TPU v7x, 128 devices: a whole 4x4x4 slice. The times are simulated.
128 devices in a mesh: dp: 8 (over z, x_hi), row: 4 (over y), col: 4 (over x_lo, core).
Axes of the slice: x: 4 (x_hi: 2, x_lo: 2; x = x_hi * 2 + x_lo), y: 4, z: 4, core: 2. Of those that a mesh axis runs over, the one named last changes fastest.
Arguments:
- tokens_in: bfloat16 [16384, 2048], P(('dp', 'row'), 'col'), may hold values from -6 to 6
- segment_ids: int32 [16384], P('dp'), may hold values from 0 to 2, as said below
- attn_gain: float32 [2048], P('col'), may hold values from 0.1 to 1.9
- w_qkv: bfloat16 [2048, 4, 640], P('col', 'row'), may hold values from -0.125 to 0.125
- w_out: bfloat16 [2048, 2048], P('row', 'col'), may hold values from -2 to 2
- mlp_gain: float32 [2048], P('col'), may hold values from 0.1 to 1.9
- w_gate: bfloat16 [2048, 5632], P('col', 'row'), may hold values from -0.125 to 0.125
- w_up: bfloat16 [2048, 5632], P('col', 'row'), may hold values from -0.125 to 0.125
- w_down: bfloat16 [5632, 2048], P('row', 'col'), may hold values from -0.078125 to 0.078125
- cotangent: bfloat16 [16384, 2048], P(('dp', 'row'), 'col'), may hold values from -6 to 6
Outputs:
- out: bfloat16 [16384, 2048], P(('dp', 'row'), 'col')
- grad_in: float32 [16384, 2048], P(('dp', 'row'), 'col')
- grad_attn_gain: float32 [2048], P('col')
- grad_qkv: float32 [2048, 4, 640], P('col', 'row')
- grad_out_proj: float32 [2048, 2048], P('row', 'col')
- grad_mlp_gain: float32 [2048], P('col')
- grad_gate_proj: float32 [2048, 5632], P('col', 'row')
- grad_up_proj: float32 [2048, 5632], P('col', 'row')
- grad_down_proj: float32 [5632, 2048], P('row', 'col')
Inputs may be any that keep to these rules, and one draw needn't show every extreme that they name: `segment_ids`: in each group of 2048 tokens the ids are 0, 1, 2 in order, each present; document 1 starts within the group's first eighth and ends within its last eighth.
All inputs are finite; a program needn't handle non-finite values.
Results may differ from a plain program's by a relative error of at most 0.024.
Values may be sent and summed in bfloat16 or wider, within the bound.
No kernel may reach another device: no remote copies, remote signals or barrier semaphores. Data moves between devices by JAX's collectives and lax.ppermute only.
A program may use at most 192 MiB of HBM per device.

v0:
```python
import math

import jax
import jax.numpy as jnp
from jax import lax
from jax.sharding import PartitionSpec as P

HD = 64


norm_eps = 1e-05
rope_base = 10000.0
key_block = 512


def col_stats(values):
    return lax.psum(values, "col")


def row_gather(values):
    return lax.all_gather(values, "row", axis=0, tiled=True)


def col_gather(values):
    return lax.all_gather(values, "col", axis=0, tiled=True)


def product_rows(left, right, contract):
    return lax.dot_general(
        left, right, (((1,), (contract,)), ((), ())), preferred_element_type=jnp.float32
    )


def col_sums(left, right, contract):
    return lax.psum_scatter(
        product_rows(left, right, contract), "col", scatter_dimension=0, tiled=True
    )


def row_sums(left, right, contract):
    return lax.psum_scatter(
        product_rows(left, right, contract).astype(jnp.bfloat16),
        "row",
        scatter_dimension=0,
        tiled=True,
    ).astype(jnp.float32)


def over_tokens(left, right):
    return lax.dot_general(
        left, right, (((0,), (0,)), ((), ())), preferred_element_type=jnp.float32
    )


def normalize(values, gain_vec):
    full_width = values.shape[1] * lax.axis_size("col")
    scale_vec = lax.rsqrt(col_stats(jnp.sum(values * values, axis=1)) / full_width + norm_eps)
    return (scale_vec, (values * scale_vec[:, None] * gain_vec).astype(jnp.bfloat16))


def norm_back(values, scale_vec, gain_vec, upstream):
    full_width = values.shape[1] * lax.axis_size("col")
    weighted = upstream * gain_vec
    inner_sum = col_stats(jnp.sum(weighted * values, axis=1))
    grad_values = (
        scale_vec[:, None] * weighted - values * (scale_vec**3 * inner_sum / full_width)[:, None]
    )
    grad_gain = jnp.sum(upstream * values * scale_vec[:, None], axis=0)
    return (grad_values, grad_gain)


def rotate(values, cosine, sine_tab):
    half_dim = values.shape[-1] // 2
    turned = jnp.concatenate([-values[..., half_dim:], values[..., :half_dim]], axis=-1)
    return values * cosine + turned * sine_tab


def unrotate(upstream, cosine, sine_tab):
    half_dim = upstream.shape[-1] // 2
    scaled_grad = upstream * sine_tab
    turned = jnp.concatenate([scaled_grad[..., half_dim:], -scaled_grad[..., :half_dim]], axis=-1)
    return upstream * cosine + turned


def on_device(
    tokens_in, segment_ids, attn_gain, w_qkv, w_out, mlp_gain, w_gate, w_up, w_down, cotangent
):
    group_len = segment_ids.shape[0]
    local_rows = group_len // lax.axis_size("col")
    local_kv = w_qkv.shape[1]
    slot_count = w_qkv.shape[2] // HD
    head_count = slot_count - 2
    width_local = tokens_in.shape[1]
    hidden_units = w_gate.shape[1]
    offset = lax.axis_index("col") * local_rows
    indices = jnp.arange(group_len, dtype=jnp.int32)
    previous = jnp.concatenate([segment_ids[:1] - 1, segment_ids[:-1]])
    positions = indices - lax.cummax(jnp.where(segment_ids != previous, indices, 0), axis=0)
    my_pos = lax.dynamic_slice_in_dim(positions, offset, local_rows, 0)
    my_seg = lax.dynamic_slice_in_dim(segment_ids, offset, local_rows, 0)
    query_place = offset + jnp.arange(local_rows, dtype=jnp.int32)
    half_dim = HD // 2
    inverse_freq = rope_base ** (-jnp.arange(half_dim, dtype=jnp.float32) * 2.0 / HD)
    angles = my_pos.astype(jnp.float32)[:, None] * inverse_freq[None, :]
    cosine = jnp.concatenate([jnp.cos(angles), jnp.cos(angles)], axis=-1)
    sine_tab = jnp.concatenate([jnp.sin(angles), jnp.sin(angles)], axis=-1)
    inputs = tokens_in.astype(jnp.float32)
    scale_one, normed_one = normalize(inputs, attn_gain)
    rows_one = row_gather(normed_one)
    flat_qkv = w_qkv.reshape(width_local, -1)
    qkv = col_sums(rows_one, flat_qkv, 0).reshape(local_rows, local_kv, slot_count, HD)
    query = rotate(qkv[:, :, :head_count], cosine[:, None, None], sine_tab[:, None, None]).astype(
        jnp.bfloat16
    )
    key_now = rotate(qkv[:, :, head_count], cosine[:, None], sine_tab[:, None]).astype(jnp.bfloat16)
    value_now = qkv[:, :, head_count + 1].astype(jnp.bfloat16)
    pairs = jnp.stack([key_now, value_now], axis=2).reshape(local_rows, -1)
    all_pairs = col_gather(pairs).reshape(group_len, local_kv, 2, HD)
    key_span = math.gcd(group_len, key_block)
    span_count = group_len // key_span
    score_scale = HD ** (-0.5)

    def block_scores(block_idx):
        key_first = block_idx * key_span
        key_vals = lax.dynamic_slice_in_dim(all_pairs, key_first, key_span, 0)
        key_seg = lax.dynamic_slice_in_dim(segment_ids, key_first, key_span, 0)
        key_place = key_first + jnp.arange(key_span, dtype=jnp.int32)
        scores = (
            jnp.einsum(
                "tgqd,kgd->tgqk", query, key_vals[:, :, 0], preferred_element_type=jnp.float32
            )
            * score_scale
        )
        allowed = (
            (my_seg[:, None] == key_seg[None, :]) & (key_place[None, :] <= query_place[:, None])
        )[:, None, None, :]
        return (key_vals, allowed, jnp.where(allowed, scores, -1e30))

    def running(carry, block_idx):
        running_top, running_sum = carry
        key_vals, allowed, scores = block_scores(block_idx)
        new_top = jnp.maximum(running_top, jnp.max(scores, axis=-1))
        block_sum = jnp.sum(jnp.where(allowed, jnp.exp(scores - new_top[..., None]), 0.0), axis=-1)
        return ((new_top, running_sum * jnp.exp(running_top - new_top) + block_sum), None)

    start_top = jnp.full((local_rows, local_kv, head_count), -1e30, jnp.float32)
    start_sum = jnp.zeros((local_rows, local_kv, head_count), jnp.float32)
    running_top, running_sum = lax.scan(running, (start_top, start_sum), jnp.arange(span_count))[0]
    log_total = running_top + jnp.log(running_sum)

    def weighted(accum, block_idx):
        key_vals, allowed, scores = block_scores(block_idx)
        probabilities = jnp.where(allowed, jnp.exp(scores - log_total[..., None]), 0.0).astype(
            jnp.bfloat16
        )
        return (
            accum
            + jnp.einsum(
                "tgqk,kgd->tgqd",
                probabilities,
                key_vals[:, :, 1],
                preferred_element_type=jnp.float32,
            ),
            None,
        )

    zero_heads = jnp.zeros((local_rows, local_kv, head_count, HD), jnp.float32)
    mixed_heads = lax.scan(weighted, zero_heads, jnp.arange(span_count))[0]
    heads_rows = col_gather(mixed_heads.reshape(local_rows, -1).astype(jnp.bfloat16))
    hidden = inputs + row_sums(heads_rows, w_out, 0)
    scale_two, normed_two = normalize(hidden, mlp_gain)
    rows_two = row_gather(normed_two)
    gate_up_w = jnp.concatenate([w_gate, w_up], axis=1)
    gate_up = col_sums(rows_two, gate_up_w, 0)
    inner_rows = col_gather(
        (jax.nn.silu(gate_up[:, :hidden_units]) * gate_up[:, hidden_units:]).astype(jnp.bfloat16)
    )
    gate_vals = gate_up[:, :hidden_units]
    up_vals = gate_up[:, hidden_units:]
    result = (hidden + row_sums(inner_rows, w_down, 0)).astype(jnp.bfloat16)
    grad_rows = row_gather(cotangent)
    grad_down = over_tokens(inner_rows, grad_rows)
    grad_inner = col_sums(grad_rows, w_down, 1)
    sigmoid_gate = jax.nn.sigmoid(gate_vals)
    grad_gate_vals = grad_inner * up_vals * sigmoid_gate * (1.0 + gate_vals * (1.0 - sigmoid_gate))
    grad_up_vals = grad_inner * gate_vals * sigmoid_gate
    pair_rows = col_gather(
        jnp.concatenate([grad_gate_vals, grad_up_vals], axis=1).astype(jnp.bfloat16)
    )
    grad_gate_up = over_tokens(rows_two, pair_rows)
    grad_part_two, gain_two = norm_back(
        hidden, scale_two, mlp_gain, row_sums(pair_rows, gate_up_w, 1)
    )
    grad_hidden = cotangent.astype(jnp.float32) + grad_part_two
    branch_rows = row_gather(grad_hidden.astype(jnp.bfloat16))
    grad_wout = over_tokens(heads_rows, branch_rows)
    grad_mixed = (
        col_sums(branch_rows, w_out, 1)
        .astype(jnp.bfloat16)
        .reshape(local_rows, local_kv, head_count, HD)
    )
    row_delta = jnp.sum(grad_mixed.astype(jnp.float32) * mixed_heads, axis=-1)

    def back_block(grad_query, block_idx):
        key_vals, allowed, scores = block_scores(block_idx)
        probabilities = jnp.where(allowed, jnp.exp(scores - log_total[..., None]), 0.0)
        grad_probs = jnp.einsum(
            "tgqd,kgd->tgqk", grad_mixed, key_vals[:, :, 1], preferred_element_type=jnp.float32
        )
        grad_scores = (probabilities * (grad_probs - row_delta[..., None])).astype(jnp.bfloat16)
        grad_query = (
            grad_query
            + jnp.einsum(
                "tgqk,kgd->tgqd", grad_scores, key_vals[:, :, 0], preferred_element_type=jnp.float32
            )
            * score_scale
        )
        grad_key = (
            jnp.einsum("tgqk,tgqd->kgd", grad_scores, query, preferred_element_type=jnp.float32)
            * score_scale
        )
        grad_value = jnp.einsum(
            "tgqk,tgqd->kgd",
            probabilities.astype(jnp.bfloat16),
            grad_mixed,
            preferred_element_type=jnp.float32,
        )
        return (grad_query, jnp.stack([grad_key, grad_value], axis=2))

    grad_query, grad_pairs = lax.scan(back_block, zero_heads, jnp.arange(span_count))
    own_pairs = (
        lax.psum_scatter(
            grad_pairs.reshape(group_len, -1).astype(jnp.bfloat16),
            "col",
            scatter_dimension=0,
            tiled=True,
        )
        .astype(jnp.float32)
        .reshape(local_rows, local_kv, 2, HD)
    )
    grad_key_rot = unrotate(own_pairs[:, :, 0], cosine[:, None], sine_tab[:, None])
    grad_query_rot = unrotate(grad_query, cosine[:, None, None], sine_tab[:, None, None])
    grad_qkv_local = jnp.concatenate(
        [grad_query_rot, grad_key_rot[:, :, None], own_pairs[:, :, 1:2]], axis=2
    )
    qkv_rows = col_gather(grad_qkv_local.astype(jnp.bfloat16).reshape(local_rows, -1))
    grad_wqkv = over_tokens(rows_one, qkv_rows).reshape(w_qkv.shape)
    grad_part_one, gain_one = norm_back(
        inputs, scale_one, attn_gain, row_sums(qkv_rows, flat_qkv, 1)
    )
    grad_in = grad_hidden + grad_part_one
    gain_one, gain_two = lax.psum((gain_one, gain_two), ("dp", "row"))
    grad_wqkv, grad_wout, grad_gate_up, grad_down = (
        lax.psum(grad_wqkv.astype(jnp.bfloat16), "dp").astype(jnp.float32),
        lax.psum(grad_wout.astype(jnp.bfloat16), "dp").astype(jnp.float32),
        lax.psum(grad_gate_up.astype(jnp.bfloat16), "dp").astype(jnp.float32),
        lax.psum(grad_down.astype(jnp.bfloat16), "dp").astype(jnp.float32),
    )
    return (
        result,
        grad_in,
        gain_one,
        grad_wqkv,
        grad_wout,
        gain_two,
        grad_gate_up[:, :hidden_units],
        grad_gate_up[:, hidden_units:],
        grad_down,
    )


def solution(mesh):
    in_specs = (
        P(("dp", "row"), "col"),
        P("dp"),
        P("col"),
        P("col", "row", None),
        P("row", "col"),
        P("col"),
        P("col", "row"),
        P("col", "row"),
        P("row", "col"),
        P(("dp", "row"), "col"),
    )
    out_specs = (
        P(("dp", "row"), "col"),
        P(("dp", "row"), "col"),
        P("col"),
        P("col", "row", None),
        P("row", "col"),
        P("col"),
        P("col", "row"),
        P("col", "row"),
        P("row", "col"),
    )
    return jax.shard_map(
        on_device, mesh=mesh, in_specs=in_specs, out_specs=out_specs, check_vma=False
    )
```

profile of v0, /device:TPU:0, one launch (start us, length us, event | category | flops | bytes accessed | tf_op | source)
XLA Modules:
  0.0 1431.0 jit_solution(5022025345648627353)
XLA Ops:
  8.6 7.0 psum.70
  17.7 33.0 %all-gather.9.cloned.1.call-done = bf16[2048,512]{1,0:T(8,128)(2,1)} async-done(((bf16[512,512]{1,0:T(8,128)(2,1)}), bf16[2048,512]{1,0:T(8,128)(2,1)}) %all-gather.9.cloned.1.call-update) | async-done | bytes 2097168 | tf_op jit(solution)/shard_map/all_gather | solution.py:21
  50.7 5.8 fusion.83
  60.5 50.1 %reduce-scatter.10.cloned.1.call-done = f32[512,640]{1,0:T(8,128)} async-done(((f32[2048,640]{1,0:T(8,128)}), f32[512,640]{1,0:T(8,128)}) %reduce-scatter.10.cloned.1.call-update) | async-done | bytes 1310736 | tf_op jit(solution)/shard_map/reduce_scatter | solution.py:35
  117.7 7.0 all_gather.28
  125.0 43.4 %while.37 = (s32[]{:T(128)}, f32[512,1,8]{0,2,1:T(8,128)S(1)}, f32[512,1,8]{0,2,1:T(8,128)S(1)}, s32[512]{0:T(512)S(1)}, s32[4]{0:T(128)S(1)}, /*index=5*/s32[20...) while((s32[]{:T(128)}, f32[512,1,8]{0,2,1:T(8,128)S(1)}, ...), condition=%wide.region_8.9_spmd.clone, body=%wide.region_5.8_spmd.clone.sunk | while | flops 286020608 | bytes 18383056 | solution.py:148
  137.5 4.7 fusion.147
  168.5 26.3 %while.38 = (s32[]{:T(128)}, f32[512,1,8,64]{0,3,2,1:T(8,128)}, s32[4]{0:T(128)S(1)}, bf16[2048,1,2,64]{0,3,2,1:T(8,128)(2,1)S(1)}, s32[512]{0:T(512)S(1)}, /*in...) while((s32[]{:T(128)}, f32[512,1,8,64]{0,3,2,1:T(8,128)}, ...), condition=%wide.region_10.11_spmd.clone, body=%wide.region_9.10_spmd.clone.sunk | while | flops 548668416 | bytes 3311840 | solution.py:168
  175.8 5.3 fusion.150
  182.6 5.3 fusion.150
  189.5 5.3 fusion.150
  197.1 30.0 %all-gather.11.cloned.1.call-done = bf16[2048,512]{0,1:T(8,128)(2,1)} async-done(((bf16[512,512]{0,1:T(8,128)(2,1)}), bf16[2048,512]{0,1:T(8,128)(2,1)}) %all-gather.11.cloned.1.call-update) | async-done | bytes 2097168 | tf_op jit(solution)/shard_map/all_gather | solution.py:25
  232.2 30.1 %reduce-scatter.12.cloned.1.call-done = bf16[512,512]{1,0:T(8,128)(2,1)} async-done(((bf16[2048,512]{1,0:T(8,128)(2,1)}), bf16[512,512]{1,0:T(8,128)(2,1)}) %reduce-scatter.12.cloned.1.call-update) | async-done | bytes 524304 | tf_op jit(solution)/shard_map/reduce_scatter | solution.py:41
  263.6 6.8 psum.71
  272.5 22.0 %all-gather.17.cloned.1.call-done = bf16[2048,512]{1,0:T(8,128)(2,1)} async-done(((bf16[512,512]{1,0:T(8,128)(2,1)}), bf16[2048,512]{1,0:T(8,128)(2,1)}) %all-gather.17.cloned.1.call-update) | async-done | bytes 2097168 | tf_op jit(solution)/shard_map/all_gather | solution.py:21
  294.5 7.9 fusion.104
  306.4 21.2 %all-gather.13.cloned.1.call-done = bf16[2048,512]{1,0:T(8,128)(2,1)} async-done(((bf16[512,512]{1,0:T(8,128)(2,1)}), bf16[2048,512]{1,0:T(8,128)(2,1)}) %all-gather.13.cloned.1.call-update) | async-done | bytes 2097168 | tf_op jit(solution)/shard_map/all_gather | solution.py:21
  327.6 13.7 fusion.103
  341.3 93.4 %reduce-scatter.18.cloned.1.call-done = f32[512,1408]{1,0:T(8,128)} async-done(((f32[2048,1408]{1,0:T(8,128)}), f32[512,1408]{1,0:T(8,128)}) %reduce-scatter.18.cloned.1.call-update) | async-done | bytes 2883600 | tf_op jit(solution)/shard_map/reduce_scatter | solution.py:35
  434.7 200.8 %reduce-scatter.14.cloned.1.call-done = f32[512,2816]{1,0:T(8,128)} async-done(((f32[2048,2816]{1,0:T(8,128)}), f32[512,2816]{1,0:T(8,128)}) %reduce-scatter.14.cloned.1.call-update) | async-done | bytes 5767184 | tf_op jit(solution)/shard_map/reduce_scatter | solution.py:35
  635.6 5.2 multiply_convert_fusion.1
  642.6 106.9 %all-gather.19.cloned.1.call-done = bf16[2048,2816]{1,0:T(8,128)(2,1)} async-done(((bf16[512,2816]{1,0:T(8,128)(2,1)}), bf16[2048,2816]{1,0:T(8,128)(2,1)}) %all-gather.19.cloned.1.call-update) | async-done | bytes 11534352 | tf_op jit(solution)/shard_map/all_gather | solution.py:25
  749.5 10.8 convolution_convert_fusion.5
  760.4 32.4 %reduce-scatter.20.cloned.1.call-done = bf16[512,512]{1,0:T(8,128)(2,1)} async-done(((bf16[2048,512]{1,0:T(8,128)(2,1)}), bf16[512,512]{1,0:T(8,128)(2,1)}) %reduce-scatter.20.cloned.1.call-update) | async-done | bytes 524304 | tf_op jit(solution)/shard_map/reduce_scatter | solution.py:41
  794.9 7.5 psum.72
  806.0 30.4 %all-gather.21.cloned.1.call-done = bf16[2048,512]{1,0:T(8,128)(2,1)} async-done(((bf16[512,512]{1,0:T(8,128)(2,1)}), bf16[2048,512]{1,0:T(8,128)(2,1)}) %all-gather.21.cloned.1.call-update) | async-done | bytes 2097168 | tf_op jit(solution)/shard_map/all_gather | solution.py:21
  836.4 4.9 fusion.105
  841.8 45.0 %reduce-scatter.22.cloned.1.call-done = f32[512,512]{1,0:T(8,128)} async-done(((f32[2048,512]{1,0:T(8,128)}), f32[512,512]{1,0:T(8,128)}) %reduce-scatter.22.cloned.1.call-update) | async-done | bytes 1048592 | tf_op jit(solution)/shard_map/reduce_scatter | solution.py:35
  893.6 91.9 %while.39 = (s32[]{:T(128)}, f32[512,1,8,64]{0,3,2,1:T(8,128)S(1)}, bf16[4,512,1,2,64]{1,4,3,2,0:T(8,128)(2,1)}, s32[4]{0:T(128)}, bf16[2048,1,2,64]{0,3,2,1:T(8...) while((s32[]{:T(128)}, f32[512,1,8,64]{0,3,2,1:T(8,128)S(1)}, ...), condition=%wide.region_23.24_spmd.clone, body=%wide.region_22.23_spmd.clone.sunk | while | flops 1369244672 | bytes 96928664 | solution.py:230
  896.6 5.3 fusion.158
  901.9 6.7 fusion.159
  919.5 5.3 fusion.158
  924.8 6.8 fusion.159
  942.5 5.3 fusion.158
  947.8 6.7 fusion.159
  965.5 5.3 fusion.158
  970.8 6.8 fusion.159
  990.3 16.5 %reduce-scatter.24.cloned.1.call-done = bf16[512,128]{0,1:T(8,128)(2,1)} async-done(((bf16[2048,128]{0,1:T(8,128)(2,1)}), bf16[512,128]{0,1:T(8,128)(2,1)}) %reduce-scatter.24.cloned.1.call-update) | async-done | bytes 131088 | tf_op jit(solution)/shard_map/reduce_scatter | solution.py:232
  1011.1 33.9 %all-gather.23.cloned.1.call-done = bf16[2048,640]{0,1:T(8,128)(2,1)} async-done(((bf16[512,640]{0,1:T(8,128)(2,1)}), bf16[2048,640]{0,1:T(8,128)(2,1)}) %all-gather.23.cloned.1.call-update) | async-done | bytes 2621456 | tf_op jit(solution)/shard_map/all_gather | solution.py:25
  1045.0 4.9 convolution_convert_fusion.3
  1050.2 56.9 %all-gather.15.cloned.1.call-done = bf16[2048,1408]{1,0:T(8,128)(2,1)} async-done(((bf16[512,1408]{1,0:T(8,128)(2,1)}), bf16[2048,1408]{1,0:T(8,128)(2,1)}) %all-gather.15.cloned.1.call-update) | async-done | bytes 5767184 | tf_op jit(solution)/shard_map/all_gather | solution.py:25
  1107.1 7.2 convolution_convert_fusion.4
  1114.4 7.7 convolution_convert_fusion.1
  1122.1 12.0 convolution_convert_fusion
  1143.4 7.5 psum.73
  1150.9 98.6 %all-reduce = (f32[512]{0:T(512)}, f32[512]{0:T(512)}) all-reduce(f32[512]{0:T(512)} %get-tuple-element.312, f32[512]{0:T(512)} %get-tuple-element.310), channel_id=1, replica_groups=mesh['dp'=8,'row'=4,'col'=4] {'dp','row'}, use_global_device_ids=true, to_apply=%region_29.30 | all-reduce | flops 1024 | bytes 8192 | tf_op jit(solution)/shard_map/psum | solution.py:252
  1253.9 160.1 %all-reduce.4.cloned.1.call-done = (bf16[512,1,640]{2,0,1:T(8,128)(2,1)}, bf16[512,2816]{1,0:T(8,128)(2,1)}, bf16[512,512]{1,0:T(8,128)(2,1)}, bf16[1408,512]{1,0:T(8,128)(2,1)}) async-done(((bf16[512,1,640]{2,0,1:T(8,128)(2,1)}, bf16[512,2816]{1,0:T(8,128)(2,1)}, bf16[512,512]{1,0:T(8,128)(2,1)}, bf16[1408,512]{1,0:T(8,128)(2,1)}), (bf16[512,1,640]{2,0,1:T(8,128)(2,1)}, bf16[512,2816]{1,0:T(8,128)(2,1)}, ...) | async-done | bytes 5505040 | tf_op jit(solution)/shard_map/psum | solution.py:254
  1414.0 4.8 fusion.101
  (293 shorter events, 156.1 us)
Async XLA Ops:
  7.2 287.3 %copy-start = (bf16[1408,512]{1,0:T(8,128)(2,1)S(1)}, bf16[1408,512]{1,0:T(8,128)(2,1)}, u32[]{:S(2)}) copy-start(bf16[1408,512]{1,0:T(8,128)(2,1)} %param.24) | copy-start | bytes 4325380
  7.2 43.5 %all-gather.9.cloned.1.call-start = ((), (), s32[]{:S(2)}) async-start(), calls=%async_computation.9 | async-start | bytes 2621440 | tf_op jit(solution)/shard_map/all_gather | solution.py:21
  15.5 41.0 %copy-start.30 = (f32[512]{0:T(512)}, f32[512]{0:T(512)S(1)}, u32[]{:S(2)}) copy-start(f32[512]{0:T(512)S(1)} %psum.70) | copy-start | bytes 6148
  15.5 41.0 %copy-start.25 = (f32[512]{0:T(512)}, f32[512]{0:T(512)S(1)}, u32[]{:S(2)}) copy-start(f32[512]{0:T(512)S(1)} %add_rsqrt_fusion.1) | copy-start | bytes 6148
  17.6 93.0 %reduce-scatter.10.cloned.1.call-start = ((), (), s32[]{:S(2)}) async-start(), calls=%async_computation.10 | async-start | bytes 6553600 | tf_op jit(solution)/shard_map/reduce_scatter | solution.py:35
  56.6 170.6 %all-gather.11.cloned.1.call-start = ((), (), s32[]{:S(2)}) async-start(), calls=%async_computation.11 | async-start | bytes 2621440 | tf_op jit(solution)/shard_map/all_gather | solution.py:25
  60.2 64.5 %copy-start.17 = (f32[512,64]{0,1:T(8,128)}, f32[512,64]{0,1:T(8,128)S(1)}, u32[]{:S(2)}) copy-start(f32[512,64]{0,1:T(8,128)S(1)} %get-tuple-element.408) | copy-start | bytes 393220
  60.2 64.5 %copy-start.18 = (f32[512,64]{0,1:T(8,128)}, f32[512,64]{0,1:T(8,128)S(1)}, u32[]{:S(2)}) copy-start(f32[512,64]{0,1:T(8,128)S(1)} %get-tuple-element.407) | copy-start | bytes 393220
  60.5 57.1 %copy-start.21 = (f32[512,1,1,32]{0,3,2,1:T(8,128)}, f32[512,1,1,32]{0,3,2,1:T(8,128)S(1)}, u32[]{:S(2)}) copy-start(f32[512,1,1,32]{0,3,2,1:T(8,128)S(1)} %multiply_cosine_fusion.1) | copy-start | bytes 196612
  113.4 11.3 copy-start.6
  168.5 58.7 %copy-start.22 = (bf16[512,512]{1,0:T(8,128)(2,1)S(1)}, bf16[512,512]{1,0:T(8,128)(2,1)}, u32[]{:S(2)}) copy-start(bf16[512,512]{1,0:T(8,128)(2,1)} %param.20) | copy-start | bytes 1572868
  194.8 32.4 %copy-start.33 = (f32[512,1,8]{0,2,1:T(8,128)}, f32[512,1,8]{0,2,1:T(8,128)S(1)}, u32[]{:S(2)}) copy-start(f32[512,1,8]{0,2,1:T(8,128)S(1)} %get-tuple-element.828) | copy-start | bytes 49156
  194.8 36.6 %copy-start.12 = (bf16[2048,1,2,64]{0,3,2,1:T(8,128)(2,1)}, bf16[2048,1,2,64]{0,3,2,1:T(8,128)(2,1)S(1)}, u32[]{:S(2)}) copy-start(bf16[2048,1,2,64]{0,3,2,1:T(8,128)(2,1)S(1)} %get-tuple-element.788) | copy-start | bytes 1572868
  197.1 65.2 %reduce-scatter.12.cloned.1.call-start = ((), (), s32[]{:S(2)}) async-start(), calls=%async_computation.12 | async-start | bytes 2621440 | tf_op jit(solution)/shard_map/reduce_scatter | solution.py:41
  231.4 30.9 %copy-start.3 = (bf16[512,512]{1,0:T(8,128)(2,1)S(1)}, bf16[512,512]{1,0:T(8,128)(2,1)}, u32[]{:S(2)}) copy-start(bf16[512,512]{1,0:T(8,128)(2,1)} %param.16) | copy-start | bytes 1572868
  231.4 39.1 %copy-start.27 = (f32[512]{0:T(512)S(1)}, f32[512]{0:T(512)}, u32[]{:S(2)}) copy-start(f32[512]{0:T(512)} %param.21) | copy-start | bytes 6148
  231.4 63.1 %all-gather.17.cloned.1.call-start = ((), (), s32[]{:S(2)}) async-start(), calls=%async_computation.17 | async-start | bytes 2621440 | tf_op jit(solution)/shard_map/all_gather | solution.py:21
  232.0 95.6 %all-gather.13.cloned.1.call-start = ((), (), s32[]{:S(2)}) async-start(), calls=%async_computation.13 | async-start | bytes 2621440 | tf_op jit(solution)/shard_map/all_gather | solution.py:21
  270.4 32.0 %copy-start.31 = (f32[512]{0:T(512)}, f32[512]{0:T(512)S(1)}, u32[]{:S(2)}) copy-start(f32[512]{0:T(512)S(1)} %psum.71) | copy-start | bytes 6148
  272.5 162.2 %reduce-scatter.18.cloned.1.call-start = ((), (), s32[]{:S(2)}) async-start(), calls=%async_computation.18 | async-start | bytes 14417920 | tf_op jit(solution)/shard_map/reduce_scatter | solution.py:35
  302.5 333.1 %reduce-scatter.14.cloned.1.call-start = ((), (), s32[]{:S(2)}) async-start(), calls=%async_computation.14 | async-start | bytes 28835840 | tf_op jit(solution)/shard_map/reduce_scatter | solution.py:35
  341.3 408.2 %all-gather.19.cloned.1.call-start = ((), (), s32[]{:S(2)}) async-start(), calls=%async_computation.19 | async-start | bytes 14417920 | tf_op jit(solution)/shard_map/all_gather | solution.py:25
  642.5 150.2 %copy-start.4 = (bf16[512,512]{1,0:T(8,128)(2,1)S(1)}, bf16[512,512]{1,0:T(8,128)(2,1)}, u32[]{:S(2)}) copy-start(bf16[512,512]{1,0:T(8,128)(2,1)} %reduce-scatter.12.cloned.1.call-done) | copy-start | bytes 1572868
  642.6 150.2 %reduce-scatter.20.cloned.1.call-start = ((), (), s32[]{:S(2)}) async-start(), calls=%async_computation.20 | async-start | bytes 2621440 | tf_op jit(solution)/shard_map/reduce_scatter | solution.py:41
  760.3 43.4 %copy-start.10 = (bf16[512,512]{1,0:T(8,128)(2,1)S(1)}, bf16[512,512]{1,0:T(8,128)(2,1)}, u32[]{:S(2)}) copy-start(bf16[512,512]{1,0:T(8,128)(2,1)} %param.25) | copy-start | bytes 1572868
  760.4 76.0 %all-gather.21.cloned.1.call-start = ((), (), s32[]{:S(2)}) async-start(), calls=%async_computation.21 | async-start | bytes 2621440 | tf_op jit(solution)/shard_map/all_gather | solution.py:21
  806.0 80.9 %reduce-scatter.22.cloned.1.call-start = ((), (), s32[]{:S(2)}) async-start(), calls=%async_computation.22 | async-start | bytes 5242880 | tf_op jit(solution)/shard_map/reduce_scatter | solution.py:35
  841.3 165.4 %reduce-scatter.24.cloned.1.call-start = ((), (), s32[]{:S(2)}) async-start(), calls=%async_computation.23 | async-start | bytes 655360 | tf_op jit(solution)/shard_map/reduce_scatter | solution.py:232
  901.9 8.2 copy-start.2
  908.6 4.1 copy-start.1
  924.8 8.2 copy-start.2
  947.8 8.2 copy-start.2
  954.6 4.1 copy-start.1
  970.8 8.2 copy-start.2
  987.9 57.2 %all-gather.23.cloned.1.call-start = ((), (), s32[]{:S(2)}) async-start(), calls=%async_computation.24 | async-start | bytes 3276800 | tf_op jit(solution)/shard_map/all_gather | solution.py:25
  990.3 54.8 %copy-start.19 = (bf16[512,1,640]{2,0,1:T(8,128)(2,1)S(1)}, bf16[512,1,640]{2,0,1:T(8,128)(2,1)}, u32[]{:S(2)}) copy-start(bf16[512,1,640]{2,0,1:T(8,128)(2,1)} %param.19) | copy-start | bytes 1966084
  1010.5 96.6 %all-gather.15.cloned.1.call-start = ((), (), s32[]{:S(2)}) async-start(), calls=%async_computation.15 | async-start | bytes 7208960 | tf_op jit(solution)/shard_map/all_gather | solution.py:25
  1011.1 130.2 %reduce-scatter.26.cloned.1.call-start = ((), (), s32[]{:S(2)}) async-start(), calls=%async_computation.25 | async-start | bytes 2621440 | tf_op jit(solution)/shard_map/reduce_scatter | solution.py:41
  1049.9 200.9 %reduce-scatter.16.cloned.1.call-start = ((), (), s32[]{:S(2)}) async-start(), calls=%async_computation.16 | async-start | bytes 2621440 | tf_op jit(solution)/shard_map/reduce_scatter | solution.py:41
  1114.3 299.7 %all-reduce.4.cloned.1.call-start = ((), (), s32[]{:S(2)}) async-start(), calls=%async_computation.26 | async-start | bytes 11010048 | tf_op jit(solution)/shard_map/psum | solution.py:254
  1114.4 7.7 copy-start.37
  1122.1 12.0 copy-start.8
  1122.1 12.0 copy-start.36
  1139.3 111.5 %copy-start.5 = (bf16[512,512]{1,0:T(8,128)(2,1)S(1)}, bf16[512,512]{1,0:T(8,128)(2,1)}, u32[]{:S(2)}) copy-start(bf16[512,512]{1,0:T(8,128)(2,1)} %reduce-scatter.12.cloned.1.call-done) | copy-start | bytes 1572868
  1139.3 111.5 %copy-start.9 = (bf16[512,512]{1,0:T(8,128)(2,1)S(1)}, bf16[512,512]{1,0:T(8,128)(2,1)}, u32[]{:S(2)}) copy-start(bf16[512,512]{1,0:T(8,128)(2,1)} %reduce-scatter.20.cloned.1.call-done) | copy-start | bytes 1572868
  1139.3 111.5 %copy-start.11 = (bf16[512,512]{1,0:T(8,128)(2,1)S(1)}, bf16[512,512]{1,0:T(8,128)(2,1)}, u32[]{:S(2)}) copy-start(bf16[512,512]{1,0:T(8,128)(2,1)} %param.25) | copy-start | bytes 1572868
  1139.4 111.5 %copy-start.28 = (f32[512]{0:T(512)S(1)}, f32[512]{0:T(512)}, u32[]{:S(2)}) copy-start(f32[512]{0:T(512)} %param.21) | copy-start | bytes 6148
  1414.0 4.8 copy-start.16
  (23 other events, 45.9 us)
Sparse Core Ops, SparseCore 0:
  17.7 32.9 all-gather.8
  56.7 53.8 reduce-scatter.9
  197.2 29.9 all-gather.10
  231.5 30.7 reduce-scatter.11
  263.9 30.5 all-gather.16
  296.7 30.8 all-gather.12
  330.2 104.4 reduce-scatter.17
  437.4 198.1 reduce-scatter.13
  642.7 106.8 all-gather.18
  760.5 32.2 reduce-scatter.19
  806.1 30.2 all-gather.20
  841.5 45.3 reduce-scatter.21
  988.0 18.7 reduce-scatter.23
  1010.6 34.3 all-gather.22
  1047.1 59.9 all-gather.14
  1109.9 31.3 reduce-scatter.25
  1144.2 29.6 reduce-scatter.15
  1177.8 236.1 all-reduce.3
where the time goes:
time: 1440 us; the launch traced here: 1430 us
  waiting for transfers between devices  966 us (67%)
  matrix products  198 us (14%)
  blocking collectives  134 us (9%)
  other arithmetic  71.2 us (5%)
  local copies, waits for them, and re-layouts  35.5 us (2%)
  between operations  15.6 us (1%)
    reduce_scatter x4, waiting for transfers between devices, col_sums(): lax.psum_scatter(product_rows(left, right, contract), 'col', scatter_dime...  389 us
    all_gather x4, waiting for transfers between devices, col_gather(): return lax.all_gather(values, 'col', axis=0, tiled=True)  228 us
    psum x1, waiting for transfers between devices, on_device(): lax.psum(grad_wqkv.astype(jnp.bfloat16), 'dp').astype(jnp.float32)  160 us
    all_gather x4, waiting for transfers between devices, row_gather(): return lax.all_gather(values, 'row', axis=0, tiled=True)  107 us
    psum x1, blocking collectives, on_device(): gain_one, gain_two = lax.psum((gain_one, gain_two), ('dp', 'row'))  98.6 us
    reduce_scatter x4, waiting for transfers between devices, row_sums(): lax.psum_scatter(product_rows(left, right, contract).astype(jnp.bfloat16)...  64.3 us
    dot_general x8, matrix products, product_rows(): lax.dot_general(left, right, (((1,), (contract,)), ((), ())), preferred_e...  59.5 us
    dot_general x8, matrix products, block_scores(): jnp.einsum('tgqd,kgd->tgqk', query, key_vals[:, :, 0], preferred_element_...  40.1 us
  transfers between devices with their start and end apart: 18, of which 17 were waited for; matrix products, arithmetic and copies ran while one was open for 5% of the time, Pallas kernels for 0%

commit v1 on v0

v1 whole, which is shorter than its diff:
```python
import functools

import jax
import jax.numpy as jnp
from jax import lax
from jax.experimental import pallas as pl
from jax.experimental.pallas import tpu as pltpu
from jax.sharding import Mesh
from jax.sharding import PartitionSpec as P

HD = 64
norm_eps = 1e-05
rope_base = 10000.0
masked = -1e30

COL = ("xl", "k")
RING = ("xh", "xl")
BF16 = jnp.bfloat16
F32 = jnp.float32


def trade(values, axes, mask, size=4):
    return lax.ppermute(values, axes, [(i, i ^ mask) for i in range(size)])


def trade_row(values, mask):
    return trade(values, "y", mask)


def trade_col(values, mask):
    return trade(values, COL, mask)


def trade_core(values):
    return trade(values, "k", 1, 2)


def trade_ring(values, mask):
    return trade(values, RING, mask)


def gather_row(values):
    return jnp.concatenate([values] + [trade_row(values, j) for j in (1, 2, 3)], axis=0)


def sum_row(partial):
    size = partial.shape[0] // 4
    own = partial[:size].astype(F32)
    for j in (2, 1, 3):
        own = own + trade_row(partial[j * size : (j + 1) * size], j).astype(F32)
    return own


def to_full_width(values, col):
    size = values.shape[0] // 4
    parts = [lax.dynamic_slice_in_dim(values, (col ^ m) * size, size, 0) for m in range(4)]
    return jnp.concatenate([parts[0]] + [trade_col(parts[m], m) for m in (1, 2, 3)], axis=1)


def to_blocks(values, core, low):
    width = values.shape[1] // 4
    parts = [values[:, :width]]
    parts += [trade_col(values[:, m * width : (m + 1) * width], m) for m in (1, 2, 3)]
    a, b, c, d = parts
    a, b = jnp.where(core == 0, a, b), jnp.where(core == 0, b, a)
    c, d = jnp.where(core == 0, c, d), jnp.where(core == 0, d, c)
    first, second = jnp.concatenate([a, b], 0), jnp.concatenate([c, d], 0)
    return jnp.concatenate(
        [jnp.where(low == 0, first, second), jnp.where(low == 0, second, first)], 0
    )


def gather_weight(shard, axis):
    half = shard.shape[0] // 2
    other = jnp.concatenate([trade_ring(shard[:half], 1), trade_ring(shard[half:], 3)], axis=0)
    return jnp.concatenate([shard, trade_core(shard), other, trade_core(other)], axis=axis)


def add_low(*terms):
    total = terms[0].astype(F32)
    for term in terms[1:]:
        total = total + term.astype(F32)
    return total.astype(BF16)


def sum_core(parts):
    return (
        add_low(parts[0], trade_core(parts[1])),
        add_low(parts[2], trade_core(parts[3])),
    )


def ring_scatter(mine, theirs, high):
    half = mine.shape[0] // 2
    take = lambda values, which: lax.dynamic_slice_in_dim(values, which * half, half, 0)
    return add_low(
        take(mine, high),
        trade_ring(take(theirs, high), 1),
        trade_ring(take(theirs, 1 - high), 3),
        trade_ring(take(mine, 1 - high), 2),
    )


def ring_gather(values, high):
    other = trade_ring(values, 2)
    return jnp.concatenate(
        [jnp.where(high == 0, values, other), jnp.where(high == 0, other, values)], axis=0
    )


def reduce_z_first(parts, high):
    mine, theirs = sum_core(parts)
    both = lax.psum_scatter(jnp.stack([mine, theirs]), "z", scatter_dimension=1, tiled=True)
    total = ring_gather(ring_scatter(both[0], both[1], high), high)
    return lax.all_gather(total, "z", axis=0, tiled=True).astype(F32)


def reduce_ring_first(parts, high):
    mine, theirs = sum_core(parts)
    part = ring_scatter(mine, theirs, high)
    total = lax.psum_scatter(part, "z", scatter_dimension=0, tiled=True)
    total = lax.all_gather(total, "z", axis=0, tiled=True)
    return ring_gather(total, high).astype(F32)


def reduce_gain(values):
    total = values
    for m in (1, 3, 2):
        total = total + trade_row(values, m)
    width = total.shape[1] // 4
    own = total[:, :width]
    for m in (1, 2, 3):
        own = own + trade_col(total[:, m * width : (m + 1) * width], m)
    whole = own
    for m in (1, 3, 2):
        whole = whole + trade(own, "z", m)
    return (whole + trade(whole, "xh", 1, 2))[0]


def product(left, right, dims, kind=F32):
    return lax.dot_general(left, right, (dims, ((), ())), preferred_element_type=F32).astype(kind)


def scale_of(values):
    return lax.rsqrt(jnp.mean(values * values, axis=1, keepdims=True) + norm_eps)


def norm_back(values, scale, gain, upstream):
    weighted = upstream * gain
    inner = jnp.mean(weighted * values, axis=1, keepdims=True)
    return scale * weighted - values * (scale**3 * inner)


def attend(place_ref, q_ref, kn_ref, vt_ref, koff_ref, qpos_ref, qstart_ref, o_ref, low_ref, lse_ref):
    row = place_ref[0]
    span = kn_ref.shape[1]
    size = span // 4
    pairs = q_ref.shape[0] // (2 * HD)

    def one_block(block, carry):
        at = pl.multiple_of(block * size, size)
        mine = block ^ row
        qpos = qpos_ref[:, pl.ds(at, size)]
        qstart = qstart_ref[:, pl.ds(at, size)]
        for pair in range(pairs):
            first = pair * 2 * HD
            query = jnp.concatenate(
                [
                    q_ref[first : first + HD, pl.ds(at, size)],
                    q_ref[first + HD : first + 2 * HD, pl.ds(at, size)],
                ],
                axis=1,
            )

            def chunk(number, state, diagonal):
                top, total, accum = state
                where = number ^ row
                scores = jnp.dot(kn_ref[where], query, preferred_element_type=F32)
                keys = koff_ref[...] + number * span
                allowed = keys >= qstart
                if diagonal:
                    allowed = allowed & (keys <= qpos)
                allowed = jnp.concatenate([allowed, allowed], axis=1)
                scores = jnp.where(allowed, scores, masked)
                new_top = jnp.maximum(top, jnp.max(scores, axis=0, keepdims=True))
                weights = jnp.exp(scores - new_top)
                shrink = jnp.exp(top - new_top)
                total = total * shrink + jnp.sum(weights, axis=0, keepdims=True)
                accum = accum * shrink + jnp.dot(
                    vt_ref[where], weights.astype(BF16), preferred_element_type=F32
                )
                return new_top, total, accum

            state = (
                jnp.full((1, 2 * size), masked, F32),
                jnp.zeros((1, 2 * size), F32),
                jnp.zeros((HD, 2 * size), F32),
            )
            state = chunk(mine, state, True)
            top, total, accum = lax.fori_loop(
                0, mine, lambda number, state: chunk(number, state, False), state
            )
            result = accum / total
            lse = top + jnp.log(total)
            for part in range(2):
                spot = first + part * HD
                piece = result[:, part * size : (part + 1) * size]
                o_ref[spot : spot + HD, pl.ds(at, size)] = piece
                low_ref[spot : spot + HD, pl.ds(at, size)] = piece.astype(BF16)
                lse_ref[pair * 2 + part : pair * 2 + part + 1, pl.ds(at, size)] = lse[
                    :, part * size : (part + 1) * size
                ]
        return carry

    lax.fori_loop(0, 4, one_block, 0)


def attend_back(
    place_ref, q_ref, kn_ref, kt_ref, vn_ref, koff_ref, qpos_ref, qstart_ref, o_ref, lse_ref, go_ref,
    gq_ref, gk_ref, gv_ref,
):
    row = place_ref[0]
    span = kn_ref.shape[1]
    size = span // 4
    pairs = q_ref.shape[0] // (2 * HD)
    gk_ref[...] = jnp.zeros_like(gk_ref)
    gv_ref[...] = jnp.zeros_like(gv_ref)
    last = (((1,), (1,)), ((), ()))

    def one_block(block, carry):
        at = pl.multiple_of(block * size, size)
        mine = block ^ row
        qpos = qpos_ref[:, pl.ds(at, size)]
        qstart = qstart_ref[:, pl.ds(at, size)]
        for pair in range(pairs):
            first = pair * 2 * HD
            both = lambda ref: jnp.concatenate(
                [
                    ref[first : first + HD, pl.ds(at, size)],
                    ref[first + HD : first + 2 * HD, pl.ds(at, size)],
                ],
                axis=1,
            )
            query, grad_out = both(q_ref), both(go_ref)
            delta = jnp.sum(grad_out.astype(F32) * both(o_ref), axis=0, keepdims=True)
            lse = jnp.concatenate(
                [
                    lse_ref[2 * pair : 2 * pair + 1, pl.ds(at, size)],
                    lse_ref[2 * pair + 1 : 2 * pair + 2, pl.ds(at, size)],
                ],
                axis=1,
            )

            def chunk(number, grad_query, diagonal):
                where = number ^ row
                scores = jnp.dot(kn_ref[where], query, preferred_element_type=F32)
                keys = koff_ref[...] + number * span
                allowed = keys >= qstart
                if diagonal:
                    allowed = allowed & (keys <= qpos)
                allowed = jnp.concatenate([allowed, allowed], axis=1)
                probs = jnp.exp(jnp.where(allowed, scores - lse, masked))
                grad_probs = jnp.dot(vn_ref[where], grad_out, preferred_element_type=F32)
                grad_scores = (probs * (grad_probs - delta)).astype(BF16)
                gv_ref[where] += lax.dot_general(
                    grad_out, probs.astype(BF16), last, preferred_element_type=F32
                )
                gk_ref[where] += lax.dot_general(
                    query, grad_scores, last, preferred_element_type=F32
                )
                return grad_query + jnp.dot(
                    kt_ref[where], grad_scores, preferred_element_type=F32
                )

            grad_query = chunk(mine, jnp.zeros((HD, 2 * size), F32), True)
            grad_query = lax.fori_loop(
                0, mine, lambda number, total: chunk(number, total, False), grad_query
            )
            for part in range(2):
                spot = first + part * HD
                gq_ref[spot : spot + HD, pl.ds(at, size)] = (
                    grad_query[:, part * size : (part + 1) * size] * HD**-0.5
                )
        return carry

    lax.fori_loop(0, 4, one_block, 0)


def kernel_call(body, out_shape, operands, flops):
    moved = sum(x.size * x.dtype.itemsize for x in operands)
    return pl.pallas_call(
        body,
        out_shape=out_shape,
        in_specs=[pl.BlockSpec(memory_space=pltpu.SMEM)]
        + [pl.BlockSpec(memory_space=pltpu.VMEM)] * (len(operands) - 1),
        out_specs=jax.tree.map(lambda _: pl.BlockSpec(memory_space=pltpu.VMEM), out_shape),
        compiler_params=pltpu.CompilerParams(vmem_limit_bytes=40 * 1024 * 1024),
        cost_estimate=pl.CostEstimate(flops=flops, bytes_accessed=moved, transcendentals=0),
    )(*operands)


def turn(pairs, cosine, sine):
    first, second = pairs[:, 0], pairs[:, 1]
    return jnp.stack([first * cosine - second * sine, second * cosine + first * sine], axis=1)


def turn_back(pairs, cosine, sine):
    first, second = pairs[:, 0], pairs[:, 1]
    return jnp.stack([first * cosine + second * sine, second * cosine - first * sine], axis=1)


def on_device(
    tokens_in, segment_ids, attn_gain, w_qkv, w_out, mlp_gain, w_gate, w_up, w_down, cotangent
):
    group = segment_ids.shape[0]
    span = group // 4
    size = span // 4
    units = w_gate.shape[1]
    slots = w_qkv.shape[2] // HD
    heads = slots - 2
    high, row = lax.axis_index("xh"), lax.axis_index("y")
    low, core = lax.axis_index("xl"), lax.axis_index("k")
    col = low * 2 + core

    gains = jnp.stack([attn_gain, mlp_gain])
    gains = jnp.concatenate([gains] + [trade_col(gains, m) for m in (1, 2, 3)], axis=1)
    inputs = to_full_width(tokens_in, col).astype(F32)
    scale_one = scale_of(inputs)
    rows_one = gather_row((inputs * scale_one * gains[0]).astype(BF16))
    full_qkv = gather_weight(w_qkv.reshape(w_qkv.shape[0], -1), 0)
    full_out = gather_weight(w_out, 1)
    full_gu = gather_weight(jnp.concatenate([w_gate, w_up], axis=1), 0)
    full_down = gather_weight(w_down, 1)
    grad_rows = gather_row(to_full_width(cotangent, col))

    indices = jnp.arange(group, dtype=jnp.int32)
    previous = jnp.concatenate([segment_ids[:1] - 1, segment_ids[:-1]])
    starts = lax.cummax(jnp.where(segment_ids != previous, indices, 0), axis=0)
    bases = [(row ^ place) * span + col * size for place in range(4)]
    my_starts = jnp.concatenate([lax.dynamic_slice_in_dim(starts, b, size, 0) for b in bases])
    lanes = jnp.arange(size, dtype=jnp.int32)
    my_index = jnp.concatenate([lanes + b for b in bases])
    half_dim = HD // 2
    inverse_freq = rope_base ** (-jnp.arange(half_dim, dtype=F32) * 2.0 / HD)
    angles = inverse_freq[:, None] * (my_index - my_starts).astype(F32)[None, :]
    cosine, sine = jnp.cos(angles), jnp.sin(angles)
    key_offset = jnp.concatenate([lanes + (col ^ m) * size for m in range(4)])
    key_offset = jnp.broadcast_to(key_offset[:, None], (span, size))
    place = jnp.stack([row, col]).astype(jnp.int32)
    qpos, qstart = my_index[None, :], my_starts[None, :]

    qkv = product(full_qkv, rows_one, ((0,), (1,)))
    turned = turn(qkv[: (heads + 1) * HD].reshape(heads + 1, 2, half_dim, span), cosine, sine)
    turned = turned.reshape(-1, span)
    query = (turned[: heads * HD] * HD**-0.5).astype(BF16)
    pairs = jnp.concatenate([turned[heads * HD :], qkv[(heads + 1) * HD :]], axis=0).astype(BF16)
    all_pairs = jnp.stack([pairs] + [trade_col(pairs, m) for m in (1, 2, 3)])
    all_pairs = all_pairs.reshape(4, 2, HD, 4, size).transpose(1, 3, 2, 0, 4)
    all_pairs = all_pairs.reshape(2, 4, HD, span)
    natural = all_pairs.swapaxes(2, 3)
    kt, vt, kn, vn = all_pairs[0], all_pairs[1], natural[0], natural[1]
    shape = lambda kind, *dims: jax.ShapeDtypeStruct(dims, kind)
    flops = 2 * 2 * heads * HD * span * group
    mixed, mixed_low, lse = kernel_call(
        attend,
        (shape(F32, heads * HD, span), shape(BF16, heads * HD, span), shape(F32, heads, span)),
        (place, query, kn, vt, key_offset, qpos, qstart),
        flops,
    )
    branch = product(mixed_low, full_out, ((0,), (0,)), BF16)
    hidden = inputs + sum_row(branch)
    scale_two = scale_of(hidden)
    rows_two = gather_row((hidden * scale_two * gains[1]).astype(BF16))
    gate_up = product(rows_two, full_gu, ((1,), (0,)))
    gate, up = gate_up[:, :units], gate_up[:, units:]
    grad_inner = product(grad_rows, full_down, ((1,), (1,)))
    sig = jax.nn.sigmoid(gate)
    inner = (gate * sig * up).astype(BF16)
    grad_gate = grad_inner * up * sig * (1.0 + gate * (1.0 - sig))
    grad_up = grad_inner * gate * sig
    grad_pair = jnp.concatenate([grad_gate, grad_up], axis=1).astype(BF16)
    part_two = product(grad_pair, full_gu, ((1,), (1,)), BF16)
    grad_n2 = sum_row(part_two)
    gain_two = jnp.sum(grad_n2 * hidden * scale_two, axis=0, keepdims=True)
    grad_hidden = grad_rows[:size].astype(F32) + norm_back(
        hidden, scale_two, gains[1], grad_n2
    )
    branch_rows = gather_row(grad_hidden.astype(BF16))
    grad_heads = product(full_out, branch_rows, ((1,), (1,)), BF16)
    gq, gk, gv = kernel_call(
        attend_back,
        (shape(F32, heads * HD, span), shape(F32, 4, HD, span), shape(F32, 4, HD, span)),
        (place, query, kn, kt, vn, key_offset, qpos, qstart, mixed, lse, grad_heads),
        flops * 5 // 2,
    )
    grad_pairs = jnp.stack([gk, gv]).astype(BF16).reshape(2, 4, HD, 4, size)
    own_pairs = grad_pairs[:, :, :, 0].astype(F32)
    for m in (1, 2, 3):
        own_pairs = own_pairs + trade_col(grad_pairs[:, :, :, m], m).astype(F32)
    own_pairs = own_pairs.transpose(0, 2, 1, 3).reshape(2, HD, span)
    grad_turned = jnp.concatenate([gq.reshape(heads, HD, span), own_pairs[:1]])
    grad_turned = turn_back(
        grad_turned.reshape(heads + 1, 2, half_dim, span), cosine, sine
    ).reshape(-1, span)
    grad_qkv = jnp.concatenate([grad_turned, own_pairs[1]], axis=0).astype(BF16)
    part_one = product(grad_qkv, full_qkv, ((0,), (1,)), BF16)
    grad_n1 = sum_row(part_one)
    gain_one = jnp.sum(grad_n1 * inputs * scale_one, axis=0, keepdims=True)
    grad_in = grad_hidden + norm_back(inputs, scale_one, gains[0], grad_n1)
    grad_in = to_blocks(grad_in, core, low)
    result = (hidden + sum_row(product(inner, full_down, ((1,), (0,)), BF16))).astype(BF16)
    result = to_blocks(result, core, low)

    width = rows_one.shape[1] // 4
    cut_d = lambda v: [v[:, m * width : (m + 1) * width] for m in range(4)]
    token_sum = lambda a, b: product(a, b, ((0,), (0,)), BF16)
    down_parts = [token_sum(inner, piece) for piece in cut_d(grad_rows)]
    gate_parts = [token_sum(piece, grad_pair[:, :units]) for piece in cut_d(rows_two)]
    up_parts = [token_sum(piece, grad_pair[:, units:]) for piece in cut_d(rows_two)]
    out_parts = [product(mixed_low, piece, ((1,), (0,)), BF16) for piece in cut_d(branch_rows)]
    qkv_parts = [product(piece, grad_qkv, ((0,), (1,)), BF16) for piece in cut_d(rows_one)]
    return (
        result,
        grad_in,
        reduce_gain(gain_one),
        reduce_z_first(qkv_parts, high).reshape(w_qkv.shape),
        reduce_ring_first(out_parts, high),
        reduce_gain(gain_two),
        reduce_z_first(gate_parts, high),
        reduce_ring_first(up_parts, high),
        reduce_z_first(down_parts, high),
    )


def solution(mesh):
    dp, rows, cols = mesh.devices.shape
    fine = Mesh(
        mesh.devices.reshape(dp // 2, 2, rows, cols // 2, 2), ("z", "xh", "y", "xl", "k")
    )
    tokens = P(("z", "xh", "y"), COL)
    in_specs = (
        tokens, P(("z", "xh")), P(COL), P(COL, "y", None), P("y", COL), P(COL),
        P(COL, "y"), P(COL, "y"), P("y", COL), tokens,
    )
    out_specs = (
        tokens, tokens, P(COL), P(COL, "y", None), P("y", COL), P(COL),
        P(COL, "y"), P(COL, "y"), P("y", COL),
    )
    return jax.shard_map(
        on_device, mesh=fine, in_specs=in_specs, out_specs=out_specs, check_vma=False
    )
```

time: 1440 us -> 625 us (0.43)
  waiting for transfers between devices: 966 us -> 206 us
  starting transfers between devices: 1.53 us -> 121 us
  matrix products: 198 us -> 84.7 us
  blocking collectives: 134 us -> 46.7 us
  Pallas kernels: 0 us -> 40.9 us
  other arithmetic: 71.2 us -> 49.9 us
    reduce_scatter x9 -> x5, waiting for transfers between devices: 470 us -> 0.04 us  [the longest x2 0.02 us: reduce_ring_first(): total = lax.psum_scatter(part, 'z', scatter_dimension=0, tiled=True)]
    all_gather x8 -> x2, waiting for transfers between devices: 334 us -> 0.01 us  [reduce_z_first(): return lax.all_gather(total, 'z', axis=0, tiled=True).astype(F32)]
    ppermute x0 -> x111, waiting for transfers between devices: none -> 206 us  [trade(): return lax.ppermute(values, axes, [(i, i ^ mask) for i in range(size)])]
    psum x1 -> x0, waiting for transfers between devices: 160 us -> none  [on_device(): lax.psum(grad_wqkv.astype(jnp.bfloat16), 'dp').astype(jnp.float32)]
    psum x5 -> x0, blocking collectives: 127 us -> none  [the longest x1 98.6 us: on_device(): gain_one, gain_two = lax.psum((gain_one, gain_two), ('dp', 'row'))]
    ppermute x0 -> x111, starting transfers between devices: none -> 121 us  [trade(): return lax.ppermute(values, axes, [(i, i ^ mask) for i in range(size)])]
    dot_general x40 -> x28, matrix products: 198 us -> 84.7 us  [product(): lax.dot_general(left, right, (dims, ((), ())), preferred_element_type=F32)]
    pallas_call x0 -> x2, Pallas kernels: none -> 40.9 us  [kernel_call(): pl.pallas_call(body, out_shape=out_shape, in_specs=[pl.BlockSpec(memory_s...]
  transfers between devices with their start and end apart: 18 -> 118, of which waited for: 17 -> 42; matrix products, arithmetic and copies ran while one was open for 5% -> 25% of each run, Pallas kernels for 0% -> 7%
where the time goes in v1:
time: 625 us; the launch traced here: 616 us
  waiting for transfers between devices  206 us (33%)
  starting transfers between devices  121 us (19%)
  matrix products  84.7 us (14%)
  other arithmetic  49.9 us (8%)
  local copies, waits for them, and re-layouts  49.5 us (8%)
  blocking collectives  46.7 us (7%)
  Pallas kernels  40.9 us (7%)
  between operations  16.9 us (3%)
    ppermute x111, waiting for transfers between devices, trade(): return lax.ppermute(values, axes, [(i, i ^ mask) for i in range(size)])  206 us
    ppermute x111, starting transfers between devices, trade(): return lax.ppermute(values, axes, [(i, i ^ mask) for i in range(size)])  121 us
    dot_general x28, matrix products, product(): lax.dot_general(left, right, (dims, ((), ())), preferred_element_type=F32)  84.7 us
    pallas_call x2, Pallas kernels, kernel_call(): pl.pallas_call(body, out_shape=out_shape, in_specs=[pl.BlockSpec(memory_s...  40.9 us
    all_gather x2, blocking collectives, reduce_ring_first(): total = lax.all_gather(total, 'z', axis=0, tiled=True)  31.3 us
    unnamed x207, local copies, waits for them, and re-layouts  21.8 us
    all_gather x1, blocking collectives, reduce_z_first(): return lax.all_gather(total, 'z', axis=0, tiled=True).astype(F32)  15.4 us
  transfers between devices with their start and end apart: 118, of which 42 were waited for; matrix products, arithmetic and copies ran while one was open for 25% of the time, Pallas kernels for 7%

profile of v1, /device:TPU:0, one launch (start us, length us, event | category | flops | bytes accessed | tf_op | source)
XLA Modules:
  0.0 615.9 jit_solution(7947978081848773258)
XLA Ops:
  22.5 3.7 fusion.102
  31.2 3.8 collective-permute-done.2
  40.5 5.8 collective-permute-done.5
  48.6 3.0 collective-permute-start.12
  54.4 3.2 collective-permute-start.11
  60.5 13.8 %collective-permute-done.12 = bf16[128,2048]{1,0:T(8,128)(2,1)S(1)} collective-permute-done((bf16[128,2048]{1,0:T(8,128)(2,1)S(1)}, bf16[128,2048]{1,0:T(8,128)(2,1)S(1)}, u32[]{:S(2)}, u32[]{:S(2)}) %collective-permute-start.12) | collective-permute-done | bytes 524320 | tf_op jit(solution)/shard_map/ppermute | solution.py:23
  74.3 5.8 collective-permute-done.10
  84.5 12.3 %collective-permute-done.15 = bf16[128,512]{1,0:T(8,128)(2,1)S(1)} collective-permute-done((bf16[128,512]{1,0:T(8,128)(2,1)S(1)}, bf16[128,512]{1,0:T(8,128)(2,1)S(1)}, u32[]{:S(2)}, u32[]{:S(2)}) %collective-permute-start.15) | collective-permute-done | bytes 131104 | tf_op jit(solution)/shard_map/ppermute | solution.py:23
  104.8 19.9 %shard_map.169 = (f32[512,512]{1,0:T(8,128)S(1)}, bf16[512,512]{1,0:T(8,128)(2,1)S(1)}, f32[8,512]{1,0:T(8,128)S(1)}) custom-call(s32[2]{0:T(128)S(1)} %pad_add_fusion.3.place_ref, bf16[512,512]{1,0:T(8,128)(2,1)S(1)} %bitcast.127, bf16[4,512,64]{2,1,0:T(8,128)(2,1)S(1)} %get-tuple-element.94.kn_ref, bf16[4,64,512]{2,1,0:T(8,128)(2,1)S(1)} %copy.52.vt_ref, ...), custom_call_target="tpu_custom_call" | custom-call | flops 2147483648 | bytes 1314824 | tf_op jit(solution)/shard_map/pallas_call | solution.py:291
  124.7 3.1 collective-permute-start.44
  131.7 9.6 %collective-permute-done.44 = bf16[128,2048]{1,0:T(8,128)(2,1)S(1)} collective-permute-done((bf16[128,2048]{1,0:T(8,128)(2,1)}, bf16[128,2048]{1,0:T(8,128)(2,1)S(1)}, u32[]{:S(2)}, u32[]{:S(2)}) %collective-permute-start.44) | collective-permute-done | bytes 524320 | tf_op jit(solution)/shard_map/ppermute | solution.py:23
  144.1 8.2 %collective-permute-done.43 = bf16[128,2048]{1,0:T(8,128)(2,1)S(1)} collective-permute-done((bf16[128,2048]{1,0:T(8,128)(2,1)}, bf16[128,2048]{1,0:T(8,128)(2,1)S(1)}, u32[]{:S(2)}, u32[]{:S(2)}) %collective-permute-start.43) | collective-permute-done | bytes 524320 | tf_op jit(solution)/shard_map/ppermute | solution.py:23
  154.3 5.1 pad_maximum_fusion.7
  159.9 3.6 pad_maximum_fusion.1
  167.1 10.1 %collective-permute-done.20 = bf16[128,2048]{1,0:T(8,128)(2,1)S(1)} collective-permute-done((bf16[128,2048]{1,0:T(8,128)(2,1)S(1)}, bf16[128,2048]{1,0:T(8,128)(2,1)S(1)}, u32[]{:S(2)}, u32[]{:S(2)}) %collective-permute-start.20) | collective-permute-done | bytes 524320 | tf_op jit(solution)/shard_map/ppermute | solution.py:23
  187.0 17.4 %collective-permute-done.25 = bf16[128,2048]{1,0:T(8,128)(2,1)} collective-permute-done((bf16[128,2048]{1,0:T(8,128)(2,1)}, bf16[128,2048]{1,0:T(8,128)(2,1)}, u32[]{:S(2)}, u32[]{:S(2)}) %collective-permute-start.25) | collective-permute-done | bytes 524320 | tf_op jit(solution)/shard_map/ppermute | solution.py:23
  206.9 4.4 constant_dynamic-update-slice_fusion.12
  216.5 3.6 constant_dynamic-update-slice_fusion.9
  220.1 11.8 %fusion.99 = f32[512,2816]{1,0:T(8,128)} fusion(bf16[2048,2816]{1,0:T(8,128)(2,1)} %constant_dynamic-update-slice_fusion.9, bf16[128,2048]{1,0:T(8,128)(2,1)} %collective-permute-done.25, bf16[128,2048]{1,0:T(8,128)(2,1)} %collective-permute-done.24, bf16[128,2048]{1,0:T(8,128)(2,1)} %collective-permute-done.23, bf16[128,2048]{1,0:T(8,128)(2,1)} %multiply_convert_fusion.3), kind=kOutput, calls=%fused_computation.293 | convolution fusion | flops 5913968640 | bytes 19398656 | tf_op jit(solution)/shard_map/dot_general | solution.py:141
  232.0 10.6 %multiply_convert_fusion.1 = (bf16[512,1408]{1,0:T(8,128)(2,1)}, bf16[512,1408]{1,0:T(8,128)(2,1)}, bf16[512,1408]{1,0:T(8,128)(2,1)}) fusion(f32[512,2816]{1,0:T(8,128)} %fusion.99, bf16[1408,512]{1,0:T(8,128)(2,1)} %collective-permute-done.33, bf16[1408,512]{1,0:T(8,128)(2,1)} %copy-done.80, bf16[1408,512]{1,0:T(8,128)(2,1)} %collective-permute-done.30, ...), kind=kOutput, calls=%fused_computation.42 | convolution fusion | flops 3002073088 | bytes 17956864 | tf_op jit(solution)/shard_map/dot_general | solution.py:141
  242.6 10.0 %convolution_convert_fusion.12 = bf16[512,2048]{1,0:T(8,128)(2,1)S(1)} fusion(bf16[2048,2816]{1,0:T(8,128)(2,1)} %constant_dynamic-update-slice_fusion.9, bf16[512,1408]{1,0:T(8,128)(2,1)} %get-tuple-element.57, bf16[512,1408]{1,0:T(8,128)(2,1)} %get-tuple-element.56), kind=kOutput, calls=%fused_computation.31 | convolution fusion | flops 5912395776 | bytes 16515072 | tf_op jit(solution)/shard_map/dot_general | solution.py:141
  257.5 5.2 convolution_convert_fusion.15
  270.4 9.9 %collective-permute-done.46 = bf16[128,2048]{1,0:T(8,128)(2,1)S(1)} collective-permute-done((bf16[128,2048]{1,0:T(8,128)(2,1)S(1)}, bf16[128,2048]{1,0:T(8,128)(2,1)S(1)}, u32[]{:S(2)}, u32[]{:S(2)}) %collective-permute-start.46) | collective-permute-done | bytes 524320 | tf_op jit(solution)/shard_map/ppermute | solution.py:23
  295.6 3.7 convolution_convert_fusion
  302.9 4.0 collective-permute-start.91
  307.9 4.6 collective-permute-done.34
  312.5 3.7 fusion.101
  325.7 3.1 convolution_convert_fusion.2
  332.6 6.7 %collective-permute-done.51 = bf16[128,2048]{1,0:T(8,128)(2,1)S(1)} collective-permute-done((bf16[128,2048]{1,0:T(8,128)(2,1)S(1)}, bf16[128,2048]{1,0:T(8,128)(2,1)S(1)}, u32[]{:S(2)}, u32[]{:S(2)}) %collective-permute-start.51) | collective-permute-done | bytes 524320 | tf_op jit(solution)/shard_map/ppermute | solution.py:23
  346.2 21.0 %shard_map.170 = (f32[512,512]{1,0:T(8,128)S(1)}, f32[4,64,512]{2,1,0:T(8,128)S(1)}, f32[4,64,512]{2,1,0:T(8,128)S(1)}) custom-call(s32[2]{0:T(128)S(1)} %pad_add_fusion.3.place_ref, bf16[512,512]{1,0:T(8,128)(2,1)S(1)} %bitcast.128, bf16[4,512,64]{2,1,0:T(8,128)(2,1)S(1)} %get-tuple-element.94.kn_ref, bf16[4,64,512]{2,1,0:T(8,128)(2,1)S(1)} %copy.53.kt_ref, ...), custom_call_target="tpu_custom_call" | custom-call | flops 5368709120 | bytes 3166216 | tf_op jit(solution)/shard_map/pallas_call | solution.py:291
  380.6 4.7 collective-permute-done.80
  416.7 3.7 collective-permute-done.57
  422.3 10.3 %collective-permute-done.55 = bf16[128,2048]{1,0:T(8,128)(2,1)S(1)} collective-permute-done((bf16[128,2048]{1,0:T(8,128)(2,1)S(1)}, bf16[128,2048]{1,0:T(8,128)(2,1)S(1)}, u32[]{:S(2)}, u32[]{:S(2)}) %collective-permute-start.55) | collective-permute-done | bytes 524320 | tf_op jit(solution)/shard_map/ppermute | solution.py:23
  442.8 9.9 %collective-permute-done.66 = f32[1,512]{1,0:T(1,128)S(1)} collective-permute-done((f32[1,512]{1,0:T(1,128)S(1)}, f32[1,512]{1,0:T(1,128)S(1)}, u32[]{:S(2)}, u32[]{:S(2)}) %collective-permute-start.66) | collective-permute-done | bytes 2080 | tf_op jit(solution)/shard_map/ppermute | solution.py:23
  457.0 4.1 collective-permute-start.69
  494.5 4.4 collective-permute-done.60
  499.0 13.9 %all_gather.16 = bf16[256,512]{1,0:T(8,128)(2,1)S(1)} all-gather(bf16[64,512]{1,0:T(8,128)(2,1)} %reduce-scatter.8.cloned.1.call-done), channel_id=1, replica_groups=mesh['z'=4,'xh'=2,'y'=4,'xl'=2,'k'=2] {'z'}, dimensions={0}, use_global_device_ids=true | all-gather | bytes 327680 | tf_op jit(solution)/shard_map/all_gather | solution.py:122
  516.5 5.5 collective-permute-done.82
  524.4 3.1 collective-permute-start.109
  528.9 17.3 %all_gather.18 = bf16[256,1408]{1,0:T(8,128)(2,1)S(1)} all-gather(bf16[64,1408]{1,0:T(8,128)(2,1)} %reduce-scatter.12.cloned.1.call-done), channel_id=1, replica_groups=mesh['z'=4,'xh'=2,'y'=4,'xl'=2,'k'=2] {'z'}, dimensions={0}, use_global_device_ids=true | all-gather | bytes 901120 | tf_op jit(solution)/shard_map/all_gather | solution.py:122
  546.2 3.5 collective-permute-start.104
  551.0 16.5 %collective-permute-done.110 = bf16[176,512]{1,0:T(8,128)(2,1)S(1)} collective-permute-done((bf16[176,512]{1,0:T(8,128)(2,1)S(1)}, bf16[176,512]{1,0:T(8,128)(2,1)S(1)}, u32[]{:S(2)}, u32[]{:S(2)}) %collective-permute-start.110) | collective-permute-done | bytes 180256 | tf_op jit(solution)/shard_map/ppermute | solution.py:23
  568.3 3.3 collective-permute-start.75
  574.9 3.4 collective-permute-done.74
  581.1 3.2 collective-permute-done.76
  584.4 15.4 %all_gather.15 = bf16[512,640]{1,0:T(8,128)(2,1)S(1)} all-gather(bf16[128,640]{1,0:T(8,128)(2,1)S(1)} %pad_maximum_fusion.29), channel_id=1, replica_groups=mesh['z'=4,'xh'=2,'y'=4,'xl'=2,'k'=2] {'z'}, dimensions={0}, use_global_device_ids=true | all-gather | bytes 819200 | tf_op jit(solution)/shard_map/all_gather | solution.py:115
  602.3 3.1 convert_element_type.459
  605.5 3.3 convert_element_type.492
  (582 shorter events, 239.5 us)
Async XLA Ops:
  7.2 469.4 %reduce-scatter.10.cloned.1.call-start = ((), (), s32[]{:S(2)}) async-start(), calls=%async_computation.7 | async-start | bytes 3604480 | tf_op jit(solution)/shard_map/reduce_scatter | solution.py:113
  9.8 21.3 %collective-permute-start.7 = (f32[2,512]{1,0:T(2,128)S(1)}, f32[2,512]{1,0:T(2,128)S(1)}, u32[]{:S(2)}, u32[]{:S(2)}) collective-permute-start(f32[2,512]{1,0:T(2,128)S(1)} %pad_maximum_fusion.34), channel_id=1, source_target_pairs={{0,1},{1,0},{2,3},{3,2},{4,5},{5,4},{6,7},{7,6},{8,9},{9,8},{10,11... | collective-permute-start | bytes 12296 | tf_op jit(solution)/shard_map/ppermute | solution.py:23
  10.0 49.8 %collective-permute-start.3 = (bf16[512,640]{1,0:T(8,128)(2,1)}, bf16[512,640]{1,0:T(8,128)(2,1)S(1)}, u32[]{:S(2)}, u32[]{:S(2)}) collective-permute-start(bf16[512,640]{1,0:T(8,128)(2,1)} %bitcast.135), channel_id=1, source_target_pairs={{0,1},{1,0},{2,3},{3,2},{4,5},{5,4},{6,7},{7,6},{8,9},{9,8},{10,11... | collective-permute-start | bytes 1966088 | tf_op jit(solution)/shard_map/ppermute | solution.py:23
  11.4 28.3 %collective-permute-start.4 = (bf16[256,640]{1,0:T(8,128)(2,1)S(1)}, bf16[256,640]{1,0:T(8,128)(2,1)S(1)}, u32[]{:S(2)}, u32[]{:S(2)}) collective-permute-start(bf16[256,640]{1,0:T(8,128)(2,1)S(1)} %get-tuple-element.107), channel_id=1, source_target_pairs={{0,2},{2,0},{16,18},{18,16},{1,3},{3,1},{17,19},{19,17},{4,6},{6,4... | collective-permute-start | bytes 983048 | tf_op jit(solution)/shard_map/ppermute | solution.py:23
  48.6 25.7 %collective-permute-start.12 = (bf16[128,2048]{1,0:T(8,128)(2,1)S(1)}, bf16[128,2048]{1,0:T(8,128)(2,1)S(1)}, u32[]{:S(2)}, u32[]{:S(2)}) collective-permute-start(bf16[128,2048]{1,0:T(8,128)(2,1)S(1)} %fusion.44), channel_id=1, source_target_pairs={{0,12},{4,8},{8,4},{12,0},{1,13},{5,9},{9,5},{13,1},{2,14},{6,10},... | collective-permute-start | bytes 1572872 | tf_op jit(solution)/shard_map/ppermute | solution.py:23
  58.3 21.8 %collective-permute-start.10 = (bf16[128,2048]{1,0:T(8,128)(2,1)S(1)}, bf16[128,2048]{1,0:T(8,128)(2,1)S(1)}, u32[]{:S(2)}, u32[]{:S(2)}) collective-permute-start(bf16[128,2048]{1,0:T(8,128)(2,1)S(1)} %fusion.44), channel_id=1, source_target_pairs={{0,4},{4,0},{8,12},{12,8},{1,5},{5,1},{9,13},{13,9},{2,6},{6,2},{1... | collective-permute-start | bytes 1572872 | tf_op jit(solution)/shard_map/ppermute | solution.py:23
  59.8 64.9 %collective-permute-start.16 = (bf16[512,512]{1,0:T(8,128)(2,1)}, bf16[512,512]{1,0:T(8,128)(2,1)}, u32[]{:S(2)}, u32[]{:S(2)}) collective-permute-start(bf16[512,512]{1,0:T(8,128)(2,1)} %param.14), channel_id=1, source_target_pairs={{0,1},{1,0},{2,3},{3,2},{4,5},{5,4},{6,7},{7,6},{8,9},{9,8},{10,11... | collective-permute-start | bytes 1572872 | tf_op jit(solution)/shard_map/ppermute | solution.py:23
  60.1 93.6 %collective-permute-start.27 = (bf16[256,2816]{1,0:T(8,128)(2,1)}, bf16[256,2816]{1,0:T(8,128)(2,1)}, u32[]{:S(2)}, u32[]{:S(2)}) collective-permute-start(bf16[256,2816]{1,0:T(8,128)(2,1)} %get-tuple-element.60), channel_id=1, source_target_pairs={{0,2},{2,0},{16,18},{18,16},{1,3},{3,1},{17,19},{19,17},{4,6},{6,4... | collective-permute-start | bytes 4325384 | tf_op jit(solution)/shard_map/ppermute | solution.py:23
  96.7 62.7 %collective-permute-start.28 = (bf16[256,2816]{1,0:T(8,128)(2,1)}, bf16[256,2816]{1,0:T(8,128)(2,1)}, u32[]{:S(2)}, u32[]{:S(2)}) collective-permute-start(bf16[256,2816]{1,0:T(8,128)(2,1)} %get-tuple-element.59), channel_id=1, source_target_pairs={{0,18},{2,16},{16,2},{18,0},{1,19},{3,17},{17,3},{19,1},{4,22},{6,... | collective-permute-start | bytes 4325384 | tf_op jit(solution)/shard_map/ppermute | solution.py:23
  100.0 31.5 %collective-permute-start.45 = (bf16[128,2048]{1,0:T(8,128)(2,1)}, bf16[128,2048]{1,0:T(8,128)(2,1)}, u32[]{:S(2)}, u32[]{:S(2)}) collective-permute-start(bf16[128,2048]{1,0:T(8,128)(2,1)} %pad_maximum_fusion.20), channel_id=1, source_target_pairs={{0,12},{4,8},{8,4},{12,0},{1,13},{5,9},{9,5},{13,1},{2,14},{6,10},... | collective-permute-start | bytes 1572872 | tf_op jit(solution)/shard_map/ppermute | solution.py:23
  101.2 26.6 %collective-permute-start.19 = (bf16[512,512]{1,0:T(8,128)(2,1)}, bf16[512,512]{1,0:T(8,128)(2,1)}, u32[]{:S(2)}, u32[]{:S(2)}) collective-permute-start(bf16[512,512]{1,0:T(8,128)(2,1)} %constant_dynamic-update-slice_fusion.5), channel_id=1, source_target_pairs={{0,1},{1,0},{2,3},{3,2},{4,5},{5,4},{6,7},{7,6},{8,9},{9,8},{10,11... | collective-permute-start | bytes 1572872 | tf_op jit(solution)/shard_map/ppermute | solution.py:23
  127.9 24.4 %collective-permute-start.43 = (bf16[128,2048]{1,0:T(8,128)(2,1)}, bf16[128,2048]{1,0:T(8,128)(2,1)S(1)}, u32[]{:S(2)}, u32[]{:S(2)}) collective-permute-start(bf16[128,2048]{1,0:T(8,128)(2,1)} %pad_maximum_fusion.20), channel_id=1, source_target_pairs={{0,4},{4,0},{8,12},{12,8},{1,5},{5,1},{9,13},{13,9},{2,6},{6,2},{1... | collective-permute-start | bytes 1572872 | tf_op jit(solution)/shard_map/ppermute | solution.py:23
  131.4 75.5 %collective-permute-start.26 = (bf16[512,2816]{1,0:T(8,128)(2,1)}, bf16[512,2816]{1,0:T(8,128)(2,1)}, u32[]{:S(2)}, u32[]{:S(2)}) collective-permute-start(bf16[512,2816]{1,0:T(8,128)(2,1)} %get-tuple-element.79), channel_id=1, source_target_pairs={{0,1},{1,0},{2,3},{3,2},{4,5},{5,4},{6,7},{7,6},{8,9},{9,8},{10,11... | collective-permute-start | bytes 8650760 | tf_op jit(solution)/shard_map/ppermute | solution.py:23
  141.3 22.2 %collective-permute-start.22 = (bf16[128,2048]{1,0:T(8,128)(2,1)S(1)}, bf16[128,2048]{1,0:T(8,128)(2,1)S(1)}, u32[]{:S(2)}, u32[]{:S(2)}) collective-permute-start(bf16[128,2048]{1,0:T(8,128)(2,1)S(1)} %get-tuple-element.71), channel_id=1, source_target_pairs={{0,12},{4,8},{8,4},{12,0},{1,13},{5,9},{9,5},{13,1},{2,14},{6,10},... | collective-permute-start | bytes 1572872 | tf_op jit(solution)/shard_map/ppermute | solution.py:23
  153.6 23.6 %collective-permute-start.20 = (bf16[128,2048]{1,0:T(8,128)(2,1)S(1)}, bf16[128,2048]{1,0:T(8,128)(2,1)S(1)}, u32[]{:S(2)}, u32[]{:S(2)}) collective-permute-start(bf16[128,2048]{1,0:T(8,128)(2,1)S(1)} %get-tuple-element.70), channel_id=1, source_target_pairs={{0,8},{4,12},{8,0},{12,4},{1,9},{5,13},{9,1},{13,5},{2,10},{6,14},... | collective-permute-start | bytes 1572872 | tf_op jit(solution)/shard_map/ppermute | solution.py:23
  159.5 21.8 %collective-permute-start.31 = (bf16[704,512]{1,0:T(8,128)(2,1)S(1)}, bf16[704,512]{1,0:T(8,128)(2,1)S(1)}, u32[]{:S(2)}, u32[]{:S(2)}) collective-permute-start(bf16[704,512]{1,0:T(8,128)(2,1)S(1)} %copy-done.60), channel_id=1, source_target_pairs={{0,2},{2,0},{16,18},{18,16},{1,3},{3,1},{17,19},{19,17},{4,6},{6,4... | collective-permute-start | bytes 2162696 | tf_op jit(solution)/shard_map/ppermute | solution.py:23
  167.1 49.3 %collective-permute-start.29 = (bf16[512,2816]{1,0:T(8,128)(2,1)}, bf16[512,2816]{1,0:T(8,128)(2,1)}, u32[]{:S(2)}, u32[]{:S(2)}) collective-permute-start(bf16[512,2816]{1,0:T(8,128)(2,1)} %pad_maximum_fusion.1), channel_id=1, source_target_pairs={{0,1},{1,0},{2,3},{3,2},{4,5},{5,4},{6,7},{7,6},{8,9},{9,8},{10,11... | collective-permute-start | bytes 8650760 | tf_op jit(solution)/shard_map/ppermute | solution.py:23
  178.7 25.8 %collective-permute-start.25 = (bf16[128,2048]{1,0:T(8,128)(2,1)}, bf16[128,2048]{1,0:T(8,128)(2,1)}, u32[]{:S(2)}, u32[]{:S(2)}) collective-permute-start(bf16[128,2048]{1,0:T(8,128)(2,1)} %multiply_convert_fusion.3), channel_id=1, source_target_pairs={{0,12},{4,8},{8,4},{12,0},{1,13},{5,9},{9,5},{13,1},{2,14},{6,10},... | collective-permute-start | bytes 1572872 | tf_op jit(solution)/shard_map/ppermute | solution.py:23
  181.3 23.2 %collective-permute-start.24 = (bf16[128,2048]{1,0:T(8,128)(2,1)}, bf16[128,2048]{1,0:T(8,128)(2,1)}, u32[]{:S(2)}, u32[]{:S(2)}) collective-permute-start(bf16[128,2048]{1,0:T(8,128)(2,1)} %multiply_convert_fusion.3), channel_id=1, source_target_pairs={{0,8},{4,12},{8,0},{12,4},{1,9},{5,13},{9,1},{13,5},{2,10},{6,14},... | collective-permute-start | bytes 1572872 | tf_op jit(solution)/shard_map/ppermute | solution.py:23
  182.0 23.1 %collective-permute-start.23 = (bf16[128,2048]{1,0:T(8,128)(2,1)}, bf16[128,2048]{1,0:T(8,128)(2,1)}, u32[]{:S(2)}, u32[]{:S(2)}) collective-permute-start(bf16[128,2048]{1,0:T(8,128)(2,1)} %multiply_convert_fusion.3), channel_id=1, source_target_pairs={{0,4},{4,0},{8,12},{12,8},{1,5},{5,1},{9,13},{13,9},{2,6},{6,2},{1... | collective-permute-start | bytes 1572872 | tf_op jit(solution)/shard_map/ppermute | solution.py:23
  204.5 27.4 %collective-permute-start.30 = (bf16[1408,512]{1,0:T(8,128)(2,1)}, bf16[1408,512]{1,0:T(8,128)(2,1)}, u32[]{:S(2)}, u32[]{:S(2)}) collective-permute-start(bf16[1408,512]{1,0:T(8,128)(2,1)} %param.18), channel_id=1, source_target_pairs={{0,1},{1,0},{2,3},{3,2},{4,5},{5,4},{6,7},{7,6},{8,9},{9,8},{10,11... | collective-permute-start | bytes 4325384 | tf_op jit(solution)/shard_map/ppermute | solution.py:23
  204.5 27.4 %collective-permute-start.33 = (bf16[1408,512]{1,0:T(8,128)(2,1)}, bf16[1408,512]{1,0:T(8,128)(2,1)}, u32[]{:S(2)}, u32[]{:S(2)}) collective-permute-start(bf16[1408,512]{1,0:T(8,128)(2,1)} %copy-done.80), channel_id=1, source_target_pairs={{0,1},{1,0},{2,3},{3,2},{4,5},{5,4},{6,7},{7,6},{8,9},{9,8},{10,11... | collective-permute-start | bytes 4325384 | tf_op jit(solution)/shard_map/ppermute | solution.py:23
  255.1 25.2 %collective-permute-start.46 = (bf16[128,2048]{1,0:T(8,128)(2,1)S(1)}, bf16[128,2048]{1,0:T(8,128)(2,1)S(1)}, u32[]{:S(2)}, u32[]{:S(2)}) collective-permute-start(bf16[128,2048]{1,0:T(8,128)(2,1)S(1)} %get-tuple-element.64), channel_id=1, source_target_pairs={{0,8},{4,12},{8,0},{12,4},{1,9},{5,13},{9,1},{13,5},{2,10},{6,14},... | collective-permute-start | bytes 1572872 | tf_op jit(solution)/shard_map/ppermute | solution.py:23
  266.2 25.2 %collective-permute-start.94 = (bf16[512,1408]{1,0:T(8,128)(2,1)S(1)}, bf16[512,1408]{1,0:T(8,128)(2,1)S(1)}, u32[]{:S(2)}, u32[]{:S(2)}) collective-permute-start(bf16[512,1408]{1,0:T(8,128)(2,1)S(1)} %convolution_convert_fusion.8), channel_id=1, source_target_pairs={{0,1},{1,0},{2,3},{3,2},{4,5},{5,4},{6,7},{7,6},{8,9},{9,8},{10,11... | collective-permute-start | bytes 4325384 | tf_op jit(solution)/shard_map/ppermute | solution.py:23
  267.6 24.9 %collective-permute-start.93 = (bf16[512,1408]{1,0:T(8,128)(2,1)S(1)}, bf16[512,1408]{1,0:T(8,128)(2,1)S(1)}, u32[]{:S(2)}, u32[]{:S(2)}) collective-permute-start(bf16[512,1408]{1,0:T(8,128)(2,1)S(1)} %convolution_convert_fusion.10), channel_id=1, source_target_pairs={{0,1},{1,0},{2,3},{3,2},{4,5},{5,4},{6,7},{7,6},{8,9},{9,8},{10,11... | collective-permute-start | bytes 4325384 | tf_op jit(solution)/shard_map/ppermute | solution.py:23
  289.2 23.3 %collective-permute-start.34 = (bf16[128,2048]{1,0:T(8,128)(2,1)}, bf16[128,2048]{1,0:T(8,128)(2,1)}, u32[]{:S(2)}, u32[]{:S(2)}) collective-permute-start(bf16[128,2048]{1,0:T(8,128)(2,1)} %get-tuple-element.67), channel_id=1, source_target_pairs={{0,8},{4,12},{8,0},{12,4},{1,9},{5,13},{9,1},{13,5},{2,10},{6,14},... | collective-permute-start | bytes 1572872 | tf_op jit(solution)/shard_map/ppermute | solution.py:23
  295.4 203.6 %reduce-scatter.8.cloned.1.call-start = ((), (), s32[]{:S(2)}) async-start(), calls=%async_computation.6 | async-start | bytes 327680 | tf_op jit(solution)/shard_map/reduce_scatter | solution.py:121
  316.3 23.0 %collective-permute-start.51 = (bf16[128,2048]{1,0:T(8,128)(2,1)S(1)}, bf16[128,2048]{1,0:T(8,128)(2,1)S(1)}, u32[]{:S(2)}, u32[]{:S(2)}) collective-permute-start(bf16[128,2048]{1,0:T(8,128)(2,1)S(1)} %get-tuple-element.52), channel_id=1, source_target_pairs={{0,12},{4,8},{8,4},{12,0},{1,13},{5,9},{9,5},{13,1},{2,14},{6,10},... | collective-permute-start | bytes 1572872 | tf_op jit(solution)/shard_map/ppermute | solution.py:23
  318.4 21.5 %collective-permute-start.49 = (bf16[128,2048]{1,0:T(8,128)(2,1)S(1)}, bf16[128,2048]{1,0:T(8,128)(2,1)S(1)}, u32[]{:S(2)}, u32[]{:S(2)}) collective-permute-start(bf16[128,2048]{1,0:T(8,128)(2,1)S(1)} %get-tuple-element.52), channel_id=1, source_target_pairs={{0,4},{4,0},{8,12},{12,8},{1,5},{5,1},{9,13},{13,9},{2,6},{6,2},{1... | collective-permute-start | bytes 1572872 | tf_op jit(solution)/shard_map/ppermute | solution.py:23
  329.3 80.6 %collective-permute-start.99 = (bf16[512,1408]{1,0:T(8,128)(2,1)}, bf16[512,1408]{1,0:T(8,128)(2,1)}, u32[]{:S(2)}, u32[]{:S(2)}) collective-permute-start(bf16[512,1408]{1,0:T(8,128)(2,1)} %convolution_convert_fusion.6), channel_id=1, source_target_pairs={{0,1},{1,0},{2,3},{3,2},{4,5},{5,4},{6,7},{7,6},{8,9},{9,8},{10,11... | collective-permute-start | bytes 4325384 | tf_op jit(solution)/shard_map/ppermute | solution.py:23
  331.5 43.1 %collective-permute-start.106 = (bf16[1408,512]{1,0:T(8,128)(2,1)}, bf16[1408,512]{1,0:T(8,128)(2,1)}, u32[]{:S(2)}, u32[]{:S(2)}) collective-permute-start(bf16[1408,512]{1,0:T(8,128)(2,1)} %convolution_convert_fusion), channel_id=1, source_target_pairs={{0,1},{1,0},{2,3},{3,2},{4,5},{5,4},{6,7},{7,6},{8,9},{9,8},{10,11... | collective-permute-start | bytes 4325384 | tf_op jit(solution)/shard_map/ppermute | solution.py:23
  339.3 47.0 %collective-permute-start.105 = (bf16[1408,512]{1,0:T(8,128)(2,1)}, bf16[1408,512]{1,0:T(8,128)(2,1)}, u32[]{:S(2)}, u32[]{:S(2)}) collective-permute-start(bf16[1408,512]{1,0:T(8,128)(2,1)} %convolution_convert_fusion.2), channel_id=1, source_target_pairs={{0,1},{1,0},{2,3},{3,2},{4,5},{5,4},{6,7},{7,6},{8,9},{9,8},{10,11... | collective-permute-start | bytes 4325384 | tf_op jit(solution)/shard_map/ppermute | solution.py:23
  341.6 26.4 %collective-permute-start.77 = (bf16[512,512]{1,0:T(8,128)(2,1)}, bf16[512,512]{1,0:T(8,128)(2,1)}, u32[]{:S(2)}, u32[]{:S(2)}) collective-permute-start(bf16[512,512]{1,0:T(8,128)(2,1)} %convolution_convert_fusion.22), channel_id=1, source_target_pairs={{0,1},{1,0},{2,3},{3,2},{4,5},{5,4},{6,7},{7,6},{8,9},{9,8},{10,11... | collective-permute-start | bytes 1572872 | tf_op jit(solution)/shard_map/ppermute | solution.py:23
  342.8 28.9 %collective-permute-start.78 = (bf16[512,512]{1,0:T(8,128)(2,1)}, bf16[512,512]{1,0:T(8,128)(2,1)}, u32[]{:S(2)}, u32[]{:S(2)}) collective-permute-start(bf16[512,512]{1,0:T(8,128)(2,1)} %convolution_convert_fusion.20), channel_id=1, source_target_pairs={{0,1},{1,0},{2,3},{3,2},{4,5},{5,4},{6,7},{7,6},{8,9},{9,8},{10,11... | collective-permute-start | bytes 1572872 | tf_op jit(solution)/shard_map/ppermute | solution.py:23
  380.6 33.6 %collective-permute-start.100 = (bf16[512,1408]{1,0:T(8,128)(2,1)}, bf16[512,1408]{1,0:T(8,128)(2,1)}, u32[]{:S(2)}, u32[]{:S(2)}) collective-permute-start(bf16[512,1408]{1,0:T(8,128)(2,1)} %convolution_convert_fusion.4), channel_id=1, source_target_pairs={{0,1},{1,0},{2,3},{3,2},{4,5},{5,4},{6,7},{7,6},{8,9},{9,8},{10,11... | collective-permute-start | bytes 4325384 | tf_op jit(solution)/shard_map/ppermute | solution.py:23
  386.3 136.9 %reduce-scatter.14.cloned.1.call-start = ((), (), s32[]{:S(2)}) async-start(), calls=%async_computation.10 | async-start | bytes 3604480 | tf_op jit(solution)/shard_map/reduce_scatter | solution.py:113
  391.1 137.7 %reduce-scatter.12.cloned.1.call-start = ((), (), s32[]{:S(2)}) async-start(), calls=%async_computation.9 | async-start | bytes 901120 | tf_op jit(solution)/shard_map/reduce_scatter | solution.py:121
  407.4 25.1 %collective-permute-start.55 = (bf16[128,2048]{1,0:T(8,128)(2,1)S(1)}, bf16[128,2048]{1,0:T(8,128)(2,1)S(1)}, u32[]{:S(2)}, u32[]{:S(2)}) collective-permute-start(bf16[128,2048]{1,0:T(8,128)(2,1)S(1)} %get-tuple-element.61), channel_id=1, source_target_pairs={{0,8},{4,12},{8,0},{12,4},{1,9},{5,13},{9,1},{13,5},{2,10},{6,14},... | collective-permute-start | bytes 1572872 | tf_op jit(solution)/shard_map/ppermute | solution.py:23
  412.4 44.6 %collective-permute-start.103 = (bf16[256,1408]{1,0:T(8,128)(2,1)S(1)}, bf16[256,1408]{1,0:T(8,128)(2,1)S(1)}, u32[]{:S(2)}, u32[]{:S(2)}) collective-permute-start(bf16[256,1408]{1,0:T(8,128)(2,1)S(1)} %constant_dynamic-slice_fusion), channel_id=1, source_target_pairs={{0,16},{2,18},{16,0},{18,2},{1,17},{3,19},{17,1},{19,3},{4,20},{6,... | collective-permute-start | bytes 2162696 | tf_op jit(solution)/shard_map/ppermute | solution.py:23
  437.0 24.1 %collective-permute-start.102 = (bf16[256,1408]{1,0:T(8,128)(2,1)S(1)}, bf16[256,1408]{1,0:T(8,128)(2,1)S(1)}, u32[]{:S(2)}, u32[]{:S(2)}) collective-permute-start(bf16[256,1408]{1,0:T(8,128)(2,1)S(1)} %get-tuple-element.76), channel_id=1, source_target_pairs={{0,18},{2,16},{16,2},{18,0},{1,19},{3,17},{17,3},{19,1},{4,22},{6,... | collective-permute-start | bytes 2162696 | tf_op jit(solution)/shard_map/ppermute | solution.py:23
  439.1 22.5 %collective-permute-start.101 = (bf16[256,1408]{1,0:T(8,128)(2,1)S(1)}, bf16[256,1408]{1,0:T(8,128)(2,1)S(1)}, u32[]{:S(2)}, u32[]{:S(2)}) collective-permute-start(bf16[256,1408]{1,0:T(8,128)(2,1)S(1)} %get-tuple-element.75), channel_id=1, source_target_pairs={{0,2},{2,0},{16,18},{18,16},{1,3},{3,1},{17,19},{19,17},{4,6},{6,4... | collective-permute-start | bytes 2162696 | tf_op jit(solution)/shard_map/ppermute | solution.py:23
  463.5 86.4 %reduce-scatter.6.cloned.1.call-start = ((), (), s32[]{:S(2)}) async-start(), calls=%async_computation.5 | async-start | bytes 1638400 | tf_op jit(solution)/shard_map/reduce_scatter | solution.py:113
  476.6 125.8 %all-gather.3.cloned.1.call-start = ((), (), s32[]{:S(2)}) async-start(), calls=%async_computation.8 | async-start | bytes 1802240 | tf_op jit(solution)/shard_map/all_gather | solution.py:115
  489.0 25.5 %collective-permute-start.98 = (bf16[64,1408]{1,0:T(8,128)(2,1)S(1)}, bf16[64,1408]{1,0:T(8,128)(2,1)S(1)}, u32[]{:S(2)}, u32[]{:S(2)}) collective-permute-start(bf16[64,1408]{1,0:T(8,128)(2,1)S(1)} %fusion.79), channel_id=1, source_target_pairs={{0,16},{2,18},{16,0},{18,2},{1,17},{3,19},{17,1},{19,3},{4,20},{6,... | collective-permute-start | bytes 540680 | tf_op jit(solution)/shard_map/ppermute | solution.py:23
  515.3 90.2 %all-gather.5.cloned.1.call-start = ((), (), s32[]{:S(2)}) async-start(), calls=%async_computation.11 | async-start | bytes 1802240 | tf_op jit(solution)/shard_map/all_gather | solution.py:115
  524.4 25.3 %collective-permute-start.109 = (bf16[176,512]{1,0:T(8,128)(2,1)S(1)}, bf16[176,512]{1,0:T(8,128)(2,1)S(1)}, u32[]{:S(2)}, u32[]{:S(2)}) collective-permute-start(bf16[176,512]{1,0:T(8,128)(2,1)S(1)} %dynamic-slice_bitcast_fusion), channel_id=1, source_target_pairs={{0,16},{2,18},{16,0},{18,2},{1,17},{3,19},{17,1},{19,3},{4,20},{6,... | collective-permute-start | bytes 540680 | tf_op jit(solution)/shard_map/ppermute | solution.py:23
  527.6 22.1 %collective-permute-start.108 = (bf16[176,512]{1,0:T(8,128)(2,1)S(1)}, bf16[176,512]{1,0:T(8,128)(2,1)S(1)}, u32[]{:S(2)}, u32[]{:S(2)}) collective-permute-start(bf16[176,512]{1,0:T(8,128)(2,1)S(1)} %get-tuple-element.134), channel_id=1, source_target_pairs={{0,18},{2,16},{16,2},{18,0},{1,19},{3,17},{17,3},{19,1},{4,22},{6,... | collective-permute-start | bytes 540680 | tf_op jit(solution)/shard_map/ppermute | solution.py:23
  546.2 25.8 %collective-permute-start.104 = (bf16[256,1408]{1,0:T(8,128)(2,1)S(1)}, bf16[256,1408]{1,0:T(8,128)(2,1)S(1)}, u32[]{:S(2)}, u32[]{:S(2)}) collective-permute-start(bf16[256,1408]{1,0:T(8,128)(2,1)S(1)} %all_gather.18), channel_id=1, source_target_pairs={{0,16},{2,18},{16,0},{18,2},{1,17},{3,19},{17,1},{19,3},{4,20},{6,... | collective-permute-start | bytes 2162696 | tf_op jit(solution)/shard_map/ppermute | solution.py:23
  (167 other events, 2359.1 us)
Sparse Core Ops, SparseCore 0:
  295.5 36.8 reduce-scatter.9
  386.4 21.3 reduce-scatter.7
  410.9 35.8 reduce-scatter.13
  463.7 22.0 reduce-scatter.11
  488.8 25.5 reduce-scatter.5
  516.5 30.8 all-gather.2
  568.4 30.1 all-gather.4

commit v2 on v1

v2 whole, which is shorter than its diff:
```python
import functools

import jax
import jax.numpy as jnp
from jax import lax
from jax.experimental import pallas as pl
from jax.experimental.pallas import tpu as pltpu
from jax.sharding import Mesh
from jax.sharding import PartitionSpec as P

HD = 64
norm_eps = 1e-05
rope_base = 10000.0
masked = -1e30

COL = ("xl", "k")
RING = ("xh", "xl")
BF16 = jnp.bfloat16
F32 = jnp.float32


def trade(values, axes, mask, size=4):
    return lax.ppermute(values, axes, [(i, i ^ mask) for i in range(size)])


def trade_row(values, mask):
    return trade(values, "y", mask)


def trade_col(values, mask):
    return trade(values, COL, mask)


def trade_core(values):
    return trade(values, "k", 1, 2)


def trade_ring(values, mask):
    return trade(values, RING, mask)


def trade_deep(values, mask):
    return trade(values, "z", mask)


def after(values, *earlier):
    return lax.optimization_barrier((values, earlier))[0]


def pick(bit, zero, one):
    return jnp.where(bit == 0, zero, one)


def in_order(parts, index):
    low, high = index % 2, index // 2
    a, b, c, d = parts
    a, b = pick(low, a, b), pick(low, b, a)
    c, d = pick(low, c, d), pick(low, d, c)
    return [pick(high, a, c), pick(high, b, d), pick(high, c, a), pick(high, d, b)]


def cut(values, count, axis):
    return jnp.split(values, count, axis)


def gather_row(values):
    return lax.all_gather(values, "y", axis=0, tiled=True)


def sum_row(partial):
    return lax.psum_scatter(partial, "y", scatter_dimension=0, tiled=True)


def spread_row(values):
    return [values] + [trade_row(values, j) for j in (1, 2, 3)]


def row_parts(partial, row):
    size = partial.shape[0] // 4
    return [lax.dynamic_slice_in_dim(partial, (row ^ j) * size, size, 0) for j in range(4)]


def collect_row(parts):
    return [parts[0]] + [trade_row(parts[j], j) for j in (1, 2, 3)]


def by_width(parts, low):
    return [
        pick(low, parts[core + 2 * place], parts[core + 2 * (1 - place)])
        for core in range(2)
        for place in range(2)
    ]


def of_width(values, low):
    blocks = cut(values, 4, 1)
    return [
        pick(low, blocks[2 * core + place], blocks[2 * core + 1 - place])
        for place in range(2)
        for core in range(2)
    ]


def to_full_width(values, col, *alongside):
    size = values[0].shape[0] // 4
    send = lambda m: jnp.concatenate(
        [lax.dynamic_slice_in_dim(v, (col ^ m) * size, size, 0) for v in values], axis=1
    )
    parts = [send(0)] + [trade_col(send(m), m) for m in (1, 2, 3)]
    parts, alongside = lax.optimization_barrier((parts, alongside))
    parts = [cut(part, len(values), 1) for part in parts]
    rows = [
        jnp.concatenate(by_width([part[i] for part in parts], col // 2), axis=1)
        for i in range(len(values))
    ]
    return rows, alongside


def to_blocks(values, col):
    parts = of_width(values, col // 2)
    kind = values.dtype
    parts = [parts[0]] + [trade_col(parts[m].astype(BF16), m).astype(kind) for m in (1, 2, 3)]
    return jnp.concatenate(in_order(parts, col), axis=0)


def ring_halves(first, second, low, axis, *earlier):
    shard = jnp.concatenate([first, second])
    other = [trade_ring(first, 1), trade_ring(second, 3)]
    other = jnp.concatenate(after(other, *earlier))
    both = [pick(low, shard, other), pick(low, other, shard)]
    return jnp.concatenate(both, axis=axis)


def add_low(*terms):
    total = terms[0].astype(F32)
    for term in terms[1:]:
        total = total + term.astype(F32)
    return total.astype(BF16)


def at(values, index):
    return lax.dynamic_index_in_dim(values, index, 0, keepdims=False)


def ring_parts(blocks, low, high):
    half = blocks[0].shape[1] // 2
    take = lambda place, which: jnp.concatenate(
        [
            lax.dynamic_slice(v, (place, which * half, 0), (1, half, v.shape[2]))[0]
            for v in blocks
        ],
        axis=1,
    )
    return [take(low, high), take(1 - low, high), take(low, 1 - high), take(1 - low, 1 - high)]


def deep_parts(blocks, deep):
    size = blocks.shape[-2] // 4
    return [
        lax.dynamic_slice_in_dim(blocks, (deep ^ j) * size, size, blocks.ndim - 2) for j in range(4)
    ]


def trade_near(parts, trader):
    return [trader(parts[1], 1), trader(parts[3], 3)]


def exchange(parts, trader):
    return add_low(parts[0], *lax.optimization_barrier([trader(parts[j], j) for j in (1, 2, 3)]))


def ring_gather(values, high):
    other = trade_ring(values, 2)
    return jnp.concatenate([pick(high, values, other), pick(high, other, values)], axis=0)


def deep_gather(values, deep):
    parts = lax.optimization_barrier([values] + [trade_deep(values, j) for j in (1, 2, 3)])
    return jnp.concatenate(in_order(parts, deep), axis=0)


def product(left, right, dims, kind=F32):
    return lax.dot_general(left, right, (dims, ((), ())), preferred_element_type=F32).astype(kind)


def scale_of(values):
    return lax.rsqrt(jnp.mean(values * values, axis=1, keepdims=True) + norm_eps)


def add_and_norm(base_ref, part_ref, hidden_ref, normed_ref):
    hidden = base_ref[...] + part_ref[...].astype(F32)
    hidden_ref[...] = hidden
    normed_ref[...] = (hidden * scale_of(hidden)).astype(BF16)


def norm_back(values, weighted, passed):
    scale = scale_of(values)
    inner = jnp.mean(weighted * values, axis=1, keepdims=True)
    return passed + (scale * weighted - values * (scale**3 * inner))


def norm_back_low(values_ref, part_ref, passed_ref, grad_ref, low_ref):
    grad = norm_back(values_ref[...], part_ref[...].astype(F32), passed_ref[...].astype(F32))
    grad_ref[...] = grad
    low_ref[...] = grad.astype(BF16)


def norm_back_sum(values_ref, p0, p1, p2, p3, passed_ref, grad_ref):
    weighted = (p0[...].astype(F32) + p1[...].astype(F32)) + (p2[...].astype(F32) + p3[...].astype(F32))
    grad_ref[...] = norm_back(values_ref[...], weighted, passed_ref[...])


def turn(first, second, cosine, sine):
    return first * cosine - second * sine, second * cosine + first * sine


def project(x_ref, mine_ref, theirs_ref, cos_ref, sin_ref, q_ref, kv_ref):
    width = mine_ref.shape[1]
    slots = kv_ref.shape[0] + q_ref.shape[0]
    total = None
    for core, weights in enumerate((mine_ref, theirs_ref)):
        for place in range(2):
            spot = (2 * core + place) * width
            term = jnp.dot(
                x_ref[:, spot : spot + width], weights[place, :, :slots], preferred_element_type=F32
            )
            total = term if total is None else total + term
    turned = total.T
    cosine, sine = cos_ref[...], sin_ref[...]
    half = HD // 2
    heads = q_ref.shape[0] // HD
    for head in range(heads + 1):
        spot = head * HD
        first, second = turn(
            turned[spot : spot + half], turned[spot + half : spot + HD], cosine, sine
        )
        if head < heads:
            q_ref[spot : spot + half, :] = (first * HD**-0.5).astype(BF16)
            q_ref[spot + half : spot + HD, :] = (second * HD**-0.5).astype(BF16)
        else:
            kv_ref[:half, :] = first.astype(BF16)
            kv_ref[half:HD, :] = second.astype(BF16)
    kv_ref[HD:, :] = turned[(heads + 1) * HD :].astype(BF16)


def lay_keys(pairs, kt_ref, vt_ref, kn_ref, vn_ref):
    size = pairs[0].shape[1] // 4
    for block in range(4):
        for m, pair in enumerate(pairs):
            piece = pair[:, block * size : (block + 1) * size]
            spot = slice(m * size, (m + 1) * size)
            kt_ref[block, :, spot] = piece[:HD]
            if vt_ref is not None:
                vt_ref[block, :, spot] = piece[HD:]
            natural = piece.astype(F32).T.astype(BF16)
            kn_ref[block, spot, :] = natural[:, :HD]
            vn_ref[block, spot, :] = natural[:, HD:]


def two_heads(ref, first, spot, size):
    return jnp.concatenate(
        [ref[first : first + HD, pl.ds(spot, size)], ref[first + HD : first + 2 * HD, pl.ds(spot, size)]],
        axis=1,
    )


def admitted(koff_ref, start, qpos, qstart, diagonal):
    keys = koff_ref[...] + start
    allowed = keys >= qstart
    if diagonal:
        allowed = allowed & (keys <= qpos)
    return jnp.concatenate([allowed, allowed], axis=1)


def attend(
    q_ref, p0, p1, p2, p3, koff_ref, qpos_ref, qstart_ref,
    o_ref, low_ref, lse_ref, kt_ref, vt_ref, kn_ref, vn_ref,
):
    span = kn_ref.shape[1]
    size = span // 4
    pairs = q_ref.shape[0] // (2 * HD)
    lay_keys((p0, p1, p2, p3), kt_ref, vt_ref, kn_ref, vn_ref)

    def one_block(block, carry):
        spot = pl.multiple_of(block * size, size)
        qpos = qpos_ref[:, pl.ds(spot, size)]
        qstart = qstart_ref[:, pl.ds(spot, size)]
        queries = [two_heads(q_ref, pair * 2 * HD, spot, size) for pair in range(pairs)]

        def chunk(number, state, diagonal):
            keys, values = kn_ref[number], vt_ref[number]
            allowed = admitted(koff_ref, number * span, qpos, qstart, diagonal)
            fresh = []
            for query, (top, total, accum) in zip(queries, state):
                scores = jnp.dot(keys, query, preferred_element_type=F32)
                scores = jnp.where(allowed, scores, masked)
                new_top = jnp.maximum(top, jnp.max(scores, axis=0, keepdims=True))
                weights = jnp.exp(scores - new_top)
                shrink = jnp.exp(top - new_top)
                total = total * shrink + jnp.sum(weights, axis=0, keepdims=True)
                accum = accum * shrink + jnp.dot(
                    values, weights.astype(BF16), preferred_element_type=F32
                )
                fresh.append((new_top, total, accum))
            return tuple(fresh)

        empty = (
            jnp.full((1, 2 * size), masked, F32),
            jnp.zeros((1, 2 * size), F32),
            jnp.zeros((HD, 2 * size), F32),
        )
        state = chunk(block, (empty,) * pairs, True)
        state = lax.fori_loop(0, block, lambda number, state: chunk(number, state, False), state)
        for pair, (top, total, accum) in enumerate(state):
            result = accum / total
            lse = top + jnp.log(total)
            for part in range(2):
                first = (2 * pair + part) * HD
                piece = result[:, part * size : (part + 1) * size]
                o_ref[first : first + HD, pl.ds(spot, size)] = piece
                low_ref[first : first + HD, pl.ds(spot, size)] = piece.astype(BF16)
                lse_ref[2 * pair + part : 2 * pair + part + 1, pl.ds(spot, size)] = lse[
                    :, part * size : (part + 1) * size
                ]
        return carry

    lax.fori_loop(0, 4, one_block, 0)


def attend_back(
    q_ref, p0, p1, p2, p3, koff_ref, qpos_ref, qstart_ref, o_ref, lse_ref, go_ref, cos_ref, sin_ref, *refs,
    first_pair, pairs, last_call,
):
    if last_call:
        gk_in, gv_in, gq_ref, g0, g1, g2, g3, kt_ref, kn_ref, vn_ref, gk_ref, gv_ref = refs
    else:
        gq_ref, gk_ref, gv_ref, kt_ref, kn_ref, vn_ref = refs
    span = kn_ref.shape[1]
    size = span // 4
    lay_keys((p0, p1, p2, p3), kt_ref, None, kn_ref, vn_ref)
    gk_ref[...] = gk_in[...] if last_call else jnp.zeros_like(gk_ref)
    gv_ref[...] = gv_in[...] if last_call else jnp.zeros_like(gv_ref)
    last = (((1,), (1,)), ((), ()))

    def one_block(block, carry):
        spot = pl.multiple_of(block * size, size)
        qpos = qpos_ref[:, pl.ds(spot, size)]
        qstart = qstart_ref[:, pl.ds(spot, size)]
        cosine, sine = cos_ref[:, pl.ds(spot, size)], sin_ref[:, pl.ds(spot, size)]
        known = []
        for pair in range(first_pair, first_pair + pairs):
            first = pair * 2 * HD
            query, grad_out = two_heads(q_ref, first, spot, size), two_heads(go_ref, first, spot, size)
            mixed = two_heads(o_ref, first, spot, size)
            delta = jnp.sum(grad_out.astype(F32) * mixed, axis=0, keepdims=True)
            lse = jnp.concatenate(
                [lse_ref[2 * pair + part : 2 * pair + part + 1, pl.ds(spot, size)] for part in range(2)],
                axis=1,
            )
            known.append((query, grad_out, delta, lse))

        def chunk(number, state, diagonal):
            keys, values, turned_keys = kn_ref[number], vn_ref[number], kt_ref[number]
            allowed = admitted(koff_ref, number * span, qpos, qstart, diagonal)
            fresh = []
            grad_keys, grad_values = gk_ref[number], gv_ref[number]
            for (query, grad_out, delta, lse), grad_query in zip(known, state):
                scores = jnp.dot(keys, query, preferred_element_type=F32)
                probs = jnp.exp(jnp.where(allowed, scores - lse, masked))
                grad_probs = jnp.dot(values, grad_out, preferred_element_type=F32)
                grad_scores = (probs * (grad_probs - delta)).astype(BF16)
                grad_values = grad_values + lax.dot_general(
                    grad_out, probs.astype(BF16), last, preferred_element_type=F32
                )
                grad_keys = grad_keys + lax.dot_general(
                    query, grad_scores, last, preferred_element_type=F32
                )
                fresh.append(
                    grad_query + jnp.dot(turned_keys, grad_scores, preferred_element_type=F32)
                )
            gk_ref[number] = grad_keys
            gv_ref[number] = grad_values
            return tuple(fresh)

        state = chunk(block, (jnp.zeros((HD, 2 * size), F32),) * pairs, True)
        state = lax.fori_loop(0, block, lambda number, state: chunk(number, state, False), state)
        for head in range(2 * pairs):
            grad = state[head // 2][:, head % 2 * size : (head % 2 + 1) * size] * HD**-0.5
            half = HD // 2
            first, second = turn(grad[:half], grad[half:], cosine, -sine)
            gq_ref[head * HD : head * HD + half, pl.ds(spot, size)] = first.astype(BF16)
            gq_ref[head * HD + half : (head + 1) * HD, pl.ds(spot, size)] = second.astype(BF16)
        return carry

    lax.fori_loop(0, 4, one_block, 0)
    if last_call:
        for block in range(4):
            for m, ref in enumerate((g0, g1, g2, g3)):
                spot, out = slice(m * size, (m + 1) * size), slice(block * size, (block + 1) * size)
                ref[:HD, out] = gk_ref[block, :, spot].astype(BF16)
                ref[HD:, out] = gv_ref[block, :, spot].astype(BF16)


def project_back(
    gq0, gq1, g0, g1, g2, g3, cos_ref, sin_ref, mine_ref, theirs_ref, gqkv_ref, part_ref
):
    pair = g0[...].astype(F32) + g1[...].astype(F32) + (g2[...].astype(F32) + g3[...].astype(F32))
    half = HD // 2
    first, second = turn(pair[:half], pair[half:HD], cos_ref[...], -sin_ref[...])
    turned = jnp.concatenate(
        [gq0[...].astype(F32), gq1[...].astype(F32), first, second, pair[HD:]], axis=0
    )
    gqkv_ref[...] = turned.astype(BF16)
    natural = turned.T.astype(BF16)
    width = mine_ref.shape[1]
    slots = turned.shape[0]
    for core, weights in enumerate((mine_ref, theirs_ref)):
        for place in range(2):
            spot = (2 * core + place) * width
            part = lax.dot_general(
                natural, weights[place, :, :slots], (((1,), (1,)), ((), ())), preferred_element_type=F32
            )
            part_ref[:, spot : spot + width] = part.astype(BF16)


def feed(h_ref, gi_ref, own_ref, other_ref, inner_ref, pair_ref, part_ref, w_ref, sems):
    units = gi_ref.shape[1]
    depth = own_ref.shape[0]
    groups = feed_groups(units)
    copies = []
    for group, (begin, end) in enumerate(groups):
        mine = []
        for core, ref in enumerate((own_ref, other_ref)):
            for start in (0, units):
                columns = pl.ds(start + begin, end - begin)
                copy = pltpu.make_async_copy(
                    ref.at[:, columns],
                    w_ref.at[pl.ds(core * depth, depth), columns],
                    sems.at[group, len(mine)],
                )
                copy.start()
                mine.append(copy)
        copies.append(mine)
    for (begin, end), mine in zip(groups, copies):
        for copy in mine:
            copy.wait()
        gate = jnp.dot(h_ref[...], w_ref[:, begin:end], preferred_element_type=F32)
        up = jnp.dot(h_ref[...], w_ref[:, units + begin : units + end], preferred_element_type=F32)
        grad_inner = gi_ref[:, begin:end]
        sig = 1.0 / (1.0 + jnp.exp(-gate))
        act = gate * sig
        inner_ref[:, begin:end] = (act * up).astype(BF16)
        grad_gate = grad_inner * up * (sig * (1.0 + gate * (1.0 - sig)))
        pair_ref[:, begin:end] = grad_gate.astype(BF16)
        pair_ref[:, units + begin : units + end] = (grad_inner * act).astype(BF16)
    for begin in range(0, 2 * depth, 512):
        part = lax.dot_general(
            pair_ref[...], w_ref[begin : begin + 512, :], (((1,), (1,)), ((), ())),
            preferred_element_type=F32,
        )
        part_ref[:, begin : begin + 512] = part.astype(BF16)


def feed_groups(units):
    ends = [128, 384] + list(range(896, units, 512)) + [units]
    return list(zip([0] + ends[:-1], ends))


def spread_heads(row_ref, w_ref, b0, b1, b2, b3, out_ref):
    size = b0.shape[0]
    for j, part in enumerate((b0, b1, b2, b3)):
        spot = pl.multiple_of((row_ref[0] ^ j) * size, size)
        piece = lax.dot_general(
            w_ref[...], part[...], (((1,), (1,)), ((), ())), preferred_element_type=F32
        )
        out_ref[:, pl.ds(spot, size)] = piece.astype(BF16)


def kernel_call(body, out_shape, operands, flops, scratch=(), scalars=0, outside=()):
    moved = sum(x.size * x.dtype.itemsize for x in operands)
    spaces = [
        pltpu.SMEM if i < scalars else pl.ANY if i in outside else pltpu.VMEM
        for i in range(len(operands))
    ]
    return pl.pallas_call(
        body,
        out_shape=out_shape,
        in_specs=[pl.BlockSpec(memory_space=space) for space in spaces],
        out_specs=jax.tree.map(lambda _: pl.BlockSpec(memory_space=pltpu.VMEM), out_shape),
        scratch_shapes=list(scratch),
        compiler_params=pltpu.CompilerParams(vmem_limit_bytes=48 * 1024 * 1024),
        cost_estimate=pl.CostEstimate(flops=flops, bytes_accessed=moved, transcendentals=0),
    )(*operands)


def on_device(
    tokens_in, segment_ids, attn_gain, w_qkv, w_out, mlp_gain, w_gate, w_up, w_down, cotangent
):
    group = segment_ids.shape[0]
    span = group // 4
    size = span // 4
    units = w_gate.shape[1]
    slots = w_qkv.shape[2] // HD
    heads = slots - 2
    deep, high, row = lax.axis_index("z"), lax.axis_index("xh"), lax.axis_index("y")
    low, core = lax.axis_index("xl"), lax.axis_index("k")
    col = low * 2 + core

    indices = jnp.arange(group, dtype=jnp.int32)
    previous = jnp.concatenate([segment_ids[:1] - 1, segment_ids[:-1]])
    starts = lax.cummax(jnp.where(segment_ids != previous, indices, 0), axis=0)
    bases = [j * span + col * size for j in range(4)]
    my_starts = jnp.concatenate([lax.dynamic_slice_in_dim(starts, b, size, 0) for b in bases])
    lanes = jnp.arange(size, dtype=jnp.int32)
    my_index = jnp.concatenate([lanes + b for b in bases])
    half_dim = HD // 2
    inverse_freq = rope_base ** (-jnp.arange(half_dim, dtype=F32) * 2.0 / HD)
    angles = inverse_freq[:, None] * (my_index - my_starts).astype(F32)[None, :]
    cosine, sine = jnp.cos(angles), jnp.sin(angles)
    key_offset = jnp.concatenate([lanes + (col ^ m) * size for m in range(4)])
    key_offset = jnp.broadcast_to(key_offset[:, None], (span, size))
    qpos, qstart = my_index[None, :], my_starts[None, :]
    cut_at = slots * HD

    flat_qkv = w_qkv.reshape(w_qkv.shape[0], -1)
    qkv_out = jnp.concatenate([(flat_qkv * attn_gain[:, None]).astype(BF16), w_out], axis=1)
    (inputs, cot_rows), alongside = to_full_width(
        [tokens_in, cotangent], col, cosine, sine, key_offset, qpos, qstart, *cut(qkv_out, 2, 0)
    )
    cosine, sine, key_offset, qpos, qstart, qkv_out_first, qkv_out_second = alongside
    inputs = inputs.astype(F32)
    normed_one = (inputs * scale_of(inputs)).astype(BF16)
    rows_one = gather_row(normed_one)

    mine = ring_halves(qkv_out_first, qkv_out_second, low, 0).reshape(2, *qkv_out.shape)
    theirs = trade_core(mine)
    down_halves = [after(v, normed_one) for v in cut(w_down, 2, 0)]
    scaled = lambda v: (v * mlp_gain[:, None]).astype(BF16)
    gate_up = jnp.concatenate([scaled(w_gate), scaled(w_up)], axis=1)
    gu_halves = [after(v, mine) for v in cut(gate_up, 2, 0)]
    full_out = jnp.concatenate(
        [mine[0, :, cut_at:], mine[1, :, cut_at:], theirs[0, :, cut_at:], theirs[1, :, cut_at:]],
        axis=1,
    )
    rows_one, gu_halves, full_out = lax.optimization_barrier((rows_one, gu_halves, full_out))
    grad_rows = gather_row(after(cot_rows, rows_one))
    down_mine = ring_halves(*down_halves, low, 1, rows_one)
    gu_mine = ring_halves(*gu_halves, low, 0)

    shape = lambda kind, *dims: jax.ShapeDtypeStruct(dims, kind)
    scratch = lambda kind, *dims: pltpu.VMEM(dims, kind)
    width = inputs.shape[1]
    matmul = lambda rows, depth, columns: 2 * rows * depth * columns
    query, pairs = kernel_call(
        project,
        (shape(BF16, heads * HD, span), shape(BF16, 2 * HD, span)),
        (rows_one, mine, theirs, cosine, sine),
        matmul(span, width, cut_at),
    )
    all_pairs = [pairs] + [trade_col(pairs, m) for m in (1, 2, 3)]
    all_pairs = lax.optimization_barrier((all_pairs, down_mine))[0]
    down_theirs = trade_core(after(down_mine, all_pairs))

    flops = 2 * matmul(heads * span, HD, group)
    keys_shape = (4, HD, span), (4, span, HD)
    mixed, mixed_low, lse = kernel_call(
        attend,
        (shape(F32, heads * HD, span), shape(BF16, heads * HD, span), shape(F32, heads, span)),
        (query, *all_pairs, key_offset, qpos, qstart),
        flops,
        scratch=[scratch(BF16, *keys_shape[i]) for i in (0, 0, 1, 1)],
    )
    mixed_low = after(mixed_low, down_theirs)
    full_down = jnp.concatenate([down_mine, down_theirs], axis=1)
    branch = product(mixed_low, full_out, ((0,), (0,)), BF16)
    grad_inner = product(grad_rows, full_down, ((1,), (1,)))
    hidden, normed_two = kernel_call(
        add_and_norm,
        (shape(F32, *inputs.shape), shape(BF16, *inputs.shape)),
        (inputs, after(sum_row(branch), grad_inner, gu_mine)),
        0,
    )
    gu_theirs = trade_core(after(gu_mine, hidden))
    rows_two = gather_row(normed_two)

    side = lambda v, which: v[:, which * width // 2 : (which + 1) * width // 2]
    both_cores = lambda v, axis=0: jnp.concatenate([v, trade_core(v)], axis=axis)
    half_of = lambda v: jnp.concatenate([side(v, 0), trade_core(side(v, 1))])

    def half_by_ring(v):
        blocks = [cut(v, 8, 1)[i] for i in (0, 2, 1, 3, 4, 6, 5, 7)]
        sides = [jnp.concatenate(blocks[:4], axis=1), jnp.concatenate(blocks[4:], axis=1)]
        return jnp.concatenate([sides[0], trade_core(sides[1])])

    token_sum = lambda a, b: product(a, b, ((0,), (0,)), BF16)
    cot_half, heads_both = half_by_ring(after(grad_rows, hidden)), both_cores(after(mixed_low, hidden), 1)
    one_half = half_of(after(rows_one, hidden))
    rows_two, cot_half, heads_both, one_half = lax.optimization_barrier(
        (rows_two, cot_half, heads_both, one_half)
    )
    two_half = half_by_ring(rows_two)
    inner, grad_pair, part_two = kernel_call(
        feed,
        (shape(BF16, span, units), shape(BF16, span, 2 * units), shape(BF16, span, width)),
        (rows_two, grad_inner, gu_mine, gu_theirs),
        2 * matmul(span, width, 2 * units),
        scratch=(scratch(BF16, width, 2 * units), pltpu.SemaphoreType.DMA((len(feed_groups(units)), 4))),
        outside=(2, 3),
    )
    inner_both = both_cores(inner)
    pair_both = both_cores(grad_pair)
    mlp_sums = jnp.concatenate([token_sum(two_half, pair_both), token_sum(cot_half, inner_both)], axis=1)
    grad_n2, mlp_sums = lax.optimization_barrier((sum_row(part_two), mlp_sums))
    mlp_sums = lax.psum_scatter(mlp_sums, ("xh", "xl", "z"), scatter_dimension=0, tiled=True)
    grad_hidden, grad_low = kernel_call(
        norm_back_low,
        (shape(F32, *hidden.shape), shape(BF16, *hidden.shape)),
        (hidden, grad_n2, cot_rows),
        0,
    )
    branch_parts = spread_row(grad_low)
    result_parts = row_parts(product(inner, full_down, ((1,), (0,)), BF16), row)
    branch_parts, result_parts = lax.optimization_barrier((branch_parts, result_parts))
    grad_heads = kernel_call(
        spread_heads,
        shape(BF16, heads * HD, span),
        (row.astype(jnp.int32)[None], full_out, *branch_parts),
        matmul(span, width, heads * HD),
        scalars=1,
    )
    pair_shape = shape(BF16, 2 * HD, span)
    known = (query, *all_pairs, key_offset, qpos, qstart, mixed, lse, grad_heads, cosine, sine)
    half_heads = shape(BF16, heads * HD // 2, span)
    keys_scratch = [scratch(BF16, *keys_shape[i]) for i in (0, 1, 1)]
    key_sums = (shape(F32, *keys_shape[0]),) * 2
    split = functools.partial(attend_back, pairs=heads // 4)
    result_near = trade_near(result_parts, trade_row)
    gq_first, *key_grads = kernel_call(
        functools.partial(split, first_pair=0, last_call=False),
        (half_heads,) + key_sums,
        known,
        flops * 5 // 4,
        scratch=keys_scratch,
    )
    key_grads, result_near = lax.optimization_barrier((key_grads, result_near))
    result_far = trade_row(after(result_parts[2], result_near), 2)
    gq_last, *grad_pairs = kernel_call(
        functools.partial(split, first_pair=heads // 4, last_call=True),
        (half_heads,) + (pair_shape,) * 4,
        (*known, *key_grads),
        flops * 5 // 4,
        scratch=keys_scratch + [scratch(F32, *keys_shape[0])] * 2,
    )
    grad_pairs, result_far = lax.optimization_barrier((grad_pairs, result_far))
    grad_pairs = [grad_pairs[0]] + [trade_col(grad_pairs[m], m) for m in (1, 2, 3)]
    grad_qkv, part_one = kernel_call(
        project_back,
        (shape(BF16, cut_at, span), shape(BF16, span, width)),
        (gq_first, gq_last, *grad_pairs, cosine, sine, mine, theirs),
        matmul(span, width, cut_at),
    )
    one_parts = collect_row(row_parts(part_one, row))
    branch_rows = jnp.concatenate(in_order(after(branch_parts, grad_qkv), row))
    branch_half = half_of(branch_rows)
    qkv_both = both_cores(grad_qkv, 1)
    qkv_sum = product(one_half, qkv_both, ((0,), (1,)), BF16).reshape(2, width // 4, -1)
    qkv_parts, mlp_sums = after((ring_parts([qkv_sum], low, high), mlp_sums), one_parts[1])
    qkv_near = trade_near(qkv_parts, trade_ring)
    mlp_total = lax.all_gather(mlp_sums, ("xh", "z"), axis=0, tiled=True).astype(F32)
    one_parts, qkv_near, branch_half = lax.optimization_barrier((one_parts, qkv_near, branch_half))

    grad_in = kernel_call(
        norm_back_sum, shape(F32, *inputs.shape), (inputs, *one_parts, grad_hidden), 0
    )
    out_sum = product(branch_half, heads_both, ((0,), (1,)), BF16).reshape(2, width // 4, -1)
    qkv_far = trade_ring(after(qkv_parts[2], qkv_near), 2)
    grad_in, qkv_far, out_sum = lax.optimization_barrier((to_blocks(grad_in, col), qkv_far, out_sum))
    qkv_total = add_low(qkv_parts[0], *qkv_near, qkv_far)
    out_parts = ring_parts([out_sum], low, high)
    out_near = trade_near(out_parts, trade_ring)
    qkv_total = exchange([qkv_total] * 4, trade_deep)
    qkv_total, out_near = lax.optimization_barrier((qkv_total, out_near))
    out_far = trade_ring(after(out_parts[2], out_near), 2)
    qkv_total = ring_gather(qkv_total, high).astype(F32)
    result = (hidden + result_parts[0].astype(F32)) + result_far.astype(F32)
    result = result + sum(part.astype(F32) for part in result_near)
    result = to_blocks(after(result.astype(BF16), grad_in), col)
    out_far, qkv_total, result = lax.optimization_barrier((out_far, qkv_total, result))
    out_total = exchange([add_low(out_parts[0], *out_near, out_far)] * 4, trade_deep)
    out_total = ring_gather(out_total, high).astype(F32)
    gu_total, down_total = mlp_total[:, : 2 * units], mlp_total[:, 2 * units :]

    gate_total, up_total = gu_total[:, :units], gu_total[:, units:]
    gain_sums = jnp.stack(
        [
            jnp.sum(flat_qkv * qkv_total, axis=1),
            jnp.sum(w_gate * gate_total + w_up * up_total, axis=1),
        ]
    )
    gain_sums = sum([trade_row(gain_sums, j) for j in (1, 2, 3)], gain_sums)
    return (
        result,
        grad_in,
        gain_sums[0],
        (qkv_total * attn_gain[:, None]).reshape(w_qkv.shape),
        out_total.T,
        gain_sums[1],
        gate_total * mlp_gain[:, None],
        up_total * mlp_gain[:, None],
        down_total.T,
    )


def solution(mesh):
    dp, rows, cols = mesh.devices.shape
    fine = Mesh(
        mesh.devices.reshape(dp // 2, 2, rows, cols // 2, 2), ("z", "xh", "y", "xl", "k")
    )
    tokens = P(("z", "xh", "y"), COL)
    in_specs = (
        tokens, P(("z", "xh")), P(COL), P(COL, "y", None), P("y", COL), P(COL),
        P(COL, "y"), P(COL, "y"), P("y", COL), tokens,
    )
    out_specs = (
        tokens, tokens, P(COL), P(COL, "y", None), P("y", COL), P(COL),
        P(COL, "y"), P(COL, "y"), P("y", COL),
    )
    return jax.shard_map(
        on_device, mesh=fine, in_specs=in_specs, out_specs=out_specs, check_vma=False
    )
```

time: 625 us -> 479 us (0.77)
  starting transfers between devices: 121 us -> 65.8 us
  matrix products: 84.7 us -> 33.9 us
  blocking collectives: 46.7 us -> 0 us
  waiting for transfers between devices: 206 us -> 177 us
  Pallas kernels: 40.9 us -> 66.8 us
  local copies, waits for them, and re-layouts: 49.5 us -> 62.5 us
    ppermute x111 -> x58, waiting for transfers between devices: 206 us -> 142 us  [trade(): return lax.ppermute(values, axes, [(i, i ^ mask) for i in range(size)])]
    ppermute x111 -> x58, starting transfers between devices: 121 us -> 65.5 us  [trade(): return lax.ppermute(values, axes, [(i, i ^ mask) for i in range(size)])]
    dot_general x28 -> x7, matrix products: 84.7 us -> 33.9 us  [product(): lax.dot_general(left, right, (dims, ((), ())), preferred_element_type=F32)]
    all_gather x3 -> x0, blocking collectives: 46.7 us -> none  [the longest x2 31.3 us: reduce_ring_first(): total = lax.all_gather(total, 'z', axis=0, tiled=True)]
    pallas_call x2 -> x10, Pallas kernels: 40.9 us -> 66.8 us  [kernel_call(): pl.pallas_call(body, out_shape=out_shape, in_specs=[pl.BlockSpec(memory_s...]
    reduce_scatter x5 -> x3, waiting for transfers between devices: 0.04 us -> 18.9 us  [the longest x2 18.9 us: sum_row(): return lax.psum_scatter(partial, 'y', scatter_dimension=0, tiled=True)]
    all_gather x2 -> x4, waiting for transfers between devices: 0.01 us -> 15.8 us  [the longest x3 15.8 us: gather_row(): return lax.all_gather(values, 'y', axis=0, tiled=True)]
    unnamed x207 -> x181, local copies, waits for them, and re-layouts: 21.8 us -> 36.4 us
  transfers between devices with their start and end apart: 118 -> 65, of which waited for: 42 -> 34; matrix products, arithmetic and copies ran while one was open for 25% -> 23% of each run, Pallas kernels for 7% -> 11%
where the time goes in v2:
time: 479 us; the launch traced here: 471 us
  waiting for transfers between devices  177 us (37%)
  Pallas kernels  66.8 us (14%)
  starting transfers between devices  65.8 us (14%)
  local copies, waits for them, and re-layouts  62.5 us (13%)
  other arithmetic  47.7 us (10%)
  matrix products  33.9 us (7%)
  between operations  16.7 us (3%)
    ppermute x58, waiting for transfers between devices, trade(): return lax.ppermute(values, axes, [(i, i ^ mask) for i in range(size)])  142 us
    pallas_call x10, Pallas kernels, kernel_call(): pl.pallas_call(body, out_shape=out_shape, in_specs=[pl.BlockSpec(memory_s...  66.8 us
    ppermute x58, starting transfers between devices, trade(): return lax.ppermute(values, axes, [(i, i ^ mask) for i in range(size)])  65.5 us
    unnamed x181, local copies, waits for them, and re-layouts  36.4 us
    dot_general x7, matrix products, product(): lax.dot_general(left, right, (dims, ((), ())), preferred_element_type=F32)  33.9 us
    reduce_scatter x2, waiting for transfers between devices, sum_row(): return lax.psum_scatter(partial, 'y', scatter_dimension=0, tiled=True)  18.9 us
    all_gather x3, waiting for transfers between devices, gather_row(): return lax.all_gather(values, 'y', axis=0, tiled=True)  15.8 us
  transfers between devices with their start and end apart: 65, of which 34 were waited for; matrix products, arithmetic and copies ran while one was open for 23% of the time, Pallas kernels for 11%

profile of v2, /device:TPU:0, one launch (start us, length us, event | category | flops | bytes accessed | tf_op | source)
XLA Modules:
  0.0 470.6 jit_solution(7022760725886732461)
XLA Ops:
  17.2 3.2 collective-permute-done.1
  20.4 4.9 %collective-permute-done.2 = bf16[128,1024]{1,0:T(8,128)(2,1)} collective-permute-done((bf16[128,1024]{1,0:T(8,128)(2,1)}, bf16[128,1024]{1,0:T(8,128)(2,1)}, u32[]{:S(2)}, u32[]{:S(2)}) %collective-permute-start.2) | collective-permute-done | bytes 262176 | tf_op jit(solution)/shard_map/ppermute | solution.py:23
  33.6 7.6 %collective-permute-done.3 = bf16[256,1152]{1,0:T(8,128)(2,1)S(1)} collective-permute-done((bf16[256,1152]{1,0:T(8,128)(2,1)}, bf16[256,1152]{1,0:T(8,128)(2,1)S(1)}, u32[]{:S(2)}, u32[]{:S(2)}) %collective-permute-start.3) | collective-permute-done | bytes 589856 | tf_op jit(solution)/shard_map/ppermute | solution.py:23
  65.5 3.6 shard_map.169
  87.4 18.0 %shard_map.170 = (f32[512,512]{1,0:T(8,128)S(1)}, bf16[512,512]{1,0:T(8,128)(2,1)S(1)}, f32[8,512]{1,0:T(8,128)S(1)}) custom-call(bf16[512,512]{1,0:T(8,128)(2,1)S(1)} %copy-done.31, bf16[128,512]{1,0:T(8,128)(2,1)S(1)} %copy-done.34, bf16[128,512]{1,0:T(8,128)(2,1)S(1)} %copy-done.37, bf16[128,512]{1,0:T(8,128)(2,1)S(1)} %copy-done.40, ...), custom_call_target="tpu_custom_call" | custom-call | flops 2147483648 | bytes 1314816 | tf_op jit(solution)/shard_map/pallas_call | solution.py:485
  106.9 2.6 convolution_convert_fusion.1
  118.9 2.8 pad_maximum_fusion.2.own_ref
  121.7 8.7 %fusion.14.gi_ref = f32[512,1408]{1,0:T(8,128)} fusion(bf16[512,2048]{1,0:T(8,128)(2,1)} %all-gather.7.cloned.1.call-done, bf16[1408,1024]{1,0:T(8,128)(2,1)} %collective-permute-done.11, bf16[1408,512]{1,0:T(8,128)(2,1)} %copy-done.51, bf16[1408,512]{1,0:T(8,128)(2,1)} %copy-done.50), kind=kOutput, calls=%fused_computation.31 | convolution fusion | flops 2970091520 | bytes 10747904 | tf_op jit(solution)/shard_map/dot_general | solution.py:183
  130.4 13.5 %reduce-scatter.4.cloned.1.call-done.part_ref = bf16[128,2048]{1,0:T(8,128)(2,1)} async-done(((bf16[512,2048]{1,0:T(8,128)(2,1)}), bf16[128,2048]{1,0:T(8,128)(2,1)}) %reduce-scatter.4.cloned.1.call-update) | async-done | bytes 524304 | tf_op jit(solution)/shard_map/reduce_scatter | solution.py:71
  151.4 8.8 %collective-permute-done.15 = bf16[512,512]{1,0:T(8,128)(2,1)S(1)} collective-permute-done((bf16[512,512]{1,0:T(8,128)(2,1)S(1)}, bf16[512,512]{1,0:T(8,128)(2,1)S(1)}, u32[]{:S(2)}, u32[]{:S(2)}) %collective-permute-start.15) | collective-permute-done | bytes 524320 | tf_op jit(solution)/shard_map/ppermute | solution.py:23
  164.4 13.5 %all-gather.9.cloned.1.call-done.h_ref = bf16[512,2048]{1,0:T(8,128)(2,1)} async-done(((bf16[128,2048]{1,0:T(8,128)(2,1)}), bf16[512,2048]{1,0:T(8,128)(2,1)}) %all-gather.9.cloned.1.call-update) | async-done | bytes 2097168 | tf_op jit(solution)/shard_map/all_gather | solution.py:67
  179.5 16.8 %shard_map.172 = (bf16[512,1408]{1,0:T(8,128)(2,1)S(1)}, bf16[512,2816]{1,0:T(8,128)(2,1)}, bf16[512,2048]{1,0:T(8,128)(2,1)S(1)}) custom-call(bf16[512,2048]{1,0:T(8,128)(2,1)S(1)} %copy-done.15, f32[512,1408]{1,0:T(8,128)} %fusion.14.gi_ref, bf16[1024,2816]{1,0:T(8,128)(2,1)} %pad_maximum_fusion.2.own_ref, bf16[1024,2816]{1,0:T(8,128)(2,1)} %collective-permute-done.17.other_ref), custom_call_target="tpu_custom_call" | custom-call | flops 11811160064 | bytes 16515072 | tf_op jit(solution)/shard_map/pallas_call | solution.py:485
  201.8 5.8 %collective-permute-done.20 = bf16[512,1408]{1,0:T(8,128)(2,1)S(1)} collective-permute-done((bf16[512,1408]{1,0:T(8,128)(2,1)}, bf16[512,1408]{1,0:T(8,128)(2,1)S(1)}, u32[]{:S(2)}, u32[]{:S(2)}) %collective-permute-start.20) | collective-permute-done | bytes 1441824 | tf_op jit(solution)/shard_map/ppermute | solution.py:23
  207.5 3.7 convolution_convert_fusion
  211.3 8.4 %fusion.4 = bf16[1024,2816]{1,0:T(8,128)(2,1)S(1)} fusion(bf16[512,2816]{1,0:T(8,128)(2,1)} %collective-permute-done.19, bf16[512,2816]{1,0:T(8,128)(2,1)S(1)} %copy-done.86, bf16[512,1024]{1,0:T(8,128)(2,1)S(1)} %collective-permute-done.18, bf16[512,256]{1,0:T(8,128)(2,1)S(1)} %get-tuple-element.300, bf16[512,256]{1,0:T(8,128)(2,1)S(1)} %get-tuple-element.301, ...), kind=kOutput, calls=%fused_computation.7 | convolution fusion | flops 5930483712 | bytes 13631488 | tf_op jit(solution)/shard_map/dot_general | solution.py:183
  219.7 3.8 pad_maximum_fusion
  223.5 5.4 %reduce-scatter.6.cloned.1.call-done.part_ref = bf16[128,2048]{1,0:T(8,128)(2,1)} async-done(((bf16[512,2048]{1,0:T(8,128)(2,1)}), bf16[128,2048]{1,0:T(8,128)(2,1)}) %reduce-scatter.6.cloned.1.call-update) | async-done | bytes 524304 | tf_op jit(solution)/shard_map/reduce_scatter | solution.py:71
  236.0 2.4 collective-permute-start.23
  238.4 6.1 %convolution_convert_fusion.2 = bf16[512,2048]{1,0:T(8,128)(2,1)S(1)} fusion(bf16[512,1408]{1,0:T(8,128)(2,1)S(1)} %copy-done.29, bf16[1408,1024]{1,0:T(8,128)(2,1)} %collective-permute-done.11, bf16[1408,512]{1,0:T(8,128)(2,1)} %copy-done.51, bf16[1408,512]{1,0:T(8,128)(2,1)} %copy-done.50), kind=kOutput, calls=%fused_computation.14 | convolution fusion | flops 2971140096 | bytes 9306112 | tf_op jit(solution)/shard_map/dot_general | solution.py:183
  245.4 3.1 collective-permute-done.21.b1
  248.5 10.5 %collective-permute-done.22.b2 = bf16[128,2048]{1,0:T(8,128)(2,1)S(1)} collective-permute-done((bf16[128,2048]{1,0:T(8,128)(2,1)S(1)}, bf16[128,2048]{1,0:T(8,128)(2,1)S(1)}, u32[]{:S(2)}, u32[]{:S(2)}) %collective-permute-start.22) | collective-permute-done | bytes 524320 | tf_op jit(solution)/shard_map/ppermute | solution.py:23
  259.0 2.6 collective-permute-done.23.b3
  266.5 10.2 %shard_map.175 = (bf16[256,512]{1,0:T(8,128)(2,1)S(1)}, f32[4,64,512]{2,1,0:T(8,128)S(1)}, f32[4,64,512]{2,1,0:T(8,128)S(1)}) custom-call(bf16[512,512]{1,0:T(8,128)(2,1)S(1)} %copy-done.32, bf16[128,512]{1,0:T(8,128)(2,1)S(1)} %copy-done.35, bf16[128,512]{1,0:T(8,128)(2,1)S(1)} %copy-done.38, bf16[128,512]{1,0:T(8,128)(2,1)S(1)} %copy-done.41, ...), custom_call_target="tpu_custom_call" | custom-call | flops 2684354560 | bytes 3035136 | tf_op jit(solution)/shard_map/pallas_call | solution.py:485
  278.7 10.2 %shard_map.176 = (bf16[256,512]{1,0:T(8,128)(2,1)S(1)}, bf16[128,512]{1,0:T(8,128)(2,1)S(1)}, bf16[128,512]{1,0:T(8,128)(2,1)S(1)}, bf16[128,512]{1,0:T(8,128)(2,1)S(1)}, bf16[128,512]{1,0:T(8,128)(2,1)S(1)}) custom-call(bf16[512,512]{1,0:T(8,128)(2,1)S(1)} %copy-done.32, bf16[128,512]{1,0:T(8,128)(2,1)S(1)} %copy-done.35, bf16[128,512]{1,0:T(8,128)(2,1)S(1)} %copy-done.38, ...), custom_call_target="tpu_custom_call" | custom-call | flops 2684354560 | bytes 4083712 | tf_op jit(solution)/shard_map/pallas_call | solution.py:485
  292.5 4.4 collective-permute-done.28.g2
  299.0 4.2 shard_map.177
  305.8 3.1 convolution_convert_fusion.3
  310.1 8.7 %collective-permute-done.30.p1 = bf16[128,2048]{1,0:T(8,128)(2,1)S(1)} collective-permute-done((bf16[128,2048]{1,0:T(8,128)(2,1)S(1)}, bf16[128,2048]{1,0:T(8,128)(2,1)S(1)}, u32[]{:S(2)}, u32[]{:S(2)}) %collective-permute-start.30) | collective-permute-done | bytes 524320 | tf_op jit(solution)/shard_map/ppermute | solution.py:23
  332.4 5.1 %collective-permute-done.31.p2 = bf16[128,2048]{1,0:T(8,128)(2,1)S(1)} collective-permute-done((bf16[128,2048]{1,0:T(8,128)(2,1)}, bf16[128,2048]{1,0:T(8,128)(2,1)S(1)}, u32[]{:S(2)}, u32[]{:S(2)}) %collective-permute-start.31) | collective-permute-done | bytes 524320 | tf_op jit(solution)/shard_map/ppermute | solution.py:23
  337.5 11.1 %collective-permute-done.32.p3 = bf16[128,2048]{1,0:T(8,128)(2,1)S(1)} collective-permute-done((bf16[128,2048]{1,0:T(8,128)(2,1)}, bf16[128,2048]{1,0:T(8,128)(2,1)S(1)}, u32[]{:S(2)}, u32[]{:S(2)}) %collective-permute-start.32) | collective-permute-done | bytes 524320 | tf_op jit(solution)/shard_map/ppermute | solution.py:23
  348.6 3.0 collective-permute-start.40
  355.9 13.1 %collective-permute-done.38 = bf16[128,512]{1,0:T(8,128)(2,1)S(1)} collective-permute-done((bf16[128,512]{1,0:T(8,128)(2,1)S(1)}, bf16[128,512]{1,0:T(8,128)(2,1)S(1)}, u32[]{:S(2)}, u32[]{:S(2)}) %collective-permute-start.38) | collective-permute-done | bytes 131104 | tf_op jit(solution)/shard_map/ppermute | solution.py:23
  369.0 4.7 %collective-permute-done.39 = bf16[128,512]{1,0:T(8,128)(2,1)S(1)} collective-permute-done((bf16[128,512]{1,0:T(8,128)(2,1)S(1)}, bf16[128,512]{1,0:T(8,128)(2,1)S(1)}, u32[]{:S(2)}, u32[]{:S(2)}) %collective-permute-start.39) | collective-permute-done | bytes 131104 | tf_op jit(solution)/shard_map/ppermute | solution.py:23
  377.5 3.2 collective-permute-start.42
  380.8 2.6 collective-permute-start.49
  387.5 3.3 collective-permute-done.49
  398.5 2.7 collective-permute-done.43
  406.2 3.4 collective-permute-start.46
  409.6 6.7 %collective-permute-done.47 = bf16[256,640]{1,0:T(8,128)(2,1)S(1)} collective-permute-done((bf16[256,640]{1,0:T(8,128)(2,1)S(1)}, bf16[256,640]{1,0:T(8,128)(2,1)S(1)}, u32[]{:S(2)}, u32[]{:S(2)}) %collective-permute-start.47) | collective-permute-done | bytes 327712 | tf_op jit(solution)/shard_map/ppermute | solution.py:23
  416.5 4.8 %collective-permute-done.46 = bf16[256,512]{0,1:T(8,128)(2,1)S(1)} collective-permute-done((bf16[256,512]{0,1:T(8,128)(2,1)S(1)}, bf16[256,512]{0,1:T(8,128)(2,1)S(1)}, u32[]{:S(2)}, u32[]{:S(2)}) %collective-permute-start.46) | collective-permute-done | bytes 262176 | tf_op jit(solution)/shard_map/ppermute | solution.py:23
  422.8 3.1 collective-permute-start.55
  426.2 4.5 collective-permute-done.54
  430.8 6.3 %collective-permute-done.55 = bf16[256,512]{0,1:T(8,128)(2,1)S(1)} collective-permute-done((bf16[256,512]{0,1:T(8,128)(2,1)S(1)}, bf16[256,512]{0,1:T(8,128)(2,1)S(1)}, u32[]{:S(2)}, u32[]{:S(2)}) %collective-permute-start.55) | collective-permute-done | bytes 262176 | tf_op jit(solution)/shard_map/ppermute | solution.py:23
  437.1 2.6 collective-permute-done.56
  442.7 5.2 %collective-permute-done.57 = bf16[256,512]{0,1:T(8,128)(2,1)S(1)} collective-permute-done((bf16[256,512]{0,1:T(8,128)(2,1)S(1)}, bf16[256,512]{0,1:T(8,128)(2,1)S(1)}, u32[]{:S(2)}, u32[]{:S(2)}) %collective-permute-start.57) | collective-permute-done | bytes 262176 | tf_op jit(solution)/shard_map/ppermute | solution.py:23
  448.0 3.0 convert_element_type.196
  451.1 3.5 slice_multiply_fusion
  455.8 3.6 collective-permute-start.53
  (385 shorter events, 161.8 us)
Async XLA Ops:
  7.2 56.7 %all-gather.5.cloned.1.call-start = ((), (), s32[]{:S(2)}) async-start(), calls=%async_computation.3 | async-start | bytes 2621440 | tf_op jit(solution)/shard_map/all_gather | solution.py:67
  13.4 12.0 %collective-permute-start.2 = (bf16[128,1024]{1,0:T(8,128)(2,1)}, bf16[128,1024]{1,0:T(8,128)(2,1)}, u32[]{:S(2)}, u32[]{:S(2)}) collective-permute-start(bf16[128,1024]{1,0:T(8,128)(2,1)} %pad_maximum_fusion.23), channel_id=1, source_target_pairs={{0,3},{1,2},{2,1},{3,0},{4,7},{5,6},{6,5},{7,4},{8,11},{9,10},{10,... | collective-permute-start | bytes 786440 | tf_op jit(solution)/shard_map/ppermute | solution.py:23
  25.5 15.7 %collective-permute-start.3 = (bf16[256,1152]{1,0:T(8,128)(2,1)}, bf16[256,1152]{1,0:T(8,128)(2,1)S(1)}, u32[]{:S(2)}, u32[]{:S(2)}) collective-permute-start(bf16[256,1152]{1,0:T(8,128)(2,1)} %get-tuple-element.130), channel_id=1, source_target_pairs={{0,2},{2,0},{16,18},{18,16},{1,3},{3,1},{17,19},{19,17},{4,6},{6,4... | collective-permute-start | bytes 1769480 | tf_op jit(solution)/shard_map/ppermute | solution.py:23
  27.2 16.5 %collective-permute-start.4 = (bf16[256,1152]{1,0:T(8,128)(2,1)S(1)}, bf16[256,1152]{1,0:T(8,128)(2,1)}, u32[]{:S(2)}, u32[]{:S(2)}) collective-permute-start(bf16[256,1152]{1,0:T(8,128)(2,1)S(1)} %get-tuple-element.131), channel_id=1, source_target_pairs={{0,18},{2,16},{16,2},{18,0},{1,19},{3,17},{17,3},{19,1},{4,22},{6,... | collective-permute-start | bytes 1769480 | tf_op jit(solution)/shard_map/ppermute | solution.py:23
  32.4 89.3 %all-gather.7.cloned.1.call-start = ((), (), s32[]{:S(2)}) async-start(), calls=%async_computation.5 | async-start | bytes 2621440 | tf_op jit(solution)/shard_map/all_gather | solution.py:67
  46.4 12.1 %collective-permute-start.5 = (bf16[2,512,1152]{2,1,0:T(8,128)(2,1)S(1)}, bf16[2,512,1152]{2,1,0:T(8,128)(2,1)S(1)}, u32[]{:S(2)}, u32[]{:S(2)}) collective-permute-start(bf16[2,512,1152]{2,1,0:T(8,128)(2,1)S(1)} %bitcast.53), channel_id=1, source_target_pairs={{0,1},{1,0},{2,3},{3,2},{4,5},{5,4},{6,7},{7,6},{8,9},{9,8},{10,11... | collective-permute-start | bytes 7077896 | tf_op jit(solution)/shard_map/ppermute | solution.py:23
  52.2 18.8 %collective-permute-start.10 = (bf16[704,512]{1,0:T(8,128)(2,1)}, bf16[704,512]{1,0:T(8,128)(2,1)}, u32[]{:S(2)}, u32[]{:S(2)}) collective-permute-start(bf16[704,512]{1,0:T(8,128)(2,1)} %get-tuple-element.142), channel_id=1, source_target_pairs={{0,18},{2,16},{16,2},{18,0},{1,19},{3,17},{17,3},{19,1},{4,22},{6,... | collective-permute-start | bytes 2162696 | tf_op jit(solution)/shard_map/ppermute | solution.py:23
  54.3 17.2 %collective-permute-start.9 = (bf16[704,512]{1,0:T(8,128)(2,1)}, bf16[704,512]{1,0:T(8,128)(2,1)}, u32[]{:S(2)}, u32[]{:S(2)}) collective-permute-start(bf16[704,512]{1,0:T(8,128)(2,1)} %get-tuple-element.141), channel_id=1, source_target_pairs={{0,2},{2,0},{16,18},{18,16},{1,3},{3,1},{17,19},{19,17},{4,6},{6,4... | collective-permute-start | bytes 2162696 | tf_op jit(solution)/shard_map/ppermute | solution.py:23
  78.0 28.1 %collective-permute-start.11 = (bf16[1408,1024]{1,0:T(8,128)(2,1)}, bf16[1408,1024]{1,0:T(8,128)(2,1)}, u32[]{:S(2)}, u32[]{:S(2)}) collective-permute-start(bf16[1408,1024]{1,0:T(8,128)(2,1)} %pad_maximum_fusion.3), channel_id=1, source_target_pairs={{0,1},{1,0},{2,3},{3,2},{4,5},{5,4},{6,7},{7,6},{8,9},{9,8},{10,11... | collective-permute-start | bytes 8650760 | tf_op jit(solution)/shard_map/ppermute | solution.py:23
  79.0 64.9 %reduce-scatter.4.cloned.1.call-start = ((), (), s32[]{:S(2)}) async-start(), calls=%async_computation.4 | async-start | bytes 2621440 | tf_op jit(solution)/shard_map/reduce_scatter | solution.py:71
  79.0 34.6 %collective-permute-start.12 = (bf16[256,2816]{1,0:T(8,128)(2,1)}, bf16[256,2816]{1,0:T(8,128)(2,1)}, u32[]{:S(2)}, u32[]{:S(2)}) collective-permute-start(bf16[256,2816]{1,0:T(8,128)(2,1)} %get-tuple-element.159), channel_id=1, source_target_pairs={{0,2},{2,0},{16,18},{18,16},{1,3},{3,1},{17,19},{19,17},{4,6},{6,4... | collective-permute-start | bytes 4325384 | tf_op jit(solution)/shard_map/ppermute | solution.py:23
  80.5 35.1 %collective-permute-start.13 = (bf16[256,2816]{1,0:T(8,128)(2,1)}, bf16[256,2816]{1,0:T(8,128)(2,1)}, u32[]{:S(2)}, u32[]{:S(2)}) collective-permute-start(bf16[256,2816]{1,0:T(8,128)(2,1)} %get-tuple-element.160), channel_id=1, source_target_pairs={{0,18},{2,16},{16,2},{18,0},{1,19},{3,17},{17,3},{19,1},{4,22},{6,... | collective-permute-start | bytes 4325384 | tf_op jit(solution)/shard_map/ppermute | solution.py:23
  109.5 68.4 %all-gather.9.cloned.1.call-start = ((), (), s32[]{:S(2)}) async-start(), calls=%async_computation.6 | async-start | bytes 2621440 | tf_op jit(solution)/shard_map/all_gather | solution.py:67
  147.0 30.9 %collective-permute-start.17 = (bf16[1024,2816]{1,0:T(8,128)(2,1)}, bf16[1024,2816]{1,0:T(8,128)(2,1)}, u32[]{:S(2)}, u32[]{:S(2)}) collective-permute-start(bf16[1024,2816]{1,0:T(8,128)(2,1)} %pad_maximum_fusion.2.own_ref), channel_id=1, source_target_pairs={{0,1},{1,0},{2,3},{3,2},{4,5},{5,4},{6,7},{7,6},{8,9},{9,8},{10,11... | collective-permute-start | bytes 17301512 | tf_op jit(solution)/shard_map/ppermute | solution.py:23
  147.1 81.8 %reduce-scatter.6.cloned.1.call-start = ((), (), s32[]{:S(2)}) async-start(), calls=%async_computation.7 | async-start | bytes 2621440 | tf_op jit(solution)/shard_map/reduce_scatter | solution.py:71
  149.0 12.4 %collective-permute-start.16 = (bf16[512,1024]{1,0:T(8,128)(2,1)S(1)}, bf16[512,1024]{1,0:T(8,128)(2,1)S(1)}, u32[]{:S(2)}, u32[]{:S(2)}) collective-permute-start(bf16[512,1024]{1,0:T(8,128)(2,1)S(1)} %get-tuple-element.304), channel_id=1, source_target_pairs={{0,1},{1,0},{2,3},{3,2},{4,5},{5,4},{6,7},{7,6},{8,9},{9,8},{10,11... | collective-permute-start | bytes 3145736 | tf_op jit(solution)/shard_map/ppermute | solution.py:23
  149.9 13.0 %collective-permute-start.14 = (bf16[512,1024]{1,0:T(8,128)(2,1)S(1)}, bf16[512,1024]{1,0:T(8,128)(2,1)S(1)}, u32[]{:S(2)}, u32[]{:S(2)}) collective-permute-start(bf16[512,1024]{1,0:T(8,128)(2,1)S(1)} %pad_maximum_fusion.13), channel_id=1, source_target_pairs={{0,1},{1,0},{2,3},{3,2},{4,5},{5,4},{6,7},{7,6},{8,9},{9,8},{10,11... | collective-permute-start | bytes 3145736 | tf_op jit(solution)/shard_map/ppermute | solution.py:23
  150.8 9.4 %collective-permute-start.15 = (bf16[512,512]{1,0:T(8,128)(2,1)S(1)}, bf16[512,512]{1,0:T(8,128)(2,1)S(1)}, u32[]{:S(2)}, u32[]{:S(2)}) collective-permute-start(bf16[512,512]{1,0:T(8,128)(2,1)S(1)} %copy-done.26), channel_id=1, source_target_pairs={{0,1},{1,0},{2,3},{3,2},{4,5},{5,4},{6,7},{7,6},{8,9},{9,8},{10,11... | collective-permute-start | bytes 1572872 | tf_op jit(solution)/shard_map/ppermute | solution.py:23
  198.9 12.4 %collective-permute-start.19 = (bf16[512,2816]{1,0:T(8,128)(2,1)}, bf16[512,2816]{1,0:T(8,128)(2,1)}, u32[]{:S(2)}, u32[]{:S(2)}) collective-permute-start(bf16[512,2816]{1,0:T(8,128)(2,1)} %get-tuple-element.172), channel_id=1, source_target_pairs={{0,1},{1,0},{2,3},{3,2},{4,5},{5,4},{6,7},{7,6},{8,9},{9,8},{10,11... | collective-permute-start | bytes 8650760 | tf_op jit(solution)/shard_map/ppermute | solution.py:23
  198.9 120.7 %reduce-scatter.8.cloned.1.call-start = ((), (), s32[]{:S(2)}) async-start(), calls=%async_computation.8 | async-start | bytes 9191424 | tf_op jit(solution)/shard_map/reduce_scatter | solution.py:614
  201.5 9.8 %collective-permute-start.18 = (bf16[512,1024]{1,0:T(8,128)(2,1)S(1)}, bf16[512,1024]{1,0:T(8,128)(2,1)S(1)}, u32[]{:S(2)}, u32[]{:S(2)}) collective-permute-start(bf16[512,1024]{1,0:T(8,128)(2,1)S(1)} %pad_maximum_fusion.15), channel_id=1, source_target_pairs={{0,1},{1,0},{2,3},{3,2},{4,5},{5,4},{6,7},{7,6},{8,9},{9,8},{10,11... | collective-permute-start | bytes 3145736 | tf_op jit(solution)/shard_map/ppermute | solution.py:23
  228.9 219.1 %all-gather.11.cloned.1.call-start = ((), (), s32[]{:S(2)}) async-start(), calls=%async_computation.9 | async-start | bytes 4866048 | tf_op jit(solution)/shard_map/all_gather | solution.py:669
  233.7 14.8 %collective-permute-start.21 = (bf16[128,2048]{1,0:T(8,128)(2,1)S(1)}, bf16[128,2048]{1,0:T(8,128)(2,1)S(1)}, u32[]{:S(2)}, u32[]{:S(2)}) collective-permute-start(bf16[128,2048]{1,0:T(8,128)(2,1)S(1)} %get-tuple-element.207.b0), channel_id=1, source_target_pairs={{0,4},{4,0},{8,12},{12,8},{1,5},{5,1},{9,13},{13,9},{2,6},{6,2},{1... | collective-permute-start | bytes 1572872 | tf_op jit(solution)/shard_map/ppermute | solution.py:23
  233.9 25.1 %collective-permute-start.22 = (bf16[128,2048]{1,0:T(8,128)(2,1)S(1)}, bf16[128,2048]{1,0:T(8,128)(2,1)S(1)}, u32[]{:S(2)}, u32[]{:S(2)}) collective-permute-start(bf16[128,2048]{1,0:T(8,128)(2,1)S(1)} %get-tuple-element.207.b0), channel_id=1, source_target_pairs={{0,8},{4,12},{8,0},{12,4},{1,9},{5,13},{9,1},{13,5},{2,10},{6,14},... | collective-permute-start | bytes 1572872 | tf_op jit(solution)/shard_map/ppermute | solution.py:23
  236.0 25.6 %collective-permute-start.23 = (bf16[128,2048]{1,0:T(8,128)(2,1)S(1)}, bf16[128,2048]{1,0:T(8,128)(2,1)S(1)}, u32[]{:S(2)}, u32[]{:S(2)}) collective-permute-start(bf16[128,2048]{1,0:T(8,128)(2,1)S(1)} %get-tuple-element.207.b0), channel_id=1, source_target_pairs={{0,12},{4,8},{8,4},{12,0},{1,13},{5,9},{9,5},{13,1},{2,14},{6,10},... | collective-permute-start | bytes 1572872 | tf_op jit(solution)/shard_map/ppermute | solution.py:23
  261.6 15.1 %collective-permute-start.24 = (bf16[128,2048]{1,0:T(8,128)(2,1)S(1)}, bf16[128,2048]{1,0:T(8,128)(2,1)S(1)}, u32[]{:S(2)}, u32[]{:S(2)}) collective-permute-start(bf16[128,2048]{1,0:T(8,128)(2,1)S(1)} %get-tuple-element.184), channel_id=1, source_target_pairs={{0,4},{4,0},{8,12},{12,8},{1,5},{5,1},{9,13},{13,9},{2,6},{6,2},{1... | collective-permute-start | bytes 1572872 | tf_op jit(solution)/shard_map/ppermute | solution.py:23
  261.6 15.1 %collective-permute-start.25 = (bf16[128,2048]{1,0:T(8,128)(2,1)S(1)}, bf16[128,2048]{1,0:T(8,128)(2,1)S(1)}, u32[]{:S(2)}, u32[]{:S(2)}) collective-permute-start(bf16[128,2048]{1,0:T(8,128)(2,1)S(1)} %get-tuple-element.185), channel_id=1, source_target_pairs={{0,12},{4,8},{8,4},{12,0},{1,13},{5,9},{9,5},{13,1},{2,14},{6,10},... | collective-permute-start | bytes 1572872 | tf_op jit(solution)/shard_map/ppermute | solution.py:23
  276.8 13.9 %collective-permute-start.26 = (bf16[128,2048]{1,0:T(8,128)(2,1)S(1)}, bf16[128,2048]{1,0:T(8,128)(2,1)S(1)}, u32[]{:S(2)}, u32[]{:S(2)}) collective-permute-start(bf16[128,2048]{1,0:T(8,128)(2,1)S(1)} %get-tuple-element.196), channel_id=1, source_target_pairs={{0,8},{4,12},{8,0},{12,4},{1,9},{5,13},{9,1},{13,5},{2,10},{6,14},... | collective-permute-start | bytes 1572872 | tf_op jit(solution)/shard_map/ppermute | solution.py:23
  304.7 14.1 %collective-permute-start.30 = (bf16[128,2048]{1,0:T(8,128)(2,1)S(1)}, bf16[128,2048]{1,0:T(8,128)(2,1)S(1)}, u32[]{:S(2)}, u32[]{:S(2)}) collective-permute-start(bf16[128,2048]{1,0:T(8,128)(2,1)S(1)} %get-tuple-element.289), channel_id=1, source_target_pairs={{0,4},{4,0},{8,12},{12,8},{1,5},{5,1},{9,13},{13,9},{2,6},{6,2},{1... | collective-permute-start | bytes 1572872 | tf_op jit(solution)/shard_map/ppermute | solution.py:23
  321.3 9.4 %collective-permute-start.36 = (bf16[512,1024]{1,0:T(8,128)(2,1)}, bf16[512,1024]{1,0:T(8,128)(2,1)}, u32[]{:S(2)}, u32[]{:S(2)}) collective-permute-start(bf16[512,1024]{1,0:T(8,128)(2,1)} %get-tuple-element.282), channel_id=1, source_target_pairs={{0,1},{1,0},{2,3},{3,2},{4,5},{5,4},{6,7},{7,6},{8,9},{9,8},{10,11... | collective-permute-start | bytes 3145736 | tf_op jit(solution)/shard_map/ppermute | solution.py:23
  321.3 16.2 %collective-permute-start.31 = (bf16[128,2048]{1,0:T(8,128)(2,1)}, bf16[128,2048]{1,0:T(8,128)(2,1)S(1)}, u32[]{:S(2)}, u32[]{:S(2)}) collective-permute-start(bf16[128,2048]{1,0:T(8,128)(2,1)} %get-tuple-element.288), channel_id=1, source_target_pairs={{0,8},{4,12},{8,0},{12,4},{1,9},{5,13},{9,1},{13,5},{2,10},{6,14},... | collective-permute-start | bytes 1572872 | tf_op jit(solution)/shard_map/ppermute | solution.py:23
  323.7 24.9 %collective-permute-start.32 = (bf16[128,2048]{1,0:T(8,128)(2,1)}, bf16[128,2048]{1,0:T(8,128)(2,1)S(1)}, u32[]{:S(2)}, u32[]{:S(2)}) collective-permute-start(bf16[128,2048]{1,0:T(8,128)(2,1)} %get-tuple-element.287), channel_id=1, source_target_pairs={{0,12},{4,8},{8,4},{12,0},{1,13},{5,9},{9,5},{13,1},{2,14},{6,10},... | collective-permute-start | bytes 1572872 | tf_op jit(solution)/shard_map/ppermute | solution.py:23
  325.1 23.5 %collective-permute-start.34 = (bf16[256,640]{1,0:T(8,128)(2,1)}, bf16[256,640]{1,0:T(8,128)(2,1)S(1)}, u32[]{:S(2)}, u32[]{:S(2)}) collective-permute-start(bf16[256,640]{1,0:T(8,128)(2,1)} %get-tuple-element.205), channel_id=1, source_target_pairs={{0,2},{2,0},{16,18},{18,16},{1,3},{3,1},{17,19},{19,17},{4,6},{6,4... | collective-permute-start | bytes 983048 | tf_op jit(solution)/shard_map/ppermute | solution.py:23
  326.6 22.0 %collective-permute-start.35 = (bf16[256,640]{1,0:T(8,128)(2,1)}, bf16[256,640]{1,0:T(8,128)(2,1)S(1)}, u32[]{:S(2)}, u32[]{:S(2)}) collective-permute-start(bf16[256,640]{1,0:T(8,128)(2,1)} %get-tuple-element.206), channel_id=1, source_target_pairs={{0,18},{2,16},{16,2},{18,0},{1,19},{3,17},{17,3},{19,1},{4,22},{6,... | collective-permute-start | bytes 983048 | tf_op jit(solution)/shard_map/ppermute | solution.py:23
  348.6 26.4 %collective-permute-start.40 = (bf16[256,640]{1,0:T(8,128)(2,1)S(1)}, bf16[256,640]{1,0:T(8,128)(2,1)S(1)}, u32[]{:S(2)}, u32[]{:S(2)}) collective-permute-start(bf16[256,640]{1,0:T(8,128)(2,1)S(1)} %copy-done.81), channel_id=1, source_target_pairs={{0,16},{2,18},{16,0},{18,2},{1,17},{3,19},{17,1},{19,3},{4,20},{6,... | collective-permute-start | bytes 983048 | tf_op jit(solution)/shard_map/ppermute | solution.py:23
  352.5 16.5 %collective-permute-start.38 = (bf16[128,512]{1,0:T(8,128)(2,1)S(1)}, bf16[128,512]{1,0:T(8,128)(2,1)S(1)}, u32[]{:S(2)}, u32[]{:S(2)}) collective-permute-start(bf16[128,512]{1,0:T(8,128)(2,1)S(1)} %get-tuple-element.328), channel_id=1, source_target_pairs={{0,2},{1,3},{2,0},{3,1},{4,6},{5,7},{6,4},{7,5},{8,10},{9,11},{10,... | collective-permute-start | bytes 393224 | tf_op jit(solution)/shard_map/ppermute | solution.py:23
  353.2 20.6 %collective-permute-start.39 = (bf16[128,512]{1,0:T(8,128)(2,1)S(1)}, bf16[128,512]{1,0:T(8,128)(2,1)S(1)}, u32[]{:S(2)}, u32[]{:S(2)}) collective-permute-start(bf16[128,512]{1,0:T(8,128)(2,1)S(1)} %get-tuple-element.327), channel_id=1, source_target_pairs={{0,3},{1,2},{2,1},{3,0},{4,7},{5,6},{6,5},{7,4},{8,11},{9,10},{10,... | collective-permute-start | bytes 393224 | tf_op jit(solution)/shard_map/ppermute | solution.py:23
  376.0 20.2 %collective-permute-start.41 = (bf16[256,640]{1,0:T(8,128)(2,1)S(1)}, bf16[256,640]{1,0:T(8,128)(2,1)}, u32[]{:S(2)}, u32[]{:S(2)}) collective-permute-start(bf16[256,640]{1,0:T(8,128)(2,1)S(1)} %add_convert_fusion.2), channel_id=1, source_target_pairs={{0,32},{32,0},{64,96},{96,64},{1,33},{33,1},{65,97},{97,65},{2,34}... | collective-permute-start | bytes 983048 | tf_op jit(solution)/shard_map/ppermute | solution.py:23
  377.5 21.0 %collective-permute-start.42 = (bf16[256,640]{1,0:T(8,128)(2,1)S(1)}, bf16[256,640]{1,0:T(8,128)(2,1)}, u32[]{:S(2)}, u32[]{:S(2)}) collective-permute-start(bf16[256,640]{1,0:T(8,128)(2,1)S(1)} %add_convert_fusion.2), channel_id=1, source_target_pairs={{0,64},{32,96},{64,0},{96,32},{1,65},{33,97},{65,1},{97,33},{2,66}... | collective-permute-start | bytes 983048 | tf_op jit(solution)/shard_map/ppermute | solution.py:23
  380.6 20.6 %collective-permute-start.43 = (bf16[256,640]{1,0:T(8,128)(2,1)S(1)}, bf16[256,640]{1,0:T(8,128)(2,1)}, u32[]{:S(2)}, u32[]{:S(2)}) collective-permute-start(bf16[256,640]{1,0:T(8,128)(2,1)S(1)} %add_convert_fusion.2), channel_id=1, source_target_pairs={{0,96},{32,64},{64,32},{96,0},{1,97},{33,65},{65,33},{97,1},{2,98}... | collective-permute-start | bytes 983048 | tf_op jit(solution)/shard_map/ppermute | solution.py:23
  380.8 10.0 %collective-permute-start.49 = (bf16[128,512]{1,0:T(8,128)(2,1)}, bf16[128,512]{1,0:T(8,128)(2,1)}, u32[]{:S(2)}, u32[]{:S(2)}) collective-permute-start(bf16[128,512]{1,0:T(8,128)(2,1)} %get-tuple-element.341), channel_id=1, source_target_pairs={{0,2},{1,3},{2,0},{3,1},{4,6},{5,7},{6,4},{7,5},{8,10},{9,11},{10,... | collective-permute-start | bytes 393224 | tf_op jit(solution)/shard_map/ppermute | solution.py:23
  384.6 9.3 %collective-permute-start.50 = (bf16[128,512]{1,0:T(8,128)(2,1)}, bf16[128,512]{1,0:T(8,128)(2,1)}, u32[]{:S(2)}, u32[]{:S(2)}) collective-permute-start(bf16[128,512]{1,0:T(8,128)(2,1)} %get-tuple-element.339), channel_id=1, source_target_pairs={{0,3},{1,2},{2,1},{3,0},{4,7},{5,6},{6,5},{7,4},{8,11},{9,10},{10,... | collective-permute-start | bytes 393224 | tf_op jit(solution)/shard_map/ppermute | solution.py:23
  390.8 11.7 %collective-permute-start.44 = (bf16[256,512]{0,1:T(8,128)(2,1)}, bf16[256,512]{0,1:T(8,128)(2,1)S(1)}, u32[]{:S(2)}, u32[]{:S(2)}) collective-permute-start(bf16[256,512]{0,1:T(8,128)(2,1)} %bitcast.18), channel_id=1, source_target_pairs={{0,2},{2,0},{16,18},{18,16},{1,3},{3,1},{17,19},{19,17},{4,6},{6,4... | collective-permute-start | bytes 786440 | tf_op jit(solution)/shard_map/ppermute | solution.py:23
  394.0 10.3 %collective-permute-start.45 = (bf16[256,512]{0,1:T(8,128)(2,1)S(1)}, bf16[256,512]{0,1:T(8,128)(2,1)S(1)}, u32[]{:S(2)}, u32[]{:S(2)}) collective-permute-start(bf16[256,512]{0,1:T(8,128)(2,1)S(1)} %bitcast.67), channel_id=1, source_target_pairs={{0,18},{2,16},{16,2},{18,0},{1,19},{3,17},{17,3},{19,1},{4,22},{6,... | collective-permute-start | bytes 786440 | tf_op jit(solution)/shard_map/ppermute | solution.py:23
  404.3 12.0 %collective-permute-start.47 = (bf16[256,640]{1,0:T(8,128)(2,1)S(1)}, bf16[256,640]{1,0:T(8,128)(2,1)S(1)}, u32[]{:S(2)}, u32[]{:S(2)}) collective-permute-start(bf16[256,640]{1,0:T(8,128)(2,1)S(1)} %add_convert_fusion.1), channel_id=1, source_target_pairs={{0,16},{2,18},{16,0},{18,2},{1,17},{3,19},{17,1},{19,3},{4,20},{6,... | collective-permute-start | bytes 983048 | tf_op jit(solution)/shard_map/ppermute | solution.py:23
  406.2 15.1 %collective-permute-start.46 = (bf16[256,512]{0,1:T(8,128)(2,1)S(1)}, bf16[256,512]{0,1:T(8,128)(2,1)S(1)}, u32[]{:S(2)}, u32[]{:S(2)}) collective-permute-start(bf16[256,512]{0,1:T(8,128)(2,1)S(1)} %bitcast.66), channel_id=1, source_target_pairs={{0,16},{2,18},{16,0},{18,2},{1,17},{3,19},{17,1},{19,3},{4,20},{6,... | collective-permute-start | bytes 786440 | tf_op jit(solution)/shard_map/ppermute | solution.py:23
  422.8 14.3 %collective-permute-start.55 = (bf16[256,512]{0,1:T(8,128)(2,1)S(1)}, bf16[256,512]{0,1:T(8,128)(2,1)S(1)}, u32[]{:S(2)}, u32[]{:S(2)}) collective-permute-start(bf16[256,512]{0,1:T(8,128)(2,1)S(1)} %fusion.33), channel_id=1, source_target_pairs={{0,64},{32,96},{64,0},{96,32},{1,65},{33,97},{65,1},{97,33},{2,66}... | collective-permute-start | bytes 786440 | tf_op jit(solution)/shard_map/ppermute | solution.py:23
  425.9 13.8 %collective-permute-start.56 = (bf16[256,512]{0,1:T(8,128)(2,1)S(1)}, bf16[256,512]{0,1:T(8,128)(2,1)S(1)}, u32[]{:S(2)}, u32[]{:S(2)}) collective-permute-start(bf16[256,512]{0,1:T(8,128)(2,1)S(1)} %fusion.33), channel_id=1, source_target_pairs={{0,96},{32,64},{64,32},{96,0},{1,97},{33,65},{65,33},{97,1},{2,98}... | collective-permute-start | bytes 786440 | tf_op jit(solution)/shard_map/ppermute | solution.py:23
  (104 other events, 669.6 us)
Sparse Core Ops, SparseCore 0:
  32.5 31.3 all-gather.4
  79.1 32.0 all-gather.6
  114.2 29.6 reduce-scatter.3
  147.2 30.7 all-gather.8
  199.0 29.8 reduce-scatter.5
  232.2 85.7 reduce-scatter.7
  320.5 85.3 all-gather.10

commit v3 on v2

--- a/solution.py
+++ b/solution.py
@@ -123,12 +123,13 @@
     return jnp.concatenate(in_order(parts, col), axis=0)
 
 
-def ring_halves(first, second, low, axis, *earlier):
-    shard = jnp.concatenate([first, second])
-    other = [trade_ring(first, 1), trade_ring(second, 3)]
-    other = jnp.concatenate(after(other, *earlier))
-    both = [pick(low, shard, other), pick(low, other, shard)]
-    return jnp.concatenate(both, axis=axis)
+def ring_send(halves):
+    return [trade_ring(halves[0], 1), trade_ring(halves[1], 3)]
+
+
+def ring_join(halves, got, low, axis):
+    shard, other = jnp.concatenate(halves), jnp.concatenate(got)
+    return jnp.concatenate([pick(low, shard, other), pick(low, other, shard)], axis=axis)
 
 
 def add_low(*terms):
@@ -187,8 +188,9 @@
     return lax.rsqrt(jnp.mean(values * values, axis=1, keepdims=True) + norm_eps)
 
 
-def add_and_norm(base_ref, part_ref, hidden_ref, normed_ref):
-    hidden = base_ref[...] + part_ref[...].astype(F32)
+def add_and_norm(base_ref, p0, p1, p2, p3, hidden_ref, normed_ref):
+    hidden = (p0[...].astype(F32) + p1[...].astype(F32)) + (p2[...].astype(F32) + p3[...].astype(F32))
+    hidden = base_ref[...] + hidden
     hidden_ref[...] = hidden
     normed_ref[...] = (hidden * scale_of(hidden)).astype(BF16)
 
@@ -205,9 +207,8 @@
     low_ref[...] = grad.astype(BF16)
 
 
-def norm_back_sum(values_ref, p0, p1, p2, p3, passed_ref, grad_ref):
-    weighted = (p0[...].astype(F32) + p1[...].astype(F32)) + (p2[...].astype(F32) + p3[...].astype(F32))
-    grad_ref[...] = norm_back(values_ref[...], weighted, passed_ref[...])
+def norm_back_high(values_ref, part_ref, passed_ref, grad_ref):
+    grad_ref[...] = norm_back(values_ref[...], part_ref[...].astype(F32), passed_ref[...])
 
 
 def turn(first, second, cosine, sine):
@@ -244,10 +245,10 @@
 
 
 def lay_keys(pairs, kt_ref, vt_ref, kn_ref, vn_ref):
-    size = pairs[0].shape[1] // 4
+    size = pairs.shape[2] // 4
     for block in range(4):
-        for m, pair in enumerate(pairs):
-            piece = pair[:, block * size : (block + 1) * size]
+        for m in range(4):
+            piece = pairs[m, :, block * size : (block + 1) * size]
             spot = slice(m * size, (m + 1) * size)
             kt_ref[block, :, spot] = piece[:HD]
             if vt_ref is not None:
@@ -257,79 +258,60 @@
             vn_ref[block, spot, :] = natural[:, HD:]
 
 
-def two_heads(ref, first, spot, size):
+def side_by_side(ref, first, count, depth, spot, size):
     return jnp.concatenate(
-        [ref[first : first + HD, pl.ds(spot, size)], ref[first + HD : first + 2 * HD, pl.ds(spot, size)]],
+        [ref[head * depth : (head + 1) * depth, spot : spot + size] for head in range(first, first + count)],
         axis=1,
     )
 
 
-def admitted(koff_ref, start, qpos, qstart, diagonal):
+def admitted(koff_ref, start, qpos, qstart, diagonal, count):
     keys = koff_ref[...] + start
     allowed = keys >= qstart
     if diagonal:
         allowed = allowed & (keys <= qpos)
-    return jnp.concatenate([allowed, allowed], axis=1)
+    return jnp.concatenate([allowed] * count, axis=1)
 
 
 def attend(
-    q_ref, p0, p1, p2, p3, koff_ref, qpos_ref, qstart_ref,
-    o_ref, low_ref, lse_ref, kt_ref, vt_ref, kn_ref, vn_ref,
+    q_ref, pairs_ref, koff_ref, qpos_ref, qstart_ref, o_ref, low_ref, lse_ref, kt_ref, vt_ref, kn_ref, vn_ref
 ):
     span = kn_ref.shape[1]
     size = span // 4
-    pairs = q_ref.shape[0] // (2 * HD)
-    lay_keys((p0, p1, p2, p3), kt_ref, vt_ref, kn_ref, vn_ref)
-
-    def one_block(block, carry):
-        spot = pl.multiple_of(block * size, size)
-        qpos = qpos_ref[:, pl.ds(spot, size)]
-        qstart = qstart_ref[:, pl.ds(spot, size)]
-        queries = [two_heads(q_ref, pair * 2 * HD, spot, size) for pair in range(pairs)]
-
-        def chunk(number, state, diagonal):
-            keys, values = kn_ref[number], vt_ref[number]
-            allowed = admitted(koff_ref, number * span, qpos, qstart, diagonal)
-            fresh = []
-            for query, (top, total, accum) in zip(queries, state):
-                scores = jnp.dot(keys, query, preferred_element_type=F32)
-                scores = jnp.where(allowed, scores, masked)
-                new_top = jnp.maximum(top, jnp.max(scores, axis=0, keepdims=True))
-                weights = jnp.exp(scores - new_top)
-                shrink = jnp.exp(top - new_top)
-                total = total * shrink + jnp.sum(weights, axis=0, keepdims=True)
-                accum = accum * shrink + jnp.dot(
-                    values, weights.astype(BF16), preferred_element_type=F32
-                )
-                fresh.append((new_top, total, accum))
-            return tuple(fresh)
-
-        empty = (
-            jnp.full((1, 2 * size), masked, F32),
-            jnp.zeros((1, 2 * size), F32),
-            jnp.zeros((HD, 2 * size), F32),
-        )
-        state = chunk(block, (empty,) * pairs, True)
-        state = lax.fori_loop(0, block, lambda number, state: chunk(number, state, False), state)
-        for pair, (top, total, accum) in enumerate(state):
-            result = accum / total
-            lse = top + jnp.log(total)
-            for part in range(2):
-                first = (2 * pair + part) * HD
-                piece = result[:, part * size : (part + 1) * size]
-                o_ref[first : first + HD, pl.ds(spot, size)] = piece
-                low_ref[first : first + HD, pl.ds(spot, size)] = piece.astype(BF16)
-                lse_ref[2 * pair + part : 2 * pair + part + 1, pl.ds(spot, size)] = lse[
-                    :, part * size : (part + 1) * size
-                ]
-        return carry
-
-    lax.fori_loop(0, 4, one_block, 0)
+    heads = q_ref.shape[0] // HD
+    lay_keys(pairs_ref, kt_ref, vt_ref, kn_ref, vn_ref)
+    for block in range(4):
+        spot = block * size
+        qpos, qstart = qpos_ref[:, spot : spot + size], qstart_ref[:, spot : spot + size]
+        query = side_by_side(q_ref, 0, heads, HD, spot, size)
+        top = jnp.full((1, heads * size), masked, F32)
+        total = jnp.zeros((1, heads * size), F32)
+        accum = jnp.zeros((HD, heads * size), F32)
+        for number in (block, *range(block)):
+            scores = jnp.dot(kn_ref[number], query, preferred_element_type=F32)
+            allowed = admitted(koff_ref, number * span, qpos, qstart, number == block, heads)
+            scores = jnp.where(allowed, scores, masked)
+            new_top = jnp.maximum(top, jnp.max(scores, axis=0, keepdims=True))
+            weights = jnp.exp(scores - new_top)
+            shrink = jnp.exp(top - new_top)
+            total = total * shrink + jnp.sum(weights, axis=0, keepdims=True)
+            accum = accum * shrink + jnp.dot(
+                vt_ref[number], weights.astype(BF16), preferred_element_type=F32
+            )
+            top = new_top
+        result = accum / total
+        lse = top + jnp.log(total)
+        for head in range(heads):
+            piece = result[:, head * size : (head + 1) * size]
+            rows = slice(head * HD, (head + 1) * HD)
+            o_ref[rows, spot : spot + size] = piece
+            low_ref[rows, spot : spot + size] = piece.astype(BF16)
+            lse_ref[head : head + 1, spot : spot + size] = lse[:, head * size : (head + 1) * size]
 
 
 def attend_back(
-    q_ref, p0, p1, p2, p3, koff_ref, qpos_ref, qstart_ref, o_ref, lse_ref, go_ref, cos_ref, sin_ref, *refs,
-    first_pair, pairs, last_call,
+    q_ref, pairs_ref, koff_ref, qpos_ref, qstart_ref, o_ref, lse_ref, go_ref, cos_ref, sin_ref, *refs,
+    first, count, last_call,
 ):
     if last_call:
         gk_in, gv_in, gq_ref, g0, g1, g2, g3, kt_ref, kn_ref, vn_ref, gk_ref, gv_ref = refs
@@ -337,62 +319,39 @@
         gq_ref, gk_ref, gv_ref, kt_ref, kn_ref, vn_ref = refs
     span = kn_ref.shape[1]
     size = span // 4
-    lay_keys((p0, p1, p2, p3), kt_ref, None, kn_ref, vn_ref)
+    lay_keys(pairs_ref, kt_ref, None, kn_ref, vn_ref)
     gk_ref[...] = gk_in[...] if last_call else jnp.zeros_like(gk_ref)
     gv_ref[...] = gv_in[...] if last_call else jnp.zeros_like(gv_ref)
     last = (((1,), (1,)), ((), ()))
-
-    def one_block(block, carry):
-        spot = pl.multiple_of(block * size, size)
-        qpos = qpos_ref[:, pl.ds(spot, size)]
-        qstart = qstart_ref[:, pl.ds(spot, size)]
-        cosine, sine = cos_ref[:, pl.ds(spot, size)], sin_ref[:, pl.ds(spot, size)]
-        known = []
-        for pair in range(first_pair, first_pair + pairs):
-            first = pair * 2 * HD
-            query, grad_out = two_heads(q_ref, first, spot, size), two_heads(go_ref, first, spot, size)
-            mixed = two_heads(o_ref, first, spot, size)
-            delta = jnp.sum(grad_out.astype(F32) * mixed, axis=0, keepdims=True)
-            lse = jnp.concatenate(
-                [lse_ref[2 * pair + part : 2 * pair + part + 1, pl.ds(spot, size)] for part in range(2)],
-                axis=1,
+    for block in range(4):
+        spot = block * size
+        here = slice(spot, spot + size)
+        qpos, qstart = qpos_ref[:, here], qstart_ref[:, here]
+        cosine, sine = cos_ref[:, here], sin_ref[:, here]
+        pick_heads = lambda ref, depth: side_by_side(ref, first, count, depth, spot, size)
+        query, grad_out = pick_heads(q_ref, HD), pick_heads(go_ref, HD)
+        lse = pick_heads(lse_ref, 1)
+        delta = jnp.sum(grad_out.astype(F32) * pick_heads(o_ref, HD), axis=0, keepdims=True)
+        grad_query = jnp.zeros((HD, count * size), F32)
+        for number in (block, *range(block)):
+            scores = jnp.dot(kn_ref[number], query, preferred_element_type=F32)
+            allowed = admitted(koff_ref, number * span, qpos, qstart, number == block, count)
+            probs = jnp.exp(jnp.where(allowed, scores - lse, masked))
+            grad_probs = jnp.dot(vn_ref[number], grad_out, preferred_element_type=F32)
+            grad_scores = (probs * (grad_probs - delta)).astype(BF16)
+            gv_ref[number] += lax.dot_general(
+                grad_out, probs.astype(BF16), last, preferred_element_type=F32
             )
-            known.append((query, grad_out, delta, lse))
-
-        def chunk(number, state, diagonal):
-            keys, values, turned_keys = kn_ref[number], vn_ref[number], kt_ref[number]
-            allowed = admitted(koff_ref, number * span, qpos, qstart, diagonal)
-            fresh = []
-            grad_keys, grad_values = gk_ref[number], gv_ref[number]
-            for (query, grad_out, delta, lse), grad_query in zip(known, state):
-                scores = jnp.dot(keys, query, preferred_element_type=F32)
-                probs = jnp.exp(jnp.where(allowed, scores - lse, masked))
-                grad_probs = jnp.dot(values, grad_out, preferred_element_type=F32)
-                grad_scores = (probs * (grad_probs - delta)).astype(BF16)
-                grad_values = grad_values + lax.dot_general(
-                    grad_out, probs.astype(BF16), last, preferred_element_type=F32
-                )
-                grad_keys = grad_keys + lax.dot_general(
-                    query, grad_scores, last, preferred_element_type=F32
-                )
-                fresh.append(
-                    grad_query + jnp.dot(turned_keys, grad_scores, preferred_element_type=F32)
-                )
-            gk_ref[number] = grad_keys
-            gv_ref[number] = grad_values
-            return tuple(fresh)
-
-        state = chunk(block, (jnp.zeros((HD, 2 * size), F32),) * pairs, True)
-        state = lax.fori_loop(0, block, lambda number, state: chunk(number, state, False), state)
-        for head in range(2 * pairs):
-            grad = state[head // 2][:, head % 2 * size : (head % 2 + 1) * size] * HD**-0.5
-            half = HD // 2
-            first, second = turn(grad[:half], grad[half:], cosine, -sine)
-            gq_ref[head * HD : head * HD + half, pl.ds(spot, size)] = first.astype(BF16)
-            gq_ref[head * HD + half : (head + 1) * HD, pl.ds(spot, size)] = second.astype(BF16)
-        return carry
-
-    lax.fori_loop(0, 4, one_block, 0)
+            gk_ref[number] += lax.dot_general(query, grad_scores, last, preferred_element_type=F32)
+            grad_query = grad_query + jnp.dot(
+                kt_ref[number], grad_scores, preferred_element_type=F32
+            )
+        half = HD // 2
+        for head in range(count):
+            grad = grad_query[:, head * size : (head + 1) * size] * HD**-0.5
+            upper, lower = turn(grad[:half], grad[half:], cosine, -sine)
+            gq_ref[head * HD : head * HD + half, here] = upper.astype(BF16)
+            gq_ref[head * HD + half : (head + 1) * HD, here] = lower.astype(BF16)
     if last_call:
         for block in range(4):
             for m, ref in enumerate((g0, g1, g2, g3)):
@@ -476,20 +435,56 @@
         out_ref[:, pl.ds(spot, size)] = piece.astype(BF16)
 
 
-def kernel_call(body, out_shape, operands, flops, scratch=(), scalars=0, outside=()):
+def kernel_call(body, out_shape, operands, flops, scratch=(), scalars=0, outside=(), staged=(), mib=48):
     moved = sum(x.size * x.dtype.itemsize for x in operands)
+    count = len(operands)
     spaces = [
-        pltpu.SMEM if i < scalars else pl.ANY if i in outside else pltpu.VMEM
-        for i in range(len(operands))
+        pltpu.SMEM if i < scalars else pl.ANY if i in outside or i in staged else pltpu.VMEM
+        for i in range(count)
     ]
+    if staged:
+        held = [pltpu.VMEM(operands[i].shape, operands[i].dtype) for i in staged]
+        scratch = [*scratch, *held, pltpu.SemaphoreType.DMA((len(staged),))]
+
+        def whole(*refs):
+            refs, buffers, sems = list(refs[: -len(staged) - 1]), refs[-len(staged) - 1 : -1], refs[-1]
+            copies = [
+                pltpu.make_async_copy(refs[i], buffer, sems.at[n])
+                for n, (i, buffer) in enumerate(zip(staged, buffers))
+            ]
+            for copy in copies:
+                copy.start()
+            for copy in copies:
+                copy.wait()
+            for i, buffer in zip(staged, buffers):
+                refs[i] = buffer
+            body(*refs)
+    else:
+        whole = body
+    out_specs = jax.tree.map(lambda _: pl.BlockSpec(memory_space=pltpu.VMEM), out_shape)
+    return pl.pallas_call(
+        whole,
+        out_shape=out_shape,
+        in_specs=[pl.BlockSpec(memory_space=space) for space in spaces],
+        out_specs=out_specs,
+        scratch_shapes=list(scratch),
+        compiler_params=pltpu.CompilerParams(vmem_limit_bytes=mib * 1024 * 1024),
+        cost_estimate=pl.CostEstimate(flops=flops, bytes_accessed=moved, transcendentals=0),
+    )(*operands)
+
+
+def rows_call(body, kinds, operands, steps=2):
+    rows, width = operands[0].shape
+    block = pl.BlockSpec((rows // steps, width), lambda i: (i, 0))
+    out_shape = tuple(jax.ShapeDtypeStruct((rows, width), kind) for kind in kinds)
+    moved = sum(x.size * x.dtype.itemsize for x in operands)
     return pl.pallas_call(
         body,
         out_shape=out_shape,
-        in_specs=[pl.BlockSpec(memory_space=space) for space in spaces],
-        out_specs=jax.tree.map(lambda _: pl.BlockSpec(memory_space=pltpu.VMEM), out_shape),
-        scratch_shapes=list(scratch),
-        compiler_params=pltpu.CompilerParams(vmem_limit_bytes=48 * 1024 * 1024),
-        cost_estimate=pl.CostEstimate(flops=flops, bytes_accessed=moved, transcendentals=0),
+        grid=(steps,),
+        in_specs=[block] * len(operands),
+        out_specs=(block,) * len(kinds),
+        cost_estimate=pl.CostEstimate(flops=0, bytes_accessed=moved, transcendentals=0),
     )(*operands)
 
 
@@ -524,28 +519,30 @@
 
     flat_qkv = w_qkv.reshape(w_qkv.shape[0], -1)
     qkv_out = jnp.concatenate([(flat_qkv * attn_gain[:, None]).astype(BF16), w_out], axis=1)
-    (inputs, cot_rows), alongside = to_full_width(
-        [tokens_in, cotangent], col, cosine, sine, key_offset, qpos, qstart, *cut(qkv_out, 2, 0)
+    (inputs,), alongside = to_full_width(
+        [tokens_in], col, cosine, sine, key_offset, qpos, qstart, *cut(qkv_out, 2, 0)
     )
     cosine, sine, key_offset, qpos, qstart, qkv_out_first, qkv_out_second = alongside
     inputs = inputs.astype(F32)
     normed_one = (inputs * scale_of(inputs)).astype(BF16)
     rows_one = gather_row(normed_one)
 
-    mine = ring_halves(qkv_out_first, qkv_out_second, low, 0).reshape(2, *qkv_out.shape)
+    qkv_out_halves = [qkv_out_first, qkv_out_second]
+    mine = ring_join(qkv_out_halves, lax.optimization_barrier(ring_send(qkv_out_halves)), low, 0)
+    mine = mine.reshape(2, *qkv_out.shape)
     theirs = trade_core(mine)
-    down_halves = [after(v, normed_one) for v in cut(w_down, 2, 0)]
+    (cot_rows,), _ = to_full_width([after(cotangent, mine)], col)
     scaled = lambda v: (v * mlp_gain[:, None]).astype(BF16)
     gate_up = jnp.concatenate([scaled(w_gate), scaled(w_up)], axis=1)
-    gu_halves = [after(v, mine) for v in cut(gate_up, 2, 0)]
+    gu_halves = [after(v, normed_one) for v in cut(gate_up, 2, 0)]
     full_out = jnp.concatenate(
         [mine[0, :, cut_at:], mine[1, :, cut_at:], theirs[0, :, cut_at:], theirs[1, :, cut_at:]],
         axis=1,
     )
-    rows_one, gu_halves, full_out = lax.optimization_barrier((rows_one, gu_halves, full_out))
-    grad_rows = gather_row(after(cot_rows, rows_one))
-    down_mine = ring_halves(*down_halves, low, 1, rows_one)
-    gu_mine = ring_halves(*gu_halves, low, 0)
+    rows_one, gu_halves, full_out, cot_rows = lax.optimization_barrier(
+        (rows_one, gu_halves, full_out, cot_rows)
+    )
+    gu_got = ring_send(gu_halves)
 
     shape = lambda kind, *dims: jax.ShapeDtypeStruct(dims, kind)
     scratch = lambda kind, *dims: pltpu.VMEM(dims, kind)
@@ -556,30 +553,29 @@
         (shape(BF16, heads * HD, span), shape(BF16, 2 * HD, span)),
         (rows_one, mine, theirs, cosine, sine),
         matmul(span, width, cut_at),
-    )
-    all_pairs = [pairs] + [trade_col(pairs, m) for m in (1, 2, 3)]
-    all_pairs = lax.optimization_barrier((all_pairs, down_mine))[0]
-    down_theirs = trade_core(after(down_mine, all_pairs))
+        staged=(0,),
+    )
+    grad_rows = gather_row(after(cot_rows, query))
+    all_pairs = jnp.stack([pairs] + [trade_col(pairs, m) for m in (1, 2, 3)])
 
     flops = 2 * matmul(heads * span, HD, group)
     keys_shape = (4, HD, span), (4, span, HD)
     mixed, mixed_low, lse = kernel_call(
         attend,
         (shape(F32, heads * HD, span), shape(BF16, heads * HD, span), shape(F32, heads, span)),
-        (query, *all_pairs, key_offset, qpos, qstart),
+        (query, all_pairs, key_offset, qpos, qstart),
         flops,
         scratch=[scratch(BF16, *keys_shape[i]) for i in (0, 0, 1, 1)],
     )
-    mixed_low = after(mixed_low, down_theirs)
-    full_down = jnp.concatenate([down_mine, down_theirs], axis=1)
     branch = product(mixed_low, full_out, ((0,), (0,)), BF16)
+    gu_mine = ring_join(gu_halves, after(gu_got, branch), low, 0)
+    down_halves = [after(v, branch, gu_got) for v in cut(w_down, 2, 0)]
+    down_got = ring_send(down_halves)
+    branch_parts = after(collect_row(row_parts(branch, row)), gu_mine, down_got)
+    hidden, normed_two = rows_call(add_and_norm, (F32, BF16), (inputs, *branch_parts))
+    down_mine = ring_join(down_halves, after(down_got, hidden), low, 1)
+    full_down = jnp.concatenate([down_mine, trade_core(down_mine)], axis=1)
     grad_inner = product(grad_rows, full_down, ((1,), (1,)))
-    hidden, normed_two = kernel_call(
-        add_and_norm,
-        (shape(F32, *inputs.shape), shape(BF16, *inputs.shape)),
-        (inputs, after(sum_row(branch), grad_inner, gu_mine)),
-        0,
-    )
     gu_theirs = trade_core(after(gu_mine, hidden))
     rows_two = gather_row(normed_two)
 
@@ -612,12 +608,7 @@
     mlp_sums = jnp.concatenate([token_sum(two_half, pair_both), token_sum(cot_half, inner_both)], axis=1)
     grad_n2, mlp_sums = lax.optimization_barrier((sum_row(part_two), mlp_sums))
     mlp_sums = lax.psum_scatter(mlp_sums, ("xh", "xl", "z"), scatter_dimension=0, tiled=True)
-    grad_hidden, grad_low = kernel_call(
-        norm_back_low,
-        (shape(F32, *hidden.shape), shape(BF16, *hidden.shape)),
-        (hidden, grad_n2, cot_rows),
-        0,
-    )
+    grad_hidden, grad_low = rows_call(norm_back_low, (F32, BF16), (hidden, grad_n2, cot_rows))
     branch_parts = spread_row(grad_low)
     result_parts = row_parts(product(inner, full_down, ((1,), (0,)), BF16), row)
     branch_parts, result_parts = lax.optimization_barrier((branch_parts, result_parts))
@@ -629,85 +620,80 @@
         scalars=1,
     )
     pair_shape = shape(BF16, 2 * HD, span)
-    known = (query, *all_pairs, key_offset, qpos, qstart, mixed, lse, grad_heads, cosine, sine)
+    known = (query, all_pairs, key_offset, qpos, qstart, mixed, lse, grad_heads, cosine, sine)
     half_heads = shape(BF16, heads * HD // 2, span)
     keys_scratch = [scratch(BF16, *keys_shape[i]) for i in (0, 1, 1)]
     key_sums = (shape(F32, *keys_shape[0]),) * 2
-    split = functools.partial(attend_back, pairs=heads // 4)
+    split = functools.partial(attend_back, count=heads // 2)
     result_near = trade_near(result_parts, trade_row)
     gq_first, *key_grads = kernel_call(
-        functools.partial(split, first_pair=0, last_call=False),
+        functools.partial(split, first=0, last_call=False),
         (half_heads,) + key_sums,
         known,
         flops * 5 // 4,
         scratch=keys_scratch,
+        staged=(1,),
     )
     key_grads, result_near = lax.optimization_barrier((key_grads, result_near))
     result_far = trade_row(after(result_parts[2], result_near), 2)
     gq_last, *grad_pairs = kernel_call(
-        functools.partial(split, first_pair=heads // 4, last_call=True),
+        functools.partial(split, first=heads // 2, last_call=True),
         (half_heads,) + (pair_shape,) * 4,
         (*known, *key_grads),
         flops * 5 // 4,
         scratch=keys_scratch + [scratch(F32, *keys_shape[0])] * 2,
-    )
-    grad_pairs, result_far = lax.optimization_barrier((grad_pairs, result_far))
+        staged=(1,),
+    )
     grad_pairs = [grad_pairs[0]] + [trade_col(grad_pairs[m], m) for m in (1, 2, 3)]
+    grad_pairs = lax.optimization_barrier(grad_pairs)
     grad_qkv, part_one = kernel_call(
         project_back,
         (shape(BF16, cut_at, span), shape(BF16, span, width)),
         (gq_first, gq_last, *grad_pairs, cosine, sine, mine, theirs),
         matmul(span, width, cut_at),
     )
-    one_parts = collect_row(row_parts(part_one, row))
+    qkv_both = both_cores(grad_qkv, 1)
     branch_rows = jnp.concatenate(in_order(after(branch_parts, grad_qkv), row))
     branch_half = half_of(branch_rows)
-    qkv_both = both_cores(grad_qkv, 1)
     qkv_sum = product(one_half, qkv_both, ((0,), (1,)), BF16).reshape(2, width // 4, -1)
-    qkv_parts, mlp_sums = after((ring_parts([qkv_sum], low, high), mlp_sums), one_parts[1])
-    qkv_near = trade_near(qkv_parts, trade_ring)
-    mlp_total = lax.all_gather(mlp_sums, ("xh", "z"), axis=0, tiled=True).astype(F32)
-    one_parts, qkv_near, branch_half = lax.optimization_barrier((one_parts, qkv_near, branch_half))
-
-    grad_in = kernel_call(
-        norm_back_sum, shape(F32, *inputs.shape), (inputs, *one_parts, grad_hidden), 0
-    )
     out_sum = product(branch_half, heads_both, ((0,), (1,)), BF16).reshape(2, width // 4, -1)
-    qkv_far = trade_ring(after(qkv_parts[2], qkv_near), 2)
-    grad_in, qkv_far, out_sum = lax.optimization_barrier((to_blocks(grad_in, col), qkv_far, out_sum))
-    qkv_total = add_low(qkv_parts[0], *qkv_near, qkv_far)
-    out_parts = ring_parts([out_sum], low, high)
-    out_near = trade_near(out_parts, trade_ring)
-    qkv_total = exchange([qkv_total] * 4, trade_deep)
-    qkv_total, out_near = lax.optimization_barrier((qkv_total, out_near))
-    out_far = trade_ring(after(out_parts[2], out_near), 2)
-    qkv_total = ring_gather(qkv_total, high).astype(F32)
+    both_parts = deep_parts(jnp.concatenate([qkv_sum, out_sum], axis=2), deep)
+    both_parts, mlp_sums = lax.optimization_barrier((both_parts, mlp_sums))
+    both_sums = exchange(both_parts, trade_deep)
+    rows_here = mlp_sums.shape[0]
+    grad_n1 = sum_row(part_one)
+    (grad_in,) = rows_call(norm_back_high, (F32,), (inputs, grad_n1, grad_hidden))
+    both_sums, grad_in, result_far = lax.optimization_barrier((both_sums, to_blocks(grad_in, col), result_far))
+    both_total = exchange(ring_parts([both_sums], low, high), trade_ring)
+    own_rows = lambda w: lax.dynamic_slice_in_dim(w, (high * 4 + deep) * rows_here, rows_here, 0)
+    own_gain = jnp.sum(own_rows(w_gate) * mlp_sums[:, :units].astype(F32), axis=1, keepdims=True)
+    own_gain += jnp.sum(own_rows(w_up) * mlp_sums[:, units : 2 * units].astype(F32), axis=1, keepdims=True)
+    own_gain = jnp.broadcast_to(own_gain, (rows_here, 128))
+    own_gain = sum([trade_row(own_gain, j) for j in (1, 2, 3)], own_gain).astype(BF16)
+    mlp_total = ring_gather(jnp.concatenate([mlp_sums, own_gain], axis=1), high)
+    mlp_total = lax.all_gather(mlp_total, "z", axis=0, tiled=True)
+    both_total = ring_gather(both_total, high)
+    both_total = deep_gather(both_total, deep).astype(F32)
     result = (hidden + result_parts[0].astype(F32)) + result_far.astype(F32)
-    result = result + sum(part.astype(F32) for part in result_near)
-    result = to_blocks(after(result.astype(BF16), grad_in), col)
-    out_far, qkv_total, result = lax.optimization_barrier((out_far, qkv_total, result))
-    out_total = exchange([add_low(out_parts[0], *out_near, out_far)] * 4, trade_deep)
-    out_total = ring_gather(out_total, high).astype(F32)
-    gu_total, down_total = mlp_total[:, : 2 * units], mlp_total[:, 2 * units :]
-
-    gate_total, up_total = gu_total[:, :units], gu_total[:, units:]
-    gain_sums = jnp.stack(
-        [
-            jnp.sum(flat_qkv * qkv_total, axis=1),
-            jnp.sum(w_gate * gate_total + w_up * up_total, axis=1),
-        ]
-    )
-    gain_sums = sum([trade_row(gain_sums, j) for j in (1, 2, 3)], gain_sums)
+    result = (result + sum(part.astype(F32) for part in result_near)).astype(BF16)
+    result = to_blocks(after(result, grad_in), col)
+    both_total, result = lax.optimization_barrier((both_total, result))
+    qkv_total, out_total = both_total[:, :cut_at], both_total[:, cut_at:]
+    qkv_gain = jnp.sum(flat_qkv * qkv_total, axis=1)[None]
+    qkv_gain = sum([trade_row(qkv_gain, j) for j in (1, 2, 3)], qkv_gain)[0]
+    mlp_total, qkv_gain = lax.optimization_barrier((mlp_total, qkv_gain))
+    mlp_total = mlp_total.reshape(4, 2, rows_here, -1).swapaxes(0, 1).reshape(mlp_total.shape)
+    piece = lambda first: mlp_total[:, first : first + units].astype(F32)
     return (
         result,
         grad_in,
-        gain_sums[0],
+        qkv_gain,
         (qkv_total * attn_gain[:, None]).reshape(w_qkv.shape),
         out_total.T,
-        gain_sums[1],
-        gate_total * mlp_gain[:, None],
-        up_total * mlp_gain[:, None],
-        down_total.T,
+        mlp_total[:, 3 * units].astype(F32),
+        piece(0) * mlp_gain[:, None],
+        piece(units) * mlp_gain[:, None],
+        piece(2 * units).T,
     )
 
 

time: 479 us -> 472 us (0.985)
  waiting for transfers between devices: 177 us -> 195 us
  local copies, waits for them, and re-layouts: 62.5 us -> 50.2 us
  Pallas kernels: 66.8 us -> 59.6 us
    ppermute x58 -> x61, waiting for transfers between devices: 142 us -> 171 us  [trade(): return lax.ppermute(values, axes, [(i, i ^ mask) for i in range(size)])]
    unnamed x181 -> x127, local copies, waits for them, and re-layouts: 36.4 us -> 23.7 us
    all_gather x3, waiting for transfers between devices: 15.8 us -> 5.57 us  [gather_row(): return lax.all_gather(values, 'y', axis=0, tiled=True)]
    reduce_scatter x1, waiting for transfers between devices: 0.01 us -> 9.71 us  [on_device(): lax.psum_scatter(mlp_sums, ('xh', 'xl', 'z'), scatter_dimension=0, tiled=...]
    reduce_scatter x2, waiting for transfers between devices: 18.9 us -> 9.24 us  [sum_row(): return lax.psum_scatter(partial, 'y', scatter_dimension=0, tiled=True)]
    pallas_call x10, Pallas kernels: 66.8 us -> 59.6 us  [the longest x7 51.4 us: kernel_call(): pl.pallas_call(whole, out_shape=out_shape, in_specs=[pl.BlockSpec(memory_...]
    ppermute x58 -> x61, starting transfers between devices: 65.5 us -> 65.9 us  [trade(): return lax.ppermute(values, axes, [(i, i ^ mask) for i in range(size)])]
  transfers between devices with their start and end apart: 65 -> 68, of which waited for: 34 -> 32; matrix products, arithmetic and copies ran while one was open for 23% -> 22% of each run, Pallas kernels for 11% -> 8%
where the time goes in v3:
time: 472 us; the launch traced here: 464 us
  waiting for transfers between devices  195 us (41%)
  starting transfers between devices  66.7 us (14%)
  Pallas kernels  59.6 us (13%)
  local copies, waits for them, and re-layouts  50.2 us (11%)
  other arithmetic  43.6 us (9%)
  matrix products  32.5 us (7%)
  between operations  16.2 us (3%)
    ppermute x61, waiting for transfers between devices, trade(): return lax.ppermute(values, axes, [(i, i ^ mask) for i in range(size)])  171 us
    ppermute x61, starting transfers between devices, trade(): return lax.ppermute(values, axes, [(i, i ^ mask) for i in range(size)])  65.9 us
    pallas_call x7, Pallas kernels, kernel_call(): pl.pallas_call(whole, out_shape=out_shape, in_specs=[pl.BlockSpec(memory_...  51.4 us
    dot_general x7, matrix products, product(): lax.dot_general(left, right, (dims, ((), ())), preferred_element_type=F32)  32.5 us
    unnamed x127, local copies, waits for them, and re-layouts  23.7 us
    reduce_scatter x1, waiting for transfers between devices, on_device(): lax.psum_scatter(mlp_sums, ('xh', 'xl', 'z'), scatter_dimension=0, tiled=...  9.71 us
  transfers between devices with their start and end apart: 68, of which 32 were waited for; matrix products, arithmetic and copies ran while one was open for 22% of the time, Pallas kernels for 8%

profile of v3, /device:TPU:0, one launch (start us, length us, event | category | flops | bytes accessed | tf_op | source)
XLA Modules:
  0.0 464.0 jit_solution(7710529346841817126)
XLA Ops:
  13.7 2.6 fusion.59
  22.5 10.5 %collective-permute-done.3 = bf16[256,1152]{1,0:T(8,128)(2,1)S(1)} collective-permute-done((bf16[256,1152]{1,0:T(8,128)(2,1)S(1)}, bf16[256,1152]{1,0:T(8,128)(2,1)S(1)}, u32[]{:S(2)}, u32[]{:S(2)}) %collective-permute-start.3) | collective-permute-done | bytes 589856 | tf_op jit(solution)/shard_map/ppermute | solution.py:23
  45.0 3.6 collective-permute-done.7
  56.0 3.8 shard_map.169
  70.5 8.6 %shard_map.170 = (f32[512,512]{1,0:T(8,128)S(1)}, bf16[512,512]{1,0:T(8,128)(2,1)S(1)}, f32[8,512]{1,0:T(8,128)S(1)}) custom-call(bf16[512,512]{1,0:T(8,128)(2,1)S(1)} %get-tuple-element.139.q_ref.refs_0_, bf16[4,128,512]{2,1,0:T(8,128)(2,1)S(1)} %pad_maximum_fusion.20.pairs_ref.refs_1_, s32[512,128]{1,0:T(8,128)S(1)} %broadcast_in_dim.17.koff_ref.refs_2_, ...), custom_call_target="tpu_custom_call" | custom-call | flops 2147483648 | bytes 1314816 | tf_op jit(solution)/shard_map/pallas_call | solution.py:465
  83.5 2.9 collective-permute-start.13
  86.6 13.3 %collective-permute-done.15 = bf16[256,2816]{1,0:T(8,128)(2,1)} collective-permute-done((bf16[256,2816]{1,0:T(8,128)(2,1)}, bf16[256,2816]{1,0:T(8,128)(2,1)}, u32[]{:S(2)}, u32[]{:S(2)}) %collective-permute-start.15) | collective-permute-done | bytes 1441824 | tf_op jit(solution)/shard_map/ppermute | solution.py:23
  107.5 2.8 pad_maximum_fusion.1.own_ref
  110.3 13.7 %collective-permute-done.13.p2 = bf16[128,2048]{1,0:T(8,128)(2,1)S(1)} collective-permute-done((bf16[128,2048]{1,0:T(8,128)(2,1)}, bf16[128,2048]{1,0:T(8,128)(2,1)S(1)}, u32[]{:S(2)}, u32[]{:S(2)}) %collective-permute-start.13) | collective-permute-done | bytes 524320 | tf_op jit(solution)/shard_map/ppermute | solution.py:23
  126.0 2.9 shard_map.171
  134.7 3.1 fusion.57
  140.5 5.8 %collective-permute-done.20 = bf16[512,512]{1,0:T(8,128)(2,1)S(1)} collective-permute-done((bf16[512,512]{1,0:T(8,128)(2,1)S(1)}, bf16[512,512]{1,0:T(8,128)(2,1)S(1)}, u32[]{:S(2)}, u32[]{:S(2)}) %collective-permute-start.20) | collective-permute-done | bytes 524320 | tf_op jit(solution)/shard_map/ppermute | solution.py:23
  147.4 2.8 pad_maximum_fusion.9
  152.8 6.9 %fusion.10.gi_ref = f32[512,1408]{1,0:T(8,128)} fusion(bf16[512,2048]{1,0:T(8,128)(2,1)S(1)} %copy-done.32, bf16[1408,1024]{1,0:T(8,128)(2,1)} %collective-permute-done.22, bf16[1408,512]{1,0:T(8,128)(2,1)S(1)} %copy-done.23, bf16[1408,512]{1,0:T(8,128)(2,1)S(1)} %copy-done.21), kind=kOutput, calls=%fused_computation.33 | convolution fusion | flops 2970091520 | bytes 10747904 | tf_op jit(solution)/shard_map/dot_general | solution.py:184
  159.8 5.6 %all-gather.7.cloned.1.call-done.h_ref = bf16[512,2048]{1,0:T(8,128)(2,1)} async-done(((bf16[128,2048]{1,0:T(8,128)(2,1)}), bf16[512,2048]{1,0:T(8,128)(2,1)}) %all-gather.7.cloned.1.call-update) | async-done | bytes 2097168 | tf_op jit(solution)/shard_map/all_gather | solution.py:67
  167.0 16.8 %shard_map.172 = (bf16[512,1408]{1,0:T(8,128)(2,1)S(1)}, bf16[512,2816]{1,0:T(8,128)(2,1)}, bf16[512,2048]{1,0:T(8,128)(2,1)S(1)}) custom-call(bf16[512,2048]{1,0:T(8,128)(2,1)S(1)} %copy-done.8, f32[512,1408]{1,0:T(8,128)} %fusion.10.gi_ref, bf16[1024,2816]{1,0:T(8,128)(2,1)} %pad_maximum_fusion.1.own_ref, bf16[1024,2816]{1,0:T(8,128)(2,1)} %collective-permute-done.23.other_ref), custom_call_target="tpu_custom_call" | custom-call | flops 11811160064 | bytes 16515072 | tf_op jit(solution)/shard_map/pallas_call | solution.py:465
  189.2 6.1 %collective-permute-done.26 = bf16[512,1408]{1,0:T(8,128)(2,1)S(1)} collective-permute-done((bf16[512,1408]{1,0:T(8,128)(2,1)}, bf16[512,1408]{1,0:T(8,128)(2,1)S(1)}, u32[]{:S(2)}, u32[]{:S(2)}) %collective-permute-start.26) | collective-permute-done | bytes 1441824 | tf_op jit(solution)/shard_map/ppermute | solution.py:23
  195.3 3.7 convolution_convert_fusion
  199.1 8.4 %fusion.4 = bf16[1024,2816]{1,0:T(8,128)(2,1)S(1)} fusion(bf16[512,2816]{1,0:T(8,128)(2,1)} %collective-permute-done.25, bf16[512,2816]{1,0:T(8,128)(2,1)S(1)} %copy-done.58, bf16[512,1024]{1,0:T(8,128)(2,1)S(1)} %collective-permute-done.24, bf16[512,256]{1,0:T(8,128)(2,1)S(1)} %get-tuple-element.292, bf16[512,256]{1,0:T(8,128)(2,1)S(1)} %get-tuple-element.293, ...), kind=kOutput, calls=%fused_computation.7 | convolution fusion | flops 5930483712 | bytes 13631488 | tf_op jit(solution)/shard_map/dot_general | solution.py:184
  207.4 3.8 pad_maximum_fusion
  211.2 5.1 %reduce-scatter.4.cloned.1.call-done.part_ref = bf16[128,2048]{1,0:T(8,128)(2,1)} async-done(((bf16[512,2048]{1,0:T(8,128)(2,1)}), bf16[128,2048]{1,0:T(8,128)(2,1)}) %reduce-scatter.4.cloned.1.call-update) | async-done | bytes 524304 | tf_op jit(solution)/shard_map/reduce_scatter | solution.py:71
  216.4 2.6 shard_map.173
  223.7 6.5 %convolution_convert_fusion.2 = bf16[512,2048]{1,0:T(8,128)(2,1)S(1)} fusion(bf16[512,1408]{1,0:T(8,128)(2,1)} %copy-done.12, bf16[1408,1024]{1,0:T(8,128)(2,1)} %collective-permute-done.22, bf16[1408,512]{1,0:T(8,128)(2,1)} %copy-done.22, bf16[1408,512]{1,0:T(8,128)(2,1)} %copy-done.20), kind=kOutput, calls=%fused_computation.18 | convolution fusion | flops 2971140096 | bytes 9306112 | tf_op jit(solution)/shard_map/dot_general | solution.py:184
  234.0 10.5 %collective-permute-done.28.b2 = bf16[128,2048]{1,0:T(8,128)(2,1)S(1)} collective-permute-done((bf16[128,2048]{1,0:T(8,128)(2,1)}, bf16[128,2048]{1,0:T(8,128)(2,1)S(1)}, u32[]{:S(2)}, u32[]{:S(2)}) %collective-permute-start.28) | collective-permute-done | bytes 524320 | tf_op jit(solution)/shard_map/ppermute | solution.py:23
  252.0 7.2 %shard_map.175 = (bf16[256,512]{1,0:T(8,128)(2,1)S(1)}, f32[4,64,512]{2,1,0:T(8,128)S(1)}, f32[4,64,512]{2,1,0:T(8,128)S(1)}) custom-call(bf16[512,512]{1,0:T(8,128)(2,1)S(1)} %copy-done.15, bf16[4,128,512]{2,1,0:T(8,128)(2,1)S(1)} %copy-done.11, s32[512,128]{1,0:T(8,128)S(1)} %broadcast_in_dim.17.koff_ref.refs_2_, s32[1,512]{1,0:T(1,128)S(1)} %bitcast.64, ...), custom_call_target="tpu_custom_call" | custom-call | flops 2684354560 | bytes 3035136 | tf_op jit(solution)/shard_map/pallas_call | solution.py:465
  260.6 6.8 %shard_map.176 = (bf16[256,512]{1,0:T(8,128)(2,1)S(1)}, bf16[128,512]{1,0:T(8,128)(2,1)S(1)}, bf16[128,512]{1,0:T(8,128)(2,1)S(1)}, bf16[128,512]{1,0:T(8,128)(2,1)S(1)}, bf16[128,512]{1,0:T(8,128)(2,1)S(1)}) custom-call(bf16[512,512]{1,0:T(8,128)(2,1)S(1)} %copy-done.15, bf16[4,128,512]{2,1,0:T(8,128)(2,1)S(1)} %copy-done.11, ...), custom_call_target="tpu_custom_call" | custom-call | flops 2684354560 | bytes 4083712 | tf_op jit(solution)/shard_map/pallas_call | solution.py:465
  269.5 6.7 %collective-permute-done.33.g2 = bf16[128,512]{1,0:T(8,128)(2,1)S(1)} collective-permute-done((bf16[128,512]{1,0:T(8,128)(2,1)S(1)}, bf16[128,512]{1,0:T(8,128)(2,1)S(1)}, u32[]{:S(2)}, u32[]{:S(2)}) %collective-permute-start.33) | collective-permute-done | bytes 131104 | tf_op jit(solution)/shard_map/ppermute | solution.py:23
  276.2 4.1 collective-permute-done.34.g3
  280.3 5.8 %shard_map.177 = (bf16[640,512]{1,0:T(8,128)(2,1)}, bf16[512,2048]{1,0:T(8,128)(2,1)}) custom-call(bf16[256,512]{1,0:T(8,128)(2,1)S(1)} %get-tuple-element.180.gq0, bf16[256,512]{1,0:T(8,128)(2,1)S(1)} %get-tuple-element.187.gq1, bf16[128,512]{1,0:T(8,128)(2,1)S(1)} %get-tuple-element.192.g0, bf16[128,512]{1,0:T(8,128)(2,1)S(1)} %collective-permute-done.32.g1, ...), custom_call_target="tpu_custom_call" | custom-call | flops 1342177280 | bytes 5898240 | tf_op jit(solution)/shard_map/pallas_call | solution.py:465
  288.6 3.3 collective-permute-done.35
  291.9 3.2 convolution_convert_fusion.3
  298.0 9.7 %reduce-scatter.6.cloned.1.call-done = bf16[64,4224]{1,0:T(8,128)(2,1)} async-done(((bf16[1024,4224]{1,0:T(8,128)(2,1)}), bf16[64,4224]{1,0:T(8,128)(2,1)}) %reduce-scatter.6.cloned.1.call-update) | async-done | bytes 540688 | tf_op jit(solution)/shard_map/reduce_scatter | solution.py:610
  310.7 2.7 collective-permute-start.55
  320.6 2.7 collective-permute-start.57
  323.3 10.8 %collective-permute-done.57 = bf16[64,4352]{1,0:T(8,128)(2,1)S(1)} collective-permute-done((bf16[64,4352]{1,0:T(8,128)(2,1)}, bf16[64,4352]{1,0:T(8,128)(2,1)S(1)}, u32[]{:S(2)}, u32[]{:S(2)}) %collective-permute-start.57) | collective-permute-done | bytes 557088 | tf_op jit(solution)/shard_map/ppermute | solution.py:23
  335.4 4.1 reduce-scatter.8.cloned.1.call-done.part_ref
  339.5 2.7 shard_map.178
  349.0 2.9 collective-permute-start.38
  355.8 17.2 %collective-permute-done.37 = bf16[2,128,1152]{2,1,0:T(8,128)(2,1)S(1)} collective-permute-done((bf16[2,128,1152]{2,1,0:T(8,128)(2,1)S(1)}, bf16[2,128,1152]{2,1,0:T(8,128)(2,1)S(1)}, u32[]{:S(2)}, u32[]{:S(2)}) %collective-permute-start.37) | collective-permute-done | bytes 589856 | tf_op jit(solution)/shard_map/ppermute | solution.py:23
  372.9 27.1 %collective-permute-done.38 = bf16[2,128,1152]{2,1,0:T(8,128)(2,1)S(1)} collective-permute-done((bf16[2,128,1152]{2,1,0:T(8,128)(2,1)S(1)}, bf16[2,128,1152]{2,1,0:T(8,128)(2,1)S(1)}, u32[]{:S(2)}, u32[]{:S(2)}) %collective-permute-start.38) | collective-permute-done | bytes 589856 | tf_op jit(solution)/shard_map/ppermute | solution.py:23
  402.4 2.7 collective-permute-start.45
  414.4 5.6 %collective-permute-done.47 = bf16[64,1152]{1,0:T(8,128)(2,1)S(1)} collective-permute-done((bf16[64,1152]{1,0:T(8,128)(2,1)S(1)}, bf16[64,1152]{1,0:T(8,128)(2,1)S(1)}, u32[]{:S(2)}, u32[]{:S(2)}) %collective-permute-start.47) | collective-permute-done | bytes 147488 | tf_op jit(solution)/shard_map/ppermute | solution.py:23
  421.2 3.6 collective-permute-start.50
  425.7 4.4 collective-permute-done.48
  430.1 4.3 collective-permute-done.49
  434.4 3.0 collective-permute-done.50
  440.6 3.1 collective-permute-start.60
  450.8 3.1 convert_multiply_fusion
  (333 shorter events, 148.6 us)
Async XLA Ops:
  7.2 47.2 %all-gather.5.cloned.1.call-start = ((), (), s32[]{:S(2)}) async-start(), calls=%async_computation.3 | async-start | bytes 2621440 | tf_op jit(solution)/shard_map/all_gather | solution.py:67
  8.5 8.7 %collective-permute-start = (bf16[128,512]{1,0:T(8,128)(2,1)S(1)}, bf16[128,512]{1,0:T(8,128)(2,1)S(1)}, u32[]{:S(2)}, u32[]{:S(2)}) collective-permute-start(bf16[128,512]{1,0:T(8,128)(2,1)S(1)} %get-tuple-element.339), channel_id=1, source_target_pairs={{0,1},{1,0},{2,3},{3,2},{4,5},{5,4},{6,7},{7,6},{8,9},{9,8},{10,11... | collective-permute-start | bytes 393224 | tf_op jit(solution)/shard_map/ppermute | solution.py:23
  8.6 8.6 %collective-permute-start.1 = (bf16[128,512]{1,0:T(8,128)(2,1)S(1)}, bf16[128,512]{1,0:T(8,128)(2,1)S(1)}, u32[]{:S(2)}, u32[]{:S(2)}) collective-permute-start(bf16[128,512]{1,0:T(8,128)(2,1)S(1)} %get-tuple-element.341), channel_id=1, source_target_pairs={{0,2},{1,3},{2,0},{3,1},{4,6},{5,7},{6,4},{7,5},{8,10},{9,11},{10,... | collective-permute-start | bytes 393224 | tf_op jit(solution)/shard_map/ppermute | solution.py:23
  17.3 15.7 %collective-permute-start.3 = (bf16[256,1152]{1,0:T(8,128)(2,1)S(1)}, bf16[256,1152]{1,0:T(8,128)(2,1)S(1)}, u32[]{:S(2)}, u32[]{:S(2)}) collective-permute-start(bf16[256,1152]{1,0:T(8,128)(2,1)S(1)} %get-tuple-element.127), channel_id=1, source_target_pairs={{0,2},{2,0},{16,18},{18,16},{1,3},{3,1},{17,19},{19,17},{4,6},{6,4... | collective-permute-start | bytes 1769480 | tf_op jit(solution)/shard_map/ppermute | solution.py:23
  19.0 16.5 %collective-permute-start.4 = (bf16[256,1152]{1,0:T(8,128)(2,1)S(1)}, bf16[256,1152]{1,0:T(8,128)(2,1)S(1)}, u32[]{:S(2)}, u32[]{:S(2)}) collective-permute-start(bf16[256,1152]{1,0:T(8,128)(2,1)S(1)} %get-tuple-element.128), channel_id=1, source_target_pairs={{0,18},{2,16},{16,2},{18,0},{1,19},{3,17},{17,3},{19,1},{4,22},{6,... | collective-permute-start | bytes 1769480 | tf_op jit(solution)/shard_map/ppermute | solution.py:23
  22.3 115.6 %all-gather.9.cloned.1.call-start = ((), (), s32[]{:S(2)}) async-start(), calls=%async_computation.5 | async-start | bytes 2621440 | tf_op jit(solution)/shard_map/all_gather | solution.py:67
  36.1 15.3 %collective-permute-start.5 = (bf16[2,512,1152]{2,1,0:T(8,128)(2,1)S(1)}, bf16[2,512,1152]{2,1,0:T(8,128)(2,1)}, u32[]{:S(2)}, u32[]{:S(2)}) collective-permute-start(bf16[2,512,1152]{2,1,0:T(8,128)(2,1)S(1)} %bitcast.55), channel_id=1, source_target_pairs={{0,1},{1,0},{2,3},{3,2},{4,5},{5,4},{6,7},{7,6},{8,9},{9,8},{10,11... | collective-permute-start | bytes 7077896 | tf_op jit(solution)/shard_map/ppermute | solution.py:23
  42.3 8.2 %collective-permute-start.8 = (bf16[128,512]{1,0:T(8,128)(2,1)S(1)}, bf16[128,512]{1,0:T(8,128)(2,1)S(1)}, u32[]{:S(2)}, u32[]{:S(2)}) collective-permute-start(bf16[128,512]{1,0:T(8,128)(2,1)S(1)} %get-tuple-element.334), channel_id=1, source_target_pairs={{0,3},{1,2},{2,1},{3,0},{4,7},{5,6},{6,5},{7,4},{8,11},{9,10},{10,... | collective-permute-start | bytes 393224 | tf_op jit(solution)/shard_map/ppermute | solution.py:23
  59.8 10.6 %collective-permute-start.9 = (bf16[128,512]{1,0:T(8,128)(2,1)S(1)}, bf16[128,512]{1,0:T(8,128)(2,1)S(1)}, u32[]{:S(2)}, u32[]{:S(2)}) collective-permute-start(bf16[128,512]{1,0:T(8,128)(2,1)S(1)} %get-tuple-element.140), channel_id=1, source_target_pairs={{0,1},{1,0},{2,3},{3,2},{4,5},{5,4},{6,7},{7,6},{8,9},{9,8},{10,11... | collective-permute-start | bytes 393224 | tf_op jit(solution)/shard_map/ppermute | solution.py:23
  60.6 9.8 %collective-permute-start.10 = (bf16[128,512]{1,0:T(8,128)(2,1)S(1)}, bf16[128,512]{1,0:T(8,128)(2,1)S(1)}, u32[]{:S(2)}, u32[]{:S(2)}) collective-permute-start(bf16[128,512]{1,0:T(8,128)(2,1)S(1)} %get-tuple-element.140), channel_id=1, source_target_pairs={{0,2},{1,3},{2,0},{3,1},{4,6},{5,7},{6,4},{7,5},{8,10},{9,11},{10,... | collective-permute-start | bytes 393224 | tf_op jit(solution)/shard_map/ppermute | solution.py:23
  60.8 9.6 %collective-permute-start.11 = (bf16[128,512]{1,0:T(8,128)(2,1)S(1)}, bf16[128,512]{1,0:T(8,128)(2,1)S(1)}, u32[]{:S(2)}, u32[]{:S(2)}) collective-permute-start(bf16[128,512]{1,0:T(8,128)(2,1)S(1)} %get-tuple-element.140), channel_id=1, source_target_pairs={{0,3},{1,2},{2,1},{3,0},{4,7},{5,6},{6,5},{7,4},{8,11},{9,10},{10,... | collective-permute-start | bytes 393224 | tf_op jit(solution)/shard_map/ppermute | solution.py:23
  62.0 37.9 %collective-permute-start.15 = (bf16[256,2816]{1,0:T(8,128)(2,1)}, bf16[256,2816]{1,0:T(8,128)(2,1)}, u32[]{:S(2)}, u32[]{:S(2)}) collective-permute-start(bf16[256,2816]{1,0:T(8,128)(2,1)} %get-tuple-element.146), channel_id=1, source_target_pairs={{0,2},{2,0},{16,18},{18,16},{1,3},{3,1},{17,19},{19,17},{4,6},{6,4... | collective-permute-start | bytes 4325384 | tf_op jit(solution)/shard_map/ppermute | solution.py:23
  62.6 37.2 %collective-permute-start.16 = (bf16[256,2816]{1,0:T(8,128)(2,1)}, bf16[256,2816]{1,0:T(8,128)(2,1)}, u32[]{:S(2)}, u32[]{:S(2)}) collective-permute-start(bf16[256,2816]{1,0:T(8,128)(2,1)} %get-tuple-element.147), channel_id=1, source_target_pairs={{0,18},{2,16},{16,2},{18,0},{1,19},{3,17},{17,3},{19,1},{4,22},{6,... | collective-permute-start | bytes 4325384 | tf_op jit(solution)/shard_map/ppermute | solution.py:23
  69.9 95.5 %all-gather.7.cloned.1.call-start = ((), (), s32[]{:S(2)}) async-start(), calls=%async_computation.4 | async-start | bytes 2621440 | tf_op jit(solution)/shard_map/all_gather | solution.py:67
  81.9 28.4 %collective-permute-start.12 = (bf16[128,2048]{1,0:T(8,128)(2,1)}, bf16[128,2048]{1,0:T(8,128)(2,1)S(1)}, u32[]{:S(2)}, u32[]{:S(2)}) collective-permute-start(bf16[128,2048]{1,0:T(8,128)(2,1)} %get-tuple-element.307), channel_id=1, source_target_pairs={{0,4},{4,0},{8,12},{12,8},{1,5},{5,1},{9,13},{13,9},{2,6},{6,2},{1... | collective-permute-start | bytes 1572872 | tf_op jit(solution)/shard_map/ppermute | solution.py:23
  83.5 40.5 %collective-permute-start.13 = (bf16[128,2048]{1,0:T(8,128)(2,1)}, bf16[128,2048]{1,0:T(8,128)(2,1)S(1)}, u32[]{:S(2)}, u32[]{:S(2)}) collective-permute-start(bf16[128,2048]{1,0:T(8,128)(2,1)} %get-tuple-element.306), channel_id=1, source_target_pairs={{0,8},{4,12},{8,0},{12,4},{1,9},{5,13},{9,1},{13,5},{2,10},{6,14},... | collective-permute-start | bytes 1572872 | tf_op jit(solution)/shard_map/ppermute | solution.py:23
  86.4 37.6 %collective-permute-start.14 = (bf16[128,2048]{1,0:T(8,128)(2,1)}, bf16[128,2048]{1,0:T(8,128)(2,1)S(1)}, u32[]{:S(2)}, u32[]{:S(2)}) collective-permute-start(bf16[128,2048]{1,0:T(8,128)(2,1)} %get-tuple-element.305), channel_id=1, source_target_pairs={{0,12},{4,8},{8,4},{12,0},{1,13},{5,9},{9,5},{13,1},{2,14},{6,10},... | collective-permute-start | bytes 1572872 | tf_op jit(solution)/shard_map/ppermute | solution.py:23
  99.9 24.1 %collective-permute-start.18 = (bf16[704,512]{1,0:T(8,128)(2,1)S(1)}, bf16[704,512]{1,0:T(8,128)(2,1)S(1)}, u32[]{:S(2)}, u32[]{:S(2)}) collective-permute-start(bf16[704,512]{1,0:T(8,128)(2,1)S(1)} %copy-done.27), channel_id=1, source_target_pairs={{0,18},{2,16},{16,2},{18,0},{1,19},{3,17},{17,3},{19,1},{4,22},{6,... | collective-permute-start | bytes 2162696 | tf_op jit(solution)/shard_map/ppermute | solution.py:23
  102.0 22.0 %collective-permute-start.17 = (bf16[704,512]{1,0:T(8,128)(2,1)S(1)}, bf16[704,512]{1,0:T(8,128)(2,1)S(1)}, u32[]{:S(2)}, u32[]{:S(2)}) collective-permute-start(bf16[704,512]{1,0:T(8,128)(2,1)S(1)} %copy-done.28), channel_id=1, source_target_pairs={{0,2},{2,0},{16,18},{18,16},{1,3},{3,1},{17,19},{19,17},{4,6},{6,4... | collective-permute-start | bytes 2162696 | tf_op jit(solution)/shard_map/ppermute | solution.py:23
  128.9 36.4 %collective-permute-start.23 = (bf16[1024,2816]{1,0:T(8,128)(2,1)}, bf16[1024,2816]{1,0:T(8,128)(2,1)}, u32[]{:S(2)}, u32[]{:S(2)}) collective-permute-start(bf16[1024,2816]{1,0:T(8,128)(2,1)} %pad_maximum_fusion.1.own_ref), channel_id=1, source_target_pairs={{0,1},{1,0},{2,3},{3,2},{4,5},{5,4},{6,7},{7,6},{8,9},{9,8},{10,11... | collective-permute-start | bytes 17301512 | tf_op jit(solution)/shard_map/ppermute | solution.py:23
  134.2 17.6 %collective-permute-start.22 = (bf16[1408,1024]{1,0:T(8,128)(2,1)}, bf16[1408,1024]{1,0:T(8,128)(2,1)}, u32[]{:S(2)}, u32[]{:S(2)}) collective-permute-start(bf16[1408,1024]{1,0:T(8,128)(2,1)} %pad_maximum_fusion.3), channel_id=1, source_target_pairs={{0,1},{1,0},{2,3},{3,2},{4,5},{5,4},{6,7},{7,6},{8,9},{9,8},{10,11... | collective-permute-start | bytes 8650760 | tf_op jit(solution)/shard_map/ppermute | solution.py:23
  134.6 81.7 %reduce-scatter.4.cloned.1.call-start = ((), (), s32[]{:S(2)}) async-start(), calls=%async_computation.6 | async-start | bytes 2621440 | tf_op jit(solution)/shard_map/reduce_scatter | solution.py:71
  137.8 9.6 %collective-permute-start.21 = (bf16[512,1024]{1,0:T(8,128)(2,1)}, bf16[512,1024]{1,0:T(8,128)(2,1)}, u32[]{:S(2)}, u32[]{:S(2)}) collective-permute-start(bf16[512,1024]{1,0:T(8,128)(2,1)} %get-tuple-element.296), channel_id=1, source_target_pairs={{0,1},{1,0},{2,3},{3,2},{4,5},{5,4},{6,7},{7,6},{8,9},{9,8},{10,11... | collective-permute-start | bytes 3145736 | tf_op jit(solution)/shard_map/ppermute | solution.py:23
  139.7 10.5 %collective-permute-start.19 = (bf16[512,1024]{1,0:T(8,128)(2,1)S(1)}, bf16[512,1024]{1,0:T(8,128)(2,1)S(1)}, u32[]{:S(2)}, u32[]{:S(2)}) collective-permute-start(bf16[512,1024]{1,0:T(8,128)(2,1)S(1)} %pad_maximum_fusion.13), channel_id=1, source_target_pairs={{0,1},{1,0},{2,3},{3,2},{4,5},{5,4},{6,7},{7,6},{8,9},{9,8},{10,11... | collective-permute-start | bytes 3145736 | tf_op jit(solution)/shard_map/ppermute | solution.py:23
  186.3 12.8 %collective-permute-start.25 = (bf16[512,2816]{1,0:T(8,128)(2,1)}, bf16[512,2816]{1,0:T(8,128)(2,1)}, u32[]{:S(2)}, u32[]{:S(2)}) collective-permute-start(bf16[512,2816]{1,0:T(8,128)(2,1)} %get-tuple-element.171), channel_id=1, source_target_pairs={{0,1},{1,0},{2,3},{3,2},{4,5},{5,4},{6,7},{7,6},{8,9},{9,8},{10,11... | collective-permute-start | bytes 8650760 | tf_op jit(solution)/shard_map/ppermute | solution.py:23
  186.3 121.4 %reduce-scatter.6.cloned.1.call-start = ((), (), s32[]{:S(2)}) async-start(), calls=%async_computation.7 | async-start | bytes 9191424 | tf_op jit(solution)/shard_map/reduce_scatter | solution.py:610
  186.3 9.0 %collective-permute-start.26 = (bf16[512,1408]{1,0:T(8,128)(2,1)}, bf16[512,1408]{1,0:T(8,128)(2,1)S(1)}, u32[]{:S(2)}, u32[]{:S(2)}) collective-permute-start(bf16[512,1408]{1,0:T(8,128)(2,1)} %copy-done.12), channel_id=1, source_target_pairs={{0,1},{1,0},{2,3},{3,2},{4,5},{5,4},{6,7},{7,6},{8,9},{9,8},{10,11... | collective-permute-start | bytes 4325384 | tf_op jit(solution)/shard_map/ppermute | solution.py:23
  189.1 9.9 %collective-permute-start.24 = (bf16[512,1024]{1,0:T(8,128)(2,1)S(1)}, bf16[512,1024]{1,0:T(8,128)(2,1)S(1)}, u32[]{:S(2)}, u32[]{:S(2)}) collective-permute-start(bf16[512,1024]{1,0:T(8,128)(2,1)S(1)} %pad_maximum_fusion.15), channel_id=1, source_target_pairs={{0,1},{1,0},{2,3},{3,2},{4,5},{5,4},{6,7},{7,6},{8,9},{9,8},{10,11... | collective-permute-start | bytes 3145736 | tf_op jit(solution)/shard_map/ppermute | solution.py:23
  216.3 123.2 %reduce-scatter.8.cloned.1.call-start = ((), (), s32[]{:S(2)}) async-start(), calls=%async_computation.8 | async-start | bytes 2621440 | tf_op jit(solution)/shard_map/reduce_scatter | solution.py:71
  219.0 15.0 %collective-permute-start.27 = (bf16[128,2048]{1,0:T(8,128)(2,1)}, bf16[128,2048]{1,0:T(8,128)(2,1)S(1)}, u32[]{:S(2)}, u32[]{:S(2)}) collective-permute-start(bf16[128,2048]{1,0:T(8,128)(2,1)} %get-tuple-element.197.b0), channel_id=1, source_target_pairs={{0,4},{4,0},{8,12},{12,8},{1,5},{5,1},{9,13},{13,9},{2,6},{6,2},{1... | collective-permute-start | bytes 1572872 | tf_op jit(solution)/shard_map/ppermute | solution.py:23
  219.2 25.3 %collective-permute-start.28 = (bf16[128,2048]{1,0:T(8,128)(2,1)}, bf16[128,2048]{1,0:T(8,128)(2,1)S(1)}, u32[]{:S(2)}, u32[]{:S(2)}) collective-permute-start(bf16[128,2048]{1,0:T(8,128)(2,1)} %get-tuple-element.197.b0), channel_id=1, source_target_pairs={{0,8},{4,12},{8,0},{12,4},{1,9},{5,13},{9,1},{13,5},{2,10},{6,14},... | collective-permute-start | bytes 1572872 | tf_op jit(solution)/shard_map/ppermute | solution.py:23
  221.3 25.8 %collective-permute-start.29 = (bf16[128,2048]{1,0:T(8,128)(2,1)}, bf16[128,2048]{1,0:T(8,128)(2,1)S(1)}, u32[]{:S(2)}, u32[]{:S(2)}) collective-permute-start(bf16[128,2048]{1,0:T(8,128)(2,1)} %get-tuple-element.197.b0), channel_id=1, source_target_pairs={{0,12},{4,8},{8,4},{12,0},{1,13},{5,9},{9,5},{13,1},{2,14},{6,10},... | collective-permute-start | bytes 1572872 | tf_op jit(solution)/shard_map/ppermute | solution.py:23
  247.1 12.2 %collective-permute-start.30 = (bf16[128,2048]{1,0:T(8,128)(2,1)S(1)}, bf16[128,2048]{1,0:T(8,128)(2,1)S(1)}, u32[]{:S(2)}, u32[]{:S(2)}) collective-permute-start(bf16[128,2048]{1,0:T(8,128)(2,1)S(1)} %get-tuple-element.183), channel_id=1, source_target_pairs={{0,4},{4,0},{8,12},{12,8},{1,5},{5,1},{9,13},{13,9},{2,6},{6,2},{1... | collective-permute-start | bytes 1572872 | tf_op jit(solution)/shard_map/ppermute | solution.py:23
  247.1 13.4 %collective-permute-start.31 = (bf16[128,2048]{1,0:T(8,128)(2,1)S(1)}, bf16[128,2048]{1,0:T(8,128)(2,1)S(1)}, u32[]{:S(2)}, u32[]{:S(2)}) collective-permute-start(bf16[128,2048]{1,0:T(8,128)(2,1)S(1)} %get-tuple-element.184), channel_id=1, source_target_pairs={{0,12},{4,8},{8,4},{12,0},{1,13},{5,9},{9,5},{13,1},{2,14},{6,10},... | collective-permute-start | bytes 1572872 | tf_op jit(solution)/shard_map/ppermute | solution.py:23
  267.5 8.7 %collective-permute-start.33 = (bf16[128,512]{1,0:T(8,128)(2,1)S(1)}, bf16[128,512]{1,0:T(8,128)(2,1)S(1)}, u32[]{:S(2)}, u32[]{:S(2)}) collective-permute-start(bf16[128,512]{1,0:T(8,128)(2,1)S(1)} %get-tuple-element.190), channel_id=1, source_target_pairs={{0,2},{1,3},{2,0},{3,1},{4,6},{5,7},{6,4},{7,5},{8,10},{9,11},{10,... | collective-permute-start | bytes 393224 | tf_op jit(solution)/shard_map/ppermute | solution.py:23
  269.2 11.1 %collective-permute-start.34 = (bf16[128,512]{1,0:T(8,128)(2,1)S(1)}, bf16[128,512]{1,0:T(8,128)(2,1)S(1)}, u32[]{:S(2)}, u32[]{:S(2)}) collective-permute-start(bf16[128,512]{1,0:T(8,128)(2,1)S(1)} %get-tuple-element.191), channel_id=1, source_target_pairs={{0,3},{1,2},{2,1},{3,0},{4,7},{5,6},{6,5},{7,4},{8,11},{9,10},{10,... | collective-permute-start | bytes 393224 | tf_op jit(solution)/shard_map/ppermute | solution.py:23
  288.5 159.6 %all-gather.11.cloned.1.call-start = ((), (), s32[]{:S(2)}) async-start(), calls=%async_computation.9 | async-start | bytes 5570560 | tf_op jit(solution)/shard_map/all_gather | solution.py:674
  320.6 13.5 %collective-permute-start.57 = (bf16[64,4352]{1,0:T(8,128)(2,1)}, bf16[64,4352]{1,0:T(8,128)(2,1)S(1)}, u32[]{:S(2)}, u32[]{:S(2)}) collective-permute-start(bf16[64,4352]{1,0:T(8,128)(2,1)} %pad_maximum_fusion.18), channel_id=1, source_target_pairs={{0,16},{2,18},{16,0},{18,2},{1,17},{3,19},{17,1},{19,3},{4,20},{6,... | collective-permute-start | bytes 1671176 | tf_op jit(solution)/shard_map/ppermute | solution.py:23
  346.0 54.3 %collective-permute-start.43 = (bf16[128,2048]{1,0:T(8,128)(2,1)S(1)}, bf16[128,2048]{1,0:T(8,128)(2,1)S(1)}, u32[]{:S(2)}, u32[]{:S(2)}) collective-permute-start(bf16[128,2048]{1,0:T(8,128)(2,1)S(1)} %copy-done.53), channel_id=1, source_target_pairs={{0,8},{4,12},{8,0},{12,4},{1,9},{5,13},{9,1},{13,5},{2,10},{6,14},... | collective-permute-start | bytes 1572872 | tf_op jit(solution)/shard_map/ppermute | solution.py:23
  347.5 25.5 %collective-permute-start.37 = (bf16[2,128,1152]{2,1,0:T(8,128)(2,1)S(1)}, bf16[2,128,1152]{2,1,0:T(8,128)(2,1)S(1)}, u32[]{:S(2)}, u32[]{:S(2)}) collective-permute-start(bf16[2,128,1152]{2,1,0:T(8,128)(2,1)S(1)} %get-tuple-element.204), channel_id=1, source_target_pairs={{0,32},{32,0},{64,96},{96,64},{1,33},{33,1},{65,97},{97,65},{2,34}... | collective-permute-start | bytes 1769480 | tf_op jit(solution)/shard_map/ppermute | solution.py:23
  349.0 51.0 %collective-permute-start.38 = (bf16[2,128,1152]{2,1,0:T(8,128)(2,1)S(1)}, bf16[2,128,1152]{2,1,0:T(8,128)(2,1)S(1)}, u32[]{:S(2)}, u32[]{:S(2)}) collective-permute-start(bf16[2,128,1152]{2,1,0:T(8,128)(2,1)S(1)} %get-tuple-element.205), channel_id=1, source_target_pairs={{0,64},{32,96},{64,0},{96,32},{1,65},{33,97},{65,1},{97,33},{2,66}... | collective-permute-start | bytes 1769480 | tf_op jit(solution)/shard_map/ppermute | solution.py:23
  351.9 48.1 %collective-permute-start.39 = (bf16[2,128,1152]{2,1,0:T(8,128)(2,1)S(1)}, bf16[2,128,1152]{2,1,0:T(8,128)(2,1)S(1)}, u32[]{:S(2)}, u32[]{:S(2)}) collective-permute-start(bf16[2,128,1152]{2,1,0:T(8,128)(2,1)S(1)} %get-tuple-element.206), channel_id=1, source_target_pairs={{0,96},{32,64},{64,32},{96,0},{1,97},{33,65},{65,33},{97,1},{2,98}... | collective-permute-start | bytes 1769480 | tf_op jit(solution)/shard_map/ppermute | solution.py:23
  411.5 8.4 %collective-permute-start.47 = (bf16[64,1152]{1,0:T(8,128)(2,1)S(1)}, bf16[64,1152]{1,0:T(8,128)(2,1)S(1)}, u32[]{:S(2)}, u32[]{:S(2)}) collective-permute-start(bf16[64,1152]{1,0:T(8,128)(2,1)S(1)} %fusion.40), channel_id=1, source_target_pairs={{0,16},{2,18},{16,0},{18,2},{1,17},{3,19},{17,1},{19,3},{4,20},{6,... | collective-permute-start | bytes 442376 | tf_op jit(solution)/shard_map/ppermute | solution.py:23
  420.1 10.0 %collective-permute-start.48 = (bf16[128,1152]{1,0:T(8,128)(2,1)S(1)}, bf16[128,1152]{1,0:T(8,128)(2,1)S(1)}, u32[]{:S(2)}, u32[]{:S(2)}) collective-permute-start(bf16[128,1152]{1,0:T(8,128)(2,1)S(1)} %pad_maximum_fusion.22), channel_id=1, source_target_pairs={{0,32},{32,0},{64,96},{96,64},{1,33},{33,1},{65,97},{97,65},{2,34}... | collective-permute-start | bytes 884744 | tf_op jit(solution)/shard_map/ppermute | solution.py:23
  420.2 14.3 %collective-permute-start.49 = (bf16[128,1152]{1,0:T(8,128)(2,1)S(1)}, bf16[128,1152]{1,0:T(8,128)(2,1)S(1)}, u32[]{:S(2)}, u32[]{:S(2)}) collective-permute-start(bf16[128,1152]{1,0:T(8,128)(2,1)S(1)} %pad_maximum_fusion.22), channel_id=1, source_target_pairs={{0,64},{32,96},{64,0},{96,32},{1,65},{33,97},{65,1},{97,33},{2,66}... | collective-permute-start | bytes 884744 | tf_op jit(solution)/shard_map/ppermute | solution.py:23
  421.2 16.2 %collective-permute-start.50 = (bf16[128,1152]{1,0:T(8,128)(2,1)S(1)}, bf16[128,1152]{1,0:T(8,128)(2,1)S(1)}, u32[]{:S(2)}, u32[]{:S(2)}) collective-permute-start(bf16[128,1152]{1,0:T(8,128)(2,1)S(1)} %pad_maximum_fusion.22), channel_id=1, source_target_pairs={{0,96},{32,64},{64,32},{96,0},{1,97},{33,65},{65,33},{97,1},{2,98}... | collective-permute-start | bytes 884744 | tf_op jit(solution)/shard_map/ppermute | solution.py:23
  438.9 8.6 %collective-permute-start.58 = (f32[1,512]{1,0:T(1,128)S(1)}, f32[1,512]{1,0:T(1,128)S(1)}, u32[]{:S(2)}, u32[]{:S(2)}) collective-permute-start(f32[1,512]{1,0:T(1,128)S(1)} %bitcast.76), channel_id=1, source_target_pairs={{0,4},{4,0},{8,12},{12,8},{1,5},{5,1},{9,13},{13,9},{2,6},{6,2},{1... | collective-permute-start | bytes 6152 | tf_op jit(solution)/shard_map/ppermute | solution.py:23
  439.0 8.5 %collective-permute-start.59 = (f32[1,512]{1,0:T(1,128)S(1)}, f32[1,512]{1,0:T(1,128)S(1)}, u32[]{:S(2)}, u32[]{:S(2)}) collective-permute-start(f32[1,512]{1,0:T(1,128)S(1)} %bitcast.77), channel_id=1, source_target_pairs={{0,8},{4,12},{8,0},{12,4},{1,9},{5,13},{9,1},{13,5},{2,10},{6,14},... | collective-permute-start | bytes 6152 | tf_op jit(solution)/shard_map/ppermute | solution.py:23
  (79 other events, 624.3 us)
Sparse Core Ops, SparseCore 0:
  22.4 31.3 all-gather.4
  70.0 46.3 all-gather.8
  134.8 30.5 all-gather.6
  186.4 29.8 reduce-scatter.3
  220.0 87.6 reduce-scatter.5
  310.5 28.9 reduce-scatter.7
  341.8 74.7 all-gather.10

commit v4 on v3

--- a/solution.py
+++ b/solution.py
@@ -658,30 +658,33 @@
     qkv_sum = product(one_half, qkv_both, ((0,), (1,)), BF16).reshape(2, width // 4, -1)
     out_sum = product(branch_half, heads_both, ((0,), (1,)), BF16).reshape(2, width // 4, -1)
     both_parts = deep_parts(jnp.concatenate([qkv_sum, out_sum], axis=2), deep)
-    both_parts, mlp_sums = lax.optimization_barrier((both_parts, mlp_sums))
     both_sums = exchange(both_parts, trade_deep)
     rows_here = mlp_sums.shape[0]
-    grad_n1 = sum_row(part_one)
-    (grad_in,) = rows_call(norm_back_high, (F32,), (inputs, grad_n1, grad_hidden))
-    both_sums, grad_in, result_far = lax.optimization_barrier((both_sums, to_blocks(grad_in, col), result_far))
-    both_total = exchange(ring_parts([both_sums], low, high), trade_ring)
+    rows_here = mlp_sums.shape[0]
     own_rows = lambda w: lax.dynamic_slice_in_dim(w, (high * 4 + deep) * rows_here, rows_here, 0)
     own_gain = jnp.sum(own_rows(w_gate) * mlp_sums[:, :units].astype(F32), axis=1, keepdims=True)
     own_gain += jnp.sum(own_rows(w_up) * mlp_sums[:, units : 2 * units].astype(F32), axis=1, keepdims=True)
     own_gain = jnp.broadcast_to(own_gain, (rows_here, 128))
-    own_gain = sum([trade_row(own_gain, j) for j in (1, 2, 3)], own_gain).astype(BF16)
-    mlp_total = ring_gather(jnp.concatenate([mlp_sums, own_gain], axis=1), high)
+    own_gain = own_gain + trade_row(own_gain, 1)
+    own_gain = (own_gain + trade_row(own_gain, 2)).astype(BF16)
+    mlp_sums = jnp.concatenate([mlp_sums, own_gain], axis=1)
+    mlp_sums, both_sums = lax.optimization_barrier((mlp_sums, both_sums))
+    mlp_total = ring_gather(mlp_sums, high)
+    both_total = exchange(ring_parts([both_sums], low, high), trade_ring)
+    mlp_total, both_total = lax.optimization_barrier((mlp_total, both_total))
     mlp_total = lax.all_gather(mlp_total, "z", axis=0, tiled=True)
     both_total = ring_gather(both_total, high)
+    grad_n1 = sum_row(part_one)
+    (grad_in,) = rows_call(norm_back_high, (F32,), (inputs, grad_n1, grad_hidden))
+    both_total, grad_in, result_far = lax.optimization_barrier((both_total, to_blocks(grad_in, col), result_far))
     both_total = deep_gather(both_total, deep).astype(F32)
     result = (hidden + result_parts[0].astype(F32)) + result_far.astype(F32)
     result = (result + sum(part.astype(F32) for part in result_near)).astype(BF16)
-    result = to_blocks(after(result, grad_in), col)
+    result = to_blocks(result, col)
     both_total, result = lax.optimization_barrier((both_total, result))
     qkv_total, out_total = both_total[:, :cut_at], both_total[:, cut_at:]
     qkv_gain = jnp.sum(flat_qkv * qkv_total, axis=1)[None]
     qkv_gain = sum([trade_row(qkv_gain, j) for j in (1, 2, 3)], qkv_gain)[0]
-    mlp_total, qkv_gain = lax.optimization_barrier((mlp_total, qkv_gain))
     mlp_total = mlp_total.reshape(4, 2, rows_here, -1).swapaxes(0, 1).reshape(mlp_total.shape)
     piece = lambda first: mlp_total[:, first : first + units].astype(F32)
     return (

time: 472 us -> 451 us (0.956)
  waiting for transfers between devices: 195 us -> 174 us
    ppermute x61 -> x60, waiting for transfers between devices: 171 us -> 157 us  [trade(): return lax.ppermute(values, axes, [(i, i ^ mask) for i in range(size)])]
    ppermute x61 -> x60, starting transfers between devices: 65.9 us -> 65.5 us  [trade(): return lax.ppermute(values, axes, [(i, i ^ mask) for i in range(size)])]
    unnamed x127 -> x123, local copies, waits for them, and re-layouts: 23.7 us -> 23.7 us
  transfers between devices with their start and end apart: 68 -> 67, of which waited for: 32 -> 33; matrix products, arithmetic and copies ran while one was open for 22% -> 24% of each run, Pallas kernels for 8% -> 9%
where the time goes in v4:
time: 451 us; the launch traced here: 442 us
  waiting for transfers between devices  174 us (39%)
  starting transfers between devices  66.3 us (15%)
  Pallas kernels  59.7 us (13%)
  local copies, waits for them, and re-layouts  49.9 us (11%)
  other arithmetic  43.6 us (10%)
  matrix products  33.3 us (7%)
  between operations  16.2 us (4%)
    ppermute x60, waiting for transfers between devices, trade(): return lax.ppermute(values, axes, [(i, i ^ mask) for i in range(size)])  157 us
    ppermute x60, starting transfers between devices, trade(): return lax.ppermute(values, axes, [(i, i ^ mask) for i in range(size)])  65.5 us
    pallas_call x7, Pallas kernels, kernel_call(): pl.pallas_call(whole, out_shape=out_shape, in_specs=[pl.BlockSpec(memory_...  51.4 us
    dot_general x7, matrix products, product(): lax.dot_general(left, right, (dims, ((), ())), preferred_element_type=F32)  33.3 us
    unnamed x123, local copies, waits for them, and re-layouts  23.7 us
  transfers between devices with their start and end apart: 67, of which 33 were waited for; matrix products, arithmetic and copies ran while one was open for 24% of the time, Pallas kernels for 9%

profile of v4, /device:TPU:0, one launch (start us, length us, event | category | flops | bytes accessed | tf_op | source)
XLA Modules:
  0.0 442.5 jit_solution(14604370338302613910)
XLA Ops:
  13.8 2.6 fusion.59
  22.5 10.5 %collective-permute-done.3 = bf16[256,1152]{1,0:T(8,128)(2,1)S(1)} collective-permute-done((bf16[256,1152]{1,0:T(8,128)(2,1)S(1)}, bf16[256,1152]{1,0:T(8,128)(2,1)S(1)}, u32[]{:S(2)}, u32[]{:S(2)}) %collective-permute-start.3) | collective-permute-done | bytes 589856 | tf_op jit(solution)/shard_map/ppermute | solution.py:23
  45.0 3.6 collective-permute-done.7
  56.0 3.8 shard_map.169
  70.5 8.6 %shard_map.170 = (f32[512,512]{1,0:T(8,128)S(1)}, bf16[512,512]{1,0:T(8,128)(2,1)S(1)}, f32[8,512]{1,0:T(8,128)S(1)}) custom-call(bf16[512,512]{1,0:T(8,128)(2,1)S(1)} %get-tuple-element.135.q_ref.refs_0_, bf16[4,128,512]{2,1,0:T(8,128)(2,1)S(1)} %pad_maximum_fusion.20.pairs_ref.refs_1_, s32[512,128]{1,0:T(8,128)S(1)} %broadcast_in_dim.17.koff_ref.refs_2_, ...), custom_call_target="tpu_custom_call" | custom-call | flops 2147483648 | bytes 1314816 | tf_op jit(solution)/shard_map/pallas_call | solution.py:465
  83.5 2.9 collective-permute-start.13
  86.6 13.3 %collective-permute-done.15 = bf16[256,2816]{1,0:T(8,128)(2,1)} collective-permute-done((bf16[256,2816]{1,0:T(8,128)(2,1)}, bf16[256,2816]{1,0:T(8,128)(2,1)}, u32[]{:S(2)}, u32[]{:S(2)}) %collective-permute-start.15) | collective-permute-done | bytes 1441824 | tf_op jit(solution)/shard_map/ppermute | solution.py:23
  104.9 2.6 broadcast_select_fusion.1
  107.5 2.8 pad_maximum_fusion.1.own_ref
  110.3 13.7 %collective-permute-done.13.p2 = bf16[128,2048]{1,0:T(8,128)(2,1)S(1)} collective-permute-done((bf16[128,2048]{1,0:T(8,128)(2,1)}, bf16[128,2048]{1,0:T(8,128)(2,1)S(1)}, u32[]{:S(2)}, u32[]{:S(2)}) %collective-permute-start.13) | collective-permute-done | bytes 524320 | tf_op jit(solution)/shard_map/ppermute | solution.py:23
  126.0 2.9 shard_map.171
  134.7 3.1 fusion.57
  140.5 5.8 %collective-permute-done.20 = bf16[512,512]{1,0:T(8,128)(2,1)S(1)} collective-permute-done((bf16[512,512]{1,0:T(8,128)(2,1)S(1)}, bf16[512,512]{1,0:T(8,128)(2,1)S(1)}, u32[]{:S(2)}, u32[]{:S(2)}) %collective-permute-start.20) | collective-permute-done | bytes 524320 | tf_op jit(solution)/shard_map/ppermute | solution.py:23
  147.4 2.9 pad_maximum_fusion.9
  153.0 6.9 %fusion.10.gi_ref = f32[512,1408]{1,0:T(8,128)} fusion(bf16[512,2048]{1,0:T(8,128)(2,1)S(1)} %copy-done.30, bf16[1408,1024]{1,0:T(8,128)(2,1)} %collective-permute-done.22, bf16[1408,512]{1,0:T(8,128)(2,1)S(1)} %copy-done.23, bf16[1408,512]{1,0:T(8,128)(2,1)S(1)} %copy-done.21), kind=kOutput, calls=%fused_computation.33 | convolution fusion | flops 2970091520 | bytes 10747904 | tf_op jit(solution)/shard_map/dot_general | solution.py:184
  159.9 5.5 %all-gather.7.cloned.1.call-done.h_ref = bf16[512,2048]{1,0:T(8,128)(2,1)} async-done(((bf16[128,2048]{1,0:T(8,128)(2,1)}), bf16[512,2048]{1,0:T(8,128)(2,1)}) %all-gather.7.cloned.1.call-update) | async-done | bytes 2097168 | tf_op jit(solution)/shard_map/all_gather | solution.py:67
  167.0 16.9 %shard_map.172 = (bf16[512,1408]{1,0:T(8,128)(2,1)S(1)}, bf16[512,2816]{1,0:T(8,128)(2,1)}, bf16[512,2048]{1,0:T(8,128)(2,1)S(1)}) custom-call(bf16[512,2048]{1,0:T(8,128)(2,1)S(1)} %copy-done.8, f32[512,1408]{1,0:T(8,128)} %fusion.10.gi_ref, bf16[1024,2816]{1,0:T(8,128)(2,1)} %pad_maximum_fusion.1.own_ref, bf16[1024,2816]{1,0:T(8,128)(2,1)} %collective-permute-done.23.other_ref), custom_call_target="tpu_custom_call" | custom-call | flops 11811160064 | bytes 16515072 | tf_op jit(solution)/shard_map/pallas_call | solution.py:465
  189.4 6.1 %collective-permute-done.26 = bf16[512,1408]{1,0:T(8,128)(2,1)S(1)} collective-permute-done((bf16[512,1408]{1,0:T(8,128)(2,1)}, bf16[512,1408]{1,0:T(8,128)(2,1)S(1)}, u32[]{:S(2)}, u32[]{:S(2)}) %collective-permute-start.26) | collective-permute-done | bytes 1441824 | tf_op jit(solution)/shard_map/ppermute | solution.py:23
  195.5 3.7 convolution_convert_fusion
  199.2 8.4 %fusion.4 = bf16[1024,2816]{1,0:T(8,128)(2,1)S(1)} fusion(bf16[512,2816]{1,0:T(8,128)(2,1)} %collective-permute-done.25, bf16[512,2816]{1,0:T(8,128)(2,1)S(1)} %copy-done.56, bf16[512,1024]{1,0:T(8,128)(2,1)S(1)} %collective-permute-done.24, bf16[512,256]{1,0:T(8,128)(2,1)S(1)} %get-tuple-element.283, bf16[512,256]{1,0:T(8,128)(2,1)S(1)} %get-tuple-element.284, ...), kind=kOutput, calls=%fused_computation.7 | convolution fusion | flops 5930483712 | bytes 13631488 | tf_op jit(solution)/shard_map/dot_general | solution.py:184
  207.7 3.8 pad_maximum_fusion
  211.5 5.0 %reduce-scatter.4.cloned.1.call-done.part_ref = bf16[128,2048]{1,0:T(8,128)(2,1)} async-done(((bf16[512,2048]{1,0:T(8,128)(2,1)}), bf16[128,2048]{1,0:T(8,128)(2,1)}) %reduce-scatter.4.cloned.1.call-update) | async-done | bytes 524304 | tf_op jit(solution)/shard_map/reduce_scatter | solution.py:71
  216.5 2.6 shard_map.173
  223.8 6.5 %convolution_convert_fusion.2 = bf16[512,2048]{1,0:T(8,128)(2,1)S(1)} fusion(bf16[512,1408]{1,0:T(8,128)(2,1)} %copy-done.12, bf16[1408,1024]{1,0:T(8,128)(2,1)} %collective-permute-done.22, bf16[1408,512]{1,0:T(8,128)(2,1)} %copy-done.22, bf16[1408,512]{1,0:T(8,128)(2,1)} %copy-done.20), kind=kOutput, calls=%fused_computation.18 | convolution fusion | flops 2971140096 | bytes 9306112 | tf_op jit(solution)/shard_map/dot_general | solution.py:184
  231.6 2.6 collective-permute-done.29.b1
  234.2 10.5 %collective-permute-done.30.b2 = bf16[128,2048]{1,0:T(8,128)(2,1)S(1)} collective-permute-done((bf16[128,2048]{1,0:T(8,128)(2,1)}, bf16[128,2048]{1,0:T(8,128)(2,1)S(1)}, u32[]{:S(2)}, u32[]{:S(2)}) %collective-permute-start.30) | collective-permute-done | bytes 524320 | tf_op jit(solution)/shard_map/ppermute | solution.py:23
  244.7 2.6 collective-permute-done.31.b3
  252.1 7.2 %shard_map.175 = (bf16[256,512]{1,0:T(8,128)(2,1)S(1)}, f32[4,64,512]{2,1,0:T(8,128)S(1)}, f32[4,64,512]{2,1,0:T(8,128)S(1)}) custom-call(bf16[512,512]{1,0:T(8,128)(2,1)S(1)} %copy-done.15, bf16[4,128,512]{2,1,0:T(8,128)(2,1)S(1)} %copy-done.11, s32[512,128]{1,0:T(8,128)S(1)} %broadcast_in_dim.17.koff_ref.refs_2_, s32[1,512]{1,0:T(1,128)S(1)} %bitcast.64, ...), custom_call_target="tpu_custom_call" | custom-call | flops 2684354560 | bytes 3035136 | tf_op jit(solution)/shard_map/pallas_call | solution.py:465
  260.7 6.8 %shard_map.176 = (bf16[256,512]{1,0:T(8,128)(2,1)S(1)}, bf16[128,512]{1,0:T(8,128)(2,1)S(1)}, bf16[128,512]{1,0:T(8,128)(2,1)S(1)}, bf16[128,512]{1,0:T(8,128)(2,1)S(1)}, bf16[128,512]{1,0:T(8,128)(2,1)S(1)}) custom-call(bf16[512,512]{1,0:T(8,128)(2,1)S(1)} %copy-done.15, bf16[4,128,512]{2,1,0:T(8,128)(2,1)S(1)} %copy-done.11, ...), custom_call_target="tpu_custom_call" | custom-call | flops 2684354560 | bytes 4083712 | tf_op jit(solution)/shard_map/pallas_call | solution.py:465
  269.7 6.8 %collective-permute-done.35.g2 = bf16[128,512]{1,0:T(8,128)(2,1)S(1)} collective-permute-done((bf16[128,512]{1,0:T(8,128)(2,1)S(1)}, bf16[128,512]{1,0:T(8,128)(2,1)S(1)}, u32[]{:S(2)}, u32[]{:S(2)}) %collective-permute-start.35) | collective-permute-done | bytes 131104 | tf_op jit(solution)/shard_map/ppermute | solution.py:23
  276.4 3.8 collective-permute-done.36.g3
  280.2 5.8 %shard_map.177 = (bf16[640,512]{1,0:T(8,128)(2,1)}, bf16[512,2048]{1,0:T(8,128)(2,1)}) custom-call(bf16[256,512]{1,0:T(8,128)(2,1)S(1)} %get-tuple-element.177.gq0, bf16[256,512]{1,0:T(8,128)(2,1)S(1)} %get-tuple-element.184.gq1, bf16[128,512]{1,0:T(8,128)(2,1)S(1)} %get-tuple-element.189.g0, bf16[128,512]{1,0:T(8,128)(2,1)S(1)} %collective-permute-done.34.g1, ...), custom_call_target="tpu_custom_call" | custom-call | flops 1342177280 | bytes 5898240 | tf_op jit(solution)/shard_map/pallas_call | solution.py:465
  288.1 3.3 collective-permute-done.37
  291.4 3.9 convolution_convert_fusion.3
  303.9 6.1 %reduce-scatter.6.cloned.1.call-done = bf16[64,4224]{1,0:T(8,128)(2,1)} async-done(((bf16[1024,4224]{1,0:T(8,128)(2,1)}), bf16[64,4224]{1,0:T(8,128)(2,1)}) %reduce-scatter.6.cloned.1.call-update) | async-done | bytes 540688 | tf_op jit(solution)/shard_map/reduce_scatter | solution.py:610
  312.8 5.0 %collective-permute-done.39 = bf16[2,128,1152]{2,1,0:T(8,128)(2,1)S(1)} collective-permute-done((bf16[2,128,1152]{2,1,0:T(8,128)(2,1)}, bf16[2,128,1152]{2,1,0:T(8,128)(2,1)S(1)}, u32[]{:S(2)}, u32[]{:S(2)}) %collective-permute-start.39) | collective-permute-done | bytes 589856 | tf_op jit(solution)/shard_map/ppermute | solution.py:23
  317.9 13.9 %collective-permute-done.40 = bf16[2,128,1152]{2,1,0:T(8,128)(2,1)} collective-permute-done((bf16[2,128,1152]{2,1,0:T(8,128)(2,1)}, bf16[2,128,1152]{2,1,0:T(8,128)(2,1)}, u32[]{:S(2)}, u32[]{:S(2)}) %collective-permute-start.40) | collective-permute-done | bytes 589856 | tf_op jit(solution)/shard_map/ppermute | solution.py:23
  331.8 3.1 collective-permute-start.28
  345.3 4.2 collective-permute-done.44
  349.5 11.5 %collective-permute-done.45 = bf16[64,1152]{1,0:T(8,128)(2,1)S(1)} collective-permute-done((bf16[64,1152]{1,0:T(8,128)(2,1)S(1)}, bf16[64,1152]{1,0:T(8,128)(2,1)S(1)}, u32[]{:S(2)}, u32[]{:S(2)}) %collective-permute-start.45) | collective-permute-done | bytes 147488 | tf_op jit(solution)/shard_map/ppermute | solution.py:23
  362.3 2.7 shard_map.178
  368.3 2.9 collective-permute-start.50
  378.9 4.9 %collective-permute-done.46 = bf16[64,1152]{1,0:T(8,128)(2,1)S(1)} collective-permute-done((bf16[64,1152]{1,0:T(8,128)(2,1)S(1)}, bf16[64,1152]{1,0:T(8,128)(2,1)S(1)}, u32[]{:S(2)}, u32[]{:S(2)}) %collective-permute-start.46) | collective-permute-done | bytes 147488 | tf_op jit(solution)/shard_map/ppermute | solution.py:23
  393.9 8.9 %collective-permute-done.51 = bf16[128,1152]{1,0:T(8,128)(2,1)S(1)} collective-permute-done((bf16[128,1152]{1,0:T(8,128)(2,1)S(1)}, bf16[128,1152]{1,0:T(8,128)(2,1)S(1)}, u32[]{:S(2)}, u32[]{:S(2)}) %collective-permute-start.51) | collective-permute-done | bytes 294944 | tf_op jit(solution)/shard_map/ppermute | solution.py:23
  402.8 13.0 %collective-permute-done.52 = bf16[128,1152]{1,0:T(8,128)(2,1)S(1)} collective-permute-done((bf16[128,1152]{1,0:T(8,128)(2,1)S(1)}, bf16[128,1152]{1,0:T(8,128)(2,1)S(1)}, u32[]{:S(2)}, u32[]{:S(2)}) %collective-permute-start.52) | collective-permute-done | bytes 294944 | tf_op jit(solution)/shard_map/ppermute | solution.py:23
  418.6 2.7 collective-permute-start.58
  426.7 2.6 copy.26
  429.2 3.1 convert_multiply_fusion
  (328 shorter events, 144.1 us)
Async XLA Ops:
  7.2 47.2 %all-gather.5.cloned.1.call-start = ((), (), s32[]{:S(2)}) async-start(), calls=%async_computation.3 | async-start | bytes 2621440 | tf_op jit(solution)/shard_map/all_gather | solution.py:67
  8.5 8.7 %collective-permute-start = (bf16[128,512]{1,0:T(8,128)(2,1)S(1)}, bf16[128,512]{1,0:T(8,128)(2,1)S(1)}, u32[]{:S(2)}, u32[]{:S(2)}) collective-permute-start(bf16[128,512]{1,0:T(8,128)(2,1)S(1)} %get-tuple-element.330), channel_id=1, source_target_pairs={{0,1},{1,0},{2,3},{3,2},{4,5},{5,4},{6,7},{7,6},{8,9},{9,8},{10,11... | collective-permute-start | bytes 393224 | tf_op jit(solution)/shard_map/ppermute | solution.py:23
  8.6 8.6 %collective-permute-start.1 = (bf16[128,512]{1,0:T(8,128)(2,1)S(1)}, bf16[128,512]{1,0:T(8,128)(2,1)S(1)}, u32[]{:S(2)}, u32[]{:S(2)}) collective-permute-start(bf16[128,512]{1,0:T(8,128)(2,1)S(1)} %get-tuple-element.332), channel_id=1, source_target_pairs={{0,2},{1,3},{2,0},{3,1},{4,6},{5,7},{6,4},{7,5},{8,10},{9,11},{10,... | collective-permute-start | bytes 393224 | tf_op jit(solution)/shard_map/ppermute | solution.py:23
  17.3 15.7 %collective-permute-start.3 = (bf16[256,1152]{1,0:T(8,128)(2,1)S(1)}, bf16[256,1152]{1,0:T(8,128)(2,1)S(1)}, u32[]{:S(2)}, u32[]{:S(2)}) collective-permute-start(bf16[256,1152]{1,0:T(8,128)(2,1)S(1)} %get-tuple-element.123), channel_id=1, source_target_pairs={{0,2},{2,0},{16,18},{18,16},{1,3},{3,1},{17,19},{19,17},{4,6},{6,4... | collective-permute-start | bytes 1769480 | tf_op jit(solution)/shard_map/ppermute | solution.py:23
  19.0 16.5 %collective-permute-start.4 = (bf16[256,1152]{1,0:T(8,128)(2,1)S(1)}, bf16[256,1152]{1,0:T(8,128)(2,1)S(1)}, u32[]{:S(2)}, u32[]{:S(2)}) collective-permute-start(bf16[256,1152]{1,0:T(8,128)(2,1)S(1)} %get-tuple-element.124), channel_id=1, source_target_pairs={{0,18},{2,16},{16,2},{18,0},{1,19},{3,17},{17,3},{19,1},{4,22},{6,... | collective-permute-start | bytes 1769480 | tf_op jit(solution)/shard_map/ppermute | solution.py:23
  22.3 115.6 %all-gather.9.cloned.1.call-start = ((), (), s32[]{:S(2)}) async-start(), calls=%async_computation.5 | async-start | bytes 2621440 | tf_op jit(solution)/shard_map/all_gather | solution.py:67
  36.1 15.3 %collective-permute-start.5 = (bf16[2,512,1152]{2,1,0:T(8,128)(2,1)S(1)}, bf16[2,512,1152]{2,1,0:T(8,128)(2,1)}, u32[]{:S(2)}, u32[]{:S(2)}) collective-permute-start(bf16[2,512,1152]{2,1,0:T(8,128)(2,1)S(1)} %bitcast.55), channel_id=1, source_target_pairs={{0,1},{1,0},{2,3},{3,2},{4,5},{5,4},{6,7},{7,6},{8,9},{9,8},{10,11... | collective-permute-start | bytes 7077896 | tf_op jit(solution)/shard_map/ppermute | solution.py:23
  59.8 10.6 %collective-permute-start.9 = (bf16[128,512]{1,0:T(8,128)(2,1)S(1)}, bf16[128,512]{1,0:T(8,128)(2,1)S(1)}, u32[]{:S(2)}, u32[]{:S(2)}) collective-permute-start(bf16[128,512]{1,0:T(8,128)(2,1)S(1)} %get-tuple-element.136), channel_id=1, source_target_pairs={{0,1},{1,0},{2,3},{3,2},{4,5},{5,4},{6,7},{7,6},{8,9},{9,8},{10,11... | collective-permute-start | bytes 393224 | tf_op jit(solution)/shard_map/ppermute | solution.py:23
  60.6 9.8 %collective-permute-start.10 = (bf16[128,512]{1,0:T(8,128)(2,1)S(1)}, bf16[128,512]{1,0:T(8,128)(2,1)S(1)}, u32[]{:S(2)}, u32[]{:S(2)}) collective-permute-start(bf16[128,512]{1,0:T(8,128)(2,1)S(1)} %get-tuple-element.136), channel_id=1, source_target_pairs={{0,2},{1,3},{2,0},{3,1},{4,6},{5,7},{6,4},{7,5},{8,10},{9,11},{10,... | collective-permute-start | bytes 393224 | tf_op jit(solution)/shard_map/ppermute | solution.py:23
  60.8 9.6 %collective-permute-start.11 = (bf16[128,512]{1,0:T(8,128)(2,1)S(1)}, bf16[128,512]{1,0:T(8,128)(2,1)S(1)}, u32[]{:S(2)}, u32[]{:S(2)}) collective-permute-start(bf16[128,512]{1,0:T(8,128)(2,1)S(1)} %get-tuple-element.136), channel_id=1, source_target_pairs={{0,3},{1,2},{2,1},{3,0},{4,7},{5,6},{6,5},{7,4},{8,11},{9,10},{10,... | collective-permute-start | bytes 393224 | tf_op jit(solution)/shard_map/ppermute | solution.py:23
  62.0 37.9 %collective-permute-start.15 = (bf16[256,2816]{1,0:T(8,128)(2,1)}, bf16[256,2816]{1,0:T(8,128)(2,1)}, u32[]{:S(2)}, u32[]{:S(2)}) collective-permute-start(bf16[256,2816]{1,0:T(8,128)(2,1)} %get-tuple-element.142), channel_id=1, source_target_pairs={{0,2},{2,0},{16,18},{18,16},{1,3},{3,1},{17,19},{19,17},{4,6},{6,4... | collective-permute-start | bytes 4325384 | tf_op jit(solution)/shard_map/ppermute | solution.py:23
  62.7 37.2 %collective-permute-start.16 = (bf16[256,2816]{1,0:T(8,128)(2,1)}, bf16[256,2816]{1,0:T(8,128)(2,1)}, u32[]{:S(2)}, u32[]{:S(2)}) collective-permute-start(bf16[256,2816]{1,0:T(8,128)(2,1)} %get-tuple-element.143), channel_id=1, source_target_pairs={{0,18},{2,16},{16,2},{18,0},{1,19},{3,17},{17,3},{19,1},{4,22},{6,... | collective-permute-start | bytes 4325384 | tf_op jit(solution)/shard_map/ppermute | solution.py:23
  69.9 95.5 %all-gather.7.cloned.1.call-start = ((), (), s32[]{:S(2)}) async-start(), calls=%async_computation.4 | async-start | bytes 2621440 | tf_op jit(solution)/shard_map/all_gather | solution.py:67
  81.9 28.4 %collective-permute-start.12 = (bf16[128,2048]{1,0:T(8,128)(2,1)}, bf16[128,2048]{1,0:T(8,128)(2,1)S(1)}, u32[]{:S(2)}, u32[]{:S(2)}) collective-permute-start(bf16[128,2048]{1,0:T(8,128)(2,1)} %get-tuple-element.298), channel_id=1, source_target_pairs={{0,4},{4,0},{8,12},{12,8},{1,5},{5,1},{9,13},{13,9},{2,6},{6,2},{1... | collective-permute-start | bytes 1572872 | tf_op jit(solution)/shard_map/ppermute | solution.py:23
  83.5 40.5 %collective-permute-start.13 = (bf16[128,2048]{1,0:T(8,128)(2,1)}, bf16[128,2048]{1,0:T(8,128)(2,1)S(1)}, u32[]{:S(2)}, u32[]{:S(2)}) collective-permute-start(bf16[128,2048]{1,0:T(8,128)(2,1)} %get-tuple-element.297), channel_id=1, source_target_pairs={{0,8},{4,12},{8,0},{12,4},{1,9},{5,13},{9,1},{13,5},{2,10},{6,14},... | collective-permute-start | bytes 1572872 | tf_op jit(solution)/shard_map/ppermute | solution.py:23
  86.4 37.5 %collective-permute-start.14 = (bf16[128,2048]{1,0:T(8,128)(2,1)}, bf16[128,2048]{1,0:T(8,128)(2,1)S(1)}, u32[]{:S(2)}, u32[]{:S(2)}) collective-permute-start(bf16[128,2048]{1,0:T(8,128)(2,1)} %get-tuple-element.296), channel_id=1, source_target_pairs={{0,12},{4,8},{8,4},{12,0},{1,13},{5,9},{9,5},{13,1},{2,14},{6,10},... | collective-permute-start | bytes 1572872 | tf_op jit(solution)/shard_map/ppermute | solution.py:23
  99.9 24.1 %collective-permute-start.18 = (bf16[704,512]{1,0:T(8,128)(2,1)S(1)}, bf16[704,512]{1,0:T(8,128)(2,1)S(1)}, u32[]{:S(2)}, u32[]{:S(2)}) collective-permute-start(bf16[704,512]{1,0:T(8,128)(2,1)S(1)} %copy-done.26), channel_id=1, source_target_pairs={{0,18},{2,16},{16,2},{18,0},{1,19},{3,17},{17,3},{19,1},{4,22},{6,... | collective-permute-start | bytes 2162696 | tf_op jit(solution)/shard_map/ppermute | solution.py:23
  102.0 22.0 %collective-permute-start.17 = (bf16[704,512]{1,0:T(8,128)(2,1)S(1)}, bf16[704,512]{1,0:T(8,128)(2,1)S(1)}, u32[]{:S(2)}, u32[]{:S(2)}) collective-permute-start(bf16[704,512]{1,0:T(8,128)(2,1)S(1)} %copy-done.27), channel_id=1, source_target_pairs={{0,2},{2,0},{16,18},{18,16},{1,3},{3,1},{17,19},{19,17},{4,6},{6,4... | collective-permute-start | bytes 2162696 | tf_op jit(solution)/shard_map/ppermute | solution.py:23
  128.9 36.5 %collective-permute-start.23 = (bf16[1024,2816]{1,0:T(8,128)(2,1)}, bf16[1024,2816]{1,0:T(8,128)(2,1)}, u32[]{:S(2)}, u32[]{:S(2)}) collective-permute-start(bf16[1024,2816]{1,0:T(8,128)(2,1)} %pad_maximum_fusion.1.own_ref), channel_id=1, source_target_pairs={{0,1},{1,0},{2,3},{3,2},{4,5},{5,4},{6,7},{7,6},{8,9},{9,8},{10,11... | collective-permute-start | bytes 17301512 | tf_op jit(solution)/shard_map/ppermute | solution.py:23
  134.2 17.7 %collective-permute-start.22 = (bf16[1408,1024]{1,0:T(8,128)(2,1)}, bf16[1408,1024]{1,0:T(8,128)(2,1)}, u32[]{:S(2)}, u32[]{:S(2)}) collective-permute-start(bf16[1408,1024]{1,0:T(8,128)(2,1)} %pad_maximum_fusion.3), channel_id=1, source_target_pairs={{0,1},{1,0},{2,3},{3,2},{4,5},{5,4},{6,7},{7,6},{8,9},{9,8},{10,11... | collective-permute-start | bytes 8650760 | tf_op jit(solution)/shard_map/ppermute | solution.py:23
  134.7 81.8 %reduce-scatter.4.cloned.1.call-start = ((), (), s32[]{:S(2)}) async-start(), calls=%async_computation.6 | async-start | bytes 2621440 | tf_op jit(solution)/shard_map/reduce_scatter | solution.py:71
  137.9 9.6 %collective-permute-start.21 = (bf16[512,1024]{1,0:T(8,128)(2,1)}, bf16[512,1024]{1,0:T(8,128)(2,1)}, u32[]{:S(2)}, u32[]{:S(2)}) collective-permute-start(bf16[512,1024]{1,0:T(8,128)(2,1)} %get-tuple-element.287), channel_id=1, source_target_pairs={{0,1},{1,0},{2,3},{3,2},{4,5},{5,4},{6,7},{7,6},{8,9},{9,8},{10,11... | collective-permute-start | bytes 3145736 | tf_op jit(solution)/shard_map/ppermute | solution.py:23
  139.8 10.6 %collective-permute-start.19 = (bf16[512,1024]{1,0:T(8,128)(2,1)S(1)}, bf16[512,1024]{1,0:T(8,128)(2,1)S(1)}, u32[]{:S(2)}, u32[]{:S(2)}) collective-permute-start(bf16[512,1024]{1,0:T(8,128)(2,1)S(1)} %pad_maximum_fusion.13), channel_id=1, source_target_pairs={{0,1},{1,0},{2,3},{3,2},{4,5},{5,4},{6,7},{7,6},{8,9},{9,8},{10,11... | collective-permute-start | bytes 3145736 | tf_op jit(solution)/shard_map/ppermute | solution.py:23
  186.4 12.8 %collective-permute-start.25 = (bf16[512,2816]{1,0:T(8,128)(2,1)}, bf16[512,2816]{1,0:T(8,128)(2,1)}, u32[]{:S(2)}, u32[]{:S(2)}) collective-permute-start(bf16[512,2816]{1,0:T(8,128)(2,1)} %get-tuple-element.164), channel_id=1, source_target_pairs={{0,1},{1,0},{2,3},{3,2},{4,5},{5,4},{6,7},{7,6},{8,9},{9,8},{10,11... | collective-permute-start | bytes 8650760 | tf_op jit(solution)/shard_map/ppermute | solution.py:23
  186.4 123.5 %reduce-scatter.6.cloned.1.call-start = ((), (), s32[]{:S(2)}) async-start(), calls=%async_computation.7 | async-start | bytes 9191424 | tf_op jit(solution)/shard_map/reduce_scatter | solution.py:610
  186.5 9.0 %collective-permute-start.26 = (bf16[512,1408]{1,0:T(8,128)(2,1)}, bf16[512,1408]{1,0:T(8,128)(2,1)S(1)}, u32[]{:S(2)}, u32[]{:S(2)}) collective-permute-start(bf16[512,1408]{1,0:T(8,128)(2,1)} %copy-done.12), channel_id=1, source_target_pairs={{0,1},{1,0},{2,3},{3,2},{4,5},{5,4},{6,7},{7,6},{8,9},{9,8},{10,11... | collective-permute-start | bytes 4325384 | tf_op jit(solution)/shard_map/ppermute | solution.py:23
  189.3 9.9 %collective-permute-start.24 = (bf16[512,1024]{1,0:T(8,128)(2,1)S(1)}, bf16[512,1024]{1,0:T(8,128)(2,1)S(1)}, u32[]{:S(2)}, u32[]{:S(2)}) collective-permute-start(bf16[512,1024]{1,0:T(8,128)(2,1)S(1)} %pad_maximum_fusion.15), channel_id=1, source_target_pairs={{0,1},{1,0},{2,3},{3,2},{4,5},{5,4},{6,7},{7,6},{8,9},{9,8},{10,11... | collective-permute-start | bytes 3145736 | tf_op jit(solution)/shard_map/ppermute | solution.py:23
  216.5 145.8 %reduce-scatter.8.cloned.1.call-start = ((), (), s32[]{:S(2)}) async-start(), calls=%async_computation.8 | async-start | bytes 2621440 | tf_op jit(solution)/shard_map/reduce_scatter | solution.py:71
  219.1 15.0 %collective-permute-start.29 = (bf16[128,2048]{1,0:T(8,128)(2,1)}, bf16[128,2048]{1,0:T(8,128)(2,1)S(1)}, u32[]{:S(2)}, u32[]{:S(2)}) collective-permute-start(bf16[128,2048]{1,0:T(8,128)(2,1)} %get-tuple-element.194.b0), channel_id=1, source_target_pairs={{0,4},{4,0},{8,12},{12,8},{1,5},{5,1},{9,13},{13,9},{2,6},{6,2},{1... | collective-permute-start | bytes 1572872 | tf_op jit(solution)/shard_map/ppermute | solution.py:23
  219.4 25.3 %collective-permute-start.30 = (bf16[128,2048]{1,0:T(8,128)(2,1)}, bf16[128,2048]{1,0:T(8,128)(2,1)S(1)}, u32[]{:S(2)}, u32[]{:S(2)}) collective-permute-start(bf16[128,2048]{1,0:T(8,128)(2,1)} %get-tuple-element.194.b0), channel_id=1, source_target_pairs={{0,8},{4,12},{8,0},{12,4},{1,9},{5,13},{9,1},{13,5},{2,10},{6,14},... | collective-permute-start | bytes 1572872 | tf_op jit(solution)/shard_map/ppermute | solution.py:23
  221.4 25.8 %collective-permute-start.31 = (bf16[128,2048]{1,0:T(8,128)(2,1)}, bf16[128,2048]{1,0:T(8,128)(2,1)S(1)}, u32[]{:S(2)}, u32[]{:S(2)}) collective-permute-start(bf16[128,2048]{1,0:T(8,128)(2,1)} %get-tuple-element.194.b0), channel_id=1, source_target_pairs={{0,12},{4,8},{8,4},{12,0},{1,13},{5,9},{9,5},{13,1},{2,14},{6,10},... | collective-permute-start | bytes 1572872 | tf_op jit(solution)/shard_map/ppermute | solution.py:23
  247.3 12.2 %collective-permute-start.32 = (bf16[128,2048]{1,0:T(8,128)(2,1)S(1)}, bf16[128,2048]{1,0:T(8,128)(2,1)S(1)}, u32[]{:S(2)}, u32[]{:S(2)}) collective-permute-start(bf16[128,2048]{1,0:T(8,128)(2,1)S(1)} %get-tuple-element.180), channel_id=1, source_target_pairs={{0,4},{4,0},{8,12},{12,8},{1,5},{5,1},{9,13},{13,9},{2,6},{6,2},{1... | collective-permute-start | bytes 1572872 | tf_op jit(solution)/shard_map/ppermute | solution.py:23
  247.3 13.4 %collective-permute-start.33 = (bf16[128,2048]{1,0:T(8,128)(2,1)S(1)}, bf16[128,2048]{1,0:T(8,128)(2,1)S(1)}, u32[]{:S(2)}, u32[]{:S(2)}) collective-permute-start(bf16[128,2048]{1,0:T(8,128)(2,1)S(1)} %get-tuple-element.181), channel_id=1, source_target_pairs={{0,12},{4,8},{8,4},{12,0},{1,13},{5,9},{9,5},{13,1},{2,14},{6,10},... | collective-permute-start | bytes 1572872 | tf_op jit(solution)/shard_map/ppermute | solution.py:23
  267.7 8.8 %collective-permute-start.35 = (bf16[128,512]{1,0:T(8,128)(2,1)S(1)}, bf16[128,512]{1,0:T(8,128)(2,1)S(1)}, u32[]{:S(2)}, u32[]{:S(2)}) collective-permute-start(bf16[128,512]{1,0:T(8,128)(2,1)S(1)} %get-tuple-element.187), channel_id=1, source_target_pairs={{0,2},{1,3},{2,0},{3,1},{4,6},{5,7},{6,4},{7,5},{8,10},{9,11},{10,... | collective-permute-start | bytes 393224 | tf_op jit(solution)/shard_map/ppermute | solution.py:23
  269.3 10.9 %collective-permute-start.36 = (bf16[128,512]{1,0:T(8,128)(2,1)S(1)}, bf16[128,512]{1,0:T(8,128)(2,1)S(1)}, u32[]{:S(2)}, u32[]{:S(2)}) collective-permute-start(bf16[128,512]{1,0:T(8,128)(2,1)S(1)} %get-tuple-element.188), channel_id=1, source_target_pairs={{0,3},{1,2},{2,1},{3,0},{4,7},{5,6},{6,5},{7,4},{8,11},{9,10},{10,... | collective-permute-start | bytes 393224 | tf_op jit(solution)/shard_map/ppermute | solution.py:23
  299.2 18.7 %collective-permute-start.39 = (bf16[2,128,1152]{2,1,0:T(8,128)(2,1)}, bf16[2,128,1152]{2,1,0:T(8,128)(2,1)S(1)}, u32[]{:S(2)}, u32[]{:S(2)}) collective-permute-start(bf16[2,128,1152]{2,1,0:T(8,128)(2,1)} %get-tuple-element.260), channel_id=1, source_target_pairs={{0,32},{32,0},{64,96},{96,64},{1,33},{33,1},{65,97},{97,65},{2,34}... | collective-permute-start | bytes 1769480 | tf_op jit(solution)/shard_map/ppermute | solution.py:23
  299.3 32.4 %collective-permute-start.40 = (bf16[2,128,1152]{2,1,0:T(8,128)(2,1)}, bf16[2,128,1152]{2,1,0:T(8,128)(2,1)}, u32[]{:S(2)}, u32[]{:S(2)}) collective-permute-start(bf16[2,128,1152]{2,1,0:T(8,128)(2,1)} %get-tuple-element.261), channel_id=1, source_target_pairs={{0,64},{32,96},{64,0},{96,32},{1,65},{33,97},{65,1},{97,33},{2,66}... | collective-permute-start | bytes 1769480 | tf_op jit(solution)/shard_map/ppermute | solution.py:23
  301.7 30.0 %collective-permute-start.41 = (bf16[2,128,1152]{2,1,0:T(8,128)(2,1)}, bf16[2,128,1152]{2,1,0:T(8,128)(2,1)}, u32[]{:S(2)}, u32[]{:S(2)}) collective-permute-start(bf16[2,128,1152]{2,1,0:T(8,128)(2,1)} %get-tuple-element.259), channel_id=1, source_target_pairs={{0,96},{32,64},{64,32},{96,0},{1,97},{33,65},{65,33},{97,1},{2,98}... | collective-permute-start | bytes 1769480 | tf_op jit(solution)/shard_map/ppermute | solution.py:23
  311.4 20.3 %collective-permute-start.27 = (f32[64,128]{1,0:T(8,128)S(1)}, f32[64,128]{1,0:T(8,128)S(1)}, u32[]{:S(2)}, u32[]{:S(2)}) collective-permute-start(f32[64,128]{1,0:T(8,128)S(1)} %broadcast_in_dim.20), channel_id=1, source_target_pairs={{0,4},{4,0},{8,12},{12,8},{1,5},{5,1},{9,13},{13,9},{2,6},{6,2},{1... | collective-permute-start | bytes 98312 | tf_op jit(solution)/shard_map/ppermute | solution.py:23
  312.8 113.9 %all-gather.11.cloned.1.call-start = ((), (), s32[]{:S(2)}) async-start(), calls=%async_computation.9 | async-start | bytes 5570560 | tf_op jit(solution)/shard_map/all_gather | solution.py:675
  340.6 8.9 %collective-permute-start.44 = (bf16[64,1152]{1,0:T(8,128)(2,1)S(1)}, bf16[64,1152]{1,0:T(8,128)(2,1)S(1)}, u32[]{:S(2)}, u32[]{:S(2)}) collective-permute-start(bf16[64,1152]{1,0:T(8,128)(2,1)S(1)} %get-tuple-element.317), channel_id=1, source_target_pairs={{0,16},{2,18},{16,0},{18,2},{1,17},{3,19},{17,1},{19,3},{4,20},{6,... | collective-permute-start | bytes 442376 | tf_op jit(solution)/shard_map/ppermute | solution.py:23
  342.6 18.4 %collective-permute-start.45 = (bf16[64,1152]{1,0:T(8,128)(2,1)S(1)}, bf16[64,1152]{1,0:T(8,128)(2,1)S(1)}, u32[]{:S(2)}, u32[]{:S(2)}) collective-permute-start(bf16[64,1152]{1,0:T(8,128)(2,1)S(1)} %get-tuple-element.316), channel_id=1, source_target_pairs={{0,18},{2,16},{16,2},{18,0},{1,19},{3,17},{17,3},{19,1},{4,22},{6,... | collective-permute-start | bytes 442376 | tf_op jit(solution)/shard_map/ppermute | solution.py:23
  343.4 17.7 %collective-permute-start.42 = (bf16[64,4352]{1,0:T(8,128)(2,1)S(1)}, bf16[64,4352]{1,0:T(8,128)(2,1)S(1)}, u32[]{:S(2)}, u32[]{:S(2)}) collective-permute-start(bf16[64,4352]{1,0:T(8,128)(2,1)S(1)} %pad_maximum_fusion.18), channel_id=1, source_target_pairs={{0,16},{2,18},{16,0},{18,2},{1,17},{3,19},{17,1},{19,3},{4,20},{6,... | collective-permute-start | bytes 1671176 | tf_op jit(solution)/shard_map/ppermute | solution.py:23
  368.3 15.7 %collective-permute-start.50 = (bf16[128,2048]{1,0:T(8,128)(2,1)S(1)}, bf16[128,2048]{1,0:T(8,128)(2,1)S(1)}, u32[]{:S(2)}, u32[]{:S(2)}) collective-permute-start(bf16[128,2048]{1,0:T(8,128)(2,1)S(1)} %copy-done.53), channel_id=1, source_target_pairs={{0,8},{4,12},{8,0},{12,4},{1,9},{5,13},{9,1},{13,5},{2,10},{6,14},... | collective-permute-start | bytes 1572872 | tf_op jit(solution)/shard_map/ppermute | solution.py:23
  386.6 16.2 %collective-permute-start.51 = (bf16[128,1152]{1,0:T(8,128)(2,1)S(1)}, bf16[128,1152]{1,0:T(8,128)(2,1)S(1)}, u32[]{:S(2)}, u32[]{:S(2)}) collective-permute-start(bf16[128,1152]{1,0:T(8,128)(2,1)S(1)} %pad_maximum_fusion.22), channel_id=1, source_target_pairs={{0,32},{32,0},{64,96},{96,64},{1,33},{33,1},{65,97},{97,65},{2,34}... | collective-permute-start | bytes 884744 | tf_op jit(solution)/shard_map/ppermute | solution.py:23
  387.2 28.6 %collective-permute-start.52 = (bf16[128,1152]{1,0:T(8,128)(2,1)S(1)}, bf16[128,1152]{1,0:T(8,128)(2,1)S(1)}, u32[]{:S(2)}, u32[]{:S(2)}) collective-permute-start(bf16[128,1152]{1,0:T(8,128)(2,1)S(1)} %pad_maximum_fusion.22), channel_id=1, source_target_pairs={{0,64},{32,96},{64,0},{96,32},{1,65},{33,97},{65,1},{97,33},{2,66}... | collective-permute-start | bytes 884744 | tf_op jit(solution)/shard_map/ppermute | solution.py:23
  389.3 26.6 %collective-permute-start.53 = (bf16[128,1152]{1,0:T(8,128)(2,1)S(1)}, bf16[128,1152]{1,0:T(8,128)(2,1)S(1)}, u32[]{:S(2)}, u32[]{:S(2)}) collective-permute-start(bf16[128,1152]{1,0:T(8,128)(2,1)S(1)} %pad_maximum_fusion.22), channel_id=1, source_target_pairs={{0,96},{32,64},{64,32},{96,0},{1,97},{33,65},{65,33},{97,1},{2,98}... | collective-permute-start | bytes 884744 | tf_op jit(solution)/shard_map/ppermute | solution.py:23
  417.4 8.6 %collective-permute-start.57 = (f32[1,512]{1,0:T(1,128)S(1)}, f32[1,512]{1,0:T(1,128)S(1)}, u32[]{:S(2)}, u32[]{:S(2)}) collective-permute-start(f32[1,512]{1,0:T(1,128)S(1)} %bitcast.78), channel_id=1, source_target_pairs={{0,4},{4,0},{8,12},{12,8},{1,5},{5,1},{9,13},{13,9},{2,6},{6,2},{1... | collective-permute-start | bytes 6152 | tf_op jit(solution)/shard_map/ppermute | solution.py:23
  (76 other events, 450.1 us)
Sparse Core Ops, SparseCore 0:
  22.4 31.3 all-gather.4
  70.0 46.3 all-gather.8
  134.8 30.5 all-gather.6
  186.6 29.8 reduce-scatter.3
  220.1 89.7 reduce-scatter.5
  312.9 29.8 reduce-scatter.7
  362.4 61.4 all-gather.10

commit v5 on v4

--- a/solution.py
+++ b/solution.py
@@ -542,7 +542,6 @@
     rows_one, gu_halves, full_out, cot_rows = lax.optimization_barrier(
         (rows_one, gu_halves, full_out, cot_rows)
     )
-    gu_got = ring_send(gu_halves)
 
     shape = lambda kind, *dims: jax.ShapeDtypeStruct(dims, kind)
     scratch = lambda kind, *dims: pltpu.VMEM(dims, kind)
@@ -557,6 +556,8 @@
     )
     grad_rows = gather_row(after(cot_rows, query))
     all_pairs = jnp.stack([pairs] + [trade_col(pairs, m) for m in (1, 2, 3)])
+    gu_halves = [after(v, all_pairs) for v in gu_halves]
+    gu_got = ring_send(gu_halves)
 
     flops = 2 * matmul(heads * span, HD, group)
     keys_shape = (4, HD, span), (4, span, HD)
@@ -567,6 +568,7 @@
         flops,
         scratch=[scratch(BF16, *keys_shape[i]) for i in (0, 0, 1, 1)],
     )
+    mixed_low, grad_rows = lax.optimization_barrier((mixed_low, grad_rows))
     branch = product(mixed_low, full_out, ((0,), (0,)), BF16)
     gu_mine = ring_join(gu_halves, after(gu_got, branch), low, 0)
     down_halves = [after(v, branch, gu_got) for v in cut(w_down, 2, 0)]

time: 451 us -> 466 us (1.033)
  waiting for transfers between devices: 174 us -> 191 us
    ppermute x60, waiting for transfers between devices: 157 us -> 166 us  [trade(): return lax.ppermute(values, axes, [(i, i ^ mask) for i in range(size)])]
    all_gather x3, waiting for transfers between devices: 5.5 us -> 14.2 us  [gather_row(): return lax.all_gather(values, 'y', axis=0, tiled=True)]
  transfers between devices with their start and end apart: 67 -> 67, of which waited for: 33 -> 39; matrix products, arithmetic and copies ran while one was open for 24% -> 23% of each run, Pallas kernels for 9% -> 8%
where the time goes in v5:
time: 466 us; the launch traced here: 458 us
  waiting for transfers between devices  191 us (41%)
  starting transfers between devices  63.8 us (14%)
  Pallas kernels  59.7 us (13%)
  local copies, waits for them, and re-layouts  50.9 us (11%)
  other arithmetic  43.1 us (9%)
  matrix products  33.1 us (7%)
  between operations  16.1 us (3%)
    ppermute x60, waiting for transfers between devices, trade(): return lax.ppermute(values, axes, [(i, i ^ mask) for i in range(size)])  166 us
    ppermute x60, starting transfers between devices, trade(): return lax.ppermute(values, axes, [(i, i ^ mask) for i in range(size)])  63.5 us
    pallas_call x7, Pallas kernels, kernel_call(): pl.pallas_call(whole, out_shape=out_shape, in_specs=[pl.BlockSpec(memory_...  51.4 us
    dot_general x7, matrix products, product(): lax.dot_general(left, right, (dims, ((), ())), preferred_element_type=F32)  33.1 us
    unnamed x123, local copies, waits for them, and re-layouts  25.3 us
    all_gather x3, waiting for transfers between devices, gather_row(): return lax.all_gather(values, 'y', axis=0, tiled=True)  14.2 us
  transfers between devices with their start and end apart: 67, of which 39 were waited for; matrix products, arithmetic and copies ran while one was open for 23% of the time, Pallas kernels for 8%

profile of v5, /device:TPU:0, one launch (start us, length us, event | category | flops | bytes accessed | tf_op | source)
XLA Modules:
  0.0 458.1 jit_solution(2601908391545892059)
XLA Ops:
  22.2 10.4 %collective-permute-done.3 = bf16[256,1152]{1,0:T(8,128)(2,1)S(1)} collective-permute-done((bf16[256,1152]{1,0:T(8,128)(2,1)S(1)}, bf16[256,1152]{1,0:T(8,128)(2,1)S(1)}, u32[]{:S(2)}, u32[]{:S(2)}) %collective-permute-start.3) | collective-permute-done | bytes 589856 | tf_op jit(solution)/shard_map/ppermute | solution.py:23
  32.5 2.6 collective-permute-done.4
  44.6 3.6 collective-permute-done.7
  55.6 3.8 shard_map.169
  71.9 8.6 %shard_map.170 = (f32[512,512]{1,0:T(8,128)S(1)}, bf16[512,512]{1,0:T(8,128)(2,1)S(1)}, f32[8,512]{1,0:T(8,128)S(1)}) custom-call(bf16[512,512]{1,0:T(8,128)(2,1)S(1)} %get-tuple-element.139.q_ref.refs_0_, bf16[4,128,512]{2,1,0:T(8,128)(2,1)S(1)} %pad_maximum_fusion.20.pairs_ref.refs_1_, s32[512,128]{1,0:T(8,128)S(1)} %broadcast_in_dim.17.koff_ref.refs_2_, ...), custom_call_target="tpu_custom_call" | custom-call | flops 2147483648 | bytes 1314816 | tf_op jit(solution)/shard_map/pallas_call | solution.py:465
  84.7 2.7 constant_dynamic-update-slice_fusion.4
  87.4 4.9 %all-gather.7.cloned.1.call-done = bf16[512,2048]{1,0:T(8,128)(2,1)} async-done(((bf16[128,2048]{1,0:T(8,128)(2,1)}), bf16[512,2048]{1,0:T(8,128)(2,1)}) %all-gather.7.cloned.1.call-update) | async-done | bytes 2097168 | tf_op jit(solution)/shard_map/all_gather | solution.py:67
  93.6 10.0 %collective-permute-done.16 = bf16[256,2816]{1,0:T(8,128)(2,1)} collective-permute-done((bf16[256,2816]{1,0:T(8,128)(2,1)}, bf16[256,2816]{1,0:T(8,128)(2,1)}, u32[]{:S(2)}, u32[]{:S(2)}) %collective-permute-start.16) | collective-permute-done | bytes 1441824 | tf_op jit(solution)/shard_map/ppermute | solution.py:23
  110.3 2.9 collective-permute-start.13
  117.4 2.8 pad_maximum_fusion.1.own_ref
  120.3 3.5 collective-permute-done.12.p1
  123.8 12.2 %collective-permute-done.13.p2 = bf16[128,2048]{1,0:T(8,128)(2,1)S(1)} collective-permute-done((bf16[128,2048]{1,0:T(8,128)(2,1)}, bf16[128,2048]{1,0:T(8,128)(2,1)S(1)}, u32[]{:S(2)}, u32[]{:S(2)}) %collective-permute-start.13) | collective-permute-done | bytes 524320 | tf_op jit(solution)/shard_map/ppermute | solution.py:23
  136.0 2.6 collective-permute-done.14.p3
  139.4 2.9 shard_map.171
  153.5 6.1 %collective-permute-done.20 = bf16[512,512]{1,0:T(8,128)(2,1)S(1)} collective-permute-done((bf16[512,512]{1,0:T(8,128)(2,1)S(1)}, bf16[512,512]{1,0:T(8,128)(2,1)S(1)}, u32[]{:S(2)}, u32[]{:S(2)}) %collective-permute-start.20) | collective-permute-done | bytes 524320 | tf_op jit(solution)/shard_map/ppermute | solution.py:23
  164.7 6.9 %fusion.10.gi_ref = f32[512,1408]{1,0:T(8,128)} fusion(bf16[512,2048]{1,0:T(8,128)(2,1)S(1)} %copy-done.28, bf16[1408,1024]{1,0:T(8,128)(2,1)} %collective-permute-done.22, bf16[1408,512]{1,0:T(8,128)(2,1)S(1)} %copy-done.23, bf16[1408,512]{1,0:T(8,128)(2,1)S(1)} %copy-done.21), kind=kOutput, calls=%fused_computation.33 | convolution fusion | flops 2970091520 | bytes 10747904 | tf_op jit(solution)/shard_map/dot_general | solution.py:184
  171.6 9.3 %all-gather.9.cloned.1.call-done.h_ref = bf16[512,2048]{1,0:T(8,128)(2,1)} async-done(((bf16[128,2048]{1,0:T(8,128)(2,1)}), bf16[512,2048]{1,0:T(8,128)(2,1)}) %all-gather.9.cloned.1.call-update) | async-done | bytes 2097168 | tf_op jit(solution)/shard_map/all_gather | solution.py:67
  182.5 16.9 %shard_map.172 = (bf16[512,1408]{1,0:T(8,128)(2,1)S(1)}, bf16[512,2816]{1,0:T(8,128)(2,1)}, bf16[512,2048]{1,0:T(8,128)(2,1)S(1)}) custom-call(bf16[512,2048]{1,0:T(8,128)(2,1)S(1)} %copy-done.8, f32[512,1408]{1,0:T(8,128)} %fusion.10.gi_ref, bf16[1024,2816]{1,0:T(8,128)(2,1)} %pad_maximum_fusion.1.own_ref, bf16[1024,2816]{1,0:T(8,128)(2,1)} %collective-permute-done.23.other_ref), custom_call_target="tpu_custom_call" | custom-call | flops 11811160064 | bytes 16515072 | tf_op jit(solution)/shard_map/pallas_call | solution.py:465
  204.9 6.1 %collective-permute-done.26 = bf16[512,1408]{1,0:T(8,128)(2,1)S(1)} collective-permute-done((bf16[512,1408]{1,0:T(8,128)(2,1)}, bf16[512,1408]{1,0:T(8,128)(2,1)S(1)}, u32[]{:S(2)}, u32[]{:S(2)}) %collective-permute-start.26) | collective-permute-done | bytes 1441824 | tf_op jit(solution)/shard_map/ppermute | solution.py:23
  211.0 3.7 convolution_convert_fusion
  214.7 8.4 %fusion.4 = bf16[1024,2816]{1,0:T(8,128)(2,1)S(1)} fusion(bf16[512,2816]{1,0:T(8,128)(2,1)} %collective-permute-done.25, bf16[512,2816]{1,0:T(8,128)(2,1)S(1)} %copy-done.56, bf16[512,1024]{1,0:T(8,128)(2,1)S(1)} %collective-permute-done.24, bf16[512,256]{1,0:T(8,128)(2,1)S(1)} %get-tuple-element.291, bf16[512,256]{1,0:T(8,128)(2,1)S(1)} %get-tuple-element.292, ...), kind=kOutput, calls=%fused_computation.7 | convolution fusion | flops 5930483712 | bytes 13631488 | tf_op jit(solution)/shard_map/dot_general | solution.py:184
  223.2 3.8 pad_maximum_fusion
  227.0 5.0 %reduce-scatter.4.cloned.1.call-done.part_ref = bf16[128,2048]{1,0:T(8,128)(2,1)} async-done(((bf16[512,2048]{1,0:T(8,128)(2,1)}), bf16[128,2048]{1,0:T(8,128)(2,1)}) %reduce-scatter.4.cloned.1.call-update) | async-done | bytes 524304 | tf_op jit(solution)/shard_map/reduce_scatter | solution.py:71
  232.0 2.6 shard_map.173
  239.3 6.5 %convolution_convert_fusion.2 = bf16[512,2048]{1,0:T(8,128)(2,1)S(1)} fusion(bf16[512,1408]{1,0:T(8,128)(2,1)} %copy-done.12, bf16[1408,1024]{1,0:T(8,128)(2,1)} %collective-permute-done.22, bf16[1408,512]{1,0:T(8,128)(2,1)} %copy-done.22, bf16[1408,512]{1,0:T(8,128)(2,1)} %copy-done.20), kind=kOutput, calls=%fused_computation.18 | convolution fusion | flops 2971140096 | bytes 9306112 | tf_op jit(solution)/shard_map/dot_general | solution.py:184
  247.1 2.6 collective-permute-done.29.b1
  249.7 10.5 %collective-permute-done.30.b2 = bf16[128,2048]{1,0:T(8,128)(2,1)S(1)} collective-permute-done((bf16[128,2048]{1,0:T(8,128)(2,1)}, bf16[128,2048]{1,0:T(8,128)(2,1)S(1)}, u32[]{:S(2)}, u32[]{:S(2)}) %collective-permute-start.30) | collective-permute-done | bytes 524320 | tf_op jit(solution)/shard_map/ppermute | solution.py:23
  260.2 2.6 collective-permute-done.31.b3
  267.6 7.2 %shard_map.175 = (bf16[256,512]{1,0:T(8,128)(2,1)S(1)}, f32[4,64,512]{2,1,0:T(8,128)S(1)}, f32[4,64,512]{2,1,0:T(8,128)S(1)}) custom-call(bf16[512,512]{1,0:T(8,128)(2,1)S(1)} %copy-done.15, bf16[4,128,512]{2,1,0:T(8,128)(2,1)S(1)} %copy-done.11, s32[512,128]{1,0:T(8,128)S(1)} %broadcast_in_dim.17.koff_ref.refs_2_, s32[1,512]{1,0:T(1,128)S(1)} %bitcast.64, ...), custom_call_target="tpu_custom_call" | custom-call | flops 2684354560 | bytes 3035136 | tf_op jit(solution)/shard_map/pallas_call | solution.py:465
  276.2 6.8 %shard_map.176 = (bf16[256,512]{1,0:T(8,128)(2,1)S(1)}, bf16[128,512]{1,0:T(8,128)(2,1)S(1)}, bf16[128,512]{1,0:T(8,128)(2,1)S(1)}, bf16[128,512]{1,0:T(8,128)(2,1)S(1)}, bf16[128,512]{1,0:T(8,128)(2,1)S(1)}) custom-call(bf16[512,512]{1,0:T(8,128)(2,1)S(1)} %copy-done.15, bf16[4,128,512]{2,1,0:T(8,128)(2,1)S(1)} %copy-done.11, ...), custom_call_target="tpu_custom_call" | custom-call | flops 2684354560 | bytes 4083712 | tf_op jit(solution)/shard_map/pallas_call | solution.py:465
  285.2 6.7 %collective-permute-done.35.g2 = bf16[128,512]{1,0:T(8,128)(2,1)S(1)} collective-permute-done((bf16[128,512]{1,0:T(8,128)(2,1)S(1)}, bf16[128,512]{1,0:T(8,128)(2,1)S(1)}, u32[]{:S(2)}, u32[]{:S(2)}) %collective-permute-start.35) | collective-permute-done | bytes 131104 | tf_op jit(solution)/shard_map/ppermute | solution.py:23
  291.9 4.1 collective-permute-done.36.g3
  296.0 5.8 %shard_map.177 = (bf16[640,512]{1,0:T(8,128)(2,1)}, bf16[512,2048]{1,0:T(8,128)(2,1)}) custom-call(bf16[256,512]{1,0:T(8,128)(2,1)S(1)} %get-tuple-element.185.gq0, bf16[256,512]{1,0:T(8,128)(2,1)S(1)} %get-tuple-element.192.gq1, bf16[128,512]{1,0:T(8,128)(2,1)S(1)} %get-tuple-element.197.g0, bf16[128,512]{1,0:T(8,128)(2,1)S(1)} %collective-permute-done.34.g1, ...), custom_call_target="tpu_custom_call" | custom-call | flops 1342177280 | bytes 5898240 | tf_op jit(solution)/shard_map/pallas_call | solution.py:465
  303.9 3.3 collective-permute-done.37
  307.2 3.8 convolution_convert_fusion.3
  315.0 3.0 collective-permute-start.40
  319.5 5.6 %reduce-scatter.6.cloned.1.call-done = bf16[64,4224]{1,0:T(8,128)(2,1)} async-done(((bf16[1024,4224]{1,0:T(8,128)(2,1)}), bf16[64,4224]{1,0:T(8,128)(2,1)}) %reduce-scatter.6.cloned.1.call-update) | async-done | bytes 540688 | tf_op jit(solution)/shard_map/reduce_scatter | solution.py:612
  328.4 4.9 %collective-permute-done.39 = bf16[2,128,1152]{2,1,0:T(8,128)(2,1)S(1)} collective-permute-done((bf16[2,128,1152]{2,1,0:T(8,128)(2,1)}, bf16[2,128,1152]{2,1,0:T(8,128)(2,1)S(1)}, u32[]{:S(2)}, u32[]{:S(2)}) %collective-permute-start.39) | collective-permute-done | bytes 589856 | tf_op jit(solution)/shard_map/ppermute | solution.py:23
  333.4 13.9 %collective-permute-done.40 = bf16[2,128,1152]{2,1,0:T(8,128)(2,1)} collective-permute-done((bf16[2,128,1152]{2,1,0:T(8,128)(2,1)}, bf16[2,128,1152]{2,1,0:T(8,128)(2,1)}, u32[]{:S(2)}, u32[]{:S(2)}) %collective-permute-start.40) | collective-permute-done | bytes 589856 | tf_op jit(solution)/shard_map/ppermute | solution.py:23
  347.5 2.9 collective-permute-start.28
  360.3 5.5 %collective-permute-done.44 = bf16[64,1152]{1,0:T(8,128)(2,1)S(1)} collective-permute-done((bf16[64,1152]{1,0:T(8,128)(2,1)S(1)}, bf16[64,1152]{1,0:T(8,128)(2,1)S(1)}, u32[]{:S(2)}, u32[]{:S(2)}) %collective-permute-start.44) | collective-permute-done | bytes 147488 | tf_op jit(solution)/shard_map/ppermute | solution.py:23
  365.8 10.9 %collective-permute-done.45 = bf16[64,1152]{1,0:T(8,128)(2,1)S(1)} collective-permute-done((bf16[64,1152]{1,0:T(8,128)(2,1)S(1)}, bf16[64,1152]{1,0:T(8,128)(2,1)S(1)}, u32[]{:S(2)}, u32[]{:S(2)}) %collective-permute-start.45) | collective-permute-done | bytes 147488 | tf_op jit(solution)/shard_map/ppermute | solution.py:23
  378.0 2.7 shard_map.178
  393.9 5.6 %collective-permute-done.46 = bf16[64,1152]{1,0:T(8,128)(2,1)S(1)} collective-permute-done((bf16[64,1152]{1,0:T(8,128)(2,1)S(1)}, bf16[64,1152]{1,0:T(8,128)(2,1)S(1)}, u32[]{:S(2)}, u32[]{:S(2)}) %collective-permute-start.46) | collective-permute-done | bytes 147488 | tf_op jit(solution)/shard_map/ppermute | solution.py:23
  409.6 8.9 %collective-permute-done.51 = bf16[128,1152]{1,0:T(8,128)(2,1)S(1)} collective-permute-done((bf16[128,1152]{1,0:T(8,128)(2,1)S(1)}, bf16[128,1152]{1,0:T(8,128)(2,1)S(1)}, u32[]{:S(2)}, u32[]{:S(2)}) %collective-permute-start.51) | collective-permute-done | bytes 294944 | tf_op jit(solution)/shard_map/ppermute | solution.py:23
  418.5 13.1 %collective-permute-done.52 = bf16[128,1152]{1,0:T(8,128)(2,1)S(1)} collective-permute-done((bf16[128,1152]{1,0:T(8,128)(2,1)S(1)}, bf16[128,1152]{1,0:T(8,128)(2,1)S(1)}, u32[]{:S(2)}, u32[]{:S(2)}) %collective-permute-start.52) | collective-permute-done | bytes 294944 | tf_op jit(solution)/shard_map/ppermute | solution.py:23
  434.1 2.7 collective-permute-start.58
  444.9 3.1 convert_multiply_fusion
  (328 shorter events, 157.0 us)
Async XLA Ops:
  7.2 46.9 %all-gather.5.cloned.1.call-start = ((), (), s32[]{:S(2)}) async-start(), calls=%async_computation.3 | async-start | bytes 2621440 | tf_op jit(solution)/shard_map/all_gather | solution.py:67
  16.9 15.6 %collective-permute-start.3 = (bf16[256,1152]{1,0:T(8,128)(2,1)S(1)}, bf16[256,1152]{1,0:T(8,128)(2,1)S(1)}, u32[]{:S(2)}, u32[]{:S(2)}) collective-permute-start(bf16[256,1152]{1,0:T(8,128)(2,1)S(1)} %get-tuple-element.127), channel_id=1, source_target_pairs={{0,2},{2,0},{16,18},{18,16},{1,3},{3,1},{17,19},{19,17},{4,6},{6,4... | collective-permute-start | bytes 1769480 | tf_op jit(solution)/shard_map/ppermute | solution.py:23
  18.6 16.6 %collective-permute-start.4 = (bf16[256,1152]{1,0:T(8,128)(2,1)S(1)}, bf16[256,1152]{1,0:T(8,128)(2,1)}, u32[]{:S(2)}, u32[]{:S(2)}) collective-permute-start(bf16[256,1152]{1,0:T(8,128)(2,1)S(1)} %get-tuple-element.128), channel_id=1, source_target_pairs={{0,18},{2,16},{16,2},{18,0},{1,19},{3,17},{17,3},{19,1},{4,22},{6,... | collective-permute-start | bytes 1769480 | tf_op jit(solution)/shard_map/ppermute | solution.py:23
  22.0 70.3 %all-gather.7.cloned.1.call-start = ((), (), s32[]{:S(2)}) async-start(), calls=%async_computation.4 | async-start | bytes 2621440 | tf_op jit(solution)/shard_map/all_gather | solution.py:67
  36.8 14.2 %collective-permute-start.5 = (bf16[2,512,1152]{2,1,0:T(8,128)(2,1)S(1)}, bf16[2,512,1152]{2,1,0:T(8,128)(2,1)}, u32[]{:S(2)}, u32[]{:S(2)}) collective-permute-start(bf16[2,512,1152]{2,1,0:T(8,128)(2,1)S(1)} %bitcast.55), channel_id=1, source_target_pairs={{0,1},{1,0},{2,3},{3,2},{4,5},{5,4},{6,7},{7,6},{8,9},{9,8},{10,11... | collective-permute-start | bytes 7077896 | tf_op jit(solution)/shard_map/ppermute | solution.py:23
  42.0 8.2 %collective-permute-start.8 = (bf16[128,512]{1,0:T(8,128)(2,1)S(1)}, bf16[128,512]{1,0:T(8,128)(2,1)S(1)}, u32[]{:S(2)}, u32[]{:S(2)}) collective-permute-start(bf16[128,512]{1,0:T(8,128)(2,1)S(1)} %get-tuple-element.333), channel_id=1, source_target_pairs={{0,3},{1,2},{2,1},{3,0},{4,7},{5,6},{6,5},{7,4},{8,11},{9,10},{10,... | collective-permute-start | bytes 393224 | tf_op jit(solution)/shard_map/ppermute | solution.py:23
  59.5 121.5 %all-gather.9.cloned.1.call-start = ((), (), s32[]{:S(2)}) async-start(), calls=%async_computation.5 | async-start | bytes 2621440 | tf_op jit(solution)/shard_map/all_gather | solution.py:67
  67.8 35.8 %collective-permute-start.16 = (bf16[256,2816]{1,0:T(8,128)(2,1)}, bf16[256,2816]{1,0:T(8,128)(2,1)}, u32[]{:S(2)}, u32[]{:S(2)}) collective-permute-start(bf16[256,2816]{1,0:T(8,128)(2,1)} %get-tuple-element.152), channel_id=1, source_target_pairs={{0,18},{2,16},{16,2},{18,0},{1,19},{3,17},{17,3},{19,1},{4,22},{6,... | collective-permute-start | bytes 4325384 | tf_op jit(solution)/shard_map/ppermute | solution.py:23
  70.0 34.7 %collective-permute-start.15 = (bf16[256,2816]{1,0:T(8,128)(2,1)}, bf16[256,2816]{1,0:T(8,128)(2,1)}, u32[]{:S(2)}, u32[]{:S(2)}) collective-permute-start(bf16[256,2816]{1,0:T(8,128)(2,1)} %get-tuple-element.150), channel_id=1, source_target_pairs={{0,2},{2,0},{16,18},{18,16},{1,3},{3,1},{17,19},{19,17},{4,6},{6,4... | collective-permute-start | bytes 4325384 | tf_op jit(solution)/shard_map/ppermute | solution.py:23
  104.7 33.9 %collective-permute-start.18 = (bf16[704,512]{1,0:T(8,128)(2,1)S(1)}, bf16[704,512]{1,0:T(8,128)(2,1)}, u32[]{:S(2)}, u32[]{:S(2)}) collective-permute-start(bf16[704,512]{1,0:T(8,128)(2,1)S(1)} %copy-done.25), channel_id=1, source_target_pairs={{0,18},{2,16},{16,2},{18,0},{1,19},{3,17},{17,3},{19,1},{4,22},{6,... | collective-permute-start | bytes 2162696 | tf_op jit(solution)/shard_map/ppermute | solution.py:23
  105.8 32.7 %collective-permute-start.17 = (bf16[704,512]{1,0:T(8,128)(2,1)S(1)}, bf16[704,512]{1,0:T(8,128)(2,1)}, u32[]{:S(2)}, u32[]{:S(2)}) collective-permute-start(bf16[704,512]{1,0:T(8,128)(2,1)S(1)} %copy-done.26), channel_id=1, source_target_pairs={{0,2},{2,0},{16,18},{18,16},{1,3},{3,1},{17,19},{19,17},{4,6},{6,4... | collective-permute-start | bytes 2162696 | tf_op jit(solution)/shard_map/ppermute | solution.py:23
  108.7 15.1 %collective-permute-start.12 = (bf16[128,2048]{1,0:T(8,128)(2,1)}, bf16[128,2048]{1,0:T(8,128)(2,1)S(1)}, u32[]{:S(2)}, u32[]{:S(2)}) collective-permute-start(bf16[128,2048]{1,0:T(8,128)(2,1)} %get-tuple-element.306), channel_id=1, source_target_pairs={{0,4},{4,0},{8,12},{12,8},{1,5},{5,1},{9,13},{13,9},{2,6},{6,2},{1... | collective-permute-start | bytes 1572872 | tf_op jit(solution)/shard_map/ppermute | solution.py:23
  110.3 25.7 %collective-permute-start.13 = (bf16[128,2048]{1,0:T(8,128)(2,1)}, bf16[128,2048]{1,0:T(8,128)(2,1)S(1)}, u32[]{:S(2)}, u32[]{:S(2)}) collective-permute-start(bf16[128,2048]{1,0:T(8,128)(2,1)} %get-tuple-element.305), channel_id=1, source_target_pairs={{0,8},{4,12},{8,0},{12,4},{1,9},{5,13},{9,1},{13,5},{2,10},{6,14},... | collective-permute-start | bytes 1572872 | tf_op jit(solution)/shard_map/ppermute | solution.py:23
  113.2 25.3 %collective-permute-start.14 = (bf16[128,2048]{1,0:T(8,128)(2,1)}, bf16[128,2048]{1,0:T(8,128)(2,1)S(1)}, u32[]{:S(2)}, u32[]{:S(2)}) collective-permute-start(bf16[128,2048]{1,0:T(8,128)(2,1)} %get-tuple-element.304), channel_id=1, source_target_pairs={{0,12},{4,8},{8,4},{12,0},{1,13},{5,9},{9,5},{13,1},{2,14},{6,10},... | collective-permute-start | bytes 1572872 | tf_op jit(solution)/shard_map/ppermute | solution.py:23
  142.3 38.7 %collective-permute-start.23 = (bf16[1024,2816]{1,0:T(8,128)(2,1)}, bf16[1024,2816]{1,0:T(8,128)(2,1)}, u32[]{:S(2)}, u32[]{:S(2)}) collective-permute-start(bf16[1024,2816]{1,0:T(8,128)(2,1)} %pad_maximum_fusion.1.own_ref), channel_id=1, source_target_pairs={{0,1},{1,0},{2,3},{3,2},{4,5},{5,4},{6,7},{7,6},{8,9},{9,8},{10,11... | collective-permute-start | bytes 17301512 | tf_op jit(solution)/shard_map/ppermute | solution.py:23
  149.6 14.2 %collective-permute-start.22 = (bf16[1408,1024]{1,0:T(8,128)(2,1)}, bf16[1408,1024]{1,0:T(8,128)(2,1)}, u32[]{:S(2)}, u32[]{:S(2)}) collective-permute-start(bf16[1408,1024]{1,0:T(8,128)(2,1)} %pad_maximum_fusion.3), channel_id=1, source_target_pairs={{0,1},{1,0},{2,3},{3,2},{4,5},{5,4},{6,7},{7,6},{8,9},{9,8},{10,11... | collective-permute-start | bytes 8650760 | tf_op jit(solution)/shard_map/ppermute | solution.py:23
  150.1 81.8 %reduce-scatter.4.cloned.1.call-start = ((), (), s32[]{:S(2)}) async-start(), calls=%async_computation.6 | async-start | bytes 2621440 | tf_op jit(solution)/shard_map/reduce_scatter | solution.py:71
  152.1 8.6 %collective-permute-start.21 = (bf16[512,1024]{1,0:T(8,128)(2,1)S(1)}, bf16[512,1024]{1,0:T(8,128)(2,1)S(1)}, u32[]{:S(2)}, u32[]{:S(2)}) collective-permute-start(bf16[512,1024]{1,0:T(8,128)(2,1)S(1)} %get-tuple-element.295), channel_id=1, source_target_pairs={{0,1},{1,0},{2,3},{3,2},{4,5},{5,4},{6,7},{7,6},{8,9},{9,8},{10,11... | collective-permute-start | bytes 3145736 | tf_op jit(solution)/shard_map/ppermute | solution.py:23
  152.7 9.5 %collective-permute-start.19 = (bf16[512,1024]{1,0:T(8,128)(2,1)S(1)}, bf16[512,1024]{1,0:T(8,128)(2,1)S(1)}, u32[]{:S(2)}, u32[]{:S(2)}) collective-permute-start(bf16[512,1024]{1,0:T(8,128)(2,1)S(1)} %pad_maximum_fusion.13), channel_id=1, source_target_pairs={{0,1},{1,0},{2,3},{3,2},{4,5},{5,4},{6,7},{7,6},{8,9},{9,8},{10,11... | collective-permute-start | bytes 3145736 | tf_op jit(solution)/shard_map/ppermute | solution.py:23
  201.9 12.8 %collective-permute-start.25 = (bf16[512,2816]{1,0:T(8,128)(2,1)}, bf16[512,2816]{1,0:T(8,128)(2,1)}, u32[]{:S(2)}, u32[]{:S(2)}) collective-permute-start(bf16[512,2816]{1,0:T(8,128)(2,1)} %get-tuple-element.172), channel_id=1, source_target_pairs={{0,1},{1,0},{2,3},{3,2},{4,5},{5,4},{6,7},{7,6},{8,9},{9,8},{10,11... | collective-permute-start | bytes 8650760 | tf_op jit(solution)/shard_map/ppermute | solution.py:23
  201.9 123.1 %reduce-scatter.6.cloned.1.call-start = ((), (), s32[]{:S(2)}) async-start(), calls=%async_computation.7 | async-start | bytes 9191424 | tf_op jit(solution)/shard_map/reduce_scatter | solution.py:612
  202.0 9.0 %collective-permute-start.26 = (bf16[512,1408]{1,0:T(8,128)(2,1)}, bf16[512,1408]{1,0:T(8,128)(2,1)S(1)}, u32[]{:S(2)}, u32[]{:S(2)}) collective-permute-start(bf16[512,1408]{1,0:T(8,128)(2,1)} %copy-done.12), channel_id=1, source_target_pairs={{0,1},{1,0},{2,3},{3,2},{4,5},{5,4},{6,7},{7,6},{8,9},{9,8},{10,11... | collective-permute-start | bytes 4325384 | tf_op jit(solution)/shard_map/ppermute | solution.py:23
  204.8 9.9 %collective-permute-start.24 = (bf16[512,1024]{1,0:T(8,128)(2,1)S(1)}, bf16[512,1024]{1,0:T(8,128)(2,1)S(1)}, u32[]{:S(2)}, u32[]{:S(2)}) collective-permute-start(bf16[512,1024]{1,0:T(8,128)(2,1)S(1)} %pad_maximum_fusion.15), channel_id=1, source_target_pairs={{0,1},{1,0},{2,3},{3,2},{4,5},{5,4},{6,7},{7,6},{8,9},{9,8},{10,11... | collective-permute-start | bytes 3145736 | tf_op jit(solution)/shard_map/ppermute | solution.py:23
  232.0 146.0 %reduce-scatter.8.cloned.1.call-start = ((), (), s32[]{:S(2)}) async-start(), calls=%async_computation.8 | async-start | bytes 2621440 | tf_op jit(solution)/shard_map/reduce_scatter | solution.py:71
  234.6 15.0 %collective-permute-start.29 = (bf16[128,2048]{1,0:T(8,128)(2,1)}, bf16[128,2048]{1,0:T(8,128)(2,1)S(1)}, u32[]{:S(2)}, u32[]{:S(2)}) collective-permute-start(bf16[128,2048]{1,0:T(8,128)(2,1)} %get-tuple-element.202.b0), channel_id=1, source_target_pairs={{0,4},{4,0},{8,12},{12,8},{1,5},{5,1},{9,13},{13,9},{2,6},{6,2},{1... | collective-permute-start | bytes 1572872 | tf_op jit(solution)/shard_map/ppermute | solution.py:23
  234.9 25.3 %collective-permute-start.30 = (bf16[128,2048]{1,0:T(8,128)(2,1)}, bf16[128,2048]{1,0:T(8,128)(2,1)S(1)}, u32[]{:S(2)}, u32[]{:S(2)}) collective-permute-start(bf16[128,2048]{1,0:T(8,128)(2,1)} %get-tuple-element.202.b0), channel_id=1, source_target_pairs={{0,8},{4,12},{8,0},{12,4},{1,9},{5,13},{9,1},{13,5},{2,10},{6,14},... | collective-permute-start | bytes 1572872 | tf_op jit(solution)/shard_map/ppermute | solution.py:23
  236.9 25.8 %collective-permute-start.31 = (bf16[128,2048]{1,0:T(8,128)(2,1)}, bf16[128,2048]{1,0:T(8,128)(2,1)S(1)}, u32[]{:S(2)}, u32[]{:S(2)}) collective-permute-start(bf16[128,2048]{1,0:T(8,128)(2,1)} %get-tuple-element.202.b0), channel_id=1, source_target_pairs={{0,12},{4,8},{8,4},{12,0},{1,13},{5,9},{9,5},{13,1},{2,14},{6,10},... | collective-permute-start | bytes 1572872 | tf_op jit(solution)/shard_map/ppermute | solution.py:23
  262.8 12.2 %collective-permute-start.32 = (bf16[128,2048]{1,0:T(8,128)(2,1)S(1)}, bf16[128,2048]{1,0:T(8,128)(2,1)S(1)}, u32[]{:S(2)}, u32[]{:S(2)}) collective-permute-start(bf16[128,2048]{1,0:T(8,128)(2,1)S(1)} %get-tuple-element.188), channel_id=1, source_target_pairs={{0,4},{4,0},{8,12},{12,8},{1,5},{5,1},{9,13},{13,9},{2,6},{6,2},{1... | collective-permute-start | bytes 1572872 | tf_op jit(solution)/shard_map/ppermute | solution.py:23
  262.8 13.4 %collective-permute-start.33 = (bf16[128,2048]{1,0:T(8,128)(2,1)S(1)}, bf16[128,2048]{1,0:T(8,128)(2,1)S(1)}, u32[]{:S(2)}, u32[]{:S(2)}) collective-permute-start(bf16[128,2048]{1,0:T(8,128)(2,1)S(1)} %get-tuple-element.189), channel_id=1, source_target_pairs={{0,12},{4,8},{8,4},{12,0},{1,13},{5,9},{9,5},{13,1},{2,14},{6,10},... | collective-permute-start | bytes 1572872 | tf_op jit(solution)/shard_map/ppermute | solution.py:23
  283.1 8.7 %collective-permute-start.35 = (bf16[128,512]{1,0:T(8,128)(2,1)S(1)}, bf16[128,512]{1,0:T(8,128)(2,1)S(1)}, u32[]{:S(2)}, u32[]{:S(2)}) collective-permute-start(bf16[128,512]{1,0:T(8,128)(2,1)S(1)} %get-tuple-element.195), channel_id=1, source_target_pairs={{0,2},{1,3},{2,0},{3,1},{4,6},{5,7},{6,4},{7,5},{8,10},{9,11},{10,... | collective-permute-start | bytes 393224 | tf_op jit(solution)/shard_map/ppermute | solution.py:23
  284.8 11.2 %collective-permute-start.36 = (bf16[128,512]{1,0:T(8,128)(2,1)S(1)}, bf16[128,512]{1,0:T(8,128)(2,1)S(1)}, u32[]{:S(2)}, u32[]{:S(2)}) collective-permute-start(bf16[128,512]{1,0:T(8,128)(2,1)S(1)} %get-tuple-element.196), channel_id=1, source_target_pairs={{0,3},{1,2},{2,1},{3,0},{4,7},{5,6},{6,5},{7,4},{8,11},{9,10},{10,... | collective-permute-start | bytes 393224 | tf_op jit(solution)/shard_map/ppermute | solution.py:23
  314.8 18.6 %collective-permute-start.39 = (bf16[2,128,1152]{2,1,0:T(8,128)(2,1)}, bf16[2,128,1152]{2,1,0:T(8,128)(2,1)S(1)}, u32[]{:S(2)}, u32[]{:S(2)}) collective-permute-start(bf16[2,128,1152]{2,1,0:T(8,128)(2,1)} %get-tuple-element.268), channel_id=1, source_target_pairs={{0,32},{32,0},{64,96},{96,64},{1,33},{33,1},{65,97},{97,65},{2,34}... | collective-permute-start | bytes 1769480 | tf_op jit(solution)/shard_map/ppermute | solution.py:23
  315.0 32.3 %collective-permute-start.40 = (bf16[2,128,1152]{2,1,0:T(8,128)(2,1)}, bf16[2,128,1152]{2,1,0:T(8,128)(2,1)}, u32[]{:S(2)}, u32[]{:S(2)}) collective-permute-start(bf16[2,128,1152]{2,1,0:T(8,128)(2,1)} %get-tuple-element.269), channel_id=1, source_target_pairs={{0,64},{32,96},{64,0},{96,32},{1,65},{33,97},{65,1},{97,33},{2,66}... | collective-permute-start | bytes 1769480 | tf_op jit(solution)/shard_map/ppermute | solution.py:23
  317.9 29.5 %collective-permute-start.41 = (bf16[2,128,1152]{2,1,0:T(8,128)(2,1)}, bf16[2,128,1152]{2,1,0:T(8,128)(2,1)}, u32[]{:S(2)}, u32[]{:S(2)}) collective-permute-start(bf16[2,128,1152]{2,1,0:T(8,128)(2,1)} %get-tuple-element.267), channel_id=1, source_target_pairs={{0,96},{32,64},{64,32},{96,0},{1,97},{33,65},{65,33},{97,1},{2,98}... | collective-permute-start | bytes 1769480 | tf_op jit(solution)/shard_map/ppermute | solution.py:23
  326.5 20.9 %collective-permute-start.27 = (f32[64,128]{1,0:T(8,128)S(1)}, f32[64,128]{1,0:T(8,128)S(1)}, u32[]{:S(2)}, u32[]{:S(2)}) collective-permute-start(f32[64,128]{1,0:T(8,128)S(1)} %broadcast_in_dim.20), channel_id=1, source_target_pairs={{0,4},{4,0},{8,12},{12,8},{1,5},{5,1},{9,13},{13,9},{2,6},{6,2},{1... | collective-permute-start | bytes 98312 | tf_op jit(solution)/shard_map/ppermute | solution.py:23
  328.4 113.9 %all-gather.11.cloned.1.call-start = ((), (), s32[]{:S(2)}) async-start(), calls=%async_computation.9 | async-start | bytes 5570560 | tf_op jit(solution)/shard_map/all_gather | solution.py:677
  355.8 10.0 %collective-permute-start.44 = (bf16[64,1152]{1,0:T(8,128)(2,1)S(1)}, bf16[64,1152]{1,0:T(8,128)(2,1)S(1)}, u32[]{:S(2)}, u32[]{:S(2)}) collective-permute-start(bf16[64,1152]{1,0:T(8,128)(2,1)S(1)} %get-tuple-element.325), channel_id=1, source_target_pairs={{0,16},{2,18},{16,0},{18,2},{1,17},{3,19},{17,1},{19,3},{4,20},{6,... | collective-permute-start | bytes 442376 | tf_op jit(solution)/shard_map/ppermute | solution.py:23
  358.1 18.6 %collective-permute-start.45 = (bf16[64,1152]{1,0:T(8,128)(2,1)S(1)}, bf16[64,1152]{1,0:T(8,128)(2,1)S(1)}, u32[]{:S(2)}, u32[]{:S(2)}) collective-permute-start(bf16[64,1152]{1,0:T(8,128)(2,1)S(1)} %get-tuple-element.324), channel_id=1, source_target_pairs={{0,18},{2,16},{16,2},{18,0},{1,19},{3,17},{17,3},{19,1},{4,22},{6,... | collective-permute-start | bytes 442376 | tf_op jit(solution)/shard_map/ppermute | solution.py:23
  358.8 18.0 %collective-permute-start.42 = (bf16[64,4352]{1,0:T(8,128)(2,1)S(1)}, bf16[64,4352]{1,0:T(8,128)(2,1)S(1)}, u32[]{:S(2)}, u32[]{:S(2)}) collective-permute-start(bf16[64,4352]{1,0:T(8,128)(2,1)S(1)} %pad_maximum_fusion.18), channel_id=1, source_target_pairs={{0,16},{2,18},{16,0},{18,2},{1,17},{3,19},{17,1},{19,3},{4,20},{6,... | collective-permute-start | bytes 1671176 | tf_op jit(solution)/shard_map/ppermute | solution.py:23
  382.2 8.2 %collective-permute-start.49 = (bf16[128,512]{1,0:T(8,128)(2,1)S(1)}, bf16[128,512]{1,0:T(8,128)(2,1)S(1)}, u32[]{:S(2)}, u32[]{:S(2)}) collective-permute-start(bf16[128,512]{1,0:T(8,128)(2,1)S(1)} %get-tuple-element.319), channel_id=1, source_target_pairs={{0,3},{1,2},{2,1},{3,0},{4,7},{5,6},{6,5},{7,4},{8,11},{9,10},{10,... | collective-permute-start | bytes 393224 | tf_op jit(solution)/shard_map/ppermute | solution.py:23
  384.0 15.7 %collective-permute-start.50 = (bf16[128,2048]{1,0:T(8,128)(2,1)S(1)}, bf16[128,2048]{1,0:T(8,128)(2,1)S(1)}, u32[]{:S(2)}, u32[]{:S(2)}) collective-permute-start(bf16[128,2048]{1,0:T(8,128)(2,1)S(1)} %copy-done.53), channel_id=1, source_target_pairs={{0,8},{4,12},{8,0},{12,4},{1,9},{5,13},{9,1},{13,5},{2,10},{6,14},... | collective-permute-start | bytes 1572872 | tf_op jit(solution)/shard_map/ppermute | solution.py:23
  391.5 8.0 %collective-permute-start.46 = (bf16[64,1152]{1,0:T(8,128)(2,1)S(1)}, bf16[64,1152]{1,0:T(8,128)(2,1)S(1)}, u32[]{:S(2)}, u32[]{:S(2)}) collective-permute-start(bf16[64,1152]{1,0:T(8,128)(2,1)S(1)} %fusion.40), channel_id=1, source_target_pairs={{0,16},{2,18},{16,0},{18,2},{1,17},{3,19},{17,1},{19,3},{4,20},{6,... | collective-permute-start | bytes 442376 | tf_op jit(solution)/shard_map/ppermute | solution.py:23
  400.6 8.1 %collective-permute-start.56 = (bf16[128,512]{1,0:T(8,128)(2,1)S(1)}, bf16[128,512]{1,0:T(8,128)(2,1)S(1)}, u32[]{:S(2)}, u32[]{:S(2)}) collective-permute-start(bf16[128,512]{1,0:T(8,128)(2,1)S(1)} %get-tuple-element.330), channel_id=1, source_target_pairs={{0,3},{1,2},{2,1},{3,0},{4,7},{5,6},{6,5},{7,4},{8,11},{9,10},{10,... | collective-permute-start | bytes 393224 | tf_op jit(solution)/shard_map/ppermute | solution.py:23
  402.3 16.2 %collective-permute-start.51 = (bf16[128,1152]{1,0:T(8,128)(2,1)S(1)}, bf16[128,1152]{1,0:T(8,128)(2,1)S(1)}, u32[]{:S(2)}, u32[]{:S(2)}) collective-permute-start(bf16[128,1152]{1,0:T(8,128)(2,1)S(1)} %pad_maximum_fusion.22), channel_id=1, source_target_pairs={{0,32},{32,0},{64,96},{96,64},{1,33},{33,1},{65,97},{97,65},{2,34}... | collective-permute-start | bytes 884744 | tf_op jit(solution)/shard_map/ppermute | solution.py:23
  402.6 28.9 %collective-permute-start.52 = (bf16[128,1152]{1,0:T(8,128)(2,1)S(1)}, bf16[128,1152]{1,0:T(8,128)(2,1)S(1)}, u32[]{:S(2)}, u32[]{:S(2)}) collective-permute-start(bf16[128,1152]{1,0:T(8,128)(2,1)S(1)} %pad_maximum_fusion.22), channel_id=1, source_target_pairs={{0,64},{32,96},{64,0},{96,32},{1,65},{33,97},{65,1},{97,33},{2,66}... | collective-permute-start | bytes 884744 | tf_op jit(solution)/shard_map/ppermute | solution.py:23
  405.0 26.6 %collective-permute-start.53 = (bf16[128,1152]{1,0:T(8,128)(2,1)S(1)}, bf16[128,1152]{1,0:T(8,128)(2,1)S(1)}, u32[]{:S(2)}, u32[]{:S(2)}) collective-permute-start(bf16[128,1152]{1,0:T(8,128)(2,1)S(1)} %pad_maximum_fusion.22), channel_id=1, source_target_pairs={{0,96},{32,64},{64,32},{96,0},{1,97},{33,65},{65,33},{97,1},{2,98}... | collective-permute-start | bytes 884744 | tf_op jit(solution)/shard_map/ppermute | solution.py:23
  433.1 8.6 %collective-permute-start.57 = (f32[1,512]{1,0:T(1,128)S(1)}, f32[1,512]{1,0:T(1,128)S(1)}, u32[]{:S(2)}, u32[]{:S(2)}) collective-permute-start(f32[1,512]{1,0:T(1,128)S(1)} %bitcast.78), channel_id=1, source_target_pairs={{0,4},{4,0},{8,12},{12,8},{1,5},{5,1},{9,13},{13,9},{2,6},{6,2},{1... | collective-permute-start | bytes 6152 | tf_op jit(solution)/shard_map/ppermute | solution.py:23
  434.1 7.7 %collective-permute-start.58 = (f32[1,512]{1,0:T(1,128)S(1)}, f32[1,512]{1,0:T(1,128)S(1)}, u32[]{:S(2)}, u32[]{:S(2)}) collective-permute-start(f32[1,512]{1,0:T(1,128)S(1)} %bitcast.79), channel_id=1, source_target_pairs={{0,8},{4,12},{8,0},{12,4},{1,9},{5,13},{9,1},{13,5},{2,10},{6,14},... | collective-permute-start | bytes 6152 | tf_op jit(solution)/shard_map/ppermute | solution.py:23
  (76 other events, 441.2 us)
Sparse Core Ops, SparseCore 0:
  22.1 31.3 all-gather.4
  59.6 32.6 all-gather.6
  150.3 30.6 all-gather.8
  202.1 29.8 reduce-scatter.3
  235.6 89.3 reduce-scatter.5
  328.5 29.7 reduce-scatter.7
  378.1 61.2 all-gather.10

commit v6 on v5

--- a/solution.py
+++ b/solution.py
@@ -570,10 +570,11 @@
     )
     mixed_low, grad_rows = lax.optimization_barrier((mixed_low, grad_rows))
     branch = product(mixed_low, full_out, ((0,), (0,)), BF16)
+    branch_parts = collect_row(row_parts(branch, row))
     gu_mine = ring_join(gu_halves, after(gu_got, branch), low, 0)
-    down_halves = [after(v, branch, gu_got) for v in cut(w_down, 2, 0)]
+    down_halves = [after(v, branch_parts[1]) for v in cut(w_down, 2, 0)]
     down_got = ring_send(down_halves)
-    branch_parts = after(collect_row(row_parts(branch, row)), gu_mine, down_got)
+    branch_parts = after(branch_parts, gu_mine)
     hidden, normed_two = rows_call(add_and_norm, (F32, BF16), (inputs, *branch_parts))
     down_mine = ring_join(down_halves, after(down_got, hidden), low, 1)
     full_down = jnp.concatenate([down_mine, trade_core(down_mine)], axis=1)

time: 466 us -> 472 us (1.013)
  waiting for transfers between devices: 191 us -> 199 us
  local copies, waits for them, and re-layouts: 50.9 us -> 44.5 us
    ppermute x60, waiting for transfers between devices: 166 us -> 183 us  [trade(): return lax.ppermute(values, axes, [(i, i ^ mask) for i in range(size)])]
    all_gather x3, waiting for transfers between devices: 14.2 us -> 6.1 us  [gather_row(): return lax.all_gather(values, 'y', axis=0, tiled=True)]
    unnamed x123 -> x115, local copies, waits for them, and re-layouts: 25.3 us -> 23.6 us
  transfers between devices with their start and end apart: 67 -> 67, of which waited for: 39 -> 42; matrix products, arithmetic and copies ran while one was open for 23% -> 21% of each run, Pallas kernels for 8% -> 8%
where the time goes in v6:
time: 472 us; the launch traced here: 464 us
  waiting for transfers between devices  199 us (42%)
  starting transfers between devices  64.1 us (14%)
  Pallas kernels  59.7 us (13%)
  other arithmetic  45.5 us (10%)
  local copies, waits for them, and re-layouts  44.5 us (9%)
  matrix products  34.7 us (7%)
  between operations  16.1 us (3%)
    ppermute x60, waiting for transfers between devices, trade(): return lax.ppermute(values, axes, [(i, i ^ mask) for i in range(size)])  183 us
    ppermute x60, starting transfers between devices, trade(): return lax.ppermute(values, axes, [(i, i ^ mask) for i in range(size)])  63.9 us
    pallas_call x7, Pallas kernels, kernel_call(): pl.pallas_call(whole, out_shape=out_shape, in_specs=[pl.BlockSpec(memory_...  51.4 us
    dot_general x7, matrix products, product(): lax.dot_general(left, right, (dims, ((), ())), preferred_element_type=F32)  34.7 us
    unnamed x115, local copies, waits for them, and re-layouts  23.6 us
  transfers between devices with their start and end apart: 67, of which 42 were waited for; matrix products, arithmetic and copies ran while one was open for 21% of the time, Pallas kernels for 8%

profile of v6, /device:TPU:0, one launch (start us, length us, event | category | flops | bytes accessed | tf_op | source)
XLA Modules:
  0.0 463.7 jit_solution(4207253714892071823)
XLA Ops:
  24.7 8.5 %collective-permute-done.3 = bf16[256,1152]{1,0:T(8,128)(2,1)S(1)} collective-permute-done((bf16[256,1152]{1,0:T(8,128)(2,1)S(1)}, bf16[256,1152]{1,0:T(8,128)(2,1)S(1)}, u32[]{:S(2)}, u32[]{:S(2)}) %collective-permute-start.3) | collective-permute-done | bytes 589856 | tf_op jit(solution)/shard_map/ppermute | solution.py:23
  44.1 3.6 collective-permute-done.7
  57.6 3.8 shard_map.169
  63.4 4.5 collective-permute-done.10
  69.8 2.8 collective-permute-start.16
  75.4 8.6 %shard_map.170 = (f32[512,512]{1,0:T(8,128)S(1)}, bf16[512,512]{1,0:T(8,128)(2,1)S(1)}, f32[8,512]{1,0:T(8,128)S(1)}) custom-call(bf16[512,512]{1,0:T(8,128)(2,1)S(1)} %get-tuple-element.139.q_ref.refs_0_, bf16[4,128,512]{2,1,0:T(8,128)(2,1)S(1)} %pad_maximum_fusion.20.pairs_ref.refs_1_, s32[512,128]{1,0:T(8,128)S(1)} %broadcast_in_dim.17.koff_ref.refs_2_, ...), custom_call_target="tpu_custom_call" | custom-call | flops 2147483648 | bytes 1314816 | tf_op jit(solution)/shard_map/pallas_call | solution.py:465
  88.7 3.7 all-gather.7.cloned.1.call-done
  93.7 11.6 %collective-permute-done.16 = bf16[256,2816]{1,0:T(8,128)(2,1)} collective-permute-done((bf16[256,2816]{1,0:T(8,128)(2,1)}, bf16[256,2816]{1,0:T(8,128)(2,1)}, u32[]{:S(2)}, u32[]{:S(2)}) %collective-permute-start.16) | collective-permute-done | bytes 1441824 | tf_op jit(solution)/shard_map/ppermute | solution.py:23
  117.6 2.8 pad_maximum_fusion.1.own_ref
  120.4 3.7 collective-permute-done.12.p1
  124.2 9.9 %collective-permute-done.13.p2 = bf16[128,2048]{1,0:T(8,128)(2,1)} collective-permute-done((bf16[128,2048]{1,0:T(8,128)(2,1)S(1)}, bf16[128,2048]{1,0:T(8,128)(2,1)}, u32[]{:S(2)}, u32[]{:S(2)}) %collective-permute-start.13) | collective-permute-done | bytes 524320 | tf_op jit(solution)/shard_map/ppermute | solution.py:23
  134.0 2.6 collective-permute-done.14.p3
  136.6 2.9 shard_map.171
  145.8 15.1 %collective-permute-done.20 = bf16[704,512]{1,0:T(8,128)(2,1)} collective-permute-done((bf16[704,512]{1,0:T(8,128)(2,1)}, bf16[704,512]{1,0:T(8,128)(2,1)}, u32[]{:S(2)}, u32[]{:S(2)}) %collective-permute-start.20) | collective-permute-done | bytes 720928 | tf_op jit(solution)/shard_map/ppermute | solution.py:23
  170.2 6.3 %collective-permute-done.18 = bf16[512,512]{1,0:T(8,128)(2,1)S(1)} collective-permute-done((bf16[512,512]{1,0:T(8,128)(2,1)S(1)}, bf16[512,512]{1,0:T(8,128)(2,1)S(1)}, u32[]{:S(2)}, u32[]{:S(2)}) %collective-permute-start.18) | collective-permute-done | bytes 524320 | tf_op jit(solution)/shard_map/ppermute | solution.py:23
  180.7 8.4 %fusion.10.gi_ref = f32[512,1408]{1,0:T(8,128)} fusion(bf16[512,2048]{1,0:T(8,128)(2,1)} %all-gather.7.cloned.1.call-done, bf16[1408,1024]{1,0:T(8,128)(2,1)} %collective-permute-done.22, bf16[1408,512]{1,0:T(8,128)(2,1)} %copy-done.24, bf16[1408,512]{1,0:T(8,128)(2,1)} %copy-done.23), kind=kOutput, calls=%fused_computation.33 | convolution fusion | flops 2970091520 | bytes 10747904 | tf_op jit(solution)/shard_map/dot_general | solution.py:184
  189.1 16.9 %shard_map.172 = (bf16[512,1408]{1,0:T(8,128)(2,1)S(1)}, bf16[512,2816]{1,0:T(8,128)(2,1)}, bf16[512,2048]{1,0:T(8,128)(2,1)S(1)}) custom-call(bf16[512,2048]{1,0:T(8,128)(2,1)S(1)} %copy-done.9, f32[512,1408]{1,0:T(8,128)} %fusion.10.gi_ref, bf16[1024,2816]{1,0:T(8,128)(2,1)} %pad_maximum_fusion.1.own_ref, bf16[1024,2816]{1,0:T(8,128)(2,1)} %collective-permute-done.23.other_ref), custom_call_target="tpu_custom_call" | custom-call | flops 11811160064 | bytes 16515072 | tf_op jit(solution)/shard_map/pallas_call | solution.py:465
  211.6 6.0 %collective-permute-done.26 = bf16[512,1408]{1,0:T(8,128)(2,1)S(1)} collective-permute-done((bf16[512,1408]{1,0:T(8,128)(2,1)}, bf16[512,1408]{1,0:T(8,128)(2,1)S(1)}, u32[]{:S(2)}, u32[]{:S(2)}) %collective-permute-start.26) | collective-permute-done | bytes 1441824 | tf_op jit(solution)/shard_map/ppermute | solution.py:23
  217.6 3.7 convolution_convert_fusion
  221.3 8.4 %fusion.4 = bf16[1024,2816]{1,0:T(8,128)(2,1)S(1)} fusion(bf16[512,2816]{1,0:T(8,128)(2,1)} %collective-permute-done.25, bf16[512,2816]{1,0:T(8,128)(2,1)S(1)} %copy-done.52, bf16[512,1024]{1,0:T(8,128)(2,1)S(1)} %collective-permute-done.24, bf16[512,256]{1,0:T(8,128)(2,1)S(1)} %get-tuple-element.291, bf16[512,256]{1,0:T(8,128)(2,1)S(1)} %get-tuple-element.292, ...), kind=kOutput, calls=%fused_computation.7 | convolution fusion | flops 5930483712 | bytes 13631488 | tf_op jit(solution)/shard_map/dot_general | solution.py:184
  229.8 3.8 pad_maximum_fusion
  233.6 4.0 reduce-scatter.4.cloned.1.call-done.part_ref
  237.6 2.6 shard_map.173
  245.0 6.5 %convolution_convert_fusion.2 = bf16[512,2048]{1,0:T(8,128)(2,1)S(1)} fusion(bf16[512,1408]{1,0:T(8,128)(2,1)} %copy-done.13, bf16[1408,1024]{1,0:T(8,128)(2,1)} %collective-permute-done.22, bf16[1408,512]{1,0:T(8,128)(2,1)} %copy-done.24, bf16[1408,512]{1,0:T(8,128)(2,1)} %copy-done.23), kind=kOutput, calls=%fused_computation.18 | convolution fusion | flops 2971140096 | bytes 9306112 | tf_op jit(solution)/shard_map/dot_general | solution.py:184
  252.6 2.6 collective-permute-done.29.b1
  255.3 10.5 %collective-permute-done.30.b2 = bf16[128,2048]{1,0:T(8,128)(2,1)S(1)} collective-permute-done((bf16[128,2048]{1,0:T(8,128)(2,1)}, bf16[128,2048]{1,0:T(8,128)(2,1)S(1)}, u32[]{:S(2)}, u32[]{:S(2)}) %collective-permute-start.30) | collective-permute-done | bytes 524320 | tf_op jit(solution)/shard_map/ppermute | solution.py:23
  265.8 2.6 collective-permute-done.31.b3
  273.2 7.2 %shard_map.175 = (bf16[256,512]{1,0:T(8,128)(2,1)S(1)}, f32[4,64,512]{2,1,0:T(8,128)S(1)}, f32[4,64,512]{2,1,0:T(8,128)S(1)}) custom-call(bf16[512,512]{1,0:T(8,128)(2,1)S(1)} %copy-done.16, bf16[4,128,512]{2,1,0:T(8,128)(2,1)S(1)} %copy-done.12, s32[512,128]{1,0:T(8,128)S(1)} %broadcast_in_dim.17.koff_ref.refs_2_, s32[1,512]{1,0:T(1,128)S(1)} %bitcast.64, ...), custom_call_target="tpu_custom_call" | custom-call | flops 2684354560 | bytes 3035136 | tf_op jit(solution)/shard_map/pallas_call | solution.py:465
  281.8 6.8 %shard_map.176 = (bf16[256,512]{1,0:T(8,128)(2,1)S(1)}, bf16[128,512]{1,0:T(8,128)(2,1)S(1)}, bf16[128,512]{1,0:T(8,128)(2,1)S(1)}, bf16[128,512]{1,0:T(8,128)(2,1)S(1)}, bf16[128,512]{1,0:T(8,128)(2,1)S(1)}) custom-call(bf16[512,512]{1,0:T(8,128)(2,1)S(1)} %copy-done.16, bf16[4,128,512]{2,1,0:T(8,128)(2,1)S(1)} %copy-done.12, ...), custom_call_target="tpu_custom_call" | custom-call | flops 2684354560 | bytes 4083712 | tf_op jit(solution)/shard_map/pallas_call | solution.py:465
  290.7 6.8 %collective-permute-done.35.g2 = bf16[128,512]{1,0:T(8,128)(2,1)S(1)} collective-permute-done((bf16[128,512]{1,0:T(8,128)(2,1)S(1)}, bf16[128,512]{1,0:T(8,128)(2,1)S(1)}, u32[]{:S(2)}, u32[]{:S(2)}) %collective-permute-start.35) | collective-permute-done | bytes 131104 | tf_op jit(solution)/shard_map/ppermute | solution.py:23
  297.5 4.0 collective-permute-done.36.g3
  301.6 5.8 %shard_map.177 = (bf16[640,512]{1,0:T(8,128)(2,1)}, bf16[512,2048]{1,0:T(8,128)(2,1)}) custom-call(bf16[256,512]{1,0:T(8,128)(2,1)S(1)} %get-tuple-element.185.gq0, bf16[256,512]{1,0:T(8,128)(2,1)S(1)} %get-tuple-element.192.gq1, bf16[128,512]{1,0:T(8,128)(2,1)S(1)} %get-tuple-element.197.g0, bf16[128,512]{1,0:T(8,128)(2,1)S(1)} %collective-permute-done.34.g1, ...), custom_call_target="tpu_custom_call" | custom-call | flops 1342177280 | bytes 5898240 | tf_op jit(solution)/shard_map/pallas_call | solution.py:465
  309.5 3.3 collective-permute-done.37
  312.8 3.8 convolution_convert_fusion.3
  320.5 2.8 collective-permute-start.40
  325.1 5.6 %reduce-scatter.6.cloned.1.call-done = bf16[64,4224]{1,0:T(8,128)(2,1)} async-done(((bf16[1024,4224]{1,0:T(8,128)(2,1)}), bf16[64,4224]{1,0:T(8,128)(2,1)}) %reduce-scatter.6.cloned.1.call-update) | async-done | bytes 540688 | tf_op jit(solution)/shard_map/reduce_scatter | solution.py:613
  334.0 5.0 %collective-permute-done.39 = bf16[2,128,1152]{2,1,0:T(8,128)(2,1)S(1)} collective-permute-done((bf16[2,128,1152]{2,1,0:T(8,128)(2,1)}, bf16[2,128,1152]{2,1,0:T(8,128)(2,1)S(1)}, u32[]{:S(2)}, u32[]{:S(2)}) %collective-permute-start.39) | collective-permute-done | bytes 589856 | tf_op jit(solution)/shard_map/ppermute | solution.py:23
  339.0 13.9 %collective-permute-done.40 = bf16[2,128,1152]{2,1,0:T(8,128)(2,1)} collective-permute-done((bf16[2,128,1152]{2,1,0:T(8,128)(2,1)}, bf16[2,128,1152]{2,1,0:T(8,128)(2,1)}, u32[]{:S(2)}, u32[]{:S(2)}) %collective-permute-start.40) | collective-permute-done | bytes 589856 | tf_op jit(solution)/shard_map/ppermute | solution.py:23
  353.2 2.8 collective-permute-start.28
  366.0 5.1 %collective-permute-done.44 = bf16[64,1152]{1,0:T(8,128)(2,1)S(1)} collective-permute-done((bf16[64,1152]{1,0:T(8,128)(2,1)S(1)}, bf16[64,1152]{1,0:T(8,128)(2,1)S(1)}, u32[]{:S(2)}, u32[]{:S(2)}) %collective-permute-start.44) | collective-permute-done | bytes 147488 | tf_op jit(solution)/shard_map/ppermute | solution.py:23
  371.1 11.0 %collective-permute-done.45 = bf16[64,1152]{1,0:T(8,128)(2,1)S(1)} collective-permute-done((bf16[64,1152]{1,0:T(8,128)(2,1)S(1)}, bf16[64,1152]{1,0:T(8,128)(2,1)S(1)}, u32[]{:S(2)}, u32[]{:S(2)}) %collective-permute-start.45) | collective-permute-done | bytes 147488 | tf_op jit(solution)/shard_map/ppermute | solution.py:23
  383.4 2.7 shard_map.178
  389.4 2.6 collective-permute-start.50
  399.4 5.5 %collective-permute-done.46 = bf16[64,1152]{1,0:T(8,128)(2,1)S(1)} collective-permute-done((bf16[64,1152]{1,0:T(8,128)(2,1)S(1)}, bf16[64,1152]{1,0:T(8,128)(2,1)S(1)}, u32[]{:S(2)}, u32[]{:S(2)}) %collective-permute-start.46) | collective-permute-done | bytes 147488 | tf_op jit(solution)/shard_map/ppermute | solution.py:23
  407.9 2.7 collective-permute-start.52
  415.1 8.9 %collective-permute-done.51 = bf16[128,1152]{1,0:T(8,128)(2,1)S(1)} collective-permute-done((bf16[128,1152]{1,0:T(8,128)(2,1)S(1)}, bf16[128,1152]{1,0:T(8,128)(2,1)S(1)}, u32[]{:S(2)}, u32[]{:S(2)}) %collective-permute-start.51) | collective-permute-done | bytes 294944 | tf_op jit(solution)/shard_map/ppermute | solution.py:23
  423.9 13.2 %collective-permute-done.52 = bf16[128,1152]{1,0:T(8,128)(2,1)S(1)} collective-permute-done((bf16[128,1152]{1,0:T(8,128)(2,1)S(1)}, bf16[128,1152]{1,0:T(8,128)(2,1)S(1)}, u32[]{:S(2)}, u32[]{:S(2)}) %collective-permute-start.52) | collective-permute-done | bytes 294944 | tf_op jit(solution)/shard_map/ppermute | solution.py:23
  450.4 3.1 convert_multiply_fusion
  (320 shorter events, 158.9 us)
Async XLA Ops:
  7.2 48.8 %all-gather.5.cloned.1.call-start = ((), (), s32[]{:S(2)}) async-start(), calls=%async_computation.3 | async-start | bytes 2621440 | tf_op jit(solution)/shard_map/all_gather | solution.py:67
  17.6 15.6 %collective-permute-start.3 = (bf16[256,1152]{1,0:T(8,128)(2,1)S(1)}, bf16[256,1152]{1,0:T(8,128)(2,1)S(1)}, u32[]{:S(2)}, u32[]{:S(2)}) collective-permute-start(bf16[256,1152]{1,0:T(8,128)(2,1)S(1)} %get-tuple-element.127), channel_id=1, source_target_pairs={{0,2},{2,0},{16,18},{18,16},{1,3},{3,1},{17,19},{19,17},{4,6},{6,4... | collective-permute-start | bytes 1769480 | tf_op jit(solution)/shard_map/ppermute | solution.py:23
  19.2 16.5 %collective-permute-start.4 = (bf16[256,1152]{1,0:T(8,128)(2,1)S(1)}, bf16[256,1152]{1,0:T(8,128)(2,1)S(1)}, u32[]{:S(2)}, u32[]{:S(2)}) collective-permute-start(bf16[256,1152]{1,0:T(8,128)(2,1)S(1)} %get-tuple-element.128), channel_id=1, source_target_pairs={{0,18},{2,16},{16,2},{18,0},{1,19},{3,17},{17,3},{19,1},{4,22},{6,... | collective-permute-start | bytes 1769480 | tf_op jit(solution)/shard_map/ppermute | solution.py:23
  24.5 67.9 %all-gather.7.cloned.1.call-start = ((), (), s32[]{:S(2)}) async-start(), calls=%async_computation.4 | async-start | bytes 2621440 | tf_op jit(solution)/shard_map/all_gather | solution.py:67
  36.3 14.2 %collective-permute-start.5 = (bf16[2,512,1152]{2,1,0:T(8,128)(2,1)S(1)}, bf16[2,512,1152]{2,1,0:T(8,128)(2,1)}, u32[]{:S(2)}, u32[]{:S(2)}) collective-permute-start(bf16[2,512,1152]{2,1,0:T(8,128)(2,1)S(1)} %bitcast.55), channel_id=1, source_target_pairs={{0,1},{1,0},{2,3},{3,2},{4,5},{5,4},{6,7},{7,6},{8,9},{9,8},{10,11... | collective-permute-start | bytes 7077896 | tf_op jit(solution)/shard_map/ppermute | solution.py:23
  41.5 8.2 %collective-permute-start.8 = (bf16[128,512]{1,0:T(8,128)(2,1)S(1)}, bf16[128,512]{1,0:T(8,128)(2,1)S(1)}, u32[]{:S(2)}, u32[]{:S(2)}) collective-permute-start(bf16[128,512]{1,0:T(8,128)(2,1)S(1)} %get-tuple-element.333), channel_id=1, source_target_pairs={{0,3},{1,2},{2,1},{3,0},{4,7},{5,6},{6,5},{7,4},{8,11},{9,10},{10,... | collective-permute-start | bytes 393224 | tf_op jit(solution)/shard_map/ppermute | solution.py:23
  61.4 119.3 %all-gather.9.cloned.1.call-start = ((), (), s32[]{:S(2)}) async-start(), calls=%async_computation.5 | async-start | bytes 2621440 | tf_op jit(solution)/shard_map/all_gather | solution.py:67
  69.8 35.4 %collective-permute-start.16 = (bf16[256,2816]{1,0:T(8,128)(2,1)}, bf16[256,2816]{1,0:T(8,128)(2,1)}, u32[]{:S(2)}, u32[]{:S(2)}) collective-permute-start(bf16[256,2816]{1,0:T(8,128)(2,1)} %get-tuple-element.152), channel_id=1, source_target_pairs={{0,18},{2,16},{16,2},{18,0},{1,19},{3,17},{17,3},{19,1},{4,22},{6,... | collective-permute-start | bytes 4325384 | tf_op jit(solution)/shard_map/ppermute | solution.py:23
  72.6 34.3 %collective-permute-start.15 = (bf16[256,2816]{1,0:T(8,128)(2,1)}, bf16[256,2816]{1,0:T(8,128)(2,1)}, u32[]{:S(2)}, u32[]{:S(2)}) collective-permute-start(bf16[256,2816]{1,0:T(8,128)(2,1)} %get-tuple-element.150), channel_id=1, source_target_pairs={{0,2},{2,0},{16,18},{18,16},{1,3},{3,1},{17,19},{19,17},{4,6},{6,4... | collective-permute-start | bytes 4325384 | tf_op jit(solution)/shard_map/ppermute | solution.py:23
  109.3 14.9 %collective-permute-start.12 = (bf16[128,2048]{1,0:T(8,128)(2,1)S(1)}, bf16[128,2048]{1,0:T(8,128)(2,1)S(1)}, u32[]{:S(2)}, u32[]{:S(2)}) collective-permute-start(bf16[128,2048]{1,0:T(8,128)(2,1)S(1)} %get-tuple-element.306), channel_id=1, source_target_pairs={{0,4},{4,0},{8,12},{12,8},{1,5},{5,1},{9,13},{13,9},{2,6},{6,2},{1... | collective-permute-start | bytes 1572872 | tf_op jit(solution)/shard_map/ppermute | solution.py:23
  109.8 24.2 %collective-permute-start.13 = (bf16[128,2048]{1,0:T(8,128)(2,1)S(1)}, bf16[128,2048]{1,0:T(8,128)(2,1)}, u32[]{:S(2)}, u32[]{:S(2)}) collective-permute-start(bf16[128,2048]{1,0:T(8,128)(2,1)S(1)} %get-tuple-element.305), channel_id=1, source_target_pairs={{0,8},{4,12},{8,0},{12,4},{1,9},{5,13},{9,1},{13,5},{2,10},{6,14},... | collective-permute-start | bytes 1572872 | tf_op jit(solution)/shard_map/ppermute | solution.py:23
  111.6 25.0 %collective-permute-start.14 = (bf16[128,2048]{1,0:T(8,128)(2,1)S(1)}, bf16[128,2048]{1,0:T(8,128)(2,1)}, u32[]{:S(2)}, u32[]{:S(2)}) collective-permute-start(bf16[128,2048]{1,0:T(8,128)(2,1)S(1)} %get-tuple-element.304), channel_id=1, source_target_pairs={{0,12},{4,8},{8,4},{12,0},{1,13},{5,9},{9,5},{13,1},{2,14},{6,10},... | collective-permute-start | bytes 1572872 | tf_op jit(solution)/shard_map/ppermute | solution.py:23
  139.5 49.6 %collective-permute-start.23 = (bf16[1024,2816]{1,0:T(8,128)(2,1)}, bf16[1024,2816]{1,0:T(8,128)(2,1)}, u32[]{:S(2)}, u32[]{:S(2)}) collective-permute-start(bf16[1024,2816]{1,0:T(8,128)(2,1)} %pad_maximum_fusion.1.own_ref), channel_id=1, source_target_pairs={{0,1},{1,0},{2,3},{3,2},{4,5},{5,4},{6,7},{7,6},{8,9},{9,8},{10,11... | collective-permute-start | bytes 17301512 | tf_op jit(solution)/shard_map/ppermute | solution.py:23
  142.0 18.9 %collective-permute-start.20 = (bf16[704,512]{1,0:T(8,128)(2,1)}, bf16[704,512]{1,0:T(8,128)(2,1)}, u32[]{:S(2)}, u32[]{:S(2)}) collective-permute-start(bf16[704,512]{1,0:T(8,128)(2,1)} %get-tuple-element.166), channel_id=1, source_target_pairs={{0,2},{2,0},{16,18},{18,16},{1,3},{3,1},{17,19},{19,17},{4,6},{6,4... | collective-permute-start | bytes 2162696 | tf_op jit(solution)/shard_map/ppermute | solution.py:23
  142.4 19.8 %collective-permute-start.21 = (bf16[704,512]{1,0:T(8,128)(2,1)}, bf16[704,512]{1,0:T(8,128)(2,1)}, u32[]{:S(2)}, u32[]{:S(2)}) collective-permute-start(bf16[704,512]{1,0:T(8,128)(2,1)} %get-tuple-element.167), channel_id=1, source_target_pairs={{0,18},{2,16},{16,2},{18,0},{1,19},{3,17},{17,3},{19,1},{4,22},{6,... | collective-permute-start | bytes 2162696 | tf_op jit(solution)/shard_map/ppermute | solution.py:23
  143.4 94.1 %reduce-scatter.4.cloned.1.call-start = ((), (), s32[]{:S(2)}) async-start(), calls=%async_computation.6 | async-start | bytes 2621440 | tf_op jit(solution)/shard_map/reduce_scatter | solution.py:71
  167.4 13.3 %collective-permute-start.22 = (bf16[1408,1024]{1,0:T(8,128)(2,1)}, bf16[1408,1024]{1,0:T(8,128)(2,1)}, u32[]{:S(2)}, u32[]{:S(2)}) collective-permute-start(bf16[1408,1024]{1,0:T(8,128)(2,1)} %pad_maximum_fusion.3), channel_id=1, source_target_pairs={{0,1},{1,0},{2,3},{3,2},{4,5},{5,4},{6,7},{7,6},{8,9},{9,8},{10,11... | collective-permute-start | bytes 8650760 | tf_op jit(solution)/shard_map/ppermute | solution.py:23
  168.1 9.5 %collective-permute-start.19 = (bf16[512,1024]{1,0:T(8,128)(2,1)S(1)}, bf16[512,1024]{1,0:T(8,128)(2,1)S(1)}, u32[]{:S(2)}, u32[]{:S(2)}) collective-permute-start(bf16[512,1024]{1,0:T(8,128)(2,1)S(1)} %get-tuple-element.295), channel_id=1, source_target_pairs={{0,1},{1,0},{2,3},{3,2},{4,5},{5,4},{6,7},{7,6},{8,9},{9,8},{10,11... | collective-permute-start | bytes 3145736 | tf_op jit(solution)/shard_map/ppermute | solution.py:23
  169.4 9.6 %collective-permute-start.17 = (bf16[512,1024]{1,0:T(8,128)(2,1)S(1)}, bf16[512,1024]{1,0:T(8,128)(2,1)S(1)}, u32[]{:S(2)}, u32[]{:S(2)}) collective-permute-start(bf16[512,1024]{1,0:T(8,128)(2,1)S(1)} %pad_maximum_fusion.13), channel_id=1, source_target_pairs={{0,1},{1,0},{2,3},{3,2},{4,5},{5,4},{6,7},{7,6},{8,9},{9,8},{10,11... | collective-permute-start | bytes 3145736 | tf_op jit(solution)/shard_map/ppermute | solution.py:23
  208.5 12.8 %collective-permute-start.25 = (bf16[512,2816]{1,0:T(8,128)(2,1)}, bf16[512,2816]{1,0:T(8,128)(2,1)}, u32[]{:S(2)}, u32[]{:S(2)}) collective-permute-start(bf16[512,2816]{1,0:T(8,128)(2,1)} %get-tuple-element.172), channel_id=1, source_target_pairs={{0,1},{1,0},{2,3},{3,2},{4,5},{5,4},{6,7},{7,6},{8,9},{9,8},{10,11... | collective-permute-start | bytes 8650760 | tf_op jit(solution)/shard_map/ppermute | solution.py:23
  208.7 121.9 %reduce-scatter.6.cloned.1.call-start = ((), (), s32[]{:S(2)}) async-start(), calls=%async_computation.7 | async-start | bytes 9191424 | tf_op jit(solution)/shard_map/reduce_scatter | solution.py:613
  208.7 8.9 %collective-permute-start.26 = (bf16[512,1408]{1,0:T(8,128)(2,1)}, bf16[512,1408]{1,0:T(8,128)(2,1)S(1)}, u32[]{:S(2)}, u32[]{:S(2)}) collective-permute-start(bf16[512,1408]{1,0:T(8,128)(2,1)} %copy-done.13), channel_id=1, source_target_pairs={{0,1},{1,0},{2,3},{3,2},{4,5},{5,4},{6,7},{7,6},{8,9},{9,8},{10,11... | collective-permute-start | bytes 4325384 | tf_op jit(solution)/shard_map/ppermute | solution.py:23
  211.4 9.9 %collective-permute-start.24 = (bf16[512,1024]{1,0:T(8,128)(2,1)S(1)}, bf16[512,1024]{1,0:T(8,128)(2,1)S(1)}, u32[]{:S(2)}, u32[]{:S(2)}) collective-permute-start(bf16[512,1024]{1,0:T(8,128)(2,1)S(1)} %pad_maximum_fusion.15), channel_id=1, source_target_pairs={{0,1},{1,0},{2,3},{3,2},{4,5},{5,4},{6,7},{7,6},{8,9},{9,8},{10,11... | collective-permute-start | bytes 3145736 | tf_op jit(solution)/shard_map/ppermute | solution.py:23
  237.6 145.8 %reduce-scatter.8.cloned.1.call-start = ((), (), s32[]{:S(2)}) async-start(), calls=%async_computation.8 | async-start | bytes 2621440 | tf_op jit(solution)/shard_map/reduce_scatter | solution.py:71
  240.3 15.0 %collective-permute-start.29 = (bf16[128,2048]{1,0:T(8,128)(2,1)}, bf16[128,2048]{1,0:T(8,128)(2,1)S(1)}, u32[]{:S(2)}, u32[]{:S(2)}) collective-permute-start(bf16[128,2048]{1,0:T(8,128)(2,1)} %get-tuple-element.202.b0), channel_id=1, source_target_pairs={{0,4},{4,0},{8,12},{12,8},{1,5},{5,1},{9,13},{13,9},{2,6},{6,2},{1... | collective-permute-start | bytes 1572872 | tf_op jit(solution)/shard_map/ppermute | solution.py:23
  240.5 25.3 %collective-permute-start.30 = (bf16[128,2048]{1,0:T(8,128)(2,1)}, bf16[128,2048]{1,0:T(8,128)(2,1)S(1)}, u32[]{:S(2)}, u32[]{:S(2)}) collective-permute-start(bf16[128,2048]{1,0:T(8,128)(2,1)} %get-tuple-element.202.b0), channel_id=1, source_target_pairs={{0,8},{4,12},{8,0},{12,4},{1,9},{5,13},{9,1},{13,5},{2,10},{6,14},... | collective-permute-start | bytes 1572872 | tf_op jit(solution)/shard_map/ppermute | solution.py:23
  242.6 25.8 %collective-permute-start.31 = (bf16[128,2048]{1,0:T(8,128)(2,1)}, bf16[128,2048]{1,0:T(8,128)(2,1)S(1)}, u32[]{:S(2)}, u32[]{:S(2)}) collective-permute-start(bf16[128,2048]{1,0:T(8,128)(2,1)} %get-tuple-element.202.b0), channel_id=1, source_target_pairs={{0,12},{4,8},{8,4},{12,0},{1,13},{5,9},{9,5},{13,1},{2,14},{6,10},... | collective-permute-start | bytes 1572872 | tf_op jit(solution)/shard_map/ppermute | solution.py:23
  268.4 12.2 %collective-permute-start.32 = (bf16[128,2048]{1,0:T(8,128)(2,1)S(1)}, bf16[128,2048]{1,0:T(8,128)(2,1)S(1)}, u32[]{:S(2)}, u32[]{:S(2)}) collective-permute-start(bf16[128,2048]{1,0:T(8,128)(2,1)S(1)} %get-tuple-element.188), channel_id=1, source_target_pairs={{0,4},{4,0},{8,12},{12,8},{1,5},{5,1},{9,13},{13,9},{2,6},{6,2},{1... | collective-permute-start | bytes 1572872 | tf_op jit(solution)/shard_map/ppermute | solution.py:23
  268.4 13.4 %collective-permute-start.33 = (bf16[128,2048]{1,0:T(8,128)(2,1)S(1)}, bf16[128,2048]{1,0:T(8,128)(2,1)S(1)}, u32[]{:S(2)}, u32[]{:S(2)}) collective-permute-start(bf16[128,2048]{1,0:T(8,128)(2,1)S(1)} %get-tuple-element.189), channel_id=1, source_target_pairs={{0,12},{4,8},{8,4},{12,0},{1,13},{5,9},{9,5},{13,1},{2,14},{6,10},... | collective-permute-start | bytes 1572872 | tf_op jit(solution)/shard_map/ppermute | solution.py:23
  288.7 8.8 %collective-permute-start.35 = (bf16[128,512]{1,0:T(8,128)(2,1)S(1)}, bf16[128,512]{1,0:T(8,128)(2,1)S(1)}, u32[]{:S(2)}, u32[]{:S(2)}) collective-permute-start(bf16[128,512]{1,0:T(8,128)(2,1)S(1)} %get-tuple-element.195), channel_id=1, source_target_pairs={{0,2},{1,3},{2,0},{3,1},{4,6},{5,7},{6,4},{7,5},{8,10},{9,11},{10,... | collective-permute-start | bytes 393224 | tf_op jit(solution)/shard_map/ppermute | solution.py:23
  290.4 11.2 %collective-permute-start.36 = (bf16[128,512]{1,0:T(8,128)(2,1)S(1)}, bf16[128,512]{1,0:T(8,128)(2,1)S(1)}, u32[]{:S(2)}, u32[]{:S(2)}) collective-permute-start(bf16[128,512]{1,0:T(8,128)(2,1)S(1)} %get-tuple-element.196), channel_id=1, source_target_pairs={{0,3},{1,2},{2,1},{3,0},{4,7},{5,6},{6,5},{7,4},{8,11},{9,10},{10,... | collective-permute-start | bytes 393224 | tf_op jit(solution)/shard_map/ppermute | solution.py:23
  309.0 7.6 %collective-permute-start.38 = (bf16[512,1024]{1,0:T(8,128)(2,1)S(1)}, bf16[512,1024]{1,0:T(8,128)(2,1)}, u32[]{:S(2)}, u32[]{:S(2)}) collective-permute-start(bf16[512,1024]{1,0:T(8,128)(2,1)S(1)} %get-tuple-element.277), channel_id=1, source_target_pairs={{0,1},{1,0},{2,3},{3,2},{4,5},{5,4},{6,7},{7,6},{8,9},{9,8},{10,11... | collective-permute-start | bytes 3145736 | tf_op jit(solution)/shard_map/ppermute | solution.py:23
  320.4 18.6 %collective-permute-start.39 = (bf16[2,128,1152]{2,1,0:T(8,128)(2,1)}, bf16[2,128,1152]{2,1,0:T(8,128)(2,1)S(1)}, u32[]{:S(2)}, u32[]{:S(2)}) collective-permute-start(bf16[2,128,1152]{2,1,0:T(8,128)(2,1)} %get-tuple-element.268), channel_id=1, source_target_pairs={{0,32},{32,0},{64,96},{96,64},{1,33},{33,1},{65,97},{97,65},{2,34}... | collective-permute-start | bytes 1769480 | tf_op jit(solution)/shard_map/ppermute | solution.py:23
  320.5 32.4 %collective-permute-start.40 = (bf16[2,128,1152]{2,1,0:T(8,128)(2,1)}, bf16[2,128,1152]{2,1,0:T(8,128)(2,1)}, u32[]{:S(2)}, u32[]{:S(2)}) collective-permute-start(bf16[2,128,1152]{2,1,0:T(8,128)(2,1)} %get-tuple-element.269), channel_id=1, source_target_pairs={{0,64},{32,96},{64,0},{96,32},{1,65},{33,97},{65,1},{97,33},{2,66}... | collective-permute-start | bytes 1769480 | tf_op jit(solution)/shard_map/ppermute | solution.py:23
  323.3 29.8 %collective-permute-start.41 = (bf16[2,128,1152]{2,1,0:T(8,128)(2,1)}, bf16[2,128,1152]{2,1,0:T(8,128)(2,1)}, u32[]{:S(2)}, u32[]{:S(2)}) collective-permute-start(bf16[2,128,1152]{2,1,0:T(8,128)(2,1)} %get-tuple-element.267), channel_id=1, source_target_pairs={{0,96},{32,64},{64,32},{96,0},{1,97},{33,65},{65,33},{97,1},{2,98}... | collective-permute-start | bytes 1769480 | tf_op jit(solution)/shard_map/ppermute | solution.py:23
  332.1 21.0 %collective-permute-start.27 = (f32[64,128]{1,0:T(8,128)S(1)}, f32[64,128]{1,0:T(8,128)S(1)}, u32[]{:S(2)}, u32[]{:S(2)}) collective-permute-start(f32[64,128]{1,0:T(8,128)S(1)} %broadcast_in_dim.20), channel_id=1, source_target_pairs={{0,4},{4,0},{8,12},{12,8},{1,5},{5,1},{9,13},{13,9},{2,6},{6,2},{1... | collective-permute-start | bytes 98312 | tf_op jit(solution)/shard_map/ppermute | solution.py:23
  333.9 113.9 %all-gather.11.cloned.1.call-start = ((), (), s32[]{:S(2)}) async-start(), calls=%async_computation.9 | async-start | bytes 5570560 | tf_op jit(solution)/shard_map/all_gather | solution.py:678
  361.7 9.4 %collective-permute-start.44 = (bf16[64,1152]{1,0:T(8,128)(2,1)S(1)}, bf16[64,1152]{1,0:T(8,128)(2,1)S(1)}, u32[]{:S(2)}, u32[]{:S(2)}) collective-permute-start(bf16[64,1152]{1,0:T(8,128)(2,1)S(1)} %get-tuple-element.325), channel_id=1, source_target_pairs={{0,16},{2,18},{16,0},{18,2},{1,17},{3,19},{17,1},{19,3},{4,20},{6,... | collective-permute-start | bytes 442376 | tf_op jit(solution)/shard_map/ppermute | solution.py:23
  363.7 18.4 %collective-permute-start.45 = (bf16[64,1152]{1,0:T(8,128)(2,1)S(1)}, bf16[64,1152]{1,0:T(8,128)(2,1)S(1)}, u32[]{:S(2)}, u32[]{:S(2)}) collective-permute-start(bf16[64,1152]{1,0:T(8,128)(2,1)S(1)} %get-tuple-element.324), channel_id=1, source_target_pairs={{0,18},{2,16},{16,2},{18,0},{1,19},{3,17},{17,3},{19,1},{4,22},{6,... | collective-permute-start | bytes 442376 | tf_op jit(solution)/shard_map/ppermute | solution.py:23
  364.5 17.7 %collective-permute-start.42 = (bf16[64,4352]{1,0:T(8,128)(2,1)S(1)}, bf16[64,4352]{1,0:T(8,128)(2,1)S(1)}, u32[]{:S(2)}, u32[]{:S(2)}) collective-permute-start(bf16[64,4352]{1,0:T(8,128)(2,1)S(1)} %pad_maximum_fusion.18), channel_id=1, source_target_pairs={{0,16},{2,18},{16,0},{18,2},{1,17},{3,19},{17,1},{19,3},{4,20},{6,... | collective-permute-start | bytes 1671176 | tf_op jit(solution)/shard_map/ppermute | solution.py:23
  387.7 8.0 %collective-permute-start.49 = (bf16[128,512]{1,0:T(8,128)(2,1)S(1)}, bf16[128,512]{1,0:T(8,128)(2,1)S(1)}, u32[]{:S(2)}, u32[]{:S(2)}) collective-permute-start(bf16[128,512]{1,0:T(8,128)(2,1)S(1)} %get-tuple-element.319), channel_id=1, source_target_pairs={{0,3},{1,2},{2,1},{3,0},{4,7},{5,6},{6,5},{7,4},{8,11},{9,10},{10,... | collective-permute-start | bytes 393224 | tf_op jit(solution)/shard_map/ppermute | solution.py:23
  389.4 15.7 %collective-permute-start.50 = (bf16[128,2048]{1,0:T(8,128)(2,1)S(1)}, bf16[128,2048]{1,0:T(8,128)(2,1)S(1)}, u32[]{:S(2)}, u32[]{:S(2)}) collective-permute-start(bf16[128,2048]{1,0:T(8,128)(2,1)S(1)} %copy-done.47), channel_id=1, source_target_pairs={{0,8},{4,12},{8,0},{12,4},{1,9},{5,13},{9,1},{13,5},{2,10},{6,14},... | collective-permute-start | bytes 1572872 | tf_op jit(solution)/shard_map/ppermute | solution.py:23
  396.9 8.0 %collective-permute-start.46 = (bf16[64,1152]{1,0:T(8,128)(2,1)S(1)}, bf16[64,1152]{1,0:T(8,128)(2,1)S(1)}, u32[]{:S(2)}, u32[]{:S(2)}) collective-permute-start(bf16[64,1152]{1,0:T(8,128)(2,1)S(1)} %fusion.40), channel_id=1, source_target_pairs={{0,16},{2,18},{16,0},{18,2},{1,17},{3,19},{17,1},{19,3},{4,20},{6,... | collective-permute-start | bytes 442376 | tf_op jit(solution)/shard_map/ppermute | solution.py:23
  406.1 8.0 %collective-permute-start.56 = (bf16[128,512]{1,0:T(8,128)(2,1)S(1)}, bf16[128,512]{1,0:T(8,128)(2,1)S(1)}, u32[]{:S(2)}, u32[]{:S(2)}) collective-permute-start(bf16[128,512]{1,0:T(8,128)(2,1)S(1)} %get-tuple-element.330), channel_id=1, source_target_pairs={{0,3},{1,2},{2,1},{3,0},{4,7},{5,6},{6,5},{7,4},{8,11},{9,10},{10,... | collective-permute-start | bytes 393224 | tf_op jit(solution)/shard_map/ppermute | solution.py:23
  407.7 16.2 %collective-permute-start.51 = (bf16[128,1152]{1,0:T(8,128)(2,1)S(1)}, bf16[128,1152]{1,0:T(8,128)(2,1)S(1)}, u32[]{:S(2)}, u32[]{:S(2)}) collective-permute-start(bf16[128,1152]{1,0:T(8,128)(2,1)S(1)} %pad_maximum_fusion.22), channel_id=1, source_target_pairs={{0,32},{32,0},{64,96},{96,64},{1,33},{33,1},{65,97},{97,65},{2,34}... | collective-permute-start | bytes 884744 | tf_op jit(solution)/shard_map/ppermute | solution.py:23
  407.9 29.2 %collective-permute-start.52 = (bf16[128,1152]{1,0:T(8,128)(2,1)S(1)}, bf16[128,1152]{1,0:T(8,128)(2,1)S(1)}, u32[]{:S(2)}, u32[]{:S(2)}) collective-permute-start(bf16[128,1152]{1,0:T(8,128)(2,1)S(1)} %pad_maximum_fusion.22), channel_id=1, source_target_pairs={{0,64},{32,96},{64,0},{96,32},{1,65},{33,97},{65,1},{97,33},{2,66}... | collective-permute-start | bytes 884744 | tf_op jit(solution)/shard_map/ppermute | solution.py:23
  410.6 26.6 %collective-permute-start.53 = (bf16[128,1152]{1,0:T(8,128)(2,1)S(1)}, bf16[128,1152]{1,0:T(8,128)(2,1)S(1)}, u32[]{:S(2)}, u32[]{:S(2)}) collective-permute-start(bf16[128,1152]{1,0:T(8,128)(2,1)S(1)} %pad_maximum_fusion.22), channel_id=1, source_target_pairs={{0,96},{32,64},{64,32},{96,0},{1,97},{33,65},{65,33},{97,1},{2,98}... | collective-permute-start | bytes 884744 | tf_op jit(solution)/shard_map/ppermute | solution.py:23
  438.6 8.6 %collective-permute-start.57 = (f32[1,512]{1,0:T(1,128)S(1)}, f32[1,512]{1,0:T(1,128)S(1)}, u32[]{:S(2)}, u32[]{:S(2)}) collective-permute-start(f32[1,512]{1,0:T(1,128)S(1)} %bitcast.78), channel_id=1, source_target_pairs={{0,4},{4,0},{8,12},{12,8},{1,5},{5,1},{9,13},{13,9},{2,6},{6,2},{1... | collective-permute-start | bytes 6152 | tf_op jit(solution)/shard_map/ppermute | solution.py:23
  (72 other events, 403.5 us)
Sparse Core Ops, SparseCore 0:
  24.6 31.3 all-gather.4
  61.5 30.8 all-gather.6
  143.6 31.2 all-gather.8
  208.8 28.7 reduce-scatter.3
  241.2 89.3 reduce-scatter.5
  334.1 29.7 reduce-scatter.7
  383.5 61.3 all-gather.10

commit v7 on v4

--- a/solution.py
+++ b/solution.py
@@ -571,9 +571,10 @@
     gu_mine = ring_join(gu_halves, after(gu_got, branch), low, 0)
     down_halves = [after(v, branch, gu_got) for v in cut(w_down, 2, 0)]
     down_got = ring_send(down_halves)
-    branch_parts = after(collect_row(row_parts(branch, row)), gu_mine, down_got)
+    down_mine = ring_join(down_halves, down_got, low, 1)
+    branch_parts = after(collect_row(row_parts(branch, row)), gu_mine, down_mine)
     hidden, normed_two = rows_call(add_and_norm, (F32, BF16), (inputs, *branch_parts))
-    down_mine = ring_join(down_halves, after(down_got, hidden), low, 1)
+    down_mine = after(down_mine, hidden)
     full_down = jnp.concatenate([down_mine, trade_core(down_mine)], axis=1)
     grad_inner = product(grad_rows, full_down, ((1,), (1,)))
     gu_theirs = trade_core(after(gu_mine, hidden))

time: 451 us -> 444 us (0.984)
    all_gather x3, waiting for transfers between devices: 5.5 us -> 0.01 us  [gather_row(): return lax.all_gather(values, 'y', axis=0, tiled=True)]
    unnamed x123 -> x110, local copies, waits for them, and re-layouts: 23.7 us -> 22 us
  transfers between devices with their start and end apart: 67 -> 67, of which waited for: 33 -> 34; matrix products, arithmetic and copies ran while one was open for 24% -> 23% of each run, Pallas kernels for 9% -> 9%
where the time goes in v7:
time: 444 us; the launch traced here: 436 us
  waiting for transfers between devices  172 us (39%)
  starting transfers between devices  64.8 us (15%)
  Pallas kernels  59.8 us (13%)
  local copies, waits for them, and re-layouts  49.7 us (11%)
  other arithmetic  43.1 us (10%)
  matrix products  30.6 us (7%)
  between operations  16.1 us (4%)
    ppermute x60, waiting for transfers between devices, trade(): return lax.ppermute(values, axes, [(i, i ^ mask) for i in range(size)])  161 us
    ppermute x60, starting transfers between devices, trade(): return lax.ppermute(values, axes, [(i, i ^ mask) for i in range(size)])  64 us
    pallas_call x7, Pallas kernels, kernel_call(): pl.pallas_call(whole, out_shape=out_shape, in_specs=[pl.BlockSpec(memory_...  51.6 us
    dot_general x7, matrix products, product(): lax.dot_general(left, right, (dims, ((), ())), preferred_element_type=F32)  30.6 us
    unnamed x110, local copies, waits for them, and re-layouts  22 us
  transfers between devices with their start and end apart: 67, of which 34 were waited for; matrix products, arithmetic and copies ran while one was open for 23% of the time, Pallas kernels for 9%

profile of v7, /device:TPU:0, one launch (start us, length us, event | category | flops | bytes accessed | tf_op | source)
XLA Modules:
  0.0 435.8 jit_solution(11237708346841205475)
XLA Ops:
  13.7 2.6 fusion.56
  22.6 10.5 %collective-permute-done.3 = bf16[256,1152]{1,0:T(8,128)(2,1)S(1)} collective-permute-done((bf16[256,1152]{1,0:T(8,128)(2,1)S(1)}, bf16[256,1152]{1,0:T(8,128)(2,1)S(1)}, u32[]{:S(2)}, u32[]{:S(2)}) %collective-permute-start.3) | collective-permute-done | bytes 589856 | tf_op jit(solution)/shard_map/ppermute | solution.py:23
  45.0 3.6 collective-permute-done.7
  56.0 3.8 shard_map.169
  70.6 8.6 %shard_map.170 = (f32[512,512]{1,0:T(8,128)S(1)}, bf16[512,512]{1,0:T(8,128)(2,1)S(1)}, f32[8,512]{1,0:T(8,128)S(1)}) custom-call(bf16[512,512]{1,0:T(8,128)(2,1)S(1)} %get-tuple-element.134.q_ref.refs_0_, bf16[4,128,512]{2,1,0:T(8,128)(2,1)S(1)} %pad_maximum_fusion.17.pairs_ref.refs_1_, s32[512,128]{1,0:T(8,128)S(1)} %broadcast_in_dim.17.koff_ref.refs_2_, ...), custom_call_target="tpu_custom_call" | custom-call | flops 2147483648 | bytes 1314816 | tf_op jit(solution)/shard_map/pallas_call | solution.py:465
  83.4 2.9 collective-permute-start.13
  86.6 13.3 %collective-permute-done.15 = bf16[256,2816]{1,0:T(8,128)(2,1)} collective-permute-done((bf16[256,2816]{1,0:T(8,128)(2,1)}, bf16[256,2816]{1,0:T(8,128)(2,1)}, u32[]{:S(2)}, u32[]{:S(2)}) %collective-permute-start.15) | collective-permute-done | bytes 1441824 | tf_op jit(solution)/shard_map/ppermute | solution.py:23
  104.9 2.6 broadcast_select_fusion.1
  107.6 2.8 pad_maximum_fusion.1.own_ref
  110.4 8.6 %collective-permute-done.17 = bf16[704,512]{1,0:T(8,128)(2,1)S(1)} collective-permute-done((bf16[704,512]{1,0:T(8,128)(2,1)S(1)}, bf16[704,512]{1,0:T(8,128)(2,1)S(1)}, u32[]{:S(2)}, u32[]{:S(2)}) %collective-permute-start.17) | collective-permute-done | bytes 720928 | tf_op jit(solution)/shard_map/ppermute | solution.py:23
  121.2 2.8 collective-permute-done.13.p2
  124.0 2.9 shard_map.171
  127.5 3.0 fusion.54
  133.7 7.2 %collective-permute-done.20 = bf16[512,512]{1,0:T(8,128)(2,1)S(1)} collective-permute-done((bf16[512,512]{1,0:T(8,128)(2,1)S(1)}, bf16[512,512]{1,0:T(8,128)(2,1)S(1)}, u32[]{:S(2)}, u32[]{:S(2)}) %collective-permute-start.20) | collective-permute-done | bytes 524320 | tf_op jit(solution)/shard_map/ppermute | solution.py:23
  142.0 2.6 collective-permute-done.21
  144.6 2.8 pad_maximum_fusion.6
  153.7 5.0 %fusion.58.gi_ref = f32[512,1408]{1,0:T(8,128)} fusion(bf16[512,2048]{1,0:T(8,128)(2,1)S(1)} %copy-done.28, bf16[1408,2048]{1,0:T(8,128)(2,1)S(1)} %constant_dynamic-update-slice_fusion.12), kind=kOutput, calls=%fused_computation.222 | convolution fusion | flops 2952790016 | bytes 10747904 | tf_op jit(solution)/shard_map/dot_general | solution.py:184
  160.3 17.0 %shard_map.172 = (bf16[512,1408]{1,0:T(8,128)(2,1)S(1)}, bf16[512,2816]{1,0:T(8,128)(2,1)}, bf16[512,2048]{1,0:T(8,128)(2,1)S(1)}) custom-call(bf16[512,2048]{1,0:T(8,128)(2,1)S(1)} %copy-done.8, f32[512,1408]{1,0:T(8,128)} %fusion.58.gi_ref, bf16[1024,2816]{1,0:T(8,128)(2,1)} %pad_maximum_fusion.1.own_ref, bf16[1024,2816]{1,0:T(8,128)(2,1)} %collective-permute-done.23.other_ref), custom_call_target="tpu_custom_call" | custom-call | flops 11811160064 | bytes 16515072 | tf_op jit(solution)/shard_map/pallas_call | solution.py:465
  182.8 6.0 %collective-permute-done.26 = bf16[512,1408]{1,0:T(8,128)(2,1)S(1)} collective-permute-done((bf16[512,1408]{1,0:T(8,128)(2,1)}, bf16[512,1408]{1,0:T(8,128)(2,1)S(1)}, u32[]{:S(2)}, u32[]{:S(2)}) %collective-permute-start.26) | collective-permute-done | bytes 1441824 | tf_op jit(solution)/shard_map/ppermute | solution.py:23
  188.7 3.7 convolution_convert_fusion
  192.5 8.4 %fusion.4 = bf16[1024,2816]{1,0:T(8,128)(2,1)S(1)} fusion(bf16[512,2816]{1,0:T(8,128)(2,1)} %collective-permute-done.25, bf16[512,2816]{1,0:T(8,128)(2,1)S(1)} %copy-done.49, bf16[512,1024]{1,0:T(8,128)(2,1)S(1)} %collective-permute-done.24, bf16[512,256]{1,0:T(8,128)(2,1)S(1)} %get-tuple-element.281, bf16[512,256]{1,0:T(8,128)(2,1)S(1)} %get-tuple-element.282, ...), kind=kOutput, calls=%fused_computation.6 | convolution fusion | flops 5930483712 | bytes 13631488 | tf_op jit(solution)/shard_map/dot_general | solution.py:184
  200.9 3.8 pad_maximum_fusion
  204.7 5.0 %reduce-scatter.4.cloned.1.call-done.part_ref = bf16[128,2048]{1,0:T(8,128)(2,1)} async-done(((bf16[512,2048]{1,0:T(8,128)(2,1)}), bf16[128,2048]{1,0:T(8,128)(2,1)}) %reduce-scatter.4.cloned.1.call-update) | async-done | bytes 524304 | tf_op jit(solution)/shard_map/reduce_scatter | solution.py:71
  209.7 2.6 shard_map.173
  217.1 6.5 %convolution_convert_fusion.2 = bf16[512,2048]{1,0:T(8,128)(2,1)S(1)} fusion(bf16[512,1408]{1,0:T(8,128)(2,1)} %copy-done.12, bf16[1408,2048]{1,0:T(8,128)(2,1)} %copy-done.35), kind=kOutput, calls=%fused_computation.17 | convolution fusion | flops 2953838592 | bytes 9306112 | tf_op jit(solution)/shard_map/dot_general | solution.py:184
  224.8 2.6 collective-permute-done.29.b1
  227.4 10.5 %collective-permute-done.30.b2 = bf16[128,2048]{1,0:T(8,128)(2,1)S(1)} collective-permute-done((bf16[128,2048]{1,0:T(8,128)(2,1)}, bf16[128,2048]{1,0:T(8,128)(2,1)S(1)}, u32[]{:S(2)}, u32[]{:S(2)}) %collective-permute-start.30) | collective-permute-done | bytes 524320 | tf_op jit(solution)/shard_map/ppermute | solution.py:23
  237.9 2.6 collective-permute-done.31.b3
  245.4 7.2 %shard_map.175 = (bf16[256,512]{1,0:T(8,128)(2,1)S(1)}, f32[4,64,512]{2,1,0:T(8,128)S(1)}, f32[4,64,512]{2,1,0:T(8,128)S(1)}) custom-call(bf16[512,512]{1,0:T(8,128)(2,1)S(1)} %copy-done.15, bf16[4,128,512]{2,1,0:T(8,128)(2,1)S(1)} %copy-done.11, s32[512,128]{1,0:T(8,128)S(1)} %broadcast_in_dim.17.koff_ref.refs_2_, s32[1,512]{1,0:T(1,128)S(1)} %bitcast.66, ...), custom_call_target="tpu_custom_call" | custom-call | flops 2684354560 | bytes 3035136 | tf_op jit(solution)/shard_map/pallas_call | solution.py:465
  253.9 6.8 %shard_map.176 = (bf16[256,512]{1,0:T(8,128)(2,1)S(1)}, bf16[128,512]{1,0:T(8,128)(2,1)S(1)}, bf16[128,512]{1,0:T(8,128)(2,1)S(1)}, bf16[128,512]{1,0:T(8,128)(2,1)S(1)}, bf16[128,512]{1,0:T(8,128)(2,1)S(1)}) custom-call(bf16[512,512]{1,0:T(8,128)(2,1)S(1)} %copy-done.15, bf16[4,128,512]{2,1,0:T(8,128)(2,1)S(1)} %copy-done.11, ...), custom_call_target="tpu_custom_call" | custom-call | flops 2684354560 | bytes 4083712 | tf_op jit(solution)/shard_map/pallas_call | solution.py:465
  262.9 6.7 %collective-permute-done.35.g2 = bf16[128,512]{1,0:T(8,128)(2,1)S(1)} collective-permute-done((bf16[128,512]{1,0:T(8,128)(2,1)S(1)}, bf16[128,512]{1,0:T(8,128)(2,1)S(1)}, u32[]{:S(2)}, u32[]{:S(2)}) %collective-permute-start.35) | collective-permute-done | bytes 131104 | tf_op jit(solution)/shard_map/ppermute | solution.py:23
  269.6 4.2 collective-permute-done.36.g3
  273.8 5.8 %shard_map.177 = (bf16[640,512]{1,0:T(8,128)(2,1)}, bf16[512,2048]{1,0:T(8,128)(2,1)}) custom-call(bf16[256,512]{1,0:T(8,128)(2,1)S(1)} %get-tuple-element.175.gq0, bf16[256,512]{1,0:T(8,128)(2,1)S(1)} %get-tuple-element.182.gq1, bf16[128,512]{1,0:T(8,128)(2,1)S(1)} %get-tuple-element.187.g0, bf16[128,512]{1,0:T(8,128)(2,1)S(1)} %collective-permute-done.34.g1, ...), custom_call_target="tpu_custom_call" | custom-call | flops 1342177280 | bytes 5898240 | tf_op jit(solution)/shard_map/pallas_call | solution.py:465
  282.0 3.4 collective-permute-done.37
  285.5 3.1 convolution_convert_fusion.3
  293.1 2.8 collective-permute-start.40
  297.1 5.5 %reduce-scatter.6.cloned.1.call-done = bf16[64,4224]{1,0:T(8,128)(2,1)} async-done(((bf16[1024,4224]{1,0:T(8,128)(2,1)}), bf16[64,4224]{1,0:T(8,128)(2,1)}) %reduce-scatter.6.cloned.1.call-update) | async-done | bytes 540688 | tf_op jit(solution)/shard_map/reduce_scatter | solution.py:611
  305.7 5.4 %collective-permute-done.39 = bf16[2,128,1152]{2,1,0:T(8,128)(2,1)S(1)} collective-permute-done((bf16[2,128,1152]{2,1,0:T(8,128)(2,1)}, bf16[2,128,1152]{2,1,0:T(8,128)(2,1)S(1)}, u32[]{:S(2)}, u32[]{:S(2)}) %collective-permute-start.39) | collective-permute-done | bytes 589856 | tf_op jit(solution)/shard_map/ppermute | solution.py:23
  311.1 13.9 %collective-permute-done.40 = bf16[2,128,1152]{2,1,0:T(8,128)(2,1)} collective-permute-done((bf16[2,128,1152]{2,1,0:T(8,128)(2,1)}, bf16[2,128,1152]{2,1,0:T(8,128)(2,1)}, u32[]{:S(2)}, u32[]{:S(2)}) %collective-permute-start.40) | collective-permute-done | bytes 589856 | tf_op jit(solution)/shard_map/ppermute | solution.py:23
  325.2 3.0 collective-permute-start.28
  338.1 5.8 %collective-permute-done.44 = bf16[64,1152]{1,0:T(8,128)(2,1)S(1)} collective-permute-done((bf16[64,1152]{1,0:T(8,128)(2,1)S(1)}, bf16[64,1152]{1,0:T(8,128)(2,1)S(1)}, u32[]{:S(2)}, u32[]{:S(2)}) %collective-permute-start.44) | collective-permute-done | bytes 147488 | tf_op jit(solution)/shard_map/ppermute | solution.py:23
  343.9 10.7 %collective-permute-done.45 = bf16[64,1152]{1,0:T(8,128)(2,1)S(1)} collective-permute-done((bf16[64,1152]{1,0:T(8,128)(2,1)S(1)}, bf16[64,1152]{1,0:T(8,128)(2,1)S(1)}, u32[]{:S(2)}, u32[]{:S(2)}) %collective-permute-start.45) | collective-permute-done | bytes 147488 | tf_op jit(solution)/shard_map/ppermute | solution.py:23
  355.9 2.7 shard_map.178
  371.7 5.6 %collective-permute-done.46 = bf16[64,1152]{1,0:T(8,128)(2,1)S(1)} collective-permute-done((bf16[64,1152]{1,0:T(8,128)(2,1)S(1)}, bf16[64,1152]{1,0:T(8,128)(2,1)S(1)}, u32[]{:S(2)}, u32[]{:S(2)}) %collective-permute-start.46) | collective-permute-done | bytes 147488 | tf_op jit(solution)/shard_map/ppermute | solution.py:23
  387.5 8.9 %collective-permute-done.51 = bf16[128,1152]{1,0:T(8,128)(2,1)S(1)} collective-permute-done((bf16[128,1152]{1,0:T(8,128)(2,1)S(1)}, bf16[128,1152]{1,0:T(8,128)(2,1)S(1)}, u32[]{:S(2)}, u32[]{:S(2)}) %collective-permute-start.51) | collective-permute-done | bytes 294944 | tf_op jit(solution)/shard_map/ppermute | solution.py:23
  396.4 12.7 %collective-permute-done.52 = bf16[128,1152]{1,0:T(8,128)(2,1)S(1)} collective-permute-done((bf16[128,1152]{1,0:T(8,128)(2,1)S(1)}, bf16[128,1152]{1,0:T(8,128)(2,1)S(1)}, u32[]{:S(2)}, u32[]{:S(2)}) %collective-permute-start.52) | collective-permute-done | bytes 294944 | tf_op jit(solution)/shard_map/ppermute | solution.py:23
  411.7 3.0 collective-permute-start.58
  422.6 3.1 convert_multiply_fusion
  (316 shorter events, 145.2 us)
Async XLA Ops:
  7.2 47.2 %all-gather.5.cloned.1.call-start = ((), (), s32[]{:S(2)}) async-start(), calls=%async_computation.3 | async-start | bytes 2621440 | tf_op jit(solution)/shard_map/all_gather | solution.py:67
  8.5 8.7 %collective-permute-start = (bf16[128,512]{1,0:T(8,128)(2,1)S(1)}, bf16[128,512]{1,0:T(8,128)(2,1)S(1)}, u32[]{:S(2)}, u32[]{:S(2)}) collective-permute-start(bf16[128,512]{1,0:T(8,128)(2,1)S(1)} %get-tuple-element.328), channel_id=1, source_target_pairs={{0,1},{1,0},{2,3},{3,2},{4,5},{5,4},{6,7},{7,6},{8,9},{9,8},{10,11... | collective-permute-start | bytes 393224 | tf_op jit(solution)/shard_map/ppermute | solution.py:23
  8.6 8.7 %collective-permute-start.1 = (bf16[128,512]{1,0:T(8,128)(2,1)S(1)}, bf16[128,512]{1,0:T(8,128)(2,1)S(1)}, u32[]{:S(2)}, u32[]{:S(2)}) collective-permute-start(bf16[128,512]{1,0:T(8,128)(2,1)S(1)} %get-tuple-element.330), channel_id=1, source_target_pairs={{0,2},{1,3},{2,0},{3,1},{4,6},{5,7},{6,4},{7,5},{8,10},{9,11},{10,... | collective-permute-start | bytes 393224 | tf_op jit(solution)/shard_map/ppermute | solution.py:23
  17.4 15.7 %collective-permute-start.3 = (bf16[256,1152]{1,0:T(8,128)(2,1)S(1)}, bf16[256,1152]{1,0:T(8,128)(2,1)S(1)}, u32[]{:S(2)}, u32[]{:S(2)}) collective-permute-start(bf16[256,1152]{1,0:T(8,128)(2,1)S(1)} %get-tuple-element.122), channel_id=1, source_target_pairs={{0,2},{2,0},{16,18},{18,16},{1,3},{3,1},{17,19},{19,17},{4,6},{6,4... | collective-permute-start | bytes 1769480 | tf_op jit(solution)/shard_map/ppermute | solution.py:23
  19.0 16.5 %collective-permute-start.4 = (bf16[256,1152]{1,0:T(8,128)(2,1)S(1)}, bf16[256,1152]{1,0:T(8,128)(2,1)S(1)}, u32[]{:S(2)}, u32[]{:S(2)}) collective-permute-start(bf16[256,1152]{1,0:T(8,128)(2,1)S(1)} %get-tuple-element.123), channel_id=1, source_target_pairs={{0,18},{2,16},{16,2},{18,0},{1,19},{3,17},{17,3},{19,1},{4,22},{6,... | collective-permute-start | bytes 1769480 | tf_op jit(solution)/shard_map/ppermute | solution.py:23
  22.4 108.3 %all-gather.9.cloned.1.call-start = ((), (), s32[]{:S(2)}) async-start(), calls=%async_computation.5 | async-start | bytes 2621440 | tf_op jit(solution)/shard_map/all_gather | solution.py:67
  36.1 15.3 %collective-permute-start.5 = (bf16[2,512,1152]{2,1,0:T(8,128)(2,1)S(1)}, bf16[2,512,1152]{2,1,0:T(8,128)(2,1)}, u32[]{:S(2)}, u32[]{:S(2)}) collective-permute-start(bf16[2,512,1152]{2,1,0:T(8,128)(2,1)S(1)} %bitcast.57), channel_id=1, source_target_pairs={{0,1},{1,0},{2,3},{3,2},{4,5},{5,4},{6,7},{7,6},{8,9},{9,8},{10,11... | collective-permute-start | bytes 7077896 | tf_op jit(solution)/shard_map/ppermute | solution.py:23
  59.8 10.6 %collective-permute-start.9 = (bf16[128,512]{1,0:T(8,128)(2,1)S(1)}, bf16[128,512]{1,0:T(8,128)(2,1)S(1)}, u32[]{:S(2)}, u32[]{:S(2)}) collective-permute-start(bf16[128,512]{1,0:T(8,128)(2,1)S(1)} %get-tuple-element.135), channel_id=1, source_target_pairs={{0,1},{1,0},{2,3},{3,2},{4,5},{5,4},{6,7},{7,6},{8,9},{9,8},{10,11... | collective-permute-start | bytes 393224 | tf_op jit(solution)/shard_map/ppermute | solution.py:23
  60.5 9.9 %collective-permute-start.10 = (bf16[128,512]{1,0:T(8,128)(2,1)S(1)}, bf16[128,512]{1,0:T(8,128)(2,1)S(1)}, u32[]{:S(2)}, u32[]{:S(2)}) collective-permute-start(bf16[128,512]{1,0:T(8,128)(2,1)S(1)} %get-tuple-element.135), channel_id=1, source_target_pairs={{0,2},{1,3},{2,0},{3,1},{4,6},{5,7},{6,4},{7,5},{8,10},{9,11},{10,... | collective-permute-start | bytes 393224 | tf_op jit(solution)/shard_map/ppermute | solution.py:23
  60.9 9.5 %collective-permute-start.11 = (bf16[128,512]{1,0:T(8,128)(2,1)S(1)}, bf16[128,512]{1,0:T(8,128)(2,1)S(1)}, u32[]{:S(2)}, u32[]{:S(2)}) collective-permute-start(bf16[128,512]{1,0:T(8,128)(2,1)S(1)} %get-tuple-element.135), channel_id=1, source_target_pairs={{0,3},{1,2},{2,1},{3,0},{4,7},{5,6},{6,5},{7,4},{8,11},{9,10},{10,... | collective-permute-start | bytes 393224 | tf_op jit(solution)/shard_map/ppermute | solution.py:23
  62.0 37.9 %collective-permute-start.15 = (bf16[256,2816]{1,0:T(8,128)(2,1)}, bf16[256,2816]{1,0:T(8,128)(2,1)}, u32[]{:S(2)}, u32[]{:S(2)}) collective-permute-start(bf16[256,2816]{1,0:T(8,128)(2,1)} %get-tuple-element.141), channel_id=1, source_target_pairs={{0,2},{2,0},{16,18},{18,16},{1,3},{3,1},{17,19},{19,17},{4,6},{6,4... | collective-permute-start | bytes 4325384 | tf_op jit(solution)/shard_map/ppermute | solution.py:23
  62.7 37.2 %collective-permute-start.16 = (bf16[256,2816]{1,0:T(8,128)(2,1)}, bf16[256,2816]{1,0:T(8,128)(2,1)}, u32[]{:S(2)}, u32[]{:S(2)}) collective-permute-start(bf16[256,2816]{1,0:T(8,128)(2,1)} %get-tuple-element.142), channel_id=1, source_target_pairs={{0,18},{2,16},{16,2},{18,0},{1,19},{3,17},{17,3},{19,1},{4,22},{6,... | collective-permute-start | bytes 4325384 | tf_op jit(solution)/shard_map/ppermute | solution.py:23
  69.9 88.8 %all-gather.7.cloned.1.call-start = ((), (), s32[]{:S(2)}) async-start(), calls=%async_computation.4 | async-start | bytes 2621440 | tf_op jit(solution)/shard_map/all_gather | solution.py:67
  81.9 39.4 %collective-permute-start.12 = (bf16[128,2048]{1,0:T(8,128)(2,1)}, bf16[128,2048]{1,0:T(8,128)(2,1)S(1)}, u32[]{:S(2)}, u32[]{:S(2)}) collective-permute-start(bf16[128,2048]{1,0:T(8,128)(2,1)} %get-tuple-element.296), channel_id=1, source_target_pairs={{0,4},{4,0},{8,12},{12,8},{1,5},{5,1},{9,13},{13,9},{2,6},{6,2},{1... | collective-permute-start | bytes 1572872 | tf_op jit(solution)/shard_map/ppermute | solution.py:23
  83.4 40.6 %collective-permute-start.13 = (bf16[128,2048]{1,0:T(8,128)(2,1)}, bf16[128,2048]{1,0:T(8,128)(2,1)}, u32[]{:S(2)}, u32[]{:S(2)}) collective-permute-start(bf16[128,2048]{1,0:T(8,128)(2,1)} %get-tuple-element.295), channel_id=1, source_target_pairs={{0,8},{4,12},{8,0},{12,4},{1,9},{5,13},{9,1},{13,5},{2,10},{6,14},... | collective-permute-start | bytes 1572872 | tf_op jit(solution)/shard_map/ppermute | solution.py:23
  86.4 37.7 %collective-permute-start.14 = (bf16[128,2048]{1,0:T(8,128)(2,1)}, bf16[128,2048]{1,0:T(8,128)(2,1)}, u32[]{:S(2)}, u32[]{:S(2)}) collective-permute-start(bf16[128,2048]{1,0:T(8,128)(2,1)} %get-tuple-element.294), channel_id=1, source_target_pairs={{0,12},{4,8},{8,4},{12,0},{1,13},{5,9},{9,5},{13,1},{2,14},{6,10},... | collective-permute-start | bytes 1572872 | tf_op jit(solution)/shard_map/ppermute | solution.py:23
  99.9 19.2 %collective-permute-start.18 = (bf16[704,512]{1,0:T(8,128)(2,1)S(1)}, bf16[704,512]{1,0:T(8,128)(2,1)S(1)}, u32[]{:S(2)}, u32[]{:S(2)}) collective-permute-start(bf16[704,512]{1,0:T(8,128)(2,1)S(1)} %copy-done.23), channel_id=1, source_target_pairs={{0,18},{2,16},{16,2},{18,0},{1,19},{3,17},{17,3},{19,1},{4,22},{6,... | collective-permute-start | bytes 2162696 | tf_op jit(solution)/shard_map/ppermute | solution.py:23
  102.0 17.0 %collective-permute-start.17 = (bf16[704,512]{1,0:T(8,128)(2,1)S(1)}, bf16[704,512]{1,0:T(8,128)(2,1)S(1)}, u32[]{:S(2)}, u32[]{:S(2)}) collective-permute-start(bf16[704,512]{1,0:T(8,128)(2,1)S(1)} %copy-done.24), channel_id=1, source_target_pairs={{0,2},{2,0},{16,18},{18,16},{1,3},{3,1},{17,19},{19,17},{4,6},{6,4... | collective-permute-start | bytes 2162696 | tf_op jit(solution)/shard_map/ppermute | solution.py:23
  127.0 31.8 %collective-permute-start.23 = (bf16[1024,2816]{1,0:T(8,128)(2,1)}, bf16[1024,2816]{1,0:T(8,128)(2,1)}, u32[]{:S(2)}, u32[]{:S(2)}) collective-permute-start(bf16[1024,2816]{1,0:T(8,128)(2,1)} %pad_maximum_fusion.1.own_ref), channel_id=1, source_target_pairs={{0,1},{1,0},{2,3},{3,2},{4,5},{5,4},{6,7},{7,6},{8,9},{9,8},{10,11... | collective-permute-start | bytes 17301512 | tf_op jit(solution)/shard_map/ppermute | solution.py:23
  127.0 22.1 %collective-permute-start.22 = (bf16[1408,1024]{1,0:T(8,128)(2,1)}, bf16[1408,1024]{1,0:T(8,128)(2,1)}, u32[]{:S(2)}, u32[]{:S(2)}) collective-permute-start(bf16[1408,1024]{1,0:T(8,128)(2,1)} %pad_maximum_fusion.2), channel_id=1, source_target_pairs={{0,1},{1,0},{2,3},{3,2},{4,5},{5,4},{6,7},{7,6},{8,9},{9,8},{10,11... | collective-permute-start | bytes 8650760 | tf_op jit(solution)/shard_map/ppermute | solution.py:23
  127.5 82.2 %reduce-scatter.4.cloned.1.call-start = ((), (), s32[]{:S(2)}) async-start(), calls=%async_computation.6 | async-start | bytes 2621440 | tf_op jit(solution)/shard_map/reduce_scatter | solution.py:71
  130.6 14.0 %collective-permute-start.21 = (bf16[512,1024]{1,0:T(8,128)(2,1)}, bf16[512,1024]{1,0:T(8,128)(2,1)}, u32[]{:S(2)}, u32[]{:S(2)}) collective-permute-start(bf16[512,1024]{1,0:T(8,128)(2,1)} %get-tuple-element.285), channel_id=1, source_target_pairs={{0,1},{1,0},{2,3},{3,2},{4,5},{5,4},{6,7},{7,6},{8,9},{9,8},{10,11... | collective-permute-start | bytes 3145736 | tf_op jit(solution)/shard_map/ppermute | solution.py:23
  132.6 14.8 %collective-permute-start.19 = (bf16[512,1024]{1,0:T(8,128)(2,1)S(1)}, bf16[512,1024]{1,0:T(8,128)(2,1)S(1)}, u32[]{:S(2)}, u32[]{:S(2)}) collective-permute-start(bf16[512,1024]{1,0:T(8,128)(2,1)S(1)} %pad_maximum_fusion.10), channel_id=1, source_target_pairs={{0,1},{1,0},{2,3},{3,2},{4,5},{5,4},{6,7},{7,6},{8,9},{9,8},{10,11... | collective-permute-start | bytes 3145736 | tf_op jit(solution)/shard_map/ppermute | solution.py:23
  179.9 12.6 %collective-permute-start.25 = (bf16[512,2816]{1,0:T(8,128)(2,1)}, bf16[512,2816]{1,0:T(8,128)(2,1)}, u32[]{:S(2)}, u32[]{:S(2)}) collective-permute-start(bf16[512,2816]{1,0:T(8,128)(2,1)} %get-tuple-element.162), channel_id=1, source_target_pairs={{0,1},{1,0},{2,3},{3,2},{4,5},{5,4},{6,7},{7,6},{8,9},{9,8},{10,11... | collective-permute-start | bytes 8650760 | tf_op jit(solution)/shard_map/ppermute | solution.py:23
  180.1 122.6 %reduce-scatter.6.cloned.1.call-start = ((), (), s32[]{:S(2)}) async-start(), calls=%async_computation.7 | async-start | bytes 9191424 | tf_op jit(solution)/shard_map/reduce_scatter | solution.py:611
  180.1 8.6 %collective-permute-start.26 = (bf16[512,1408]{1,0:T(8,128)(2,1)}, bf16[512,1408]{1,0:T(8,128)(2,1)S(1)}, u32[]{:S(2)}, u32[]{:S(2)}) collective-permute-start(bf16[512,1408]{1,0:T(8,128)(2,1)} %copy-done.12), channel_id=1, source_target_pairs={{0,1},{1,0},{2,3},{3,2},{4,5},{5,4},{6,7},{7,6},{8,9},{9,8},{10,11... | collective-permute-start | bytes 4325384 | tf_op jit(solution)/shard_map/ppermute | solution.py:23
  182.5 9.9 %collective-permute-start.24 = (bf16[512,1024]{1,0:T(8,128)(2,1)S(1)}, bf16[512,1024]{1,0:T(8,128)(2,1)S(1)}, u32[]{:S(2)}, u32[]{:S(2)}) collective-permute-start(bf16[512,1024]{1,0:T(8,128)(2,1)S(1)} %pad_maximum_fusion.12), channel_id=1, source_target_pairs={{0,1},{1,0},{2,3},{3,2},{4,5},{5,4},{6,7},{7,6},{8,9},{9,8},{10,11... | collective-permute-start | bytes 3145736 | tf_op jit(solution)/shard_map/ppermute | solution.py:23
  209.7 146.2 %reduce-scatter.8.cloned.1.call-start = ((), (), s32[]{:S(2)}) async-start(), calls=%async_computation.8 | async-start | bytes 2621440 | tf_op jit(solution)/shard_map/reduce_scatter | solution.py:71
  212.3 15.0 %collective-permute-start.29 = (bf16[128,2048]{1,0:T(8,128)(2,1)}, bf16[128,2048]{1,0:T(8,128)(2,1)S(1)}, u32[]{:S(2)}, u32[]{:S(2)}) collective-permute-start(bf16[128,2048]{1,0:T(8,128)(2,1)} %get-tuple-element.192.b0), channel_id=1, source_target_pairs={{0,4},{4,0},{8,12},{12,8},{1,5},{5,1},{9,13},{13,9},{2,6},{6,2},{1... | collective-permute-start | bytes 1572872 | tf_op jit(solution)/shard_map/ppermute | solution.py:23
  212.6 25.3 %collective-permute-start.30 = (bf16[128,2048]{1,0:T(8,128)(2,1)}, bf16[128,2048]{1,0:T(8,128)(2,1)S(1)}, u32[]{:S(2)}, u32[]{:S(2)}) collective-permute-start(bf16[128,2048]{1,0:T(8,128)(2,1)} %get-tuple-element.192.b0), channel_id=1, source_target_pairs={{0,8},{4,12},{8,0},{12,4},{1,9},{5,13},{9,1},{13,5},{2,10},{6,14},... | collective-permute-start | bytes 1572872 | tf_op jit(solution)/shard_map/ppermute | solution.py:23
  214.7 25.8 %collective-permute-start.31 = (bf16[128,2048]{1,0:T(8,128)(2,1)}, bf16[128,2048]{1,0:T(8,128)(2,1)S(1)}, u32[]{:S(2)}, u32[]{:S(2)}) collective-permute-start(bf16[128,2048]{1,0:T(8,128)(2,1)} %get-tuple-element.192.b0), channel_id=1, source_target_pairs={{0,12},{4,8},{8,4},{12,0},{1,13},{5,9},{9,5},{13,1},{2,14},{6,10},... | collective-permute-start | bytes 1572872 | tf_op jit(solution)/shard_map/ppermute | solution.py:23
  240.5 12.2 %collective-permute-start.32 = (bf16[128,2048]{1,0:T(8,128)(2,1)S(1)}, bf16[128,2048]{1,0:T(8,128)(2,1)S(1)}, u32[]{:S(2)}, u32[]{:S(2)}) collective-permute-start(bf16[128,2048]{1,0:T(8,128)(2,1)S(1)} %get-tuple-element.178), channel_id=1, source_target_pairs={{0,4},{4,0},{8,12},{12,8},{1,5},{5,1},{9,13},{13,9},{2,6},{6,2},{1... | collective-permute-start | bytes 1572872 | tf_op jit(solution)/shard_map/ppermute | solution.py:23
  240.5 13.5 %collective-permute-start.33 = (bf16[128,2048]{1,0:T(8,128)(2,1)S(1)}, bf16[128,2048]{1,0:T(8,128)(2,1)S(1)}, u32[]{:S(2)}, u32[]{:S(2)}) collective-permute-start(bf16[128,2048]{1,0:T(8,128)(2,1)S(1)} %get-tuple-element.179), channel_id=1, source_target_pairs={{0,12},{4,8},{8,4},{12,0},{1,13},{5,9},{9,5},{13,1},{2,14},{6,10},... | collective-permute-start | bytes 1572872 | tf_op jit(solution)/shard_map/ppermute | solution.py:23
  260.9 8.7 %collective-permute-start.35 = (bf16[128,512]{1,0:T(8,128)(2,1)S(1)}, bf16[128,512]{1,0:T(8,128)(2,1)S(1)}, u32[]{:S(2)}, u32[]{:S(2)}) collective-permute-start(bf16[128,512]{1,0:T(8,128)(2,1)S(1)} %get-tuple-element.185), channel_id=1, source_target_pairs={{0,2},{1,3},{2,0},{3,1},{4,6},{5,7},{6,4},{7,5},{8,10},{9,11},{10,... | collective-permute-start | bytes 393224 | tf_op jit(solution)/shard_map/ppermute | solution.py:23
  262.5 11.3 %collective-permute-start.36 = (bf16[128,512]{1,0:T(8,128)(2,1)S(1)}, bf16[128,512]{1,0:T(8,128)(2,1)S(1)}, u32[]{:S(2)}, u32[]{:S(2)}) collective-permute-start(bf16[128,512]{1,0:T(8,128)(2,1)S(1)} %get-tuple-element.186), channel_id=1, source_target_pairs={{0,3},{1,2},{2,1},{3,0},{4,7},{5,6},{6,5},{7,4},{8,11},{9,10},{10,... | collective-permute-start | bytes 393224 | tf_op jit(solution)/shard_map/ppermute | solution.py:23
  292.4 18.6 %collective-permute-start.39 = (bf16[2,128,1152]{2,1,0:T(8,128)(2,1)}, bf16[2,128,1152]{2,1,0:T(8,128)(2,1)S(1)}, u32[]{:S(2)}, u32[]{:S(2)}) collective-permute-start(bf16[2,128,1152]{2,1,0:T(8,128)(2,1)} %get-tuple-element.258), channel_id=1, source_target_pairs={{0,32},{32,0},{64,96},{96,64},{1,33},{33,1},{65,97},{97,65},{2,34}... | collective-permute-start | bytes 1769480 | tf_op jit(solution)/shard_map/ppermute | solution.py:23
  293.1 31.9 %collective-permute-start.40 = (bf16[2,128,1152]{2,1,0:T(8,128)(2,1)}, bf16[2,128,1152]{2,1,0:T(8,128)(2,1)}, u32[]{:S(2)}, u32[]{:S(2)}) collective-permute-start(bf16[2,128,1152]{2,1,0:T(8,128)(2,1)} %get-tuple-element.259), channel_id=1, source_target_pairs={{0,64},{32,96},{64,0},{96,32},{1,65},{33,97},{65,1},{97,33},{2,66}... | collective-permute-start | bytes 1769480 | tf_op jit(solution)/shard_map/ppermute | solution.py:23
  295.9 29.2 %collective-permute-start.41 = (bf16[2,128,1152]{2,1,0:T(8,128)(2,1)}, bf16[2,128,1152]{2,1,0:T(8,128)(2,1)}, u32[]{:S(2)}, u32[]{:S(2)}) collective-permute-start(bf16[2,128,1152]{2,1,0:T(8,128)(2,1)} %get-tuple-element.257), channel_id=1, source_target_pairs={{0,96},{32,64},{64,32},{96,0},{1,97},{33,65},{65,33},{97,1},{2,98}... | collective-permute-start | bytes 1769480 | tf_op jit(solution)/shard_map/ppermute | solution.py:23
  304.1 21.0 %collective-permute-start.27 = (f32[64,128]{1,0:T(8,128)S(1)}, f32[64,128]{1,0:T(8,128)S(1)}, u32[]{:S(2)}, u32[]{:S(2)}) collective-permute-start(f32[64,128]{1,0:T(8,128)S(1)} %broadcast_in_dim.20), channel_id=1, source_target_pairs={{0,4},{4,0},{8,12},{12,8},{1,5},{5,1},{9,13},{13,9},{2,6},{6,2},{1... | collective-permute-start | bytes 98312 | tf_op jit(solution)/shard_map/ppermute | solution.py:23
  305.7 114.4 %all-gather.11.cloned.1.call-start = ((), (), s32[]{:S(2)}) async-start(), calls=%async_computation.9 | async-start | bytes 5570560 | tf_op jit(solution)/shard_map/all_gather | solution.py:676
  333.7 10.2 %collective-permute-start.44 = (bf16[64,1152]{1,0:T(8,128)(2,1)S(1)}, bf16[64,1152]{1,0:T(8,128)(2,1)S(1)}, u32[]{:S(2)}, u32[]{:S(2)}) collective-permute-start(bf16[64,1152]{1,0:T(8,128)(2,1)S(1)} %get-tuple-element.315), channel_id=1, source_target_pairs={{0,16},{2,18},{16,0},{18,2},{1,17},{3,19},{17,1},{19,3},{4,20},{6,... | collective-permute-start | bytes 442376 | tf_op jit(solution)/shard_map/ppermute | solution.py:23
  335.9 18.6 %collective-permute-start.45 = (bf16[64,1152]{1,0:T(8,128)(2,1)S(1)}, bf16[64,1152]{1,0:T(8,128)(2,1)S(1)}, u32[]{:S(2)}, u32[]{:S(2)}) collective-permute-start(bf16[64,1152]{1,0:T(8,128)(2,1)S(1)} %get-tuple-element.314), channel_id=1, source_target_pairs={{0,18},{2,16},{16,2},{18,0},{1,19},{3,17},{17,3},{19,1},{4,22},{6,... | collective-permute-start | bytes 442376 | tf_op jit(solution)/shard_map/ppermute | solution.py:23
  336.5 18.2 %collective-permute-start.42 = (bf16[64,4352]{1,0:T(8,128)(2,1)S(1)}, bf16[64,4352]{1,0:T(8,128)(2,1)S(1)}, u32[]{:S(2)}, u32[]{:S(2)}) collective-permute-start(bf16[64,4352]{1,0:T(8,128)(2,1)S(1)} %pad_maximum_fusion.15), channel_id=1, source_target_pairs={{0,16},{2,18},{16,0},{18,2},{1,17},{3,19},{17,1},{19,3},{4,20},{6,... | collective-permute-start | bytes 1671176 | tf_op jit(solution)/shard_map/ppermute | solution.py:23
  361.9 15.7 %collective-permute-start.50 = (bf16[128,2048]{1,0:T(8,128)(2,1)S(1)}, bf16[128,2048]{1,0:T(8,128)(2,1)S(1)}, u32[]{:S(2)}, u32[]{:S(2)}) collective-permute-start(bf16[128,2048]{1,0:T(8,128)(2,1)S(1)} %copy-done.46), channel_id=1, source_target_pairs={{0,8},{4,12},{8,0},{12,4},{1,9},{5,13},{9,1},{13,5},{2,10},{6,14},... | collective-permute-start | bytes 1572872 | tf_op jit(solution)/shard_map/ppermute | solution.py:23
  380.2 16.2 %collective-permute-start.51 = (bf16[128,1152]{1,0:T(8,128)(2,1)S(1)}, bf16[128,1152]{1,0:T(8,128)(2,1)S(1)}, u32[]{:S(2)}, u32[]{:S(2)}) collective-permute-start(bf16[128,1152]{1,0:T(8,128)(2,1)S(1)} %pad_maximum_fusion.19), channel_id=1, source_target_pairs={{0,32},{32,0},{64,96},{96,64},{1,33},{33,1},{65,97},{97,65},{2,34}... | collective-permute-start | bytes 884744 | tf_op jit(solution)/shard_map/ppermute | solution.py:23
  380.4 28.7 %collective-permute-start.52 = (bf16[128,1152]{1,0:T(8,128)(2,1)S(1)}, bf16[128,1152]{1,0:T(8,128)(2,1)S(1)}, u32[]{:S(2)}, u32[]{:S(2)}) collective-permute-start(bf16[128,1152]{1,0:T(8,128)(2,1)S(1)} %pad_maximum_fusion.19), channel_id=1, source_target_pairs={{0,64},{32,96},{64,0},{96,32},{1,65},{33,97},{65,1},{97,33},{2,66}... | collective-permute-start | bytes 884744 | tf_op jit(solution)/shard_map/ppermute | solution.py:23
  382.5 26.6 %collective-permute-start.53 = (bf16[128,1152]{1,0:T(8,128)(2,1)S(1)}, bf16[128,1152]{1,0:T(8,128)(2,1)S(1)}, u32[]{:S(2)}, u32[]{:S(2)}) collective-permute-start(bf16[128,1152]{1,0:T(8,128)(2,1)S(1)} %pad_maximum_fusion.19), channel_id=1, source_target_pairs={{0,96},{32,64},{64,32},{96,0},{1,97},{33,65},{65,33},{97,1},{2,98}... | collective-permute-start | bytes 884744 | tf_op jit(solution)/shard_map/ppermute | solution.py:23
  410.6 8.6 %collective-permute-start.57 = (f32[1,512]{1,0:T(1,128)S(1)}, f32[1,512]{1,0:T(1,128)S(1)}, u32[]{:S(2)}, u32[]{:S(2)}) collective-permute-start(f32[1,512]{1,0:T(1,128)S(1)} %bitcast.80), channel_id=1, source_target_pairs={{0,4},{4,0},{8,12},{12,8},{1,5},{5,1},{9,13},{13,9},{2,6},{6,2},{1... | collective-permute-start | bytes 6152 | tf_op jit(solution)/shard_map/ppermute | solution.py:23
  (69 other events, 435.6 us)
Sparse Core Ops, SparseCore 0:
  22.5 31.3 all-gather.4
  70.0 46.3 all-gather.8
  127.6 30.5 all-gather.6
  180.2 29.4 reduce-scatter.3
  213.3 89.2 reduce-scatter.5
  305.8 29.9 reduce-scatter.7
  356.0 60.9 all-gather.10
